TPU v7x, 32 devices: a whole 2x2x4 slice. The times are simulated.
32 devices in a mesh: groups: 2 (over x), wide: 8 (over z, y), tp: 2 (over core).
Axes of the slice: x: 2, y: 2, z: 4, core: 2. Of those that a mesh axis runs over, the one named last changes fastest.
Arguments:
- normed_layer_input: bfloat16 [512, 8192], P(('groups', 'wide')), parts along dimension 0, may hold values from -6 to 6
- plain_query_rows: bfloat16 [512, 8192], P(('groups', 'wide'), 'tp'), parts along dimension 0, may hold values from -10 to 10
- plain_key_rows: bfloat16 [512, 1024], P(('groups', 'wide'), 'tp'), parts along dimension 0, may hold values from -6 to 6
- plain_value_rows: bfloat16 [512, 1024], P(('groups', 'wide'), 'tp'), parts along dimension 0, may hold values from -6 to 6
- cached_key_rows: bfloat16 [512, 8, 96, 128], P(('groups', 'wide'), 'tp'), parts along dimension 0, may hold values from -61 to 61
- cached_value_rows: bfloat16 [512, 8, 96, 128], P(('groups', 'wide'), 'tp'), parts along dimension 0, may hold values from -6 to 6
- live_cache_length: int32 [512], P(('groups', 'wide')), parts along dimension 0, may hold values from 2 to 96, as said below
- tenant: int32 [512], P('groups'), parts along dimension 0, may hold values from 0 to 7, as said below
- slot_of_adapter: int32 [16], P('groups'), parts along dimension 0, may hold values from 0 to 7, as said below
- stacked_down_weight: bfloat16 [8, 192, 8192], P('wide'), may hold values from -0.0625 to 0.0625
- query_up_weight: bfloat16 [8, 64, 8192], P('wide', None, 'tp'), may hold values from -0.75 to 0.75
- key_value_up_weight: bfloat16 [8, 2, 64, 1024], P('wide', None, None, 'tp'), may hold values from -0.75 to 0.75
- output_down_weight: bfloat16 [8, 64, 8192], P('wide', None, 'tp'), may hold values from -0.375 to 0.375
- output_up_weight: bfloat16 [8, 64, 8192], P('wide', None, 'tp'), may hold values from -0.75 to 0.75
Outputs:
- context: bfloat16 [512, 8192], P(('groups', 'wide'), 'tp'), parts along dimension 0
- adapter_output_term: bfloat16 [512, 8192], P(('groups', 'wide'), 'tp'), parts along dimension 0
There are 2 independent parts, one for each index of `groups`. A program takes and returns all parts, laid end to end along the dimension named above; an argument that names none is the same for every part. Nothing has to cross between parts.
Inputs may be any that keep to these rules, and one draw needn't show every extreme that they name: `tenant`: within each aligned block of 32 rows (the rows of one device along wide) no adapter is used by more than 8 rows, and one adapter is used by exactly 8 rows of every block. `slot_of_adapter`: A permutation; the slot of index s lies on the device of index s along wide. `live_cache_length`: every aligned block of 32 rows has a row with 96.
All inputs are finite; a program needn't handle non-finite values.
Results may differ from a plain program's by a relative error of at most 0.0095.
Values may be sent and summed in bfloat16 or wider, within the bound.
No kernel may reach another device: no remote copies, remote signals or barrier semaphores. Data moves between devices by JAX's collectives and lax.ppermute only.
A program may use at most 64 MiB of HBM per device.

v0:
```python
import jax
import jax.numpy as jnp
from jax import lax
from jax.sharding import PartitionSpec as P

ADAPTER_SCALE = 0.5


def rank_total(partial_value):
    return lax.psum(partial_value, "tp")


def from_owners(payload):
    return lax.all_to_all(payload, "wide", split_axis=0, concat_axis=0, tiled=True)


def shards(
    normed_layer_input,
    plain_query_rows,
    plain_key_rows,
    plain_value_rows,
    cached_key_rows,
    cached_value_rows,
    live_cache_length,
    tenant,
    slot_of_adapter,
    stacked_down_weight,
    query_up_weight,
    key_value_up_weight,
    output_down_weight,
    output_up_weight,
):
    wide_count = lax.axis_size("wide")
    wide_index = lax.axis_index("wide")
    row_count = normed_layer_input.shape[0]
    capacity = max(2, 2 * row_count // wide_count)
    number_of_slots = wide_count * capacity
    adapter_rank_width = query_up_weight.shape[1]
    tenant_here = lax.dynamic_slice_in_dim(tenant, wide_index * row_count, row_count)
    adapter_ids = jnp.arange(slot_of_adapter.shape[0], dtype=jnp.int32)
    matches = tenant_here[:, None] == adapter_ids[None, :]
    holder = jnp.sum(jnp.where(matches, slot_of_adapter[None, :], 0), axis=1)
    same_holder = holder[:, None] == holder[None, :]
    row_ids = jnp.arange(row_count, dtype=jnp.int32)
    earlier = row_ids[None, :] < row_ids[:, None]
    place_in = jnp.sum(same_holder & earlier, axis=1)
    destination = holder * capacity + place_in

    def pack_rows(rows_in):
        filled = (
            jnp.zeros((number_of_slots, rows_in.shape[1]), rows_in.dtype)
            .at[destination]
            .set(rows_in)
        )
        return filled.reshape(wide_count, capacity, rows_in.shape[1])

    down_panel = stacked_down_weight[0]
    received = lax.all_to_all(
        pack_rows(normed_layer_input), "wide", split_axis=0, concat_axis=0, tiled=True
    )
    item_count = received.shape[1]
    flattened_rows = received.reshape(wide_count * item_count, received.shape[2])
    shrink = lax.dot_general(
        flattened_rows, down_panel, (((1,), (1,)), ((), ())), preferred_element_type=jnp.float32
    )
    stacked_rank_rows = shrink.astype(jnp.bfloat16)
    query_correction = jnp.dot(
        stacked_rank_rows[:, :adapter_rank_width],
        query_up_weight[0],
        preferred_element_type=jnp.float32,
    ).astype(jnp.bfloat16)
    key_correction = jnp.dot(
        stacked_rank_rows[:, adapter_rank_width : 2 * adapter_rank_width],
        key_value_up_weight[0, 0],
        preferred_element_type=jnp.float32,
    ).astype(jnp.bfloat16)
    value_correction = jnp.dot(
        stacked_rank_rows[:, 2 * adapter_rank_width :],
        key_value_up_weight[0, 1],
        preferred_element_type=jnp.float32,
    ).astype(jnp.bfloat16)
    joined = jnp.concatenate([query_correction, key_correction, value_correction], axis=1)
    returned = from_owners(joined.reshape(wide_count, item_count, joined.shape[1]))
    local_terms = returned.reshape(number_of_slots, returned.shape[2])[destination]
    query_width = plain_query_rows.shape[1]
    key_value_width = plain_key_rows.shape[1]
    query_matrix = (
        plain_query_rows.astype(jnp.float32)
        + ADAPTER_SCALE * local_terms[:, :query_width].astype(jnp.float32)
    ).astype(jnp.bfloat16)
    fresh_key = (
        plain_key_rows.astype(jnp.float32)
        + ADAPTER_SCALE
        * local_terms[:, query_width : query_width + key_value_width].astype(jnp.float32)
    ).astype(jnp.bfloat16)
    fresh_value = (
        plain_value_rows.astype(jnp.float32)
        + ADAPTER_SCALE * local_terms[:, query_width + key_value_width :].astype(jnp.float32)
    ).astype(jnp.bfloat16)
    kv_heads = cached_key_rows.shape[1]
    cache_size = cached_key_rows.shape[2]
    head_dim = cached_key_rows.shape[3]
    group_size = query_width // head_dim // kv_heads
    inverse_root = head_dim ** (-0.5)
    grouped = query_matrix.reshape(row_count, kv_heads, group_size, head_dim)
    cache_scores = (
        jnp.einsum("rgqd,rgcd->rgqc", grouped, cached_key_rows, preferred_element_type=jnp.float32)
        * inverse_root
    )
    own_scores = (
        jnp.einsum(
            "rgqd,rgd->rgq",
            grouped,
            fresh_key.reshape(row_count, kv_heads, head_dim),
            preferred_element_type=jnp.float32,
        )
        * inverse_root
    )
    valid_cache = jnp.arange(cache_size, dtype=jnp.int32)[None, :] < live_cache_length[:, None]
    cache_scores = jnp.where(valid_cache[:, None, None, :], cache_scores, -jnp.inf)
    highest = jnp.maximum(jnp.max(cache_scores, axis=-1), own_scores)
    cache_exp = jnp.exp(cache_scores - highest[..., None])
    own_exp = jnp.exp(own_scores - highest)
    denominator = jnp.sum(cache_exp, axis=-1) + own_exp
    cache_weight = (cache_exp / denominator[..., None]).astype(jnp.bfloat16)
    own_weight = (own_exp / denominator).astype(jnp.bfloat16)
    attended = jnp.einsum(
        "rgqc,rgcd->rgqd", cache_weight, cached_value_rows, preferred_element_type=jnp.float32
    )
    attended = attended + own_weight.astype(jnp.float32)[..., None] * fresh_value.reshape(
        row_count, kv_heads, 1, head_dim
    ).astype(jnp.float32)
    context = attended.reshape(row_count, query_width).astype(jnp.bfloat16)
    received = lax.all_to_all(pack_rows(context), "wide", split_axis=0, concat_axis=0, tiled=True)
    item_count = received.shape[1]
    flattened_rows = received.reshape(wide_count * item_count, received.shape[2])
    partial_value = lax.dot_general(
        flattened_rows,
        output_down_weight[0],
        (((1,), (1,)), ((), ())),
        preferred_element_type=jnp.float32,
    )
    output_rank_rows = rank_total(partial_value).astype(jnp.bfloat16)
    correction_term = (
        ADAPTER_SCALE
        * jnp.dot(output_rank_rows, output_up_weight[0], preferred_element_type=jnp.float32)
    ).astype(jnp.bfloat16)
    gathered_terms = from_owners(
        correction_term.reshape(wide_count, item_count, correction_term.shape[1])
    )
    adapter_output_term = gathered_terms.reshape(number_of_slots, gathered_terms.shape[2])[
        destination
    ]
    return (context, adapter_output_term)


def solution(mesh):
    return jax.shard_map(
        shards,
        mesh=mesh,
        in_specs=(
            P(("groups", "wide"), None),
            P(("groups", "wide"), "tp"),
            P(("groups", "wide"), "tp"),
            P(("groups", "wide"), "tp"),
            P(("groups", "wide"), "tp", None, None),
            P(("groups", "wide"), "tp", None, None),
            P(("groups", "wide")),
            P("groups"),
            P("groups"),
            P("wide", None, None),
            P("wide", None, "tp"),
            P("wide", None, None, "tp"),
            P("wide", None, "tp"),
            P("wide", None, "tp"),
        ),
        out_specs=(P(("groups", "wide"), "tp"), P(("groups", "wide"), "tp")),
        check_vma=False,
    )
```

profile of v0, /device:TPU:0, one launch (start us, length us, event | category | flops | bytes accessed | tf_op | source)
XLA Modules:
  0.0 128.6 jit_solution(7357441880044600530)
XLA Ops:
  0.6 0.0 copy-start
  0.6 0.9 dynamic_slice.3
  1.6 0.8 select_reduce_fusion
  2.3 0.2 convert_reduce_fusion
  2.5 2.9 %scatter_custom_fusion = bf16[64,8192]{1,0:T(8,128)(2,1)} fusion(s32[32]{0:T(128)S(1)} %fusion.35, bf16[32,8192]{1,0:T(8,128)(2,1)} %param.14, bf16[]{:T(256)} %constant.12.clone.1), kind=kCustom, calls=%fused_computation.27 | custom fusion | bytes 1049088 | tf_op jit(solution)/shard_map/scatter | solution.py:53
  5.4 0.0 copy-start.3
  5.4 0.0 copy-start.2
  5.4 33.2 %all_to_all.20 = bf16[8,8,8192]{2,1,0:T(8,128)(2,1)S(1)} all-to-all(bf16[8,8,8192]{2,1,0:T(8,128)(2,1)} %bitcast.56), channel_id=1, replica_groups=mesh['groups'=2,'wide'=8,'tp'=2] {'wide'}, dimensions={0} | all-to-all | bytes 2097152 | tf_op jit(solution)/shard_map/all_to_all | solution.py:58
  38.6 0.0 copy-start.4
  38.6 3.0 %fusion.6 = bf16[64,192]{1,0:T(8,128)(2,1)S(1)} fusion(bf16[1,192,8192]{2,1,0:T(8,128)(2,1)} %param.23, bf16[8,8,8192]{2,1,0:T(8,128)(2,1)S(1)} %all_to_all.20), kind=kOutput, calls=%fused_computation.16 | convolution fusion | flops 201338880 | bytes 4218880 | tf_op jit(solution)/shard_map/dot_general | solution.py:63
  41.6 0.0 copy-done.3
  41.7 0.1 convolution_convert_fusion.1
  41.8 0.2 convolution_convert_fusion.2
  42.0 0.0 copy-done.2
  42.0 0.3 convolution_convert_fusion
  42.3 0.9 maximum_bitcast_fusion
  43.2 4.2 %all-to-all-start.1 = ((bf16[8,8,5120]{2,1,0:T(8,128)(2,1)}), bf16[8,8,5120]{2,1,0:T(8,128)(2,1)}, u32[]{:S(2)}, u32[]{:S(2)}) async-start(bf16[8,8,5120]{2,1,0:T(8,128)(2,1)} %maximum_bitcast_fusion), calls=%async_computation.1 | async-start | bytes 1310720 | tf_op jit(solution)/shard_map/all_to_all | solution.py:14
  47.4 0.0 copy-done.4
  47.4 0.1 iota_compare_fusion.1
  47.5 16.4 %all-to-all-done.1 = bf16[8,8,5120]{2,1,0:T(8,128)(2,1)} async-done(((bf16[8,8,5120]{2,1,0:T(8,128)(2,1)}), bf16[8,8,5120]{2,1,0:T(8,128)(2,1)}, u32[]{:S(2)}, u32[]{:S(2)}) %all-to-all-start.1) | async-done | bytes 655392 | tf_op jit(solution)/shard_map/all_to_all | solution.py:14
  63.9 2.2 %gather_fusion = bf16[32,5120]{1,0:T(8,128)(2,1)S(1)} fusion(bf16[64,5120]{1,0:T(8,128)(2,1)} %bitcast.9, s32[1024]{0:T(1024)S(1)} %pad_clamp_fusion), kind=kCustom, calls=%fused_computation | custom fusion | bytes 655488 | tf_op jit(solution)/shard_map/gather | solution.py:84
  66.1 1.0 fusion.18
  67.2 0.7 copy.18
  67.9 1.4 %add_convert_fusion.2 = (bf16[32,512]{1,0:T(8,128)(2,1)}, f32[32,512]{1,0:T(8,128)S(1)}) fusion(bf16[32,512]{1,0:T(8,128)(2,1)} %param.16, bf16[32,5120]{1,0:T(8,128)(2,1)S(1)} %gather_fusion, bf16[32,512]{1,0:T(8,128)(2,1)} %param.17), kind=kLoop, calls=%fused_computation.40 | loop fusion | flops 180224 | bytes 229376 | tf_op jit(solution)/shard_map/convert_element_type | solution.py:95
  69.3 0.8 reshape.142
  70.1 1.2 fusion.37
  71.3 3.8 %fusion.36 = (f32[32,4,8]{2,1,0:T(4,128)S(1)}, f32[32,4,8,96]{3,2,1,0:T(8,128)S(1)}) fusion(bf16[32,4,8,128]{3,2,1,0:T(8,128)(2,1)} %bitcast.59, bf16[32,4,96,128]{3,2,1,0:T(8,128)(2,1)} %param.18, pred[32,96]{1,0:T(8,128)(4,1)S(1)} %iota_compare_fusion.1), kind=kOutput, calls=%fused_computation.61 | convolution fusion | flops 25459712 | bytes 3808256 | tf_op jit(solution)/shard_map/rgqd,rgcd->rgqc/dot_general | solution.py:107
  75.2 0.0 copy-start.1
  75.2 0.7 copy-done.1
  76.0 0.4 fusion.17
  76.4 0.7 fusion.34
  77.1 0.7 reshape.106
  77.7 0.0 copy-done
  77.7 2.1 %fusion.5 = bf16[32,4,8,128]{3,2,1,0:T(8,128)(2,1)S(1)} fusion(bf16[32,4,96,128]{3,2,1,0:T(8,128)(2,1)S(1)} %copy-done, f32[32,4,8,96]{3,2,1,0:T(8,128)} %copy-done.1, f32[32,4,128]{2,1,0:T(4,128)} %reshape.106, f32[32,4,8]{2,1,0:T(4,128)} %get-tuple-element.5, f32[32,4,8]{2,1,0:T(4,128)} %get-tuple-element.4, f32[32,4,8]{2,1,0:T(4,128)S(1)} %multiply_maximum_fusion), kind=kOutput, calls=%fused_computation.13 | convolution fusion | flops 25853952 | bytes 3878912 | tf_op jit(solution)/shard_map/rgqc,rgcd->rgqd/dot_general | solution.py:127
  79.8 1.8 %scatter_custom_fusion.1 = bf16[64,4096]{1,0:T(8,128)(2,1)} fusion(s32[32]{0:T(128)S(1)} %fusion.35, bf16[]{:T(256)} %constant.12.clone.1, bf16[4,8,32,128]{3,2,1,0:T(8,128)(2,1)S(1)} %bitcast.60), kind=kCustom, calls=%fused_computation.32 | custom fusion | bytes 786434 | tf_op jit(solution)/shard_map/scatter | solution.py:53
  81.6 17.9 %all_to_all.21 = bf16[8,8,4096]{2,1,0:T(8,128)(2,1)S(1)} all-to-all(bf16[8,8,4096]{2,1,0:T(8,128)(2,1)} %bitcast.57), channel_id=1, replica_groups=mesh['groups'=2,'wide'=8,'tp'=2] {'wide'}, dimensions={0} | all-to-all | bytes 1048576 | tf_op jit(solution)/shard_map/all_to_all | solution.py:134
  99.5 1.4 %fusion.11 = f32[64,64]{1,0:T(8,128)S(1)} fusion(bf16[1,64,4096]{2,1,0:T(8,128)(2,1)} %param.26, bf16[8,8,4096]{2,1,0:T(8,128)(2,1)S(1)} %all_to_all.21), kind=kOutput, calls=%fused_computation.20 | convolution fusion | flops 33554432 | bytes 1064960 | tf_op jit(solution)/shard_map/dot_general | solution.py:137
  100.9 3.4 %psum.7 = bf16[64,64]{1,0:T(8,128)(2,1)S(1)} all-reduce(f32[64,64]{1,0:T(8,128)S(1)} %fusion.11), channel_id=1, replica_groups=mesh['groups'=2,'wide'=8,'tp'=2] {'tp'}, use_global_device_ids=true, to_apply=%region_6.7 | all-reduce | flops 4096 | bytes 24576 | tf_op jit(solution)/shard_map/psum | solution.py:10
  104.3 2.1 %fusion.1 = bf16[8,8,4096]{2,1,0:T(8,128)(2,1)} fusion(bf16[1,64,4096]{2,1,0:T(8,128)(2,1)} %param.27, bf16[64,64]{1,0:T(8,128)(2,1)S(1)} %psum.7), kind=kOutput, calls=%fused_computation.7 | convolution fusion | flops 34078720 | bytes 1056768 | tf_op jit(solution)/shard_map/dot_general | solution.py:146
  106.4 4.1 %all-to-all-start.3 = ((bf16[8,8,4096]{2,1,0:T(8,128)(2,1)}), bf16[8,8,4096]{2,1,0:T(8,128)(2,1)}, u32[]{:S(2)}, u32[]{:S(2)}) async-start(bf16[8,8,4096]{2,1,0:T(8,128)(2,1)} %fusion.1), calls=%async_computation.3 | async-start | bytes 1048576 | tf_op jit(solution)/shard_map/all_to_all | solution.py:14
  110.6 0.8 copy.22
  111.4 14.5 %all-to-all-done.3 = bf16[8,8,4096]{2,1,0:T(8,128)(2,1)} async-done(((bf16[8,8,4096]{2,1,0:T(8,128)(2,1)}), bf16[8,8,4096]{2,1,0:T(8,128)(2,1)}, u32[]{:S(2)}, u32[]{:S(2)}) %all-to-all-start.3) | async-done | bytes 524320 | tf_op jit(solution)/shard_map/all_to_all | solution.py:14
  125.8 2.8 %gather_fusion.1 = bf16[32,4096]{1,0:T(8,128)(2,1)} fusion(bf16[64,4096]{1,0:T(8,128)(2,1)} %bitcast.17, s32[1024]{0:T(1024)S(1)} %pad_clamp_fusion), kind=kCustom, calls=%fused_computation.1 | custom fusion | bytes 524416 | tf_op jit(solution)/shard_map/gather | solution.py:151
  (3 shorter events, 0.0 us)
Async XLA Ops:
  0.6 77.1 %copy-start = (bf16[32,4,96,128]{3,2,1,0:T(8,128)(2,1)S(1)}, bf16[32,4,96,128]{3,2,1,0:T(8,128)(2,1)}, u32[]{:S(2)}) copy-start(bf16[32,4,96,128]{3,2,1,0:T(8,128)(2,1)} %param.19) | copy-start | bytes 9437188
  5.4 36.2 %copy-start.3 = (bf16[1,2,64,512]{3,2,1,0:T(8,128)(2,1)S(1)}, bf16[1,2,64,512]{3,2,1,0:T(8,128)(2,1)}, u32[]{:S(2)}) copy-start(bf16[1,2,64,512]{3,2,1,0:T(8,128)(2,1)} %param.25) | copy-start | bytes 393220
  5.4 36.6 %copy-start.2 = (bf16[1,64,4096]{2,1,0:T(8,128)(2,1)S(1)}, bf16[1,64,4096]{2,1,0:T(8,128)(2,1)}, u32[]{:S(2)}) copy-start(bf16[1,64,4096]{2,1,0:T(8,128)(2,1)} %param.24) | copy-start | bytes 1572868
  38.6 8.8 %copy-start.4 = (s32[32]{0:T(128)S(1)}, s32[32]{0:T(128)}, u32[]{:S(2)}) copy-start(s32[32]{0:T(128)} %param.20) | copy-start | bytes 388
  43.2 20.7 %all-to-all-start.1 = ((bf16[8,8,5120]{2,1,0:T(8,128)(2,1)}), bf16[8,8,5120]{2,1,0:T(8,128)(2,1)}, u32[]{:S(2)}, u32[]{:S(2)}) async-start(bf16[8,8,5120]{2,1,0:T(8,128)(2,1)} %maximum_bitcast_fusion), calls=%async_computation.1 | async-start | bytes 1310720 | tf_op jit(solution)/shard_map/all_to_all | solution.py:14
  75.2 0.8 copy-start.1
  106.4 19.4 %all-to-all-start.3 = ((bf16[8,8,4096]{2,1,0:T(8,128)(2,1)}), bf16[8,8,4096]{2,1,0:T(8,128)(2,1)}, u32[]{:S(2)}, u32[]{:S(2)}) async-start(bf16[8,8,4096]{2,1,0:T(8,128)(2,1)} %fusion.1), calls=%async_computation.3 | async-start | bytes 1048576 | tf_op jit(solution)/shard_map/all_to_all | solution.py:14
where the time goes:
time: 130 us; the launch traced here: 129 us
  blocking collectives  54.4 us (42%)
  waiting for transfers between devices  30.9 us (24%)
  local copies, waits for them, and re-layouts  14.4 us (11%)
  matrix products  14.3 us (11%)
  starting transfers between devices  8.33 us (6%)
  other arithmetic  5.55 us (4%)
    all_to_all x1, blocking collectives, shards(): lax.all_to_all(pack_rows(normed_layer_input), 'wide', split_axis=0, conca...  33.2 us
    all_to_all x2, waiting for transfers between devices, from_owners(): lax.all_to_all(payload, 'wide', split_axis=0, concat_axis=0, tiled=True)  30.9 us
    all_to_all x1, blocking collectives, shards(): lax.all_to_all(pack_rows(context), 'wide', split_axis=0, concat_axis=0, t...  17.9 us
    all_to_all x2, starting transfers between devices, from_owners(): lax.all_to_all(payload, 'wide', split_axis=0, concat_axis=0, tiled=True)  8.33 us
    scatter x2, local copies, waits for them, and re-layouts, pack_rows(): filled = jnp.zeros((number_of_slots, rows_in.shape[1]), rows_in.dtype).at...  4.75 us
    dot_general x1, matrix products, shards(): jnp.einsum('rgqd,rgcd->rgqc', grouped, cached_key_rows, preferred_element...  3.82 us
    psum x1, blocking collectives, rank_total(): return lax.psum(partial_value, 'tp')  3.41 us
    dot_general x1, matrix products, shards(): lax.dot_general(flattened_rows, down_panel, (((1,), (1,)), ((), ())), pre...  3.02 us
  transfers between devices with their start and end apart: 2, of which 2 were waited for; matrix products, arithmetic and copies ran while one was open for 1% of the time, Pallas kernels for 0%

commit v1 on v0

v1 whole, which is shorter than its diff:
```python
import functools

import jax
import jax.numpy as jnp
from jax import lax
from jax.experimental import pallas as pl
from jax.experimental.pallas import tpu as pltpu
from jax.sharding import PartitionSpec as P

ADAPTER_SCALE = 0.5
CHUNKS = 2
F32 = jnp.float32
BF16 = jnp.bfloat16
VMEM = pl.BlockSpec(memory_space=pltpu.VMEM)
SMEM = pl.BlockSpec(memory_space=pltpu.SMEM)


def call(body, out_shape, in_specs, out_specs=None, scratch=(), flops=0, moved=0, limit=24):
    return pl.pallas_call(
        body,
        out_shape=out_shape,
        in_specs=in_specs,
        out_specs=jax.tree.map(lambda _: VMEM, out_shape) if out_specs is None else out_specs,
        scratch_shapes=scratch,
        cost_estimate=pl.CostEstimate(flops=flops, bytes_accessed=moved, transcendentals=0),
        compiler_params=pltpu.CompilerParams(vmem_limit_bytes=limit * 1024 * 1024),
    )


def iota(shape, dim):
    return lax.broadcasted_iota(jnp.int32, shape, dim)


def dot(a, b):
    return lax.dot_general(a, b, (((1,), (0,)), ((), ())), preferred_element_type=F32)


def dot_t(a, b):
    return lax.dot_general(a, b, (((1,), (1,)), ((), ())), preferred_element_type=F32)


def scalars_to_row(read, rows):
    lane = iota((1, rows), 1)
    row = jnp.zeros((1, rows), jnp.int32)
    for r in range(rows):
        row = jnp.where(lane == r, read(r), row)
    return row


def pack_body(capacity, tenant_ref, slot_ref, x_ref, dest_ref, packed_ref, count_ref):
    rows = x_ref.shape[0]
    slots, width = packed_ref.shape
    first = lax.axis_index("wide") * rows
    for d in range(slots // capacity):
        count_ref[d] = 0
    for r in range(rows):
        holder = slot_ref[tenant_ref[first + r]]
        place = count_ref[holder]
        count_ref[holder] = place + 1
        dest_ref[r] = holder * capacity + place
    dest = scalars_to_row(lambda r: dest_ref[r], rows)
    chosen = (iota((slots, rows), 0) == dest).astype(F32).astype(BF16)
    start = pl.multiple_of(lax.axis_index("tp") * width, width)
    packed_ref[...] = dot(chosen, x_ref[:, pl.ds(start, width)]).astype(BF16)


def prep_body(
    group, dest_ref, len_ref, pq_ref, pk_ref, pv_ref,
    pqt_ref, pkt_ref, pvt_ref, spread_ref, take_ref, place_ref, home_ref, bias_ref,
):
    rows, kv_width = pk_ref.shape
    head_dim = pqt_ref.shape[2]
    kv_heads = pqt_ref.shape[0]
    lines = rows * group
    slots = home_ref.shape[1]
    shift = group.bit_length() - 1
    dest_row = scalars_to_row(lambda r: dest_ref[r], rows)
    len_row = scalars_to_row(lambda r: len_ref[r], rows)
    mine = (iota((lines, rows), 0) >> shift) == iota((lines, rows), 1)
    dest_line = jnp.sum(jnp.where(mine, dest_row, 0), axis=1, keepdims=True)
    len_line = jnp.sum(jnp.where(mine, len_row, 0), axis=1, keepdims=True)
    head_line = iota((lines, 1), 0) & (group - 1)
    row_line = iota((lines, 1), 0) >> shift
    to_line = (iota((lines, group * rows), 1) == head_line * rows + row_line).astype(F32).astype(BF16)
    repeat = mine.astype(F32).astype(BF16)
    for g in range(kv_heads):
        stacked = jnp.concatenate(
            [pq_ref[:, (g * group + h) * head_dim : (g * group + h + 1) * head_dim] for h in range(group)], axis=0
        )
        pqt_ref[g] = dot(to_line, stacked).astype(BF16)
        pkt_ref[g] = dot(repeat, pk_ref[:, g * head_dim : (g + 1) * head_dim]).astype(BF16)
        pvt_ref[g] = dot(repeat, pv_ref[:, g * head_dim : (g + 1) * head_dim]).astype(BF16)
    spread_ref[...] = jnp.where(
        iota((lines, group * slots), 1) == head_line * slots + dest_line, ADAPTER_SCALE, 0.0
    ).astype(BF16)
    take_ref[...] = jnp.where(iota((lines, slots), 1) == dest_line, ADAPTER_SCALE, 0.0).astype(BF16)
    here = iota((rows, lines), 0) == (iota((rows, lines), 1) >> shift)
    eye = iota((rows, rows), 0) == iota((rows, rows), 1)
    dest_col = jnp.sum(jnp.where(eye, dest_row, 0), axis=1, keepdims=True)
    dest_lane = jnp.sum(jnp.where(here, dest_col, 0), axis=0, keepdims=True)
    head_lane = iota((1, lines), 1) & (group - 1)
    row_lane = iota((1, lines), 1) >> shift
    place_ref[: group * slots] = (
        (iota((group * slots, lines), 0) == head_lane * slots + dest_lane).astype(F32).astype(BF16)
    )
    place_ref[group * slots :] = (
        (iota((group * rows, lines), 0) == head_lane * rows + row_lane).astype(F32).astype(BF16)
    )
    home_ref[...] = (iota((rows, slots), 1) == dest_col).astype(F32).astype(BF16)
    bias_ref[...] = jnp.where(iota(bias_ref.shape, 1) < len_line, 0.0, -jnp.inf)


def up_body(group, mine_ref, other_ref, uq_ref, ukv_ref, *out_refs):
    rank = uq_ref.shape[1]
    total = (mine_ref[...] + other_ref[...]).astype(BF16)
    kv_width = ukv_ref.shape[3]
    width = kv_width // len(out_refs)
    q_width = width * group
    for c, out_ref in enumerate(out_refs):
        out_ref[:, :q_width] = dot(
            total[:, :rank], uq_ref[0, :, c * q_width : (c + 1) * q_width]
        ).astype(BF16)
        for i in range(2):
            out_ref[:, q_width + i * width : q_width + (i + 1) * width] = dot(
                total[:, (i + 1) * rank : (i + 2) * rank], ukv_ref[0, i, :, c * width : (c + 1) * width]
            ).astype(BF16)


def attend_body(
    first_head, heads, group, ret_ref, pqt_ref, pkt_ref, pvt_ref, k_ref, v_ref,
    spread_ref, take_ref, place_ref, bias_ref, packed_ref, context_ref,
):
    rows = context_ref.shape[0]
    slots = packed_ref.shape[0]
    head_dim = pqt_ref.shape[2]
    scale = head_dim ** (-0.5)
    spread, take, place = spread_ref[...], take_ref[...], place_ref[...]
    bias = bias_ref[...]
    k_base = heads * group * head_dim
    v_base = k_base + heads * head_dim
    for i in range(heads):
        g = first_head + i
        stacked = jnp.concatenate(
            [ret_ref[:, (i * group + h) * head_dim : (i * group + h + 1) * head_dim] for h in range(group)], axis=0
        )
        query = (pqt_ref[g].astype(F32) + dot(spread, stacked)).astype(BF16).astype(F32)
        new_key = (
            pkt_ref[g].astype(F32) + dot(take, ret_ref[:, k_base + i * head_dim : k_base + (i + 1) * head_dim])
        ).astype(BF16).astype(F32)
        new_value = (
            pvt_ref[g].astype(F32) + dot(take, ret_ref[:, v_base + i * head_dim : v_base + (i + 1) * head_dim])
        ).astype(BF16).astype(F32)
        own = jnp.sum(query * new_key, axis=1, keepdims=True) * scale
        score = jnp.concatenate(
            [dot_t(query[r * group : (r + 1) * group].astype(BF16), k_ref[r, g]) for r in range(rows)], axis=0
        )
        score = score * scale + bias
        highest = jnp.maximum(jnp.max(score, axis=1, keepdims=True), own)
        raised = jnp.exp(score - highest)
        own_raised = jnp.exp(own - highest)
        inverse = 1.0 / (jnp.sum(raised, axis=1, keepdims=True) + own_raised)
        weight = raised * inverse
        own_weight = (own_raised * inverse).astype(BF16).astype(F32)
        attended = jnp.concatenate(
            [dot(weight[r * group : (r + 1) * group].astype(BF16), v_ref[r, g]) for r in range(rows)], axis=0
        )
        context = (attended + own_weight * new_value).astype(BF16)
        laid = dot(place, context).astype(BF16)
        for h in range(group):
            columns = slice((i * group + h) * head_dim, (i * group + h + 1) * head_dim)
            packed_ref[:, columns] = laid[h * slots : (h + 1) * slots]
            base = group * slots + h * rows
            context_ref[:, columns] = laid[base : base + rows]


def output_up_body(mine_ref, other_ref, uo_ref, out_ref):
    total = (mine_ref[...] + other_ref[...]).astype(BF16)
    out_ref[...] = (ADAPTER_SCALE * dot(total, uo_ref[0])).astype(BF16)


def unpack_body(home_ref, ret_ref, out_ref):
    out_ref[...] = dot(home_ref[...], ret_ref[...]).astype(BF16)


def exchange(rows, wide_count):
    slots, width = rows.shape
    moved = lax.all_to_all(
        rows.reshape(wide_count, slots // wide_count, width), "wide", split_axis=0, concat_axis=0, tiled=True
    )
    return moved.reshape(slots, width)


def other_core(value):
    return lax.ppermute(value, "tp", [(0, 1), (1, 0)])


def shards(
    normed_layer_input,
    plain_query_rows,
    plain_key_rows,
    plain_value_rows,
    cached_key_rows,
    cached_value_rows,
    live_cache_length,
    tenant,
    slot_of_adapter,
    stacked_down_weight,
    query_up_weight,
    key_value_up_weight,
    output_down_weight,
    output_up_weight,
):
    wide_count = lax.axis_size("wide")
    rows, features = normed_layer_input.shape
    half = features // lax.axis_size("tp")
    capacity = max(2, 2 * rows // wide_count)
    slots = wide_count * capacity
    kv_heads, cache_size, head_dim = cached_key_rows.shape[1:]
    query_width = plain_query_rows.shape[1]
    group = query_width // head_dim // kv_heads
    lines = rows * group
    struct = jax.ShapeDtypeStruct

    dest, packed = call(
        functools.partial(pack_body, capacity),
        (struct((rows,), jnp.int32), struct((slots, half), BF16)),
        [SMEM, SMEM, VMEM],
        (SMEM, VMEM),
        scratch=[pltpu.SMEM((wide_count,), jnp.int32)],
        moved=4 * slots * half,
    )(tenant, slot_of_adapter, normed_layer_input)
    received = exchange(packed, wide_count)

    pqt, pkt, pvt, spread, take, place, home, bias = call(
        functools.partial(prep_body, group),
        (
            struct((kv_heads, lines, head_dim), BF16),
            struct((kv_heads, lines, head_dim), BF16),
            struct((kv_heads, lines, head_dim), BF16),
            struct((lines, group * slots), BF16),
            struct((lines, slots), BF16),
            struct((group * (slots + rows), lines), BF16),
            struct((rows, slots), BF16),
            struct((lines, cache_size), F32),
        ),
        [SMEM, SMEM, VMEM, VMEM, VMEM],
        moved=6000000,
    )(dest, live_cache_length, plain_query_rows, plain_key_rows, plain_value_rows)

    down_here = lax.dynamic_slice_in_dim(stacked_down_weight[0], lax.axis_index("tp") * half, half, axis=1)
    rank_part = dot_t(received, down_here)
    width = kv_heads // CHUNKS
    terms = call(
        functools.partial(up_body, group),
        tuple(struct((slots, width * (group + 2) * head_dim), BF16) for _ in range(CHUNKS)),
        [VMEM] * 4,
        moved=2000000,
    )(rank_part, other_core(rank_part), query_up_weight, key_value_up_weight)
    returned = [exchange(term, wide_count) for term in terms]
    contexts = []
    rank_o = None
    for c in range(CHUNKS):
        chunk_width = width * group * head_dim
        outgoing, context = call(
            functools.partial(attend_body, c * width, width, group),
            (struct((slots, chunk_width), BF16), struct((rows, chunk_width), BF16)),
            [VMEM] * 10,
            moved=8000000,
            limit=32,
        )(returned[c], pqt, pkt, pvt, cached_key_rows, cached_value_rows, spread, take, place, bias)
        contexts.append(context)
        arrived = exchange(outgoing, wide_count)
        part = dot_t(arrived, output_down_weight[0][:, c * chunk_width : (c + 1) * chunk_width])
        rank_o = part if rank_o is None else rank_o + part
    out_terms = call(
        output_up_body, struct((slots, query_width), BF16), [VMEM] * 3, moved=1200000
    )(rank_o, other_core(rank_o), output_up_weight)
    adapter_output_term = call(
        unpack_body, struct((rows, query_width), BF16), [VMEM] * 2, moved=1000000
    )(home, exchange(out_terms, wide_count))
    return jnp.concatenate(contexts, axis=1), adapter_output_term


def solution(mesh):
    return jax.shard_map(
        shards,
        mesh=mesh,
        in_specs=(
            P(("groups", "wide"), None),
            P(("groups", "wide"), "tp"),
            P(("groups", "wide"), "tp"),
            P(("groups", "wide"), "tp"),
            P(("groups", "wide"), "tp", None, None),
            P(("groups", "wide"), "tp", None, None),
            P(("groups", "wide")),
            P("groups"),
            P("groups"),
            P("wide", None, None),
            P("wide", None, "tp"),
            P("wide", None, None, "tp"),
            P("wide", None, "tp"),
            P("wide", None, "tp"),
        ),
        out_specs=(P(("groups", "wide"), "tp"), P(("groups", "wide"), "tp")),
        check_vma=False,
    )
```

time: 130 us -> 129 us (level)
  blocking collectives: 54.4 us -> 14.8 us
  starting transfers between devices: 8.33 us -> 27.7 us
  local copies, waits for them, and re-layouts: 14.4 us -> 29.6 us
  Pallas kernels: 0 us -> 11.4 us
  matrix products: 14.3 us -> 4.15 us
  waiting for transfers between devices: 30.9 us -> 38.4 us
  other arithmetic: 5.55 us -> 0.72 us
    all_to_all x2 -> x1, blocking collectives: 51 us -> 14.8 us  [exchange(): lax.all_to_all(rows.reshape(wide_count, slots // wide_count, width), 'wid...]
    unnamed x12 -> x72, local copies, waits for them, and re-layouts: 2.32 us -> 29.6 us
    all_to_all x2 -> x5, starting transfers between devices: 8.33 us -> 27.5 us  [exchange(): lax.all_to_all(rows.reshape(wide_count, slots // wide_count, width), 'wid...]
    pallas_call x0 -> x7, Pallas kernels: none -> 11.4 us  [the longest x2 5.66 us: shards(): call(functools.partial(attend_body, c * width, width, group), (struct((sl...]
    dot_general x9 -> x3, matrix products: 14.3 us -> 4.15 us  [dot_t(): lax.dot_general(a, b, (((1,), (1,)), ((), ())), preferred_element_type=F32)]
    all_to_all x2 -> x5, waiting for transfers between devices: 30.9 us -> 36 us  [exchange(): lax.all_to_all(rows.reshape(wide_count, slots // wide_count, width), 'wid...]
    gather x2 -> x0, local copies, waits for them, and re-layouts: 4.99 us -> none  [the longest x1 2.76 us: shards(): gathered_terms.reshape(number_of_slots, gathered_terms.shape[2])]
    scatter x2 -> x0, local copies, waits for them, and re-layouts: 4.75 us -> none  [pack_rows(): filled = jnp.zeros((number_of_slots, rows_in.shape[1]), rows_in.dtype).at...]
  transfers between devices with their start and end apart: 2 -> 7, of which waited for: 2 -> 5; matrix products, arithmetic and copies ran while one was open for 1% -> 2% of each run, Pallas kernels for 0% -> 5%
where the time goes in v1:
time: 129 us; the launch traced here: 128 us
  waiting for transfers between devices  38.4 us (30%)
  local copies, waits for them, and re-layouts  29.6 us (23%)
  starting transfers between devices  27.7 us (21%)
  blocking collectives  14.8 us (11%)
  Pallas kernels  11.4 us (9%)
  matrix products  4.15 us (3%)
    all_to_all x5, waiting for transfers between devices, exchange(): lax.all_to_all(rows.reshape(wide_count, slots // wide_count, width), 'wid...  36 us
    unnamed x72, local copies, waits for them, and re-layouts  29.6 us
    all_to_all x5, starting transfers between devices, exchange(): lax.all_to_all(rows.reshape(wide_count, slots // wide_count, width), 'wid...  27.5 us
    all_to_all x1, blocking collectives, exchange(): lax.all_to_all(rows.reshape(wide_count, slots // wide_count, width), 'wid...  14.8 us
    pallas_call x2, Pallas kernels, shards(): call(functools.partial(attend_body, c * width, width, group), (struct((sl...  5.66 us
    dot_general x3, matrix products, dot_t(): lax.dot_general(a, b, (((1,), (1,)), ((), ())), preferred_element_type=F32)  4.15 us
  transfers between devices with their start and end apart: 7, of which 5 were waited for; matrix products, arithmetic and copies ran while one was open for 2% of the time, Pallas kernels for 5%

profile of v1, /device:TPU:0, one launch (start us, length us, event | category | flops | bytes accessed | tf_op | source)
XLA Modules:
  0.0 127.6 jit_solution(457559221746790977)
XLA Ops:
  0.6 0.0 copy-start
  0.6 0.0 copy-start.17
  0.7 1.2 copy-done.17
  1.8 0.7 copy-done.33
  2.5 0.7 copy-done.34
  3.2 1.3 %shard_map.149 = (s32[32]{0:T(128)S(1)}, bf16[64,4096]{1,0:T(8,128)(2,1)S(1)}) custom-call(s32[256]{0:T(256)S(1)} %copy-done.33, s32[8]{0:T(128)S(1)} %copy-done.34, bf16[32,8192]{1,0:T(8,128)(2,1)S(1)} %copy-done.17), custom_call_target="tpu_custom_call" | custom-call | bytes 1048576 | tf_op jit(solution)/shard_map/pallas_call | solution.py:224
  4.5 0.0 copy-start.20
  4.5 0.8 copy-done.20
  5.3 7.3 %all-to-all-start = ((bf16[8,8,4096]{2,1,0:T(8,128)(2,1)}), bf16[8,8,4096]{2,1,0:T(8,128)(2,1)}, u32[]{:S(2)}, u32[]{:S(2)}) async-start(bf16[8,8,4096]{2,1,0:T(8,128)(2,1)} %bitcast.24), calls=%async_computation | async-start | bytes 1048576 | tf_op jit(solution)/shard_map/all_to_all | solution.py:187
  12.6 14.6 %all-to-all-done = bf16[8,8,4096]{2,1,0:T(8,128)(2,1)} async-done(((bf16[8,8,4096]{2,1,0:T(8,128)(2,1)}), bf16[8,8,4096]{2,1,0:T(8,128)(2,1)}, u32[]{:S(2)}, u32[]{:S(2)}) %all-to-all-start) | async-done | bytes 524320 | tf_op jit(solution)/shard_map/all_to_all | solution.py:187
  27.2 1.7 %fusion.mine_ref = f32[64,192]{1,0:T(8,128)S(1)} fusion(bf16[1,192,8192]{2,1,0:T(8,128)(2,1)S(1)} %copy-done, s32[]{:T(128)S(6)} %select_n.3, bf16[8,8,4096]{2,1,0:T(8,128)(2,1)} %all-to-all-done), kind=kOutput, calls=%fused_computation | convolution fusion | flops 100663296 | bytes 2146308 | tf_op jit(solution)/shard_map/dot_general | solution.py:39
  28.9 0.1 collective-permute-start
  28.9 1.2 collective-permute-done.other_ref
  30.2 1.0 copy-done.18
  31.2 1.1 shard_map.150
  32.3 14.8 %all_to_all.30 = bf16[8,8,2560]{2,1,0:T(8,128)(2,1)} all-to-all(bf16[8,8,2560]{2,1,0:T(8,128)(2,1)S(1)} %bitcast.25), channel_id=1, replica_groups=mesh['groups'=2,'wide'=8,'tp'=2] {'wide'}, dimensions={0} | all-to-all | bytes 655360 | tf_op jit(solution)/shard_map/all_to_all | solution.py:187
  47.1 4.1 %all-to-all-start.2 = ((bf16[8,8,2560]{2,1,0:T(8,128)(2,1)}), bf16[8,8,2560]{2,1,0:T(8,128)(2,1)}, u32[]{:S(2)}, u32[]{:S(2)}) async-start(bf16[8,8,2560]{2,1,0:T(8,128)(2,1)} %bitcast.5), calls=%async_computation.2 | async-start | bytes 655360 | tf_op jit(solution)/shard_map/all_to_all | solution.py:187
  51.1 0.0 copy-start.23
  51.2 0.9 copy-done.23
  52.1 0.8 copy-done.31
  52.9 0.8 copy-done.32
  53.6 1.1 shard_map.151
  54.7 0.0 copy-start.1
  54.7 1.9 %copy-done.1 = bf16[32,4,96,128]{3,2,1,0:T(8,128)(2,1)S(1)} copy-done((bf16[32,4,96,128]{3,2,1,0:T(8,128)(2,1)S(1)}, bf16[32,4,96,128]{3,2,1,0:T(8,128)(2,1)}, u32[]{:S(2)}) %copy-start.1) | copy-done | bytes 3145752
  56.6 1.9 %copy-done.3 = bf16[32,4,96,128]{3,2,1,0:T(8,128)(2,1)S(1)} copy-done((bf16[32,4,96,128]{3,2,1,0:T(8,128)(2,1)S(1)}, bf16[32,4,96,128]{3,2,1,0:T(8,128)(2,1)}, u32[]{:S(2)}) %copy-start.3) | copy-done | bytes 3145752
  58.5 1.0 copy-done.6
  59.5 2.3 %shard_map.152 = (bf16[64,2048]{1,0:T(8,128)(2,1)S(1)}, bf16[32,2048]{1,0:T(8,128)(2,1)S(1)}) custom-call(bf16[64,2560]{1,0:T(8,128)(2,1)S(1)} %bitcast.23, bf16[4,256,128]{2,1,0:T(8,128)(2,1)S(1)} %get-tuple-element.21.pqt_ref, bf16[4,256,128]{2,1,0:T(8,128)(2,1)S(1)} %get-tuple-element.22.pkt_ref, bf16[4,256,128]{2,1,0:T(8,128)(2,1)S(1)} %get-tuple-element.23.pvt_ref, ...), custom_call_target="tpu_custom_call" | custom-call | bytes 8000000 | tf_op jit(solution)/shard_map/pallas_call | solution.py:264
  61.8 0.0 copy-start.7
  61.8 0.7 copy-done.7
  62.5 0.7 copy-done.9
  63.2 0.7 copy-done.11
  64.0 0.7 copy-done.13
  64.7 0.6 copy-done.15
  65.3 0.6 copy-done.21
  66.0 0.7 copy-done.24
  66.7 0.6 copy-done.27
  67.3 0.0 all-to-all-done.2
  67.3 5.9 %all-to-all-start.3 = ((bf16[8,8,2048]{2,1,0:T(8,128)(2,1)}), bf16[8,8,2048]{2,1,0:T(8,128)(2,1)}, u32[]{:S(2)}, u32[]{:S(2)}) async-start(bf16[8,8,2048]{2,1,0:T(8,128)(2,1)} %bitcast.26), calls=%async_computation.3 | async-start | bytes 524288 | tf_op jit(solution)/shard_map/all_to_all | solution.py:187
  73.2 1.9 %copy-done.2 = bf16[32,4,96,128]{3,2,1,0:T(8,128)(2,1)S(1)} copy-done((bf16[32,4,96,128]{3,2,1,0:T(8,128)(2,1)S(1)}, bf16[32,4,96,128]{3,2,1,0:T(8,128)(2,1)}, u32[]{:S(2)}) %copy-start.2) | copy-done | bytes 3145752
  75.1 1.9 %copy-done.4 = bf16[32,4,96,128]{3,2,1,0:T(8,128)(2,1)S(1)} copy-done((bf16[32,4,96,128]{3,2,1,0:T(8,128)(2,1)S(1)}, bf16[32,4,96,128]{3,2,1,0:T(8,128)(2,1)}, u32[]{:S(2)}) %copy-start.4) | copy-done | bytes 3145752
  77.0 0.9 copy-done.8
  77.9 0.9 copy-done.10
  78.9 0.9 copy-done.12
  79.8 0.9 copy-done.14
  80.8 0.9 copy-done.16
  81.7 0.8 copy-done.22
  82.5 3.3 %shard_map.153 = (bf16[64,2048]{1,0:T(8,128)(2,1)S(1)}, bf16[32,2048]{1,0:T(8,128)(2,1)S(1)}) custom-call(bf16[64,2560]{1,0:T(8,128)(2,1)} %bitcast.6.ret_ref, bf16[4,256,128]{2,1,0:T(8,128)(2,1)S(1)} %copy-done.8, bf16[4,256,128]{2,1,0:T(8,128)(2,1)S(1)} %copy-done.10, bf16[4,256,128]{2,1,0:T(8,128)(2,1)S(1)} %copy-done.12, ...), custom_call_target="tpu_custom_call" | custom-call | bytes 8000000 | tf_op jit(solution)/shard_map/pallas_call | solution.py:264
  85.9 0.0 copy-start.25
  85.9 0.7 copy-done.25
  86.6 0.7 copy-done.29
  87.2 0.0 all-to-all-done.3
  87.2 6.1 %all-to-all-start.4 = ((bf16[8,8,2048]{2,1,0:T(8,128)(2,1)}), bf16[8,8,2048]{2,1,0:T(8,128)(2,1)}, u32[]{:S(2)}, u32[]{:S(2)}) async-start(bf16[8,8,2048]{2,1,0:T(8,128)(2,1)} %bitcast.27), calls=%async_computation.4 | async-start | bytes 524288 | tf_op jit(solution)/shard_map/all_to_all | solution.py:187
  93.4 1.2 fusion.5
  94.6 7.1 %all-to-all-done.4 = bf16[8,8,2048]{2,1,0:T(8,128)(2,1)} async-done(((bf16[8,8,2048]{2,1,0:T(8,128)(2,1)}), bf16[8,8,2048]{2,1,0:T(8,128)(2,1)}, u32[]{:S(2)}, u32[]{:S(2)}) %all-to-all-start.4) | async-done | bytes 262176 | tf_op jit(solution)/shard_map/all_to_all | solution.py:187
  101.7 1.2 convolution_add_fusion.mine_ref
  102.9 0.1 collective-permute-start.1
  103.0 1.2 collective-permute-done.1.other_ref
  104.2 1.0 copy-done.19
  105.3 0.3 shard_map.154
  105.6 0.8 copy-done.5
  106.4 4.2 %all-to-all-start.5 = ((bf16[8,8,4096]{2,1,0:T(8,128)(2,1)}), bf16[8,8,4096]{2,1,0:T(8,128)(2,1)}, u32[]{:S(2)}, u32[]{:S(2)}) async-start(bf16[8,8,4096]{2,1,0:T(8,128)(2,1)} %bitcast.22), calls=%async_computation.5 | async-start | bytes 1048576 | tf_op jit(solution)/shard_map/all_to_all | solution.py:187
  110.5 0.7 pad_maximum_fusion
  111.3 14.3 %all-to-all-done.5 = bf16[8,8,4096]{2,1,0:T(8,128)(2,1)} async-done(((bf16[8,8,4096]{2,1,0:T(8,128)(2,1)}), bf16[8,8,4096]{2,1,0:T(8,128)(2,1)}, u32[]{:S(2)}, u32[]{:S(2)}) %all-to-all-start.5) | async-done | bytes 524320 | tf_op jit(solution)/shard_map/all_to_all | solution.py:187
  125.6 2.0 %shard_map.155 = bf16[32,4096]{1,0:T(8,128)(2,1)} custom-call(bf16[32,64]{1,0:T(8,128)(2,1)S(1)} %get-tuple-element.31.home_ref, bf16[64,4096]{1,0:T(8,128)(2,1)} %bitcast.13.ret_ref), custom_call_target="tpu_custom_call" | custom-call | bytes 1000000 | tf_op jit(solution)/shard_map/pallas_call | solution.py:278
  (34 shorter events, 0.1 us)
Async XLA Ops:
  0.6 26.6 %copy-start = (bf16[1,192,8192]{2,1,0:T(8,128)(2,1)S(1)}, bf16[1,192,8192]{2,1,0:T(8,128)(2,1)}, u32[]{:S(2)}) copy-start(bf16[1,192,8192]{2,1,0:T(8,128)(2,1)} %param.23) | copy-start | bytes 9437188
  0.6 1.2 copy-start.17
  1.8 0.7 copy-start.33
  2.5 0.7 copy-start.34
  3.2 27.0 %copy-start.26 = (bf16[1,2,64,512]{3,2,1,0:T(8,128)(2,1)S(1)}, bf16[1,2,64,512]{3,2,1,0:T(8,128)(2,1)}, u32[]{:S(2)}) copy-start(bf16[1,2,64,512]{3,2,1,0:T(8,128)(2,1)} %ukv_ref.1) | copy-start | bytes 393220
  3.2 48.0 %copy-start.35 = (s32[32]{0:T(128)S(1)}, s32[32]{0:T(128)}, u32[]{:S(2)}) copy-start(s32[32]{0:T(128)} %len_ref.1) | copy-start | bytes 388
  4.5 0.8 copy-start.20
  5.3 21.9 %all-to-all-start = ((bf16[8,8,4096]{2,1,0:T(8,128)(2,1)}), bf16[8,8,4096]{2,1,0:T(8,128)(2,1)}, u32[]{:S(2)}, u32[]{:S(2)}) async-start(bf16[8,8,4096]{2,1,0:T(8,128)(2,1)} %bitcast.24), calls=%async_computation | async-start | bytes 1048576 | tf_op jit(solution)/shard_map/all_to_all | solution.py:187
  28.9 1.3 %collective-permute-start = (f32[64,192]{1,0:T(8,128)S(1)}, f32[64,192]{1,0:T(8,128)S(1)}, u32[]{:S(2)}, u32[]{:S(2)}) collective-permute-start(f32[64,192]{1,0:T(8,128)S(1)} %fusion.mine_ref), channel_id=1, source_target_pairs={{0,1},{1,0},{2,3},{3,2},{4,5},{5,4},{6,7},{7,6},{8,9},{9,8},{10,11... | collective-permute-start | bytes 147464 | tf_op jit(solution)/shard_map/ppermute | solution.py:194
  30.2 1.0 copy-start.18
  47.1 20.3 %all-to-all-start.2 = ((bf16[8,8,2560]{2,1,0:T(8,128)(2,1)}), bf16[8,8,2560]{2,1,0:T(8,128)(2,1)}, u32[]{:S(2)}, u32[]{:S(2)}) async-start(bf16[8,8,2560]{2,1,0:T(8,128)(2,1)} %bitcast.5), calls=%async_computation.2 | async-start | bytes 655360 | tf_op jit(solution)/shard_map/all_to_all | solution.py:187
  51.1 1.0 copy-start.23
  52.1 0.8 copy-start.31
  52.9 0.8 copy-start.32
  54.7 1.9 %copy-start.1 = (bf16[32,4,96,128]{3,2,1,0:T(8,128)(2,1)S(1)}, bf16[32,4,96,128]{3,2,1,0:T(8,128)(2,1)}, u32[]{:S(2)}) copy-start(bf16[32,4,96,128]{3,2,1,0:T(8,128)(2,1)} %k_ref.3) | copy-start | bytes 9437188
  56.6 1.9 %copy-start.3 = (bf16[32,4,96,128]{3,2,1,0:T(8,128)(2,1)S(1)}, bf16[32,4,96,128]{3,2,1,0:T(8,128)(2,1)}, u32[]{:S(2)}) copy-start(bf16[32,4,96,128]{3,2,1,0:T(8,128)(2,1)} %v_ref.3) | copy-start | bytes 9437188
  58.5 1.0 copy-start.6
  61.8 0.7 copy-start.7
  62.5 0.7 copy-start.9
  63.2 0.7 copy-start.11
  64.0 0.7 copy-start.13
  64.7 0.6 copy-start.15
  65.3 0.6 copy-start.21
  66.0 0.7 copy-start.24
  66.7 0.6 copy-start.27
  67.3 19.9 %all-to-all-start.3 = ((bf16[8,8,2048]{2,1,0:T(8,128)(2,1)}), bf16[8,8,2048]{2,1,0:T(8,128)(2,1)}, u32[]{:S(2)}, u32[]{:S(2)}) async-start(bf16[8,8,2048]{2,1,0:T(8,128)(2,1)} %bitcast.26), calls=%async_computation.3 | async-start | bytes 524288 | tf_op jit(solution)/shard_map/all_to_all | solution.py:187
  73.2 1.9 %copy-start.2 = (bf16[32,4,96,128]{3,2,1,0:T(8,128)(2,1)S(1)}, bf16[32,4,96,128]{3,2,1,0:T(8,128)(2,1)}, u32[]{:S(2)}) copy-start(bf16[32,4,96,128]{3,2,1,0:T(8,128)(2,1)} %k_ref.3) | copy-start | bytes 9437188
  75.1 1.9 %copy-start.4 = (bf16[32,4,96,128]{3,2,1,0:T(8,128)(2,1)S(1)}, bf16[32,4,96,128]{3,2,1,0:T(8,128)(2,1)}, u32[]{:S(2)}) copy-start(bf16[32,4,96,128]{3,2,1,0:T(8,128)(2,1)} %v_ref.3) | copy-start | bytes 9437188
  77.0 0.9 copy-start.8
  77.9 0.9 copy-start.10
  78.9 0.9 copy-start.12
  79.8 0.9 copy-start.14
  80.8 0.9 copy-start.16
  81.7 0.8 copy-start.22
  85.9 0.7 copy-start.25
  86.6 0.7 copy-start.29
  87.2 23.3 %copy-start.28 = (bf16[32,2048]{1,0:T(8,128)(2,1)S(1)}, bf16[32,2048]{1,0:T(8,128)(2,1)}, u32[]{:S(2)}) copy-start(bf16[32,2048]{1,0:T(8,128)(2,1)} %copy-done.27) | copy-start | bytes 393220
  87.2 23.3 %copy-start.30 = (bf16[32,2048]{1,0:T(8,128)(2,1)S(1)}, bf16[32,2048]{1,0:T(8,128)(2,1)}, u32[]{:S(2)}) copy-start(bf16[32,2048]{1,0:T(8,128)(2,1)} %copy-done.29) | copy-start | bytes 393220
  87.2 14.5 %all-to-all-start.4 = ((bf16[8,8,2048]{2,1,0:T(8,128)(2,1)}), bf16[8,8,2048]{2,1,0:T(8,128)(2,1)}, u32[]{:S(2)}, u32[]{:S(2)}) async-start(bf16[8,8,2048]{2,1,0:T(8,128)(2,1)} %bitcast.27), calls=%async_computation.4 | async-start | bytes 524288 | tf_op jit(solution)/shard_map/all_to_all | solution.py:187
  102.9 1.3 collective-permute-start.1
  104.2 1.0 copy-start.19
  105.5 0.8 copy-start.5
  106.4 19.2 %all-to-all-start.5 = ((bf16[8,8,4096]{2,1,0:T(8,128)(2,1)}), bf16[8,8,4096]{2,1,0:T(8,128)(2,1)}, u32[]{:S(2)}, u32[]{:S(2)}) async-start(bf16[8,8,4096]{2,1,0:T(8,128)(2,1)} %bitcast.22), calls=%async_computation.5 | async-start | bytes 1048576 | tf_op jit(solution)/shard_map/all_to_all | solution.py:187

commit v2 on v1

--- a/solution.py
+++ b/solution.py
@@ -8,14 +8,15 @@
 from jax.sharding import PartitionSpec as P
 
 ADAPTER_SCALE = 0.5
-CHUNKS = 2
 F32 = jnp.float32
 BF16 = jnp.bfloat16
 VMEM = pl.BlockSpec(memory_space=pltpu.VMEM)
 SMEM = pl.BlockSpec(memory_space=pltpu.SMEM)
-
-
-def call(body, out_shape, in_specs, out_specs=None, scratch=(), flops=0, moved=0, limit=24):
+HBM = pl.BlockSpec(memory_space=pltpu.HBM)
+DMA = pltpu.SemaphoreType.DMA
+
+
+def call(body, out_shape, in_specs, out_specs=None, scratch=(), flops=0, moved=0, limit=58):
     return pl.pallas_call(
         body,
         out_shape=out_shape,
@@ -47,28 +48,51 @@
     return row
 
 
-def pack_body(capacity, tenant_ref, slot_ref, x_ref, dest_ref, packed_ref, count_ref):
+def pack_body(
+    capacity, tenant_hbm, slot_hbm, x_hbm, dest_ref, packed_ref, tenant_ref, slot_ref, count_ref, x_ref, sems
+):
+    slots, width = packed_ref.shape
     rows = x_ref.shape[0]
-    slots, width = packed_ref.shape
-    first = lax.axis_index("wide") * rows
+    start = pl.multiple_of(lax.axis_index("tp") * width, width)
+    copies = [
+        pltpu.make_async_copy(tenant_hbm, tenant_ref, sems.at[0]),
+        pltpu.make_async_copy(slot_hbm, slot_ref, sems.at[1]),
+        pltpu.make_async_copy(x_hbm.at[:, pl.ds(start, width)], x_ref, sems.at[2]),
+    ]
+    for copy in copies:
+        copy.start()
     for d in range(slots // capacity):
         count_ref[d] = 0
+    copies[0].wait()
+    copies[1].wait()
+    first = lax.axis_index("wide") * rows
+    lane = iota((1, rows), 1)
+    dest = jnp.zeros((1, rows), jnp.int32)
     for r in range(rows):
         holder = slot_ref[tenant_ref[first + r]]
         place = count_ref[holder]
         count_ref[holder] = place + 1
-        dest_ref[r] = holder * capacity + place
-    dest = scalars_to_row(lambda r: dest_ref[r], rows)
+        slot = holder * capacity + place
+        dest_ref[r] = slot
+        dest = jnp.where(lane == r, slot, dest)
     chosen = (iota((slots, rows), 0) == dest).astype(F32).astype(BF16)
-    start = pl.multiple_of(lax.axis_index("tp") * width, width)
-    packed_ref[...] = dot(chosen, x_ref[:, pl.ds(start, width)]).astype(BF16)
+    copies[2].wait()
+    packed_ref[...] = dot(chosen, x_ref[...]).astype(BF16)
 
 
 def prep_body(
-    group, dest_ref, len_ref, pq_ref, pk_ref, pv_ref,
-    pqt_ref, pkt_ref, pvt_ref, spread_ref, take_ref, place_ref, home_ref, bias_ref,
+    group, dest_ref, len_ref, pq_hbm, pk_hbm, pv_hbm, *refs
 ):
-    rows, kv_width = pk_ref.shape
+    outs, refs = refs[:8], refs[8:]
+    pqt_ref, pkt_ref, pvt_ref, spread_ref, take_ref, place_ref, home_ref, bias_ref = refs[:8]
+    pq_ref, pk_ref, pv_ref, sems = refs[8:]
+    plain = [
+        pltpu.make_async_copy(source, target, sems.at[i])
+        for i, (source, target) in enumerate(((pq_hbm, pq_ref), (pk_hbm, pk_ref), (pv_hbm, pv_ref)))
+    ]
+    for copy in plain:
+        copy.start()
+    rows = pk_ref.shape[0]
     head_dim = pqt_ref.shape[2]
     kv_heads = pqt_ref.shape[0]
     lines = rows * group
@@ -83,6 +107,8 @@
     row_line = iota((lines, 1), 0) >> shift
     to_line = (iota((lines, group * rows), 1) == head_line * rows + row_line).astype(F32).astype(BF16)
     repeat = mine.astype(F32).astype(BF16)
+    for copy in plain:
+        copy.wait()
     for g in range(kv_heads):
         stacked = jnp.concatenate(
             [pq_ref[:, (g * group + h) * head_dim : (g * group + h + 1) * head_dim] for h in range(group)], axis=0
@@ -108,38 +134,59 @@
     )
     home_ref[...] = (iota((rows, slots), 1) == dest_col).astype(F32).astype(BF16)
     bias_ref[...] = jnp.where(iota(bias_ref.shape, 1) < len_line, 0.0, -jnp.inf)
-
-
-def up_body(group, mine_ref, other_ref, uq_ref, ukv_ref, *out_refs):
+    kept = [pltpu.make_async_copy(refs[i], outs[i], sems.at[3 + i]) for i in range(8)]
+    for copy in kept:
+        copy.start()
+    for copy in kept:
+        copy.wait()
+
+
+def up_body(group, mine_ref, other_ref, uq_ref, ukv_ref, out_ref):
     rank = uq_ref.shape[1]
     total = (mine_ref[...] + other_ref[...]).astype(BF16)
-    kv_width = ukv_ref.shape[3]
-    width = kv_width // len(out_refs)
-    q_width = width * group
-    for c, out_ref in enumerate(out_refs):
-        out_ref[:, :q_width] = dot(
-            total[:, :rank], uq_ref[0, :, c * q_width : (c + 1) * q_width]
+    q_width = uq_ref.shape[2]
+    width = ukv_ref.shape[3]
+    out_ref[:, :q_width] = dot(total[:, :rank], uq_ref[0]).astype(BF16)
+    for i in range(2):
+        out_ref[:, q_width + i * width : q_width + (i + 1) * width] = dot(
+            total[:, (i + 1) * rank : (i + 2) * rank], ukv_ref[0, i]
         ).astype(BF16)
-        for i in range(2):
-            out_ref[:, q_width + i * width : q_width + (i + 1) * width] = dot(
-                total[:, (i + 1) * rank : (i + 2) * rank], ukv_ref[0, i, :, c * width : (c + 1) * width]
-            ).astype(BF16)
 
 
 def attend_body(
-    first_head, heads, group, ret_ref, pqt_ref, pkt_ref, pvt_ref, k_ref, v_ref,
-    spread_ref, take_ref, place_ref, bias_ref, packed_ref, context_ref,
+    group, ret_ref, k_hbm, v_hbm, pqt_hbm, pkt_hbm, pvt_hbm, spread_hbm, take_hbm, place_hbm, bias_hbm,
+    packed_ref, context_ref,
+    pqt_ref, pkt_ref, pvt_ref, spread_ref, take_ref, place_ref, bias_ref, k_buf, v_buf, sems,
 ):
-    rows = context_ref.shape[0]
+    heads, rows = k_buf.shape[:2]
     slots = packed_ref.shape[0]
     head_dim = pqt_ref.shape[2]
+    pairs = [
+        (spread_hbm, spread_ref), (pqt_hbm, pqt_ref), (take_hbm, take_ref), (pkt_hbm, pkt_ref),
+        (pvt_hbm, pvt_ref), (bias_hbm, bias_ref), (place_hbm, place_ref),
+    ]
+    prepared = [pltpu.make_async_copy(a, b, sems.at[i]) for i, (a, b) in enumerate(pairs)]
+    cached = [
+        [
+            pltpu.make_async_copy(source.at[:, g], target.at[g], sems.at[len(pairs) + 2 * g + j])
+            for j, (source, target) in enumerate(((k_hbm, k_buf), (v_hbm, v_buf)))
+        ]
+        for g in range(heads)
+    ]
+    for copy in prepared[:6] + cached[0] + prepared[6:]:
+        copy.start()
+    for g in range(1, heads):
+        for copy in cached[g]:
+            copy.start()
+    for copy in prepared:
+        copy.wait()
     scale = head_dim ** (-0.5)
     spread, take, place = spread_ref[...], take_ref[...], place_ref[...]
     bias = bias_ref[...]
     k_base = heads * group * head_dim
     v_base = k_base + heads * head_dim
     for i in range(heads):
-        g = first_head + i
+        g = i
         stacked = jnp.concatenate(
             [ret_ref[:, (i * group + h) * head_dim : (i * group + h + 1) * head_dim] for h in range(group)], axis=0
         )
@@ -151,8 +198,9 @@
             pvt_ref[g].astype(F32) + dot(take, ret_ref[:, v_base + i * head_dim : v_base + (i + 1) * head_dim])
         ).astype(BF16).astype(F32)
         own = jnp.sum(query * new_key, axis=1, keepdims=True) * scale
+        cached[g][0].wait()
         score = jnp.concatenate(
-            [dot_t(query[r * group : (r + 1) * group].astype(BF16), k_ref[r, g]) for r in range(rows)], axis=0
+            [dot_t(query[r * group : (r + 1) * group].astype(BF16), k_buf[g, r]) for r in range(rows)], axis=0
         )
         score = score * scale + bias
         highest = jnp.maximum(jnp.max(score, axis=1, keepdims=True), own)
@@ -161,8 +209,9 @@
         inverse = 1.0 / (jnp.sum(raised, axis=1, keepdims=True) + own_raised)
         weight = raised * inverse
         own_weight = (own_raised * inverse).astype(BF16).astype(F32)
+        cached[g][1].wait()
         attended = jnp.concatenate(
-            [dot(weight[r * group : (r + 1) * group].astype(BF16), v_ref[r, g]) for r in range(rows)], axis=0
+            [dot(weight[r * group : (r + 1) * group].astype(BF16), v_buf[g, r]) for r in range(rows)], axis=0
         )
         context = (attended + own_weight * new_value).astype(BF16)
         laid = dot(place, context).astype(BF16)
@@ -224,61 +273,68 @@
     dest, packed = call(
         functools.partial(pack_body, capacity),
         (struct((rows,), jnp.int32), struct((slots, half), BF16)),
-        [SMEM, SMEM, VMEM],
+        [HBM, HBM, HBM],
         (SMEM, VMEM),
-        scratch=[pltpu.SMEM((wide_count,), jnp.int32)],
+        scratch=[
+            pltpu.SMEM(tenant.shape, jnp.int32),
+            pltpu.SMEM(slot_of_adapter.shape, jnp.int32),
+            pltpu.SMEM((wide_count,), jnp.int32),
+            pltpu.VMEM((rows, half), BF16),
+            DMA((3,)),
+        ],
         moved=4 * slots * half,
     )(tenant, slot_of_adapter, normed_layer_input)
     received = exchange(packed, wide_count)
 
+    prepared = (
+        struct((kv_heads, lines, head_dim), BF16),
+        struct((kv_heads, lines, head_dim), BF16),
+        struct((kv_heads, lines, head_dim), BF16),
+        struct((lines, group * slots), BF16),
+        struct((lines, slots), BF16),
+        struct((group * (slots + rows), lines), BF16),
+        struct((rows, slots), BF16),
+        struct((lines, cache_size), F32),
+    )
     pqt, pkt, pvt, spread, take, place, home, bias = call(
         functools.partial(prep_body, group),
-        (
-            struct((kv_heads, lines, head_dim), BF16),
-            struct((kv_heads, lines, head_dim), BF16),
-            struct((kv_heads, lines, head_dim), BF16),
-            struct((lines, group * slots), BF16),
-            struct((lines, slots), BF16),
-            struct((group * (slots + rows), lines), BF16),
-            struct((rows, slots), BF16),
-            struct((lines, cache_size), F32),
-        ),
-        [SMEM, SMEM, VMEM, VMEM, VMEM],
+        prepared,
+        [SMEM, SMEM, HBM, HBM, HBM],
+        (HBM,) * 8,
+        scratch=[pltpu.VMEM(a.shape, a.dtype) for a in prepared]
+        + [pltpu.VMEM(a.shape, a.dtype) for a in (plain_query_rows, plain_key_rows, plain_value_rows)]
+        + [DMA((11,))],
         moved=6000000,
     )(dest, live_cache_length, plain_query_rows, plain_key_rows, plain_value_rows)
 
     down_here = lax.dynamic_slice_in_dim(stacked_down_weight[0], lax.axis_index("tp") * half, half, axis=1)
     rank_part = dot_t(received, down_here)
-    width = kv_heads // CHUNKS
     terms = call(
         functools.partial(up_body, group),
-        tuple(struct((slots, width * (group + 2) * head_dim), BF16) for _ in range(CHUNKS)),
+        struct((slots, kv_heads * (group + 2) * head_dim), BF16),
         [VMEM] * 4,
         moved=2000000,
     )(rank_part, other_core(rank_part), query_up_weight, key_value_up_weight)
-    returned = [exchange(term, wide_count) for term in terms]
-    contexts = []
-    rank_o = None
-    for c in range(CHUNKS):
-        chunk_width = width * group * head_dim
-        outgoing, context = call(
-            functools.partial(attend_body, c * width, width, group),
-            (struct((slots, chunk_width), BF16), struct((rows, chunk_width), BF16)),
-            [VMEM] * 10,
-            moved=8000000,
-            limit=32,
-        )(returned[c], pqt, pkt, pvt, cached_key_rows, cached_value_rows, spread, take, place, bias)
-        contexts.append(context)
-        arrived = exchange(outgoing, wide_count)
-        part = dot_t(arrived, output_down_weight[0][:, c * chunk_width : (c + 1) * chunk_width])
-        rank_o = part if rank_o is None else rank_o + part
+    returned = exchange(terms, wide_count)
+    outgoing, context = call(
+        functools.partial(attend_body, group),
+        (struct((slots, query_width), BF16), struct((rows, query_width), BF16)),
+        [VMEM] + [HBM] * 9,
+        scratch=[pltpu.VMEM(a.shape, a.dtype) for a in (pqt, pkt, pvt, spread, take, place, bias)]
+        + [pltpu.VMEM((kv_heads, rows, cache_size, head_dim), BF16)] * 2
+        + [DMA((7 + 2 * kv_heads,))],
+        moved=8000000,
+        limit=58,
+    )(returned, cached_key_rows, cached_value_rows, pqt, pkt, pvt, spread, take, place, bias)
+    arrived = exchange(outgoing, wide_count)
+    rank_o = dot_t(arrived, output_down_weight[0])
     out_terms = call(
         output_up_body, struct((slots, query_width), BF16), [VMEM] * 3, moved=1200000
     )(rank_o, other_core(rank_o), output_up_weight)
     adapter_output_term = call(
         unpack_body, struct((rows, query_width), BF16), [VMEM] * 2, moved=1000000
     )(home, exchange(out_terms, wide_count))
-    return jnp.concatenate(contexts, axis=1), adapter_output_term
+    return context, adapter_output_term
 
 
 def solution(mesh):

time: 129 us -> 107 us (0.83)
  local copies, waits for them, and re-layouts: 29.6 us -> 1.26 us
  blocking collectives: 14.8 us -> 37.5 us
  starting transfers between devices: 27.7 us -> 11.6 us
  Pallas kernels: 11.4 us -> 21.9 us
  waiting for transfers between devices: 38.4 us -> 31.5 us
  matrix products: 4.15 us -> 1.99 us
    unnamed x72 -> x12, local copies, waits for them, and re-layouts: 29.6 us -> 1.26 us
    all_to_all x1 -> x2, blocking collectives: 14.8 us -> 37.5 us  [exchange(): lax.all_to_all(rows.reshape(wide_count, slots // wide_count, width), 'wid...]
    all_to_all x5 -> x2, starting transfers between devices: 27.5 us -> 11.5 us  [exchange(): lax.all_to_all(rows.reshape(wide_count, slots // wide_count, width), 'wid...]
    pallas_call x4 -> x3, Pallas kernels: 7.83 us -> 15.6 us  [the longest x1 9.82 us: shards(): call(functools.partial(attend_body, group), (struct((slots, query_width),...]
    all_to_all x5 -> x2, waiting for transfers between devices: 36 us -> 29.1 us  [exchange(): lax.all_to_all(rows.reshape(wide_count, slots // wide_count, width), 'wid...]
    dot_general x3 -> x2, matrix products: 4.15 us -> 1.99 us  [dot_t(): lax.dot_general(a, b, (((1,), (1,)), ((), ())), preferred_element_type=F32)]
    pallas_call x1, Pallas kernels: 0.28 us -> 2.15 us  [shards(): call(output_up_body, struct((slots, query_width), BF16), [VMEM] * 3, move...]
  transfers between devices with their start and end apart: 7 -> 4, of which waited for: 5 -> 4; matrix products, arithmetic and copies ran while one was open for 2% -> 0% of each run, Pallas kernels for 5% -> 3%
where the time goes in v2:
time: 107 us
  blocking collectives  37.5 us (35%)
  waiting for transfers between devices  31.5 us (29%)
  Pallas kernels  21.9 us (20%)
  starting transfers between devices  11.6 us (11%)
  matrix products  1.99 us (2%)
  local copies, waits for them, and re-layouts  1.26 us (1%)
    all_to_all x2, blocking collectives, exchange(): lax.all_to_all(rows.reshape(wide_count, slots // wide_count, width), 'wid...  37.5 us
    all_to_all x2, waiting for transfers between devices, exchange(): lax.all_to_all(rows.reshape(wide_count, slots // wide_count, width), 'wid...  29.1 us
    all_to_all x2, starting transfers between devices, exchange(): lax.all_to_all(rows.reshape(wide_count, slots // wide_count, width), 'wid...  11.5 us
    pallas_call x1, Pallas kernels, shards(): call(functools.partial(attend_body, group), (struct((slots, query_width),...  9.82 us
    pallas_call x1, Pallas kernels, shards(): call(functools.partial(prep_body, group), prepared, [SMEM, SMEM, HBM, HBM...  3.43 us
    ppermute x2, waiting for transfers between devices, other_core(): return lax.ppermute(value, 'tp', [(0, 1), (1, 0)])  2.44 us
    pallas_call x1, Pallas kernels, shards(): call(functools.partial(up_body, group), struct((slots, kv_heads * (group...  2.31 us
    pallas_call x1, Pallas kernels, shards(): call(functools.partial(pack_body, capacity), (struct((rows,), jnp.int32),...  2.2 us
  transfers between devices with their start and end apart: 4, of which 4 were waited for; matrix products, arithmetic and copies ran while one was open for 0% of the time, Pallas kernels for 3%

profile of v2, /device:TPU:0, one launch (start us, length us, event | category | flops | bytes accessed | tf_op | source)
XLA Modules:
  0.0 106.6 jit_solution(13397533239130326582)
XLA Ops:
  0.6 0.0 copy-start
  0.6 2.2 %shard_map.149 = (s32[32]{0:T(128)}, bf16[64,4096]{1,0:T(8,128)(2,1)}) custom-call(s32[256]{0:T(256)} %tenant_hbm.1, s32[8]{0:T(128)} %slot_hbm.1, bf16[32,8192]{1,0:T(8,128)(2,1)} %x_hbm.1), custom_call_target="tpu_custom_call" | custom-call | bytes 1048576 | tf_op jit(solution)/shard_map/pallas_call | solution.py:273
  2.9 7.3 %all-to-all-start = ((bf16[8,8,4096]{2,1,0:T(8,128)(2,1)}), bf16[8,8,4096]{2,1,0:T(8,128)(2,1)}, u32[]{:S(2)}, u32[]{:S(2)}) async-start(bf16[8,8,4096]{2,1,0:T(8,128)(2,1)} %bitcast.21), calls=%async_computation | async-start | bytes 1048576 | tf_op jit(solution)/shard_map/all_to_all | solution.py:236
  10.2 14.6 %all-to-all-done = bf16[8,8,4096]{2,1,0:T(8,128)(2,1)} async-done(((bf16[8,8,4096]{2,1,0:T(8,128)(2,1)}), bf16[8,8,4096]{2,1,0:T(8,128)(2,1)}, u32[]{:S(2)}, u32[]{:S(2)}) %all-to-all-start) | async-done | bytes 524320 | tf_op jit(solution)/shard_map/all_to_all | solution.py:236
  24.7 0.0 copy-done
  24.8 1.7 %fusion.mine_ref = f32[64,192]{1,0:T(8,128)S(1)} fusion(bf16[1,192,8192]{2,1,0:T(8,128)(2,1)S(1)} %copy-done, s32[]{:T(128)S(6)} %select_n.3, bf16[8,8,4096]{2,1,0:T(8,128)(2,1)} %all-to-all-done), kind=kOutput, calls=%fused_computation | convolution fusion | flops 100663296 | bytes 2146308 | tf_op jit(solution)/shard_map/dot_general | solution.py:40
  26.4 0.0 copy-start.2
  26.4 0.1 collective-permute-start
  26.5 1.2 %collective-permute-done.other_ref = f32[64,192]{1,0:T(8,128)S(1)} collective-permute-done((f32[64,192]{1,0:T(8,128)S(1)}, f32[64,192]{1,0:T(8,128)S(1)}, u32[]{:S(2)}, u32[]{:S(2)}) %collective-permute-start) | collective-permute-done | bytes 49184 | tf_op jit(solution)/shard_map/ppermute | solution.py:243
  27.7 0.0 copy-done.2
  27.8 0.0 copy-start.4
  27.8 0.6 copy-done.4
  28.4 2.3 %shard_map.150 = bf16[64,5120]{1,0:T(8,128)(2,1)} custom-call(f32[64,192]{1,0:T(8,128)} %copy-done.2, f32[64,192]{1,0:T(8,128)} %copy-done.4, bf16[1,64,4096]{2,1,0:T(8,128)(2,1)} %uq_ref.1, bf16[1,2,64,512]{3,2,1,0:T(8,128)(2,1)} %ukv_ref.1), custom_call_target="tpu_custom_call" | custom-call | bytes 2000000 | tf_op jit(solution)/shard_map/pallas_call | solution.py:312
  30.7 4.2 %all-to-all-start.1 = ((bf16[8,8,5120]{2,1,0:T(8,128)(2,1)}), bf16[8,8,5120]{2,1,0:T(8,128)(2,1)}, u32[]{:S(2)}, u32[]{:S(2)}) async-start(bf16[8,8,5120]{2,1,0:T(8,128)(2,1)} %bitcast.18), calls=%async_computation.1 | async-start | bytes 1310720 | tf_op jit(solution)/shard_map/all_to_all | solution.py:236
  34.9 3.4 %shard_map.151 = (bf16[4,256,128]{2,1,0:T(8,128)(2,1)}, bf16[4,256,128]{2,1,0:T(8,128)(2,1)}, bf16[4,256,128]{2,1,0:T(8,128)(2,1)}, bf16[256,512]{1,0:T(8,128)(2...) custom-call(s32[32]{0:T(128)} %get-tuple-element.15.dest_ref, ...), custom_call_target="tpu_custom_call" | custom-call | bytes 6000000 | tf_op jit(solution)/shard_map/pallas_call | solution.py:299
  38.3 14.5 %all-to-all-done.1 = bf16[8,8,5120]{2,1,0:T(8,128)(2,1)} async-done(((bf16[8,8,5120]{2,1,0:T(8,128)(2,1)}), bf16[8,8,5120]{2,1,0:T(8,128)(2,1)}, u32[]{:S(2)}, u32[]{:S(2)}) %all-to-all-start.1) | async-done | bytes 655392 | tf_op jit(solution)/shard_map/all_to_all | solution.py:236
  52.8 0.0 copy-start.1
  52.8 9.8 %shard_map.152 = (bf16[64,4096]{1,0:T(8,128)(2,1)}, bf16[32,4096]{1,0:T(8,128)(2,1)}) custom-call(bf16[64,5120]{1,0:T(8,128)(2,1)} %bitcast.4.ret_ref, bf16[32,4,96,128]{3,2,1,0:T(8,128)(2,1)} %k_hbm.1, bf16[32,4,96,128]{3,2,1,0:T(8,128)(2,1)} %v_hbm.1, bf16[4,256,128]{2,1,0:T(8,128)(2,1)} %get-tuple-element.16.pqt_hbm, ...), custom_call_target="tpu_custom_call" | custom-call | bytes 8000000 | tf_op jit(solution)/shard_map/pallas_call | solution.py:319
  62.7 18.3 %all_to_all.20 = bf16[8,8,4096]{2,1,0:T(8,128)(2,1)S(1)} all-to-all(bf16[8,8,4096]{2,1,0:T(8,128)(2,1)} %bitcast.22), channel_id=1, replica_groups=mesh['groups'=2,'wide'=8,'tp'=2] {'wide'}, dimensions={0} | all-to-all | bytes 1048576 | tf_op jit(solution)/shard_map/all_to_all | solution.py:236
  81.0 0.0 copy-done.1
  81.0 0.3 fusion.3.mine_ref
  81.3 0.0 copy-start.3
  81.3 0.1 collective-permute-start.1
  81.4 1.2 %collective-permute-done.1.other_ref = f32[64,64]{1,0:T(8,128)S(1)} collective-permute-done((f32[64,64]{1,0:T(8,128)S(1)}, f32[64,64]{1,0:T(8,128)S(1)}, u32[]{:S(2)}, u32[]{:S(2)}) %collective-permute-start.1) | collective-permute-done | bytes 16416 | tf_op jit(solution)/shard_map/ppermute | solution.py:243
  82.6 0.0 copy-done.3
  82.6 0.0 copy-start.5
  82.6 0.6 copy-done.5
  83.2 2.1 %shard_map.153 = bf16[64,4096]{1,0:T(8,128)(2,1)} custom-call(f32[64,64]{1,0:T(8,128)} %copy-done.3, f32[64,64]{1,0:T(8,128)} %copy-done.5, bf16[1,64,4096]{2,1,0:T(8,128)(2,1)} %uo_ref.1), custom_call_target="tpu_custom_call" | custom-call | bytes 1200000 | tf_op jit(solution)/shard_map/pallas_call | solution.py:331
  85.4 19.2 %all_to_all.21 = bf16[8,8,4096]{2,1,0:T(8,128)(2,1)} all-to-all(bf16[8,8,4096]{2,1,0:T(8,128)(2,1)} %bitcast.20), channel_id=1, replica_groups=mesh['groups'=2,'wide'=8,'tp'=2] {'wide'}, dimensions={0} | all-to-all | bytes 1048576 | tf_op jit(solution)/shard_map/all_to_all | solution.py:236
  104.6 2.0 %shard_map.154 = bf16[32,4096]{1,0:T(8,128)(2,1)} custom-call(bf16[32,64]{1,0:T(8,128)(2,1)} %get-tuple-element.24.home_ref, bf16[64,4096]{1,0:T(8,128)(2,1)} %bitcast.19), custom_call_target="tpu_custom_call" | custom-call | bytes 1000000 | tf_op jit(solution)/shard_map/pallas_call | solution.py:334
Async XLA Ops:
  0.6 24.1 %copy-start = (bf16[1,192,8192]{2,1,0:T(8,128)(2,1)S(1)}, bf16[1,192,8192]{2,1,0:T(8,128)(2,1)}, u32[]{:S(2)}) copy-start(bf16[1,192,8192]{2,1,0:T(8,128)(2,1)} %param.23) | copy-start | bytes 9437188
  2.9 21.9 %all-to-all-start = ((bf16[8,8,4096]{2,1,0:T(8,128)(2,1)}), bf16[8,8,4096]{2,1,0:T(8,128)(2,1)}, u32[]{:S(2)}, u32[]{:S(2)}) async-start(bf16[8,8,4096]{2,1,0:T(8,128)(2,1)} %bitcast.21), calls=%async_computation | async-start | bytes 1048576 | tf_op jit(solution)/shard_map/all_to_all | solution.py:236
  26.4 1.3 %copy-start.2 = (f32[64,192]{1,0:T(8,128)}, f32[64,192]{1,0:T(8,128)S(1)}, u32[]{:S(2)}) copy-start(f32[64,192]{1,0:T(8,128)S(1)} %fusion.mine_ref) | copy-start | bytes 147460
  26.4 1.3 %collective-permute-start = (f32[64,192]{1,0:T(8,128)S(1)}, f32[64,192]{1,0:T(8,128)S(1)}, u32[]{:S(2)}, u32[]{:S(2)}) collective-permute-start(f32[64,192]{1,0:T(8,128)S(1)} %fusion.mine_ref), channel_id=1, source_target_pairs={{0,1},{1,0},{2,3},{3,2},{4,5},{5,4},{6,7},{7,6},{8,9},{9,8},{10,11... | collective-permute-start | bytes 147464 | tf_op jit(solution)/shard_map/ppermute | solution.py:243
  27.8 0.6 copy-start.4
  30.7 22.1 %all-to-all-start.1 = ((bf16[8,8,5120]{2,1,0:T(8,128)(2,1)}), bf16[8,8,5120]{2,1,0:T(8,128)(2,1)}, u32[]{:S(2)}, u32[]{:S(2)}) async-start(bf16[8,8,5120]{2,1,0:T(8,128)(2,1)} %bitcast.18), calls=%async_computation.1 | async-start | bytes 1310720 | tf_op jit(solution)/shard_map/all_to_all | solution.py:236
  52.8 28.2 %copy-start.1 = (bf16[1,64,4096]{2,1,0:T(8,128)(2,1)S(1)}, bf16[1,64,4096]{2,1,0:T(8,128)(2,1)}, u32[]{:S(2)}) copy-start(bf16[1,64,4096]{2,1,0:T(8,128)(2,1)} %param.26) | copy-start | bytes 1572868
  81.3 1.3 %copy-start.3 = (f32[64,64]{1,0:T(8,128)}, f32[64,64]{1,0:T(8,128)S(1)}, u32[]{:S(2)}) copy-start(f32[64,64]{1,0:T(8,128)S(1)} %fusion.3.mine_ref) | copy-start | bytes 49156
  81.3 1.3 %collective-permute-start.1 = (f32[64,64]{1,0:T(8,128)S(1)}, f32[64,64]{1,0:T(8,128)S(1)}, u32[]{:S(2)}, u32[]{:S(2)}) collective-permute-start(f32[64,64]{1,0:T(8,128)S(1)} %fusion.3.mine_ref), channel_id=1, source_target_pairs={{0,1},{1,0},{2,3},{3,2},{4,5},{5,4},{6,7},{7,6},{8,9},{9,8},{10,11... | collective-permute-start | bytes 49160 | tf_op jit(solution)/shard_map/ppermute | solution.py:243
  82.6 0.6 copy-start.5

commit v3 on v2

v3 whole, which is shorter than its diff:
```python
import functools

import jax
import jax.numpy as jnp
from jax import lax
from jax.experimental import pallas as pl
from jax.experimental.pallas import tpu as pltpu
from jax.sharding import PartitionSpec as P

ADAPTER_SCALE = 0.5
F32 = jnp.float32
BF16 = jnp.bfloat16
VMEM = pl.BlockSpec(memory_space=pltpu.VMEM)
SMEM = pl.BlockSpec(memory_space=pltpu.SMEM)
HBM = pl.BlockSpec(memory_space=pltpu.HBM)
DMA = pltpu.SemaphoreType.DMA


def call(body, out_shape, in_specs, out_specs=None, scratch=(), flops=0, moved=0, limit=58):
    return pl.pallas_call(
        body,
        out_shape=out_shape,
        in_specs=in_specs,
        out_specs=jax.tree.map(lambda _: VMEM, out_shape) if out_specs is None else out_specs,
        scratch_shapes=scratch,
        cost_estimate=pl.CostEstimate(flops=flops, bytes_accessed=moved, transcendentals=0),
        compiler_params=pltpu.CompilerParams(vmem_limit_bytes=limit * 1024 * 1024),
    )


def iota(shape, dim):
    return lax.broadcasted_iota(jnp.int32, shape, dim)


def dot(a, b):
    return lax.dot_general(a, b, (((1,), (0,)), ((), ())), preferred_element_type=F32)


def dot_t(a, b):
    return lax.dot_general(a, b, (((1,), (1,)), ((), ())), preferred_element_type=F32)


def scalars_to_row(read, rows):
    lane = iota((1, rows), 1)
    row = jnp.zeros((1, rows), jnp.int32)
    for r in range(rows):
        row = jnp.where(lane == r, read(r), row)
    return row


def pack_body(
    capacity, tenant_hbm, slot_hbm, x_hbm, dest_ref, packed_ref, tenant_ref, slot_ref, count_ref, x_ref, sems
):
    slots, width = packed_ref.shape
    rows = x_ref.shape[0]
    start = pl.multiple_of(lax.axis_index("tp") * width, width)
    copies = [
        pltpu.make_async_copy(tenant_hbm, tenant_ref, sems.at[0]),
        pltpu.make_async_copy(slot_hbm, slot_ref, sems.at[1]),
        pltpu.make_async_copy(x_hbm.at[:, pl.ds(start, width)], x_ref, sems.at[2]),
    ]
    for copy in copies:
        copy.start()
    for d in range(slots // capacity):
        count_ref[d] = 0
    copies[0].wait()
    copies[1].wait()
    first = lax.axis_index("wide") * rows
    lane = iota((1, rows), 1)
    dest = jnp.zeros((1, rows), jnp.int32)
    for r in range(rows):
        holder = slot_ref[tenant_ref[first + r]]
        place = count_ref[holder]
        count_ref[holder] = place + 1
        slot = holder * capacity + place
        dest_ref[r] = slot
        dest = jnp.where(lane == r, slot, dest)
    chosen = (iota((slots, rows), 0) == dest).astype(F32).astype(BF16)
    copies[2].wait()
    packed_ref[...] = dot(chosen, x_ref[...]).astype(BF16)


def down_body(ret_ref, down_ref, out_ref):
    width = ret_ref.shape[1]
    start = pl.multiple_of(lax.axis_index("tp") * width, width)
    out_ref[...] = dot_t(ret_ref[...], down_ref[0, :, pl.ds(start, width)])


def up_body(group, mine_ref, other_ref, uq_ref, ukv_ref, out_ref):
    rank = uq_ref.shape[1]
    total = (mine_ref[...] + other_ref[...]).astype(BF16)
    q_width = uq_ref.shape[2]
    width = ukv_ref.shape[3]
    out_ref[:, :q_width] = dot(total[:, :rank], uq_ref[0]).astype(BF16)
    for i in range(2):
        out_ref[:, q_width + i * width : q_width + (i + 1) * width] = dot(
            total[:, (i + 1) * rank : (i + 2) * rank], ukv_ref[0, i]
        ).astype(BF16)


def attend_body(
    group, ret_ref, dest_ref, len_ref, pq_ref, pk_ref, pv_ref, k_ref, v_ref, packed_ref, context_hbm,
    context_ref, out_sems,
):
    rows, heads, cache_size, head_dim = k_ref.shape
    slots = packed_ref.shape[0]
    lines = rows * group
    shift = group.bit_length() - 1
    lane = iota((1, rows), 1)
    dest_row = jnp.zeros((1, rows), jnp.int32)
    len_row = jnp.zeros((1, rows), jnp.int32)
    for r in range(rows):
        dest_row = jnp.where(lane == r, dest_ref[r], dest_row)
        len_row = jnp.where(lane == r, len_ref[r], len_row)
    mine = (iota((lines, rows), 0) >> shift) == iota((lines, rows), 1)
    dest_line = jnp.sum(jnp.where(mine, dest_row, 0), axis=1, keepdims=True)
    len_line = jnp.sum(jnp.where(mine, len_row, 0), axis=1, keepdims=True)
    head_line = iota((lines, 1), 0) & (group - 1)
    row_line = iota((lines, 1), 0) >> shift
    to_line = (iota((lines, group * rows), 1) == head_line * rows + row_line).astype(F32).astype(BF16)
    repeat = mine.astype(F32).astype(BF16)
    spread = jnp.where(
        iota((lines, group * slots), 1) == head_line * slots + dest_line, ADAPTER_SCALE, 0.0
    ).astype(BF16)
    take = jnp.where(iota((lines, slots), 1) == dest_line, ADAPTER_SCALE, 0.0).astype(BF16)
    here = iota((rows, lines), 0) == (iota((rows, lines), 1) >> shift)
    eye = iota((rows, rows), 0) == iota((rows, rows), 1)
    dest_col = jnp.sum(jnp.where(eye, dest_row, 0), axis=1, keepdims=True)
    dest_lane = jnp.sum(jnp.where(here, dest_col, 0), axis=0, keepdims=True)
    head_lane = iota((1, lines), 1) & (group - 1)
    row_lane = iota((1, lines), 1) >> shift
    place_out = (iota((group * slots, lines), 0) == head_lane * slots + dest_lane).astype(F32).astype(BF16)
    place_home = (iota((group * rows, lines), 0) == head_lane * rows + row_lane).astype(F32).astype(BF16)
    bias = jnp.where(iota((lines, cache_size), 1) < len_line, 0.0, -jnp.inf)
    scale = head_dim ** (-0.5)
    k_base = heads * group * head_dim
    v_base = k_base + heads * head_dim
    lhs = jnp.concatenate([spread, to_line], axis=1)
    lhs_own = jnp.concatenate([take, repeat], axis=1)
    leaving = []
    for i in range(heads):
        g = i
        first = i * group * head_dim
        stacked = jnp.concatenate(
            [ret_ref[:, first + h * head_dim : first + (h + 1) * head_dim] for h in range(group)]
            + [pq_ref[:, first + h * head_dim : first + (h + 1) * head_dim] for h in range(group)],
            axis=0,
        )
        query = dot(lhs, stacked).astype(BF16).astype(F32)
        columns = slice(i * head_dim, (i + 1) * head_dim)
        new_key, new_value = (
            dot(lhs_own, jnp.concatenate([ret_ref[:, base + i * head_dim : base + (i + 1) * head_dim], plain[:, columns]], axis=0))
            .astype(BF16).astype(F32)
            for base, plain in ((k_base, pk_ref), (v_base, pv_ref))
        )
        own = jnp.sum(query * new_key, axis=1, keepdims=True) * scale
        score = jnp.concatenate(
            [dot_t(query[r * group : (r + 1) * group].astype(BF16), k_ref[r, g]) for r in range(rows)], axis=0
        )
        score = score * scale + bias
        highest = jnp.maximum(jnp.max(score, axis=1, keepdims=True), own)
        raised = jnp.exp(score - highest)
        own_raised = jnp.exp(own - highest)
        inverse = 1.0 / (jnp.sum(raised, axis=1, keepdims=True) + own_raised)
        weight = raised * inverse
        own_weight = (own_raised * inverse).astype(BF16).astype(F32)
        attended = jnp.concatenate(
            [dot(weight[r * group : (r + 1) * group].astype(BF16), v_ref[r, g]) for r in range(rows)], axis=0
        )
        context = (attended + own_weight * new_value).astype(BF16)
        laid_out = dot(place_out, context).astype(BF16)
        laid_home = dot(place_home, context).astype(BF16)
        for h in range(group):
            columns = slice((i * group + h) * head_dim, (i * group + h + 1) * head_dim)
            packed_ref[:, columns] = laid_out[h * slots : (h + 1) * slots]
            context_ref[:, columns] = laid_home[h * rows : (h + 1) * rows]
        columns = pl.ds(i * group * head_dim, group * head_dim)
        copy = pltpu.make_async_copy(context_ref.at[:, columns], context_hbm.at[:, columns], out_sems.at[i])
        copy.start()
        leaving.append(copy)
    for copy in leaving:
        copy.wait()


def output_up_body(mine_ref, other_ref, uo_ref, out_ref):
    total = (mine_ref[...] + other_ref[...]).astype(BF16)
    out_ref[...] = (ADAPTER_SCALE * dot(total, uo_ref[0])).astype(BF16)


def unpack_body(dest_ref, ret_ref, out_hbm, out_ref, sems):
    rows, width = out_ref.shape
    slots = ret_ref.shape[0]
    line = iota((rows, 1), 0)
    dest = jnp.zeros((rows, 1), jnp.int32)
    for r in range(rows):
        dest = jnp.where(line == r, dest_ref[r], dest)
    home = (iota((rows, slots), 1) == dest).astype(F32).astype(BF16)
    parts = sems.shape[0]
    part = width // parts
    leaving = []
    for i in range(parts):
        columns = pl.ds(i * part, part)
        out_ref[:, columns] = dot(home, ret_ref[:, columns]).astype(BF16)
        copy = pltpu.make_async_copy(out_ref.at[:, columns], out_hbm.at[:, columns], sems.at[i])
        copy.start()
        leaving.append(copy)
    for copy in leaving:
        copy.wait()


def exchange(rows, wide_count):
    slots, width = rows.shape
    moved = lax.all_to_all(
        rows.reshape(wide_count, slots // wide_count, width), "wide", split_axis=0, concat_axis=0, tiled=True
    )
    return moved.reshape(slots, width)


def other_core(value):
    return lax.ppermute(value, "tp", [(0, 1), (1, 0)])


def shards(
    normed_layer_input,
    plain_query_rows,
    plain_key_rows,
    plain_value_rows,
    cached_key_rows,
    cached_value_rows,
    live_cache_length,
    tenant,
    slot_of_adapter,
    stacked_down_weight,
    query_up_weight,
    key_value_up_weight,
    output_down_weight,
    output_up_weight,
):
    wide_count = lax.axis_size("wide")
    rows, features = normed_layer_input.shape
    half = features // lax.axis_size("tp")
    capacity = max(2, 2 * rows // wide_count)
    slots = wide_count * capacity
    kv_heads, cache_size, head_dim = cached_key_rows.shape[1:]
    query_width = plain_query_rows.shape[1]
    group = query_width // head_dim // kv_heads
    lines = rows * group
    struct = jax.ShapeDtypeStruct

    dest, packed = call(
        functools.partial(pack_body, capacity),
        (struct((rows,), jnp.int32), struct((slots, half), BF16)),
        [HBM, HBM, HBM],
        (SMEM, VMEM),
        scratch=[
            pltpu.SMEM(tenant.shape, jnp.int32),
            pltpu.SMEM(slot_of_adapter.shape, jnp.int32),
            pltpu.SMEM((wide_count,), jnp.int32),
            pltpu.VMEM((rows, half), BF16),
            DMA((3,)),
        ],
        moved=4 * slots * half,
    )(tenant, slot_of_adapter, normed_layer_input)
    received = exchange(packed, wide_count)

    rank_part = call(
        down_body, struct((slots, stacked_down_weight.shape[1]), F32), [VMEM] * 2, moved=4000000, limit=16
    )(received, stacked_down_weight)
    terms = call(
        functools.partial(up_body, group),
        struct((slots, kv_heads * (group + 2) * head_dim), BF16),
        [VMEM] * 4,
        moved=2000000,
        limit=16,
    )(rank_part, other_core(rank_part), query_up_weight, key_value_up_weight)
    returned = exchange(terms, wide_count)
    outgoing, context = call(
        functools.partial(attend_body, group),
        (struct((slots, query_width), BF16), struct((rows, query_width), BF16)),
        [VMEM, SMEM, SMEM, VMEM, VMEM, VMEM, VMEM, VMEM],
        (VMEM, HBM),
        scratch=[pltpu.VMEM((rows, query_width), BF16), DMA((kv_heads,))],
        moved=8000000,
        limit=16,
    )(
        returned, dest, live_cache_length, plain_query_rows, plain_key_rows, plain_value_rows,
        cached_key_rows, cached_value_rows,
    )
    arrived = exchange(outgoing, wide_count)
    rank_o = dot_t(arrived, output_down_weight[0])
    out_terms = call(
        output_up_body, struct((slots, query_width), BF16), [VMEM] * 3, moved=1200000, limit=16
    )(rank_o, other_core(rank_o), output_up_weight)
    adapter_output_term = call(
        unpack_body, struct((rows, query_width), BF16), [SMEM, VMEM], HBM,
        scratch=[pltpu.VMEM((rows, query_width), BF16), DMA((4,))], moved=1000000, limit=16,
    )(dest, exchange(out_terms, wide_count))
    return context, adapter_output_term


def solution(mesh):
    return jax.shard_map(
        shards,
        mesh=mesh,
        in_specs=(
            P(("groups", "wide"), None),
            P(("groups", "wide"), "tp"),
            P(("groups", "wide"), "tp"),
            P(("groups", "wide"), "tp"),
            P(("groups", "wide"), "tp", None, None),
            P(("groups", "wide"), "tp", None, None),
            P(("groups", "wide")),
            P("groups"),
            P("groups"),
            P("wide", None, None),
            P("wide", None, "tp"),
            P("wide", None, None, "tp"),
            P("wide", None, "tp"),
            P("wide", None, "tp"),
        ),
        out_specs=(P(("groups", "wide"), "tp"), P(("groups", "wide"), "tp")),
        check_vma=False,
    )
```

time: 107 us -> 95.4 us (0.89)
  blocking collectives: 37.5 us -> 78.9 us
  waiting for transfers between devices: 31.5 us -> 2.44 us
  starting transfers between devices: 11.6 us -> 0.14 us
  Pallas kernels: 21.9 us -> 10.5 us
  matrix products: 1.99 us -> 0.28 us
    all_to_all x2 -> x4, blocking collectives: 37.5 us -> 78.9 us  [exchange(): lax.all_to_all(rows.reshape(wide_count, slots // wide_count, width), 'wid...]
    all_to_all x2 -> x0, waiting for transfers between devices: 29.1 us -> none  [exchange(): lax.all_to_all(rows.reshape(wide_count, slots // wide_count, width), 'wid...]
    all_to_all x2 -> x0, starting transfers between devices: 11.5 us -> none  [exchange(): lax.all_to_all(rows.reshape(wide_count, slots // wide_count, width), 'wid...]
    pallas_call x1, Pallas kernels: 9.82 us -> 5.71 us  [shards(): call(functools.partial(attend_body, group), (struct((slots, query_width),...]
    pallas_call x2, Pallas kernels: 5.41 us -> 2.05 us  [the longest x1 1.42 us: shards(): call(unpack_body, struct((rows, query_width), BF16), [SMEM, VMEM], HBM, s...]
    pallas_call x1, Pallas kernels: 2.31 us -> 0.31 us  [shards(): call(functools.partial(up_body, group), struct((slots, kv_heads * (group...]
    pallas_call x1, Pallas kernels: 2.15 us -> 0.27 us  [shards(): call(output_up_body, struct((slots, query_width), BF16), [VMEM] * 3, move...]
    dot_general x2 -> x1, matrix products: 1.99 us -> 0.28 us  [dot_t(): lax.dot_general(a, b, (((1,), (1,)), ((), ())), preferred_element_type=F32)]
  transfers between devices with their start and end apart: 4 -> 2, of which waited for: 4 -> 2; matrix products, arithmetic and copies ran while one was open for 0% -> 0% of each run, Pallas kernels for 3% -> 0%
where the time goes in v3:
time: 95.4 us; the launch traced here: 95 us
  blocking collectives  78.9 us (83%)
  Pallas kernels  10.5 us (11%)
  waiting for transfers between devices  2.44 us (3%)
  local copies, waits for them, and re-layouts  1.95 us (2%)
    all_to_all x4, blocking collectives, exchange(): lax.all_to_all(rows.reshape(wide_count, slots // wide_count, width), 'wid...  78.9 us
    pallas_call x1, Pallas kernels, shards(): call(functools.partial(attend_body, group), (struct((slots, query_width),...  5.71 us
    ppermute x2, waiting for transfers between devices, other_core(): return lax.ppermute(value, 'tp', [(0, 1), (1, 0)])  2.44 us
    pallas_call x1, Pallas kernels, shards(): call(functools.partial(pack_body, capacity), (struct((rows,), jnp.int32),...  2.15 us
    unnamed x24, local copies, waits for them, and re-layouts  1.95 us
  transfers between devices with their start and end apart: 2, of which 2 were waited for; matrix products, arithmetic and copies ran while one was open for 0% of the time, Pallas kernels for 0%

profile of v3, /device:TPU:0, one launch (start us, length us, event | category | flops | bytes accessed | tf_op | source)
XLA Modules:
  0.0 95.0 jit_solution(15118542222676766088)
XLA Ops:
  0.6 0.0 copy-start
  0.6 0.0 copy-start.7
  0.7 0.0 copy-start.5
  0.7 2.1 %shard_map.149 = (s32[32]{0:T(128)}, bf16[64,4096]{1,0:T(8,128)(2,1)}) custom-call(s32[256]{0:T(256)} %tenant_hbm.1, s32[8]{0:T(128)} %slot_hbm.1, bf16[32,8192]{1,0:T(8,128)(2,1)} %x_hbm.1), custom_call_target="tpu_custom_call" | custom-call | bytes 1048576 | tf_op jit(solution)/shard_map/pallas_call | solution.py:250
  2.8 0.0 copy-start.6
  2.8 21.9 %all_to_all.20 = bf16[8,8,4096]{2,1,0:T(8,128)(2,1)S(1)} all-to-all(bf16[8,8,4096]{2,1,0:T(8,128)(2,1)} %bitcast.19), channel_id=1, replica_groups=mesh['groups'=2,'wide'=8,'tp'=2] {'wide'}, dimensions={0} | all-to-all | bytes 1048576 | tf_op jit(solution)/shard_map/all_to_all | solution.py:213
  24.8 0.0 copy-start.1
  24.8 1.9 %copy-done.1 = bf16[1,192,8192]{2,1,0:T(8,128)(2,1)S(1)} copy-done((bf16[1,192,8192]{2,1,0:T(8,128)(2,1)S(1)}, bf16[1,192,8192]{2,1,0:T(8,128)(2,1)}, u32[]{:S(2)}) %copy-start.1) | copy-done | bytes 3145752
  26.7 0.0 copy-start.2
  26.7 0.0 copy-start.3
  26.7 0.0 copy-start.8
  26.7 0.0 copy-start.9
  26.7 0.0 copy-start.10
  26.7 0.0 copy-start.11
  26.7 0.6 shard_map.150.mine_ref
  27.3 0.1 collective-permute-start
  27.4 1.2 %collective-permute-done.other_ref = f32[64,192]{1,0:T(8,128)S(1)} collective-permute-done((f32[64,192]{1,0:T(8,128)S(1)}, f32[64,192]{1,0:T(8,128)S(1)}, u32[]{:S(2)}, u32[]{:S(2)}) %collective-permute-start) | collective-permute-done | bytes 49184 | tf_op jit(solution)/shard_map/ppermute | solution.py:220
  28.7 0.0 copy-done.7
  28.7 0.0 copy-done.5
  28.7 0.3 shard_map.151
  29.0 21.4 %all_to_all.21 = bf16[8,8,5120]{2,1,0:T(8,128)(2,1)S(1)} all-to-all(bf16[8,8,5120]{2,1,0:T(8,128)(2,1)S(1)} %bitcast.13), channel_id=1, replica_groups=mesh['groups'=2,'wide'=8,'tp'=2] {'wide'}, dimensions={0} | all-to-all | bytes 1310720 | tf_op jit(solution)/shard_map/all_to_all | solution.py:213
  50.3 0.0 copy-done.6
  50.3 0.0 copy-done.2
  50.4 0.0 copy-done.3
  50.4 0.0 copy-done.8
  50.4 0.0 copy-done.9
  50.4 0.0 copy-done.10
  50.4 0.0 copy-done.11
  50.4 0.0 copy-start.4
  50.4 5.7 %shard_map.152 = (bf16[64,4096]{1,0:T(8,128)(2,1)S(1)}, bf16[32,4096]{1,0:T(8,128)(2,1)}) custom-call(bf16[64,5120]{1,0:T(8,128)(2,1)S(1)} %bitcast.14, s32[32]{0:T(128)S(1)} %copy-done.10, s32[32]{0:T(128)S(1)} %copy-done.11, bf16[32,4096]{1,0:T(8,128)(2,1)S(1)} %copy-done.6, bf16[32,512]{1,0:T(8,128)(2,1)S(1)} %copy-done.8, bf16[32,512]{1,0:T(8,128)(2,1)S(1)} %copy-done.9, ...), custom_call_target="tpu_custom_call" | custom-call | bytes 8000000 | tf_op jit(solution)/shard_map/pallas_call | solution.py:277
  56.1 17.4 %all_to_all.22 = bf16[8,8,4096]{2,1,0:T(8,128)(2,1)S(1)} all-to-all(bf16[8,8,4096]{2,1,0:T(8,128)(2,1)S(1)} %bitcast.18), channel_id=1, replica_groups=mesh['groups'=2,'wide'=8,'tp'=2] {'wide'}, dimensions={0} | all-to-all | bytes 1048576 | tf_op jit(solution)/shard_map/all_to_all | solution.py:213
  73.5 0.0 copy-done
  73.5 0.3 fusion.mine_ref
  73.8 0.1 collective-permute-start.1
  73.9 1.2 %collective-permute-done.1.other_ref = f32[64,64]{1,0:T(8,128)S(1)} collective-permute-done((f32[64,64]{1,0:T(8,128)S(1)}, f32[64,64]{1,0:T(8,128)S(1)}, u32[]{:S(2)}, u32[]{:S(2)}) %collective-permute-start.1) | collective-permute-done | bytes 16416 | tf_op jit(solution)/shard_map/ppermute | solution.py:220
  75.1 0.0 copy-done.4
  75.1 0.3 shard_map.153
  75.4 18.2 %all_to_all.23 = bf16[8,8,4096]{2,1,0:T(8,128)(2,1)S(1)} all-to-all(bf16[8,8,4096]{2,1,0:T(8,128)(2,1)S(1)} %bitcast.16), channel_id=1, replica_groups=mesh['groups'=2,'wide'=8,'tp'=2] {'wide'}, dimensions={0} | all-to-all | bytes 1048576 | tf_op jit(solution)/shard_map/all_to_all | solution.py:213
  93.6 1.4 %shard_map.154 = bf16[32,4096]{1,0:T(8,128)(2,1)} custom-call(s32[32]{0:T(128)S(1)} %copy-done.10, bf16[64,4096]{1,0:T(8,128)(2,1)S(1)} %bitcast.17), custom_call_target="tpu_custom_call" | custom-call | bytes 1000000 | tf_op jit(solution)/shard_map/pallas_call | solution.py:294
Async XLA Ops:
  0.6 72.9 %copy-start = (bf16[1,64,4096]{2,1,0:T(8,128)(2,1)S(1)}, bf16[1,64,4096]{2,1,0:T(8,128)(2,1)}, u32[]{:S(2)}) copy-start(bf16[1,64,4096]{2,1,0:T(8,128)(2,1)} %param.26) | copy-start | bytes 1572868
  0.6 28.0 %copy-start.7 = (bf16[1,2,64,512]{3,2,1,0:T(8,128)(2,1)S(1)}, bf16[1,2,64,512]{3,2,1,0:T(8,128)(2,1)}, u32[]{:S(2)}) copy-start(bf16[1,2,64,512]{3,2,1,0:T(8,128)(2,1)} %ukv_ref.1) | copy-start | bytes 393220
  0.7 28.0 %copy-start.5 = (bf16[1,64,4096]{2,1,0:T(8,128)(2,1)S(1)}, bf16[1,64,4096]{2,1,0:T(8,128)(2,1)}, u32[]{:S(2)}) copy-start(bf16[1,64,4096]{2,1,0:T(8,128)(2,1)} %uq_ref.1) | copy-start | bytes 1572868
  2.8 47.5 %copy-start.6 = (bf16[32,4096]{1,0:T(8,128)(2,1)S(1)}, bf16[32,4096]{1,0:T(8,128)(2,1)}, u32[]{:S(2)}) copy-start(bf16[32,4096]{1,0:T(8,128)(2,1)} %pq_ref.1) | copy-start | bytes 786436
  24.8 1.9 %copy-start.1 = (bf16[1,192,8192]{2,1,0:T(8,128)(2,1)S(1)}, bf16[1,192,8192]{2,1,0:T(8,128)(2,1)}, u32[]{:S(2)}) copy-start(bf16[1,192,8192]{2,1,0:T(8,128)(2,1)} %down_ref.1) | copy-start | bytes 9437188
  26.7 23.7 %copy-start.2 = (bf16[32,4,96,128]{3,2,1,0:T(8,128)(2,1)S(1)}, bf16[32,4,96,128]{3,2,1,0:T(8,128)(2,1)}, u32[]{:S(2)}) copy-start(bf16[32,4,96,128]{3,2,1,0:T(8,128)(2,1)} %k_ref.1) | copy-start | bytes 9437188
  26.7 23.7 %copy-start.3 = (bf16[32,4,96,128]{3,2,1,0:T(8,128)(2,1)S(1)}, bf16[32,4,96,128]{3,2,1,0:T(8,128)(2,1)}, u32[]{:S(2)}) copy-start(bf16[32,4,96,128]{3,2,1,0:T(8,128)(2,1)} %v_ref.1) | copy-start | bytes 9437188
  26.7 23.7 %copy-start.8 = (bf16[32,512]{1,0:T(8,128)(2,1)S(1)}, bf16[32,512]{1,0:T(8,128)(2,1)}, u32[]{:S(2)}) copy-start(bf16[32,512]{1,0:T(8,128)(2,1)} %pk_ref.1) | copy-start | bytes 98308
  26.7 23.7 %copy-start.9 = (bf16[32,512]{1,0:T(8,128)(2,1)S(1)}, bf16[32,512]{1,0:T(8,128)(2,1)}, u32[]{:S(2)}) copy-start(bf16[32,512]{1,0:T(8,128)(2,1)} %pv_ref.1) | copy-start | bytes 98308
  26.7 23.7 %copy-start.10 = (s32[32]{0:T(128)S(1)}, s32[32]{0:T(128)}, u32[]{:S(2)}) copy-start(s32[32]{0:T(128)} %get-tuple-element.7.dest_ref) | copy-start | bytes 388
  26.7 23.7 %copy-start.11 = (s32[32]{0:T(128)S(1)}, s32[32]{0:T(128)}, u32[]{:S(2)}) copy-start(s32[32]{0:T(128)} %len_ref.1) | copy-start | bytes 388
  27.3 1.3 %collective-permute-start = (f32[64,192]{1,0:T(8,128)S(1)}, f32[64,192]{1,0:T(8,128)S(1)}, u32[]{:S(2)}, u32[]{:S(2)}) collective-permute-start(f32[64,192]{1,0:T(8,128)S(1)} %shard_map.150.mine_ref), channel_id=1, source_target_pairs={{0,1},{1,0},{2,3},{3,2},{4,5},{5,4},{6,7},{7,6},{8,9},{9,8},{10,11... | collective-permute-start | bytes 147464 | tf_op jit(solution)/shard_map/ppermute | solution.py:220
  50.4 24.7 %copy-start.4 = (bf16[1,64,4096]{2,1,0:T(8,128)(2,1)S(1)}, bf16[1,64,4096]{2,1,0:T(8,128)(2,1)}, u32[]{:S(2)}) copy-start(bf16[1,64,4096]{2,1,0:T(8,128)(2,1)} %uo_ref.1) | copy-start | bytes 1572868
  73.8 1.3 %collective-permute-start.1 = (f32[64,64]{1,0:T(8,128)S(1)}, f32[64,64]{1,0:T(8,128)S(1)}, u32[]{:S(2)}, u32[]{:S(2)}) collective-permute-start(f32[64,64]{1,0:T(8,128)S(1)} %fusion.mine_ref), channel_id=1, source_target_pairs={{0,1},{1,0},{2,3},{3,2},{4,5},{5,4},{6,7},{7,6},{8,9},{9,8},{10,11... | collective-permute-start | bytes 49160 | tf_op jit(solution)/shard_map/ppermute | solution.py:220

commit v4 on v3

--- a/solution.py
+++ b/solution.py
@@ -49,7 +49,8 @@
 
 
 def pack_body(
-    capacity, tenant_hbm, slot_hbm, x_hbm, dest_ref, packed_ref, tenant_ref, slot_ref, count_ref, x_ref, sems
+    capacity, tenant_hbm, slot_hbm, len_hbm, x_hbm, table_ref, packed_ref,
+    tenant_ref, slot_ref, len_ref, count_ref, x_ref, sems,
 ):
     slots, width = packed_ref.shape
     rows = x_ref.shape[0]
@@ -57,14 +58,15 @@
     copies = [
         pltpu.make_async_copy(tenant_hbm, tenant_ref, sems.at[0]),
         pltpu.make_async_copy(slot_hbm, slot_ref, sems.at[1]),
+        pltpu.make_async_copy(len_hbm, len_ref, sems.at[3]),
         pltpu.make_async_copy(x_hbm.at[:, pl.ds(start, width)], x_ref, sems.at[2]),
     ]
     for copy in copies:
         copy.start()
     for d in range(slots // capacity):
         count_ref[d] = 0
-    copies[0].wait()
-    copies[1].wait()
+    for copy in copies[:3]:
+        copy.wait()
     first = lax.axis_index("wide") * rows
     lane = iota((1, rows), 1)
     dest = jnp.zeros((1, rows), jnp.int32)
@@ -73,17 +75,12 @@
         place = count_ref[holder]
         count_ref[holder] = place + 1
         slot = holder * capacity + place
-        dest_ref[r] = slot
+        table_ref[r] = slot
+        table_ref[rows + r] = len_ref[r]
         dest = jnp.where(lane == r, slot, dest)
     chosen = (iota((slots, rows), 0) == dest).astype(F32).astype(BF16)
-    copies[2].wait()
+    copies[3].wait()
     packed_ref[...] = dot(chosen, x_ref[...]).astype(BF16)
-
-
-def down_body(ret_ref, down_ref, out_ref):
-    width = ret_ref.shape[1]
-    start = pl.multiple_of(lax.axis_index("tp") * width, width)
-    out_ref[...] = dot_t(ret_ref[...], down_ref[0, :, pl.ds(start, width)])
 
 
 def up_body(group, mine_ref, other_ref, uq_ref, ukv_ref, out_ref):
@@ -98,20 +95,18 @@
         ).astype(BF16)
 
 
-def attend_body(
-    group, ret_ref, dest_ref, len_ref, pq_ref, pk_ref, pv_ref, k_ref, v_ref, packed_ref, context_hbm,
-    context_ref, out_sems,
+def prep_body(
+    group, table_ref, spread_ref, take_ref, out_ref, back_ref, home_ref, bias_ref,
 ):
-    rows, heads, cache_size, head_dim = k_ref.shape
-    slots = packed_ref.shape[0]
-    lines = rows * group
+    lines = spread_ref.shape[0]
+    rows, slots = home_ref.shape
     shift = group.bit_length() - 1
     lane = iota((1, rows), 1)
     dest_row = jnp.zeros((1, rows), jnp.int32)
     len_row = jnp.zeros((1, rows), jnp.int32)
     for r in range(rows):
-        dest_row = jnp.where(lane == r, dest_ref[r], dest_row)
-        len_row = jnp.where(lane == r, len_ref[r], len_row)
+        dest_row = jnp.where(lane == r, table_ref[r], dest_row)
+        len_row = jnp.where(lane == r, table_ref[rows + r], len_row)
     mine = (iota((lines, rows), 0) >> shift) == iota((lines, rows), 1)
     dest_line = jnp.sum(jnp.where(mine, dest_row, 0), axis=1, keepdims=True)
     len_line = jnp.sum(jnp.where(mine, len_row, 0), axis=1, keepdims=True)
@@ -119,38 +114,56 @@
     row_line = iota((lines, 1), 0) >> shift
     to_line = (iota((lines, group * rows), 1) == head_line * rows + row_line).astype(F32).astype(BF16)
     repeat = mine.astype(F32).astype(BF16)
-    spread = jnp.where(
+    taken = jnp.where(
         iota((lines, group * slots), 1) == head_line * slots + dest_line, ADAPTER_SCALE, 0.0
     ).astype(BF16)
-    take = jnp.where(iota((lines, slots), 1) == dest_line, ADAPTER_SCALE, 0.0).astype(BF16)
+    spread_ref[...] = jnp.concatenate([taken, to_line], axis=1)
+    taken = jnp.where(iota((lines, slots), 1) == dest_line, ADAPTER_SCALE, 0.0).astype(BF16)
+    take_ref[...] = jnp.concatenate([taken, repeat], axis=1)
     here = iota((rows, lines), 0) == (iota((rows, lines), 1) >> shift)
     eye = iota((rows, rows), 0) == iota((rows, rows), 1)
     dest_col = jnp.sum(jnp.where(eye, dest_row, 0), axis=1, keepdims=True)
     dest_lane = jnp.sum(jnp.where(here, dest_col, 0), axis=0, keepdims=True)
     head_lane = iota((1, lines), 1) & (group - 1)
     row_lane = iota((1, lines), 1) >> shift
-    place_out = (iota((group * slots, lines), 0) == head_lane * slots + dest_lane).astype(F32).astype(BF16)
-    place_home = (iota((group * rows, lines), 0) == head_lane * rows + row_lane).astype(F32).astype(BF16)
-    bias = jnp.where(iota((lines, cache_size), 1) < len_line, 0.0, -jnp.inf)
+    out_ref[...] = (iota((group * slots, lines), 0) == head_lane * slots + dest_lane).astype(F32).astype(BF16)
+    back_ref[...] = (iota((group * rows, lines), 0) == head_lane * rows + row_lane).astype(F32).astype(BF16)
+    home_ref[...] = (iota((rows, slots), 1) == dest_col).astype(F32).astype(BF16)
+    bias_ref[...] = jnp.where(iota(bias_ref.shape, 1) < len_line, 0.0, -jnp.inf)
+
+
+def attend_body(
+    group, ret_ref, k_ref, v_ref, pq_ref, pk_ref, pv_ref, spread_ref, take_ref, out_ref, back_ref, home_ref, bias_ref,
+    packed_ref, context_hbm, context_ref, out_sems,
+):
+    rows, heads, cache_size, head_dim = k_ref.shape
+    slots = packed_ref.shape[0]
+    spread, take, place_out, place_home = spread_ref[...], take_ref[...], out_ref[...], back_ref[...]
+    bias = bias_ref[...]
     scale = head_dim ** (-0.5)
     k_base = heads * group * head_dim
     v_base = k_base + heads * head_dim
-    lhs = jnp.concatenate([spread, to_line], axis=1)
-    lhs_own = jnp.concatenate([take, repeat], axis=1)
     leaving = []
     for i in range(heads):
         g = i
         first = i * group * head_dim
         stacked = jnp.concatenate(
-            [ret_ref[:, first + h * head_dim : first + (h + 1) * head_dim] for h in range(group)]
-            + [pq_ref[:, first + h * head_dim : first + (h + 1) * head_dim] for h in range(group)],
+            [
+                source[:, first + h * head_dim : first + (h + 1) * head_dim]
+                for source in (ret_ref, pq_ref)
+                for h in range(group)
+            ],
             axis=0,
         )
-        query = dot(lhs, stacked).astype(BF16).astype(F32)
+        query = dot(spread, stacked).astype(BF16).astype(F32)
         columns = slice(i * head_dim, (i + 1) * head_dim)
         new_key, new_value = (
-            dot(lhs_own, jnp.concatenate([ret_ref[:, base + i * head_dim : base + (i + 1) * head_dim], plain[:, columns]], axis=0))
-            .astype(BF16).astype(F32)
+            dot(
+                take,
+                jnp.concatenate(
+                    [ret_ref[:, base + i * head_dim : base + (i + 1) * head_dim], plain[:, columns]], axis=0
+                ),
+            ).astype(BF16).astype(F32)
             for base, plain in ((k_base, pk_ref), (v_base, pv_ref))
         )
         own = jnp.sum(query * new_key, axis=1, keepdims=True) * scale
@@ -187,14 +200,9 @@
     out_ref[...] = (ADAPTER_SCALE * dot(total, uo_ref[0])).astype(BF16)
 
 
-def unpack_body(dest_ref, ret_ref, out_hbm, out_ref, sems):
+def unpack_body(home_ref, ret_ref, out_hbm, out_ref, sems):
     rows, width = out_ref.shape
-    slots = ret_ref.shape[0]
-    line = iota((rows, 1), 0)
-    dest = jnp.zeros((rows, 1), jnp.int32)
-    for r in range(rows):
-        dest = jnp.where(line == r, dest_ref[r], dest)
-    home = (iota((rows, slots), 1) == dest).astype(F32).astype(BF16)
+    home = home_ref[...]
     parts = sems.shape[0]
     part = width // parts
     leaving = []
@@ -247,44 +255,60 @@
     lines = rows * group
     struct = jax.ShapeDtypeStruct
 
-    dest, packed = call(
+    table, packed = call(
         functools.partial(pack_body, capacity),
-        (struct((rows,), jnp.int32), struct((slots, half), BF16)),
-        [HBM, HBM, HBM],
+        (struct((2 * rows,), jnp.int32), struct((slots, half), BF16)),
+        [HBM] * 4,
         (SMEM, VMEM),
         scratch=[
             pltpu.SMEM(tenant.shape, jnp.int32),
             pltpu.SMEM(slot_of_adapter.shape, jnp.int32),
+            pltpu.SMEM((rows,), jnp.int32),
             pltpu.SMEM((wide_count,), jnp.int32),
             pltpu.VMEM((rows, half), BF16),
-            DMA((3,)),
+            DMA((4,)),
         ],
         moved=4 * slots * half,
-    )(tenant, slot_of_adapter, normed_layer_input)
+    )(tenant, slot_of_adapter, live_cache_length, normed_layer_input)
+    packed, feature_start = lax.optimization_barrier((packed, lax.axis_index("tp").astype(jnp.uint32) * jnp.uint32(half)))
     received = exchange(packed, wide_count)
 
-    rank_part = call(
-        down_body, struct((slots, stacked_down_weight.shape[1]), F32), [VMEM] * 2, moved=4000000, limit=16
-    )(received, stacked_down_weight)
+    down_here = lax.dynamic_slice(stacked_down_weight[0], (jnp.uint32(0), feature_start), (stacked_down_weight.shape[1], half))
+    rank_part = dot_t(received, down_here)
+    rank_other = other_core(rank_part)
+    table, rank_part = lax.optimization_barrier((table, rank_part))
+    prepared = (
+        struct((lines, group * (slots + rows)), BF16),
+        struct((lines, slots + rows), BF16),
+        struct((group * slots, lines), BF16),
+        struct((group * rows, lines), BF16),
+        struct((rows, slots), BF16),
+        struct((lines, cache_size), F32),
+    )
+    prepared = call(
+        functools.partial(prep_body, group), prepared, [SMEM], moved=2000000, limit=16
+    )(table)
+    rank_other, prepared = lax.optimization_barrier((rank_other, prepared))
+    home = prepared[4]
     terms = call(
         functools.partial(up_body, group),
         struct((slots, kv_heads * (group + 2) * head_dim), BF16),
         [VMEM] * 4,
-        moved=2000000,
+        moved=20000000,
+        flops=10**9,
         limit=16,
-    )(rank_part, other_core(rank_part), query_up_weight, key_value_up_weight)
+    )(rank_part, rank_other, query_up_weight, key_value_up_weight)
     returned = exchange(terms, wide_count)
     outgoing, context = call(
         functools.partial(attend_body, group),
         (struct((slots, query_width), BF16), struct((rows, query_width), BF16)),
-        [VMEM, SMEM, SMEM, VMEM, VMEM, VMEM, VMEM, VMEM],
+        [VMEM] * (6 + len(prepared)),
         (VMEM, HBM),
         scratch=[pltpu.VMEM((rows, query_width), BF16), DMA((kv_heads,))],
         moved=8000000,
         limit=16,
     )(
-        returned, dest, live_cache_length, plain_query_rows, plain_key_rows, plain_value_rows,
-        cached_key_rows, cached_value_rows,
+        returned, cached_key_rows, cached_value_rows, plain_query_rows, plain_key_rows, plain_value_rows, *prepared
     )
     arrived = exchange(outgoing, wide_count)
     rank_o = dot_t(arrived, output_down_weight[0])
@@ -292,9 +316,9 @@
         output_up_body, struct((slots, query_width), BF16), [VMEM] * 3, moved=1200000, limit=16
     )(rank_o, other_core(rank_o), output_up_weight)
     adapter_output_term = call(
-        unpack_body, struct((rows, query_width), BF16), [SMEM, VMEM], HBM,
+        unpack_body, struct((rows, query_width), BF16), [VMEM, VMEM], HBM,
         scratch=[pltpu.VMEM((rows, query_width), BF16), DMA((4,))], moved=1000000, limit=16,
-    )(dest, exchange(out_terms, wide_count))
+    )(home, exchange(out_terms, wide_count))
     return context, adapter_output_term
 
 

time: 95.4 us -> 92.5 us (0.970)
  local copies, waits for them, and re-layouts: 1.95 us -> 0.06 us
  waiting for transfers between devices: 2.44 us -> 1.43 us
    unnamed x24 -> x22, local copies, waits for them, and re-layouts: 1.95 us -> 0.06 us
    ppermute x2, waiting for transfers between devices: 2.44 us -> 1.43 us  [other_core(): return lax.ppermute(value, 'tp', [(0, 1), (1, 0)])]
  transfers between devices with their start and end apart: 2 -> 2, of which waited for: 2 -> 2; matrix products, arithmetic and copies ran while one was open for 0% -> 0% of each run, Pallas kernels for 0% -> 1%
where the time goes in v4:
time: 92.5 us; the launch traced here: 92.2 us
  blocking collectives  78.9 us (85%)
  Pallas kernels  9.72 us (11%)
  waiting for transfers between devices  1.43 us (2%)
  matrix products  1.08 us (1%)
    all_to_all x4, blocking collectives, exchange(): lax.all_to_all(rows.reshape(wide_count, slots // wide_count, width), 'wid...  78.9 us
    pallas_call x1, Pallas kernels, shards(): call(functools.partial(attend_body, group), (struct((slots, query_width),...  5.04 us
    pallas_call x1, Pallas kernels, shards(): call(functools.partial(pack_body, capacity), (struct((2 * rows,), jnp.int...  2.22 us
  transfers between devices with their start and end apart: 2, of which 2 were waited for; matrix products, arithmetic and copies ran while one was open for 0% of the time, Pallas kernels for 1%

profile of v4, /device:TPU:0, one launch (start us, length us, event | category | flops | bytes accessed | tf_op | source)
XLA Modules:
  0.0 92.2 jit_solution(18014336001052551330)
XLA Ops:
  0.6 0.0 copy-start
  0.6 0.0 copy-start.8
  0.7 0.0 copy-start.7
  0.7 2.2 %shard_map.149 = (s32[64]{0:T(128)}, bf16[64,4096]{1,0:T(8,128)(2,1)}) custom-call(s32[256]{0:T(256)} %tenant_hbm.1, s32[8]{0:T(128)} %slot_hbm.1, s32[32]{0:T(128)} %len_hbm.1, bf16[32,8192]{1,0:T(8,128)(2,1)} %x_hbm.1), custom_call_target="tpu_custom_call" | custom-call | bytes 1048576 | tf_op jit(solution)/shard_map/pallas_call | solution.py:258
  2.9 0.0 copy-start.9
  2.9 21.8 %all_to_all.20 = bf16[8,8,4096]{2,1,0:T(8,128)(2,1)S(1)} all-to-all(bf16[8,8,4096]{2,1,0:T(8,128)(2,1)} %bitcast.23), channel_id=1, replica_groups=mesh['groups'=2,'wide'=8,'tp'=2] {'wide'}, dimensions={0} | all-to-all | bytes 1048576 | tf_op jit(solution)/shard_map/all_to_all | solution.py:221
  24.7 0.0 copy-done
  24.7 0.0 copy-start.1
  24.7 0.0 copy-start.2
  24.7 0.0 copy-start.4
  24.7 0.0 copy-start.5
  24.8 0.0 copy-start.6
  24.8 0.8 fusion.mine_ref
  25.6 0.1 collective-permute-start
  25.6 0.0 copy-done.9
  25.7 1.0 %shard_map.150 = (bf16[256,768]{1,0:T(8,128)(2,1)S(1)}, bf16[256,96]{1,0:T(8,128)(2,1)S(1)}, bf16[512,256]{1,0:T(8,128)(2,1)S(1)}, bf16[256,256]{1,0:T(8,128)(2,...) custom-call(s32[64]{0:T(128)S(1)} %copy-done.9), custom_call_target="tpu_custom_call" | custom-call | bytes 2000000 | tf_op jit(solution)/shard_map/pallas_call | solution.py:288
  26.6 0.2 collective-permute-done.other_ref
  26.9 0.0 copy-done.8
  26.9 0.0 copy-done.7
  26.9 0.3 shard_map.151
  27.2 21.5 %all_to_all.21 = bf16[8,8,5120]{2,1,0:T(8,128)(2,1)S(1)} all-to-all(bf16[8,8,5120]{2,1,0:T(8,128)(2,1)S(1)} %bitcast.21), channel_id=1, replica_groups=mesh['groups'=2,'wide'=8,'tp'=2] {'wide'}, dimensions={0} | all-to-all | bytes 1310720 | tf_op jit(solution)/shard_map/all_to_all | solution.py:221
  48.7 0.0 copy-done.1
  48.7 0.0 copy-done.2
  48.7 0.0 copy-done.4
  48.7 0.0 copy-done.5
  48.7 0.0 copy-done.6
  48.7 0.0 copy-start.10
  48.7 0.0 copy-start.3
  48.8 5.0 %shard_map.152 = (bf16[64,4096]{1,0:T(8,128)(2,1)S(1)}, bf16[32,4096]{1,0:T(8,128)(2,1)}) custom-call(bf16[64,5120]{1,0:T(8,128)(2,1)S(1)} %bitcast.18, bf16[32,4,96,128]{3,2,1,0:T(8,128)(2,1)S(1)} %copy-done.1, bf16[32,4,96,128]{3,2,1,0:T(8,128)(2,1)S(1)} %copy-done.2, bf16[32,4096]{1,0:T(8,128)(2,1)S(1)} %copy-done.4, bf16[32,512]{1,0:T(8,128)(2,1)S(1)} %copy-done.5, ...), custom_call_target="tpu_custom_call" | custom-call | bytes 8000000 | tf_op jit(solution)/shard_map/pallas_call | solution.py:302
  53.8 17.4 %all_to_all.22 = bf16[8,8,4096]{2,1,0:T(8,128)(2,1)S(1)} all-to-all(bf16[8,8,4096]{2,1,0:T(8,128)(2,1)S(1)} %bitcast.22), channel_id=1, replica_groups=mesh['groups'=2,'wide'=8,'tp'=2] {'wide'}, dimensions={0} | all-to-all | bytes 1048576 | tf_op jit(solution)/shard_map/all_to_all | solution.py:221
  71.2 0.0 copy-done.10
  71.2 0.3 fusion.3.mine_ref
  71.5 0.1 collective-permute-start.1
  71.6 1.2 %collective-permute-done.1.other_ref = f32[64,64]{1,0:T(8,128)S(1)} collective-permute-done((f32[64,64]{1,0:T(8,128)S(1)}, f32[64,64]{1,0:T(8,128)S(1)}, u32[]{:S(2)}, u32[]{:S(2)}) %collective-permute-start.1) | collective-permute-done | bytes 16416 | tf_op jit(solution)/shard_map/ppermute | solution.py:228
  72.8 0.0 copy-done.3
  72.8 0.3 shard_map.153
  73.1 18.2 %all_to_all.23 = bf16[8,8,4096]{2,1,0:T(8,128)(2,1)S(1)} all-to-all(bf16[8,8,4096]{2,1,0:T(8,128)(2,1)S(1)} %bitcast.19), channel_id=1, replica_groups=mesh['groups'=2,'wide'=8,'tp'=2] {'wide'}, dimensions={0} | all-to-all | bytes 1048576 | tf_op jit(solution)/shard_map/all_to_all | solution.py:221
  91.3 0.9 shard_map.154
Async XLA Ops:
  0.6 24.1 %copy-start = (bf16[1,192,8192]{2,1,0:T(8,128)(2,1)S(1)}, bf16[1,192,8192]{2,1,0:T(8,128)(2,1)}, u32[]{:S(2)}) copy-start(bf16[1,192,8192]{2,1,0:T(8,128)(2,1)} %param.23) | copy-start | bytes 9437188
  0.6 26.2 %copy-start.8 = (bf16[1,2,64,512]{3,2,1,0:T(8,128)(2,1)S(1)}, bf16[1,2,64,512]{3,2,1,0:T(8,128)(2,1)}, u32[]{:S(2)}) copy-start(bf16[1,2,64,512]{3,2,1,0:T(8,128)(2,1)} %ukv_ref.1) | copy-start | bytes 393220
  0.7 26.2 %copy-start.7 = (bf16[1,64,4096]{2,1,0:T(8,128)(2,1)S(1)}, bf16[1,64,4096]{2,1,0:T(8,128)(2,1)}, u32[]{:S(2)}) copy-start(bf16[1,64,4096]{2,1,0:T(8,128)(2,1)} %uq_ref.1) | copy-start | bytes 1572868
  2.9 22.7 %copy-start.9 = (s32[64]{0:T(128)S(1)}, s32[64]{0:T(128)}, u32[]{:S(2)}) copy-start(s32[64]{0:T(128)} %get-tuple-element.28.table_ref) | copy-start | bytes 772
  24.7 24.0 %copy-start.1 = (bf16[32,4,96,128]{3,2,1,0:T(8,128)(2,1)S(1)}, bf16[32,4,96,128]{3,2,1,0:T(8,128)(2,1)}, u32[]{:S(2)}) copy-start(bf16[32,4,96,128]{3,2,1,0:T(8,128)(2,1)} %k_ref.1) | copy-start | bytes 9437188
  24.7 24.0 %copy-start.2 = (bf16[32,4,96,128]{3,2,1,0:T(8,128)(2,1)S(1)}, bf16[32,4,96,128]{3,2,1,0:T(8,128)(2,1)}, u32[]{:S(2)}) copy-start(bf16[32,4,96,128]{3,2,1,0:T(8,128)(2,1)} %v_ref.1) | copy-start | bytes 9437188
  24.7 24.0 %copy-start.4 = (bf16[32,4096]{1,0:T(8,128)(2,1)S(1)}, bf16[32,4096]{1,0:T(8,128)(2,1)}, u32[]{:S(2)}) copy-start(bf16[32,4096]{1,0:T(8,128)(2,1)} %pq_ref.1) | copy-start | bytes 786436
  24.7 24.0 %copy-start.5 = (bf16[32,512]{1,0:T(8,128)(2,1)S(1)}, bf16[32,512]{1,0:T(8,128)(2,1)}, u32[]{:S(2)}) copy-start(bf16[32,512]{1,0:T(8,128)(2,1)} %pk_ref.1) | copy-start | bytes 98308
  24.8 24.0 %copy-start.6 = (bf16[32,512]{1,0:T(8,128)(2,1)S(1)}, bf16[32,512]{1,0:T(8,128)(2,1)}, u32[]{:S(2)}) copy-start(bf16[32,512]{1,0:T(8,128)(2,1)} %pv_ref.1) | copy-start | bytes 98308
  25.6 1.3 %collective-permute-start = (f32[64,192]{1,0:T(8,128)S(1)}, f32[64,192]{1,0:T(8,128)S(1)}, u32[]{:S(2)}, u32[]{:S(2)}) collective-permute-start(f32[64,192]{1,0:T(8,128)S(1)} %fusion.mine_ref), channel_id=1, source_target_pairs={{0,1},{1,0},{2,3},{3,2},{4,5},{5,4},{6,7},{7,6},{8,9},{9,8},{10,11... | collective-permute-start | bytes 147464 | tf_op jit(solution)/shard_map/ppermute | solution.py:228
  48.7 22.5 %copy-start.10 = (bf16[1,64,4096]{2,1,0:T(8,128)(2,1)S(1)}, bf16[1,64,4096]{2,1,0:T(8,128)(2,1)}, u32[]{:S(2)}) copy-start(bf16[1,64,4096]{2,1,0:T(8,128)(2,1)} %param.26) | copy-start | bytes 1572868
  48.7 24.1 %copy-start.3 = (bf16[1,64,4096]{2,1,0:T(8,128)(2,1)S(1)}, bf16[1,64,4096]{2,1,0:T(8,128)(2,1)}, u32[]{:S(2)}) copy-start(bf16[1,64,4096]{2,1,0:T(8,128)(2,1)} %uo_ref.1) | copy-start | bytes 1572868
  71.5 1.3 %collective-permute-start.1 = (f32[64,64]{1,0:T(8,128)S(1)}, f32[64,64]{1,0:T(8,128)S(1)}, u32[]{:S(2)}, u32[]{:S(2)}) collective-permute-start(f32[64,64]{1,0:T(8,128)S(1)} %fusion.3.mine_ref), channel_id=1, source_target_pairs={{0,1},{1,0},{2,3},{3,2},{4,5},{5,4},{6,7},{7,6},{8,9},{9,8},{10,11... | collective-permute-start | bytes 49160 | tf_op jit(solution)/shard_map/ppermute | solution.py:228

commit v5 on v4

v5 whole, which is shorter than its diff:
```python
import functools

import jax
import jax.numpy as jnp
from jax import lax
from jax.experimental import pallas as pl
from jax.experimental.pallas import tpu as pltpu
from jax.sharding import PartitionSpec as P

ADAPTER_SCALE = 0.5
F32 = jnp.float32
BF16 = jnp.bfloat16
VMEM = pl.BlockSpec(memory_space=pltpu.VMEM)
SMEM = pl.BlockSpec(memory_space=pltpu.SMEM)
HBM = pl.BlockSpec(memory_space=pltpu.HBM)
DMA = pltpu.SemaphoreType.DMA


def call(body, out_shape, in_specs, out_specs=None, scratch=(), flops=0, moved=0, limit=58):
    return pl.pallas_call(
        body,
        out_shape=out_shape,
        in_specs=in_specs,
        out_specs=jax.tree.map(lambda _: VMEM, out_shape) if out_specs is None else out_specs,
        scratch_shapes=scratch,
        cost_estimate=pl.CostEstimate(flops=flops, bytes_accessed=moved, transcendentals=0),
        compiler_params=pltpu.CompilerParams(vmem_limit_bytes=limit * 1024 * 1024),
    )


def iota(shape, dim):
    return lax.broadcasted_iota(jnp.int32, shape, dim)


def dot(a, b):
    return lax.dot_general(a, b, (((1,), (0,)), ((), ())), preferred_element_type=F32)


def dot_t(a, b):
    return lax.dot_general(a, b, (((1,), (1,)), ((), ())), preferred_element_type=F32)


def scalars(read, rows):
    lane = iota((1, rows), 1)
    row = jnp.zeros((1, rows), jnp.int32)
    for r in range(rows):
        row = jnp.where(lane == r, read(r), row)
    return row


def joined(refs):
    if len(refs) == 1:
        return refs[0][...]
    return jnp.concatenate([ref[...].astype(F32) for ref in reversed(refs)], axis=0).astype(BF16)


def store_blocks(refs, value, columns=slice(None)):
    rows = value.shape[0] // len(refs)
    for i, ref in enumerate(refs):
        first = (len(refs) - 1 - i) * rows
        ref[:, columns] = value[first : first + rows].astype(BF16)


def pack_body(capacity, by_distance, tenant_hbm, slot_hbm, len_hbm, x_hbm, table_ref, *refs):
    packed_refs, (tenant_ref, slot_ref, len_ref, count_ref, x_ref, sems) = refs[:-6], refs[-6:]
    slots = sum(ref.shape[0] for ref in packed_refs)
    rows, width = x_ref.shape
    here = lax.axis_index("wide") if by_distance else 0
    start = pl.multiple_of(lax.axis_index("tp") * width, width)
    copies = [
        pltpu.make_async_copy(tenant_hbm, tenant_ref, sems.at[0]),
        pltpu.make_async_copy(slot_hbm, slot_ref, sems.at[1]),
        pltpu.make_async_copy(len_hbm, len_ref, sems.at[3]),
        pltpu.make_async_copy(x_hbm.at[:, pl.ds(start, width)], x_ref, sems.at[2]),
    ]
    for copy in copies:
        copy.start()
    for d in range(slots // capacity):
        count_ref[d] = 0
    for copy in copies[:3]:
        copy.wait()
    first = lax.axis_index("wide") * rows
    lane = iota((1, rows), 1)
    dest = jnp.zeros((1, rows), jnp.int32)
    for r in range(rows):
        holder = slot_ref[tenant_ref[first + r]]
        place = count_ref[holder]
        count_ref[holder] = place + 1
        slot = (holder ^ here) * capacity + place
        table_ref[r] = slot
        table_ref[rows + r] = len_ref[r]
        dest = jnp.where(lane == r, slot, dest)
    chosen = (iota((slots, rows), 0) == dest).astype(F32).astype(BF16)
    copies[3].wait()
    store_blocks(packed_refs, dot(chosen, x_ref[...]))


def down_body(ret_refs, down_ref, out_ref):
    rows = joined(ret_refs)
    width = rows.shape[1]
    start = pl.multiple_of(lax.axis_index("tp") * width, width)
    out_ref[...] = dot_t(rows, down_ref[0, :, pl.ds(start, width)])


def output_down_body(ret_refs, down_ref, out_ref):
    out_ref[...] = dot_t(joined(ret_refs), down_ref[0])


def up_body(group, mine_ref, other_ref, uq_ref, ukv_ref, *out_refs):
    rank = uq_ref.shape[1]
    total = (mine_ref[...] + other_ref[...]).astype(BF16)
    q_width = uq_ref.shape[2]
    width = ukv_ref.shape[3]
    store_blocks(out_refs, dot(total[:, :rank], uq_ref[0]), slice(0, q_width))
    for i in range(2):
        store_blocks(
            out_refs,
            dot(total[:, (i + 1) * rank : (i + 2) * rank], ukv_ref[0, i]),
            slice(q_width + i * width, q_width + (i + 1) * width),
        )


def prep_body(group, table_ref, bias_ref, take_ref, send_ref, home_ref):
    lines = bias_ref.shape[0]
    rows, slots = home_ref.shape
    shift = group.bit_length() - 1
    dest_row = scalars(lambda r: table_ref[r], rows)
    len_row = scalars(lambda r: table_ref[rows + r], rows)
    mine = (iota((lines, rows), 0) >> shift) == iota((lines, rows), 1)
    len_line = jnp.sum(jnp.where(mine, len_row, 0), axis=1, keepdims=True)
    eye = iota((rows, rows), 0) == iota((rows, rows), 1)
    dest_col = jnp.sum(jnp.where(eye, dest_row, 0), axis=1, keepdims=True)
    bias_ref[...] = jnp.where(iota(bias_ref.shape, 1) < len_line, 0.0, -jnp.inf)
    at_home = iota((rows, slots), 1) == dest_col
    take_ref[...] = jnp.where(at_home, ADAPTER_SCALE, 0.0).astype(BF16)
    send_ref[...] = (iota((slots, rows), 0) == dest_row).astype(F32).astype(BF16)
    home_ref[...] = at_home.astype(F32).astype(BF16)


def attend_body(
    group, ret_refs, k_ref, v_ref, pq_ref, pk_ref, pv_ref, bias_ref, take_ref, send_ref, home_ref, *refs,
):
    packed_refs, (context_ref, ret_ref, line_ref) = refs[:-3], refs[-3:]
    ret_ref[...] = joined(ret_refs)
    rows, heads, cache_size, head_dim = k_ref.shape
    take, send = take_ref[...], send_ref[...]
    bias = bias_ref[...]
    scale = head_dim ** (-0.5)
    k_base = heads * group * head_dim
    v_base = k_base + heads * head_dim

    def lines_of(slot, part):
        for h in range(group):
            line_ref[slot, pl.ds(h, rows, stride=group), :] = part(h)
        return line_ref[slot]

    for g in range(heads):
        slot = 4 * (g % 2)
        columns = slice(g * group * head_dim, (g + 1) * group * head_dim)
        query_rows = pq_ref[:, columns].astype(F32) + dot(take, ret_ref[:, columns])
        query = lines_of(slot, lambda h: query_rows[:, h * head_dim : (h + 1) * head_dim])
        query = query.astype(BF16).astype(F32)
        key_columns = slice(g * head_dim, (g + 1) * head_dim)
        new_key, new_value = (
            (
                plain[:, key_columns].astype(F32)
                + dot(take, ret_ref[:, base + g * head_dim : base + (g + 1) * head_dim])
            ).astype(BF16).astype(F32)
            for base, plain in ((k_base, pk_ref), (v_base, pv_ref))
        )
        new_key = lines_of(slot + 1, lambda h: new_key)
        new_value = lines_of(slot + 2, lambda h: new_value)
        own = jnp.sum(query * new_key, axis=1, keepdims=True) * scale
        score = jnp.concatenate(
            [dot_t(query[r * group : (r + 1) * group].astype(BF16), k_ref[r, g]) for r in range(rows)], axis=0
        )
        score = score * scale + bias
        highest = jnp.maximum(jnp.max(score, axis=1, keepdims=True), own)
        raised = jnp.exp(score - highest)
        own_raised = jnp.exp(own - highest)
        inverse = 1.0 / (jnp.sum(raised, axis=1, keepdims=True) + own_raised)
        weight = raised * inverse
        own_weight = (own_raised * inverse).astype(BF16).astype(F32)
        attended = jnp.concatenate(
            [dot(weight[r * group : (r + 1) * group].astype(BF16), v_ref[r, g]) for r in range(rows)], axis=0
        )
        line_ref[slot + 3] = attended + own_weight * new_value
        context = jnp.concatenate(
            [line_ref[slot + 3, pl.ds(h, rows, stride=group), :] for h in range(group)], axis=1
        ).astype(BF16)
        context_ref[:, columns] = context
        store_blocks(packed_refs, dot(send, context), columns)


def output_up_body(mine_ref, other_ref, uo_ref, *out_refs):
    total = (mine_ref[...] + other_ref[...]).astype(BF16)
    store_blocks(out_refs, ADAPTER_SCALE * dot(total, uo_ref[0]))


def unpack_body(home_ref, ret_refs, out_hbm, out_ref, sems):
    rows, width = out_ref.shape
    home = home_ref[...]
    returned = joined(ret_refs)
    parts = sems.shape[0]
    part = width // parts
    leaving = []
    for i in range(parts):
        columns = slice(i * part, (i + 1) * part)
        out_ref[:, columns] = dot(home, returned[:, columns]).astype(BF16)
        copy = pltpu.make_async_copy(out_ref.at[:, columns], out_hbm.at[:, columns], sems.at[i])
        copy.start()
        leaving.append(copy)
    for copy in leaving:
        copy.wait()


def exchange(blocks, wide_count):
    if len(blocks) == 1:
        slots, width = blocks[0].shape
        moved = lax.all_to_all(
            blocks[0].reshape(wide_count, slots // wide_count, width), "wide", split_axis=0, concat_axis=0, tiled=True
        )
        return (moved.reshape(slots, width),)
    moved = [
        lax.ppermute(block, "wide", [(k, k ^ (wide_count - 1 - i)) for k in range(wide_count)])
        for i, block in enumerate(blocks[:-1])
    ]
    return (*moved, blocks[-1])


def other_core(value):
    return lax.ppermute(value, "tp", [(0, 1), (1, 0)])


def shards(
    normed_layer_input,
    plain_query_rows,
    plain_key_rows,
    plain_value_rows,
    cached_key_rows,
    cached_value_rows,
    live_cache_length,
    tenant,
    slot_of_adapter,
    stacked_down_weight,
    query_up_weight,
    key_value_up_weight,
    output_down_weight,
    output_up_weight,
):
    wide_count = lax.axis_size("wide")
    rows, features = normed_layer_input.shape
    half = features // lax.axis_size("tp")
    capacity = max(2, 2 * rows // wide_count)
    slots = wide_count * capacity
    kv_heads, cache_size, head_dim = cached_key_rows.shape[1:]
    query_width = plain_query_rows.shape[1]
    group = query_width // head_dim // kv_heads
    lines = rows * group
    by_distance = wide_count <= 8 and wide_count & (wide_count - 1) == 0
    count = wide_count if by_distance else 1
    struct = jax.ShapeDtypeStruct

    def blocks_of(width):
        return [struct((slots // count, width), BF16)] * count


    table, *packed = call(
        functools.partial(pack_body, capacity, by_distance),
        (struct((2 * rows,), jnp.int32), *blocks_of(half)),
        [HBM] * 4,
        (SMEM, *[VMEM] * count),
        scratch=[
            pltpu.SMEM(tenant.shape, jnp.int32),
            pltpu.SMEM(slot_of_adapter.shape, jnp.int32),
            pltpu.SMEM((rows,), jnp.int32),
            pltpu.SMEM((wide_count,), jnp.int32),
            pltpu.VMEM((rows, half), BF16),
            DMA((4,)),
        ],
        flops=10**9,
        moved=40000000,
    )(tenant, slot_of_adapter, live_cache_length, normed_layer_input)
    received = exchange(packed, wide_count)
    rank_part = call(
        down_body, struct((slots, stacked_down_weight.shape[1]), F32), [(VMEM,) * count, VMEM], moved=4000000, limit=16
    )(received, stacked_down_weight)
    rank_other = other_core(rank_part)
    table, rank_part = lax.optimization_barrier((table, rank_part))
    prepared = (
        struct((lines, cache_size), F32),
        struct((rows, slots), BF16),
        struct((slots, rows), BF16),
        struct((rows, slots), BF16),
    )
    prepared = call(
        functools.partial(prep_body, group), prepared, [SMEM], flops=10**9, moved=20000000, limit=16
    )(table)
    rank_other, prepared = lax.optimization_barrier((rank_other, prepared))
    home = prepared[3]
    terms = call(
        functools.partial(up_body, group),
        blocks_of(kv_heads * (group + 2) * head_dim),
        [VMEM] * 4,
        moved=20000000,
        flops=10**9,
        limit=16,
    )(rank_part, rank_other, query_up_weight, key_value_up_weight)
    returned = exchange(terms, wide_count)
    *outgoing, context = call(
        functools.partial(attend_body, group),
        [*blocks_of(query_width), struct((rows, query_width), BF16)],
        [(VMEM,) * count] + [VMEM] * (5 + len(prepared)),
        scratch=[
            pltpu.VMEM((slots, kv_heads * (group + 2) * head_dim), BF16),
            pltpu.VMEM((8, lines, head_dim), F32),
        ],
        moved=8000000,
        limit=16,
    )(
        returned, cached_key_rows, cached_value_rows, plain_query_rows, plain_key_rows, plain_value_rows, *prepared
    )
    arrived = exchange(outgoing, wide_count)
    rank_o = call(
        output_down_body, struct((slots, output_down_weight.shape[1]), F32), [(VMEM,) * count, VMEM], moved=4000000, limit=16
    )(arrived, output_down_weight)
    out_terms = call(
        output_up_body, blocks_of(query_width), [VMEM] * 3, moved=1200000, limit=16
    )(rank_o, other_core(rank_o), output_up_weight)
    adapter_output_term = call(
        unpack_body, struct((rows, query_width), BF16), [VMEM, (VMEM,) * count], HBM,
        scratch=[pltpu.VMEM((rows, query_width), BF16), DMA((4,))], moved=1000000, limit=16,
    )(home, exchange(out_terms, wide_count))
    return context, adapter_output_term


def solution(mesh):
    return jax.shard_map(
        shards,
        mesh=mesh,
        in_specs=(
            P(("groups", "wide"), None),
            P(("groups", "wide"), "tp"),
            P(("groups", "wide"), "tp"),
            P(("groups", "wide"), "tp"),
            P(("groups", "wide"), "tp", None, None),
            P(("groups", "wide"), "tp", None, None),
            P(("groups", "wide")),
            P("groups"),
            P("groups"),
            P("wide", None, None),
            P("wide", None, "tp"),
            P("wide", None, None, "tp"),
            P("wide", None, "tp"),
            P("wide", None, "tp"),
        ),
        out_specs=(P(("groups", "wide"), "tp"), P(("groups", "wide"), "tp")),
        check_vma=False,
    )
```

time: 92.5 us -> 82.3 us (0.89)
  blocking collectives: 78.9 us -> 0 us
  starting transfers between devices: 0.14 us -> 52.1 us
  waiting for transfers between devices: 1.43 us -> 18.3 us
  matrix products: 1.08 us -> 0 us
    all_to_all x4 -> x0, blocking collectives: 78.9 us -> none  [exchange(): lax.all_to_all(rows.reshape(wide_count, slots // wide_count, width), 'wid...]
    ppermute x0 -> x28, starting transfers between devices: none -> 52 us  [exchange(): lax.ppermute(block, 'wide', [(k, k ^ wide_count - 1 - i) for k in range(w...]
    ppermute x0 -> x28, waiting for transfers between devices: none -> 16.6 us  [exchange(): lax.ppermute(block, 'wide', [(k, k ^ wide_count - 1 - i) for k in range(w...]
    dot_general x2 -> x0, matrix products: 1.08 us -> none  [dot_t(): lax.dot_general(a, b, (((1,), (1,)), ((), ())), preferred_element_type=F32)]
    pallas_call x6 -> x8, Pallas kernels: 9.72 us -> 9.97 us  [the longest x1 4.65 us: shards(): call(functools.partial(attend_body, group), [*blocks_of(query_width), str...]
  transfers between devices with their start and end apart: 2 -> 30, of which waited for: 2 -> 16; matrix products, arithmetic and copies ran while one was open for 0% -> 0% of each run, Pallas kernels for 1% -> 1%
where the time goes in v5:
time: 82.3 us; the launch traced here: 82.1 us
  starting transfers between devices  52.1 us (63%)
  waiting for transfers between devices  18.3 us (22%)
  Pallas kernels  9.97 us (12%)
  local copies, waits for them, and re-layouts  0.9 us (1%)
  between operations  0.83 us (1%)
    ppermute x28, starting transfers between devices, exchange(): lax.ppermute(block, 'wide', [(k, k ^ wide_count - 1 - i) for k in range(w...  52 us
    ppermute x28, waiting for transfers between devices, exchange(): lax.ppermute(block, 'wide', [(k, k ^ wide_count - 1 - i) for k in range(w...  16.6 us
    pallas_call x1, Pallas kernels, shards(): call(functools.partial(attend_body, group), [*blocks_of(query_width), str...  4.65 us
    pallas_call x1, Pallas kernels, shards(): call(functools.partial(pack_body, capacity, by_distance), (struct((2 * ro...  2.2 us
  transfers between devices with their start and end apart: 30, of which 16 were waited for; matrix products, arithmetic and copies ran while one was open for 0% of the time, Pallas kernels for 1%

profile of v5, /device:TPU:0, one launch (start us, length us, event | category | flops | bytes accessed | tf_op | source)
XLA Modules:
  0.0 82.1 jit_solution(6303963295133078372)
XLA Ops:
  0.6 2.2 %shard_map.149 = (s32[64]{0:T(128)}, bf16[8,4096]{1,0:T(8,128)(2,1)}, bf16[8,4096]{1,0:T(8,128)(2,1)}, bf16[8,4096]{1,0:T(8,128)(2,1)}, bf16[8,4096]{1,0:T(8,128...) custom-call(s32[256]{0:T(256)} %tenant_hbm.1, ...), custom_call_target="tpu_custom_call" | custom-call | flops 1000000000 | bytes 40000000 | tf_op jit(solution)/shard_map/pallas_call | solution.py:268
  2.9 6.1 %collective-permute-start = (bf16[8,4096]{1,0:T(8,128)(2,1)}, bf16[8,4096]{1,0:T(8,128)(2,1)S(1)}, u32[]{:S(2)}, u32[]{:S(2)}) collective-permute-start(bf16[8,4096]{1,0:T(8,128)(2,1)} %get-tuple-element.48), channel_id=1, source_target_pairs={{0,14},{2,12},{4,10},{6,8},{8,6},{10,4},{12,2},{14,0},{1,15},{3,13... | collective-permute-start | bytes 196616 | tf_op jit(solution)/shard_map/ppermute | solution.py:225
  8.9 0.2 collective-permute-start.1
  9.2 0.7 collective-permute-start.2
  9.9 2.0 %collective-permute-start.3 = (bf16[8,4096]{1,0:T(8,128)(2,1)}, bf16[8,4096]{1,0:T(8,128)(2,1)S(1)}, u32[]{:S(2)}, u32[]{:S(2)}) collective-permute-start(bf16[8,4096]{1,0:T(8,128)(2,1)} %get-tuple-element.51), channel_id=1, source_target_pairs={{0,8},{2,10},{4,12},{6,14},{8,0},{10,2},{12,4},{14,6},{1,9},{3,11}... | collective-permute-start | bytes 196616 | tf_op jit(solution)/shard_map/ppermute | solution.py:225
  11.9 2.3 %collective-permute-start.4 = (bf16[8,4096]{1,0:T(8,128)(2,1)}, bf16[8,4096]{1,0:T(8,128)(2,1)S(1)}, u32[]{:S(2)}, u32[]{:S(2)}) collective-permute-start(bf16[8,4096]{1,0:T(8,128)(2,1)} %get-tuple-element.52), channel_id=1, source_target_pairs={{0,6},{2,4},{4,2},{6,0},{8,14},{10,12},{12,10},{14,8},{1,7},{3,5},... | collective-permute-start | bytes 196616 | tf_op jit(solution)/shard_map/ppermute | solution.py:225
  14.2 0.0 collective-permute-done.ret_refs_0_
  14.2 0.8 collective-permute-start.5
  15.0 0.4 collective-permute-done.1.ret_refs_1_
  15.4 0.5 collective-permute-start.6
  15.9 3.4 %collective-permute-done.2.ret_refs_2_ = bf16[8,4096]{1,0:T(8,128)(2,1)S(1)} collective-permute-done((bf16[8,4096]{1,0:T(8,128)(2,1)}, bf16[8,4096]{1,0:T(8,128)(2,1)S(1)}, u32[]{:S(2)}, u32[]{:S(2)}) %collective-permute-start.2) | collective-permute-done | bytes 65568 | tf_op jit(solution)/shard_map/ppermute | solution.py:225
  19.3 1.1 %collective-permute-done.3.ret_refs_3_ = bf16[8,4096]{1,0:T(8,128)(2,1)S(1)} collective-permute-done((bf16[8,4096]{1,0:T(8,128)(2,1)}, bf16[8,4096]{1,0:T(8,128)(2,1)S(1)}, u32[]{:S(2)}, u32[]{:S(2)}) %collective-permute-start.3) | collective-permute-done | bytes 65568 | tf_op jit(solution)/shard_map/ppermute | solution.py:225
  20.4 0.0 collective-permute-done.4.ret_refs_4_
  20.4 0.4 collective-permute-done.5.ret_refs_5_
  20.8 0.8 %copy-done.6 = bf16[8,4096]{1,0:T(8,128)(2,1)S(1)} copy-done((bf16[8,4096]{1,0:T(8,128)(2,1)S(1)}, bf16[8,4096]{1,0:T(8,128)(2,1)}, u32[]{:S(2)}) %copy-start.6) | copy-done | bytes 65560
  21.7 0.6 shard_map.150.mine_ref
  22.3 0.1 collective-permute-start.7
  22.4 0.0 copy-start
  22.4 0.0 copy-start.1
  22.4 0.0 copy-start.5
  22.4 0.0 copy-start.7
  22.4 0.0 copy-start.8
  22.4 0.7 shard_map.151
  23.2 0.4 collective-permute-done.7.other_ref
  23.6 0.3 shard_map.152
  23.9 4.1 %collective-permute-start.8 = (bf16[8,5120]{1,0:T(8,128)(2,1)S(1)}, bf16[8,5120]{1,0:T(8,128)(2,1)S(1)}, u32[]{:S(2)}, u32[]{:S(2)}) collective-permute-start(bf16[8,5120]{1,0:T(8,128)(2,1)S(1)} %get-tuple-element.63), channel_id=1, source_target_pairs={{0,14},{2,12},{4,10},{6,8},{8,6},{10,4},{12,2},{14,0},{1,15},{3,13... | collective-permute-start | bytes 245768 | tf_op jit(solution)/shard_map/ppermute | solution.py:225
  28.0 0.0 collective-permute-start.9
  28.0 2.3 %collective-permute-start.10 = (bf16[8,5120]{1,0:T(8,128)(2,1)S(1)}, bf16[8,5120]{1,0:T(8,128)(2,1)S(1)}, u32[]{:S(2)}, u32[]{:S(2)}) collective-permute-start(bf16[8,5120]{1,0:T(8,128)(2,1)S(1)} %get-tuple-element.65), channel_id=1, source_target_pairs={{0,10},{2,8},{4,14},{6,12},{8,2},{10,0},{12,6},{14,4},{1,11},{3,9}... | collective-permute-start | bytes 245768 | tf_op jit(solution)/shard_map/ppermute | solution.py:225
  30.3 1.3 %collective-permute-start.11 = (bf16[8,5120]{1,0:T(8,128)(2,1)S(1)}, bf16[8,5120]{1,0:T(8,128)(2,1)S(1)}, u32[]{:S(2)}, u32[]{:S(2)}) collective-permute-start(bf16[8,5120]{1,0:T(8,128)(2,1)S(1)} %get-tuple-element.66), channel_id=1, source_target_pairs={{0,8},{2,10},{4,12},{6,14},{8,0},{10,2},{12,4},{14,6},{1,9},{3,11}... | collective-permute-start | bytes 245768 | tf_op jit(solution)/shard_map/ppermute | solution.py:225
  31.6 1.7 %collective-permute-start.12 = (bf16[8,5120]{1,0:T(8,128)(2,1)S(1)}, bf16[8,5120]{1,0:T(8,128)(2,1)S(1)}, u32[]{:S(2)}, u32[]{:S(2)}) collective-permute-start(bf16[8,5120]{1,0:T(8,128)(2,1)S(1)} %get-tuple-element.67), channel_id=1, source_target_pairs={{0,6},{2,4},{4,2},{6,0},{8,14},{10,12},{12,10},{14,8},{1,7},{3,5},... | collective-permute-start | bytes 245768 | tf_op jit(solution)/shard_map/ppermute | solution.py:225
  33.3 4.9 %collective-permute-start.13 = (bf16[8,5120]{1,0:T(8,128)(2,1)S(1)}, bf16[8,5120]{1,0:T(8,128)(2,1)S(1)}, u32[]{:S(2)}, u32[]{:S(2)}) collective-permute-start(bf16[8,5120]{1,0:T(8,128)(2,1)S(1)} %get-tuple-element.68), channel_id=1, source_target_pairs={{0,4},{2,6},{4,0},{6,2},{8,12},{10,14},{12,8},{14,10},{1,5},{3,7},... | collective-permute-start | bytes 245768 | tf_op jit(solution)/shard_map/ppermute | solution.py:225
  38.2 1.0 %collective-permute-start.14 = (bf16[8,5120]{1,0:T(8,128)(2,1)S(1)}, bf16[8,5120]{1,0:T(8,128)(2,1)S(1)}, u32[]{:S(2)}, u32[]{:S(2)}) collective-permute-start(bf16[8,5120]{1,0:T(8,128)(2,1)S(1)} %get-tuple-element.69), channel_id=1, source_target_pairs={{0,2},{2,0},{4,6},{6,4},{8,10},{10,8},{12,14},{14,12},{1,3},{3,1},... | collective-permute-start | bytes 245768 | tf_op jit(solution)/shard_map/ppermute | solution.py:225
  39.2 2.7 %collective-permute-done.10.ret_refs_2_ = bf16[8,5120]{1,0:T(8,128)(2,1)S(1)} collective-permute-done((bf16[8,5120]{1,0:T(8,128)(2,1)S(1)}, bf16[8,5120]{1,0:T(8,128)(2,1)S(1)}, u32[]{:S(2)}, u32[]{:S(2)}) %collective-permute-start.10) | collective-permute-done | bytes 81952 | tf_op jit(solution)/shard_map/ppermute | solution.py:225
  41.9 0.6 collective-permute-done.11.ret_refs_3_
  42.5 1.1 %collective-permute-done.13.ret_refs_5_ = bf16[8,5120]{1,0:T(8,128)(2,1)S(1)} collective-permute-done((bf16[8,5120]{1,0:T(8,128)(2,1)S(1)}, bf16[8,5120]{1,0:T(8,128)(2,1)S(1)}, u32[]{:S(2)}, u32[]{:S(2)}) %collective-permute-start.13) | collective-permute-done | bytes 81952 | tf_op jit(solution)/shard_map/ppermute | solution.py:225
  43.7 0.0 copy-start.4
  43.7 0.0 copy-start.3
  43.7 4.7 %shard_map.153 = (bf16[8,4096]{1,0:T(8,128)(2,1)S(1)}, bf16[8,4096]{1,0:T(8,128)(2,1)S(1)}, bf16[8,4096]{1,0:T(8,128)(2,1)S(1)}, bf16[8,4096]{1,0:T(8,128)(2,1)S...) custom-call(bf16[8,5120]{1,0:T(8,128)(2,1)S(1)} %collective-permute-, ...), custom_call_target="tpu_custom_call" | custom-call | bytes 8000000 | tf_op jit(solution)/shard_map/pallas_call | solution.py:310
  48.4 3.2 %collective-permute-start.15 = (bf16[8,4096]{1,0:T(8,128)(2,1)S(1)}, bf16[8,4096]{1,0:T(8,128)(2,1)S(1)}, u32[]{:S(2)}, u32[]{:S(2)}) collective-permute-start(bf16[8,4096]{1,0:T(8,128)(2,1)S(1)} %get-tuple-element.76), channel_id=1, source_target_pairs={{0,14},{2,12},{4,10},{6,8},{8,6},{10,4},{12,2},{14,0},{1,15},{3,13... | collective-permute-start | bytes 196616 | tf_op jit(solution)/shard_map/ppermute | solution.py:225
  51.6 1.2 %collective-permute-start.16 = (bf16[8,4096]{1,0:T(8,128)(2,1)S(1)}, bf16[8,4096]{1,0:T(8,128)(2,1)S(1)}, u32[]{:S(2)}, u32[]{:S(2)}) collective-permute-start(bf16[8,4096]{1,0:T(8,128)(2,1)S(1)} %get-tuple-element.77), channel_id=1, source_target_pairs={{0,12},{2,14},{4,8},{6,10},{8,4},{10,6},{12,0},{14,2},{1,13},{3,15... | collective-permute-start | bytes 196616 | tf_op jit(solution)/shard_map/ppermute | solution.py:225
  52.7 0.8 collective-permute-start.17
  53.5 2.6 %collective-permute-start.18 = (bf16[8,4096]{1,0:T(8,128)(2,1)S(1)}, bf16[8,4096]{1,0:T(8,128)(2,1)S(1)}, u32[]{:S(2)}, u32[]{:S(2)}) collective-permute-start(bf16[8,4096]{1,0:T(8,128)(2,1)S(1)} %get-tuple-element.79), channel_id=1, source_target_pairs={{0,8},{2,10},{4,12},{6,14},{8,0},{10,2},{12,4},{14,6},{1,9},{3,11}... | collective-permute-start | bytes 196616 | tf_op jit(solution)/shard_map/ppermute | solution.py:225
  56.0 0.8 collective-permute-start.19
  56.9 1.7 %collective-permute-start.20 = (bf16[8,4096]{1,0:T(8,128)(2,1)S(1)}, bf16[8,4096]{1,0:T(8,128)(2,1)S(1)}, u32[]{:S(2)}, u32[]{:S(2)}) collective-permute-start(bf16[8,4096]{1,0:T(8,128)(2,1)S(1)} %get-tuple-element.81), channel_id=1, source_target_pairs={{0,4},{2,6},{4,0},{6,2},{8,12},{10,14},{12,8},{14,10},{1,5},{3,7},... | collective-permute-start | bytes 196616 | tf_op jit(solution)/shard_map/ppermute | solution.py:225
  58.6 1.0 %collective-permute-start.21 = (bf16[8,4096]{1,0:T(8,128)(2,1)S(1)}, bf16[8,4096]{1,0:T(8,128)(2,1)S(1)}, u32[]{:S(2)}, u32[]{:S(2)}) collective-permute-start(bf16[8,4096]{1,0:T(8,128)(2,1)S(1)} %get-tuple-element.82), channel_id=1, source_target_pairs={{0,2},{2,0},{4,6},{6,4},{8,10},{10,8},{12,14},{14,12},{1,3},{3,1},... | collective-permute-start | bytes 196616 | tf_op jit(solution)/shard_map/ppermute | solution.py:225
  59.6 2.8 %collective-permute-done.17.ret_refs_2_ = bf16[8,4096]{1,0:T(8,128)(2,1)S(1)} collective-permute-done((bf16[8,4096]{1,0:T(8,128)(2,1)S(1)}, bf16[8,4096]{1,0:T(8,128)(2,1)S(1)}, u32[]{:S(2)}, u32[]{:S(2)}) %collective-permute-start.17) | collective-permute-done | bytes 65568 | tf_op jit(solution)/shard_map/ppermute | solution.py:225
  62.4 0.3 collective-permute-done.18.ret_refs_3_
  62.7 0.6 collective-permute-done.20.ret_refs_5_
  63.3 0.3 shard_map.154.mine_ref
  63.6 0.1 collective-permute-start.22
  63.7 1.2 %collective-permute-done.22.other_ref = f32[64,64]{1,0:T(8,128)S(1)} collective-permute-done((f32[64,64]{1,0:T(8,128)S(1)}, f32[64,64]{1,0:T(8,128)S(1)}, u32[]{:S(2)}, u32[]{:S(2)}) %collective-permute-start.22) | collective-permute-done | bytes 16416 | tf_op jit(solution)/shard_map/ppermute | solution.py:232
  64.9 0.3 shard_map.155
  65.2 4.1 %collective-permute-start.23 = (bf16[8,4096]{1,0:T(8,128)(2,1)S(1)}, bf16[8,4096]{1,0:T(8,128)(2,1)S(1)}, u32[]{:S(2)}, u32[]{:S(2)}) collective-permute-start(bf16[8,4096]{1,0:T(8,128)(2,1)S(1)} %get-tuple-element.84), channel_id=1, source_target_pairs={{0,14},{2,12},{4,10},{6,8},{8,6},{10,4},{12,2},{14,0},{1,15},{3,13... | collective-permute-start | bytes 196616 | tf_op jit(solution)/shard_map/ppermute | solution.py:225
  69.3 0.2 collective-permute-start.24
  69.5 2.2 %collective-permute-start.25 = (bf16[8,4096]{1,0:T(8,128)(2,1)S(1)}, bf16[8,4096]{1,0:T(8,128)(2,1)S(1)}, u32[]{:S(2)}, u32[]{:S(2)}) collective-permute-start(bf16[8,4096]{1,0:T(8,128)(2,1)S(1)} %get-tuple-element.86), channel_id=1, source_target_pairs={{0,10},{2,8},{4,14},{6,12},{8,2},{10,0},{12,6},{14,4},{1,11},{3,9}... | collective-permute-start | bytes 196616 | tf_op jit(solution)/shard_map/ppermute | solution.py:225
  71.7 1.2 %collective-permute-start.26 = (bf16[8,4096]{1,0:T(8,128)(2,1)S(1)}, bf16[8,4096]{1,0:T(8,128)(2,1)S(1)}, u32[]{:S(2)}, u32[]{:S(2)}) collective-permute-start(bf16[8,4096]{1,0:T(8,128)(2,1)S(1)} %get-tuple-element.87), channel_id=1, source_target_pairs={{0,8},{2,10},{4,12},{6,14},{8,0},{10,2},{12,4},{14,6},{1,9},{3,11}... | collective-permute-start | bytes 196616 | tf_op jit(solution)/shard_map/ppermute | solution.py:225
  72.9 1.7 %collective-permute-start.27 = (bf16[8,4096]{1,0:T(8,128)(2,1)S(1)}, bf16[8,4096]{1,0:T(8,128)(2,1)S(1)}, u32[]{:S(2)}, u32[]{:S(2)}) collective-permute-start(bf16[8,4096]{1,0:T(8,128)(2,1)S(1)} %get-tuple-element.88), channel_id=1, source_target_pairs={{0,6},{2,4},{4,2},{6,0},{8,14},{10,12},{12,10},{14,8},{1,7},{3,5},... | collective-permute-start | bytes 196616 | tf_op jit(solution)/shard_map/ppermute | solution.py:225
  74.6 0.8 collective-permute-start.28
  75.4 0.5 collective-permute-done.24.ret_refs_1_
  75.9 2.7 %collective-permute-start.29 = (bf16[8,4096]{1,0:T(8,128)(2,1)S(1)}, bf16[8,4096]{1,0:T(8,128)(2,1)S(1)}, u32[]{:S(2)}, u32[]{:S(2)}) collective-permute-start(bf16[8,4096]{1,0:T(8,128)(2,1)S(1)} %get-tuple-element.90), channel_id=1, source_target_pairs={{0,2},{2,0},{4,6},{6,4},{8,10},{10,8},{12,14},{14,12},{1,3},{3,1},... | collective-permute-start | bytes 196616 | tf_op jit(solution)/shard_map/ppermute | solution.py:225
  78.6 1.8 %collective-permute-done.25.ret_refs_2_ = bf16[8,4096]{1,0:T(8,128)(2,1)S(1)} collective-permute-done((bf16[8,4096]{1,0:T(8,128)(2,1)S(1)}, bf16[8,4096]{1,0:T(8,128)(2,1)S(1)}, u32[]{:S(2)}, u32[]{:S(2)}) %collective-permute-start.25) | collective-permute-done | bytes 65568 | tf_op jit(solution)/shard_map/ppermute | solution.py:225
  80.4 0.7 collective-permute-done.26.ret_refs_3_
  81.1 0.1 collective-permute-done.28.ret_refs_5_
  81.2 0.9 %shard_map.156 = bf16[32,4096]{1,0:T(8,128)(2,1)} custom-call(bf16[32,64]{1,0:T(8,128)(2,1)S(1)} %get-tuple-element.74.home_ref, bf16[8,4096]{1,0:T(8,128)(2,1)S(1)} %collective-permute-done.23.ret_refs_0_, bf16[8,4096]{1,0:T(8,128)(2,1)S(1)} %collective-permute-done.24.ret_refs_1_, bf16[8,4096]{1,0:T(8,128)(2,1)S(1)} %collective-permute-done.25.ret_refs_2_, ...), custom_call_target="tpu_custom_call" | custom-call | bytes 1000000 | tf_op jit(solution)/shard_map/pallas_call | solution.py:330
  (28 shorter events, 0.1 us)
Async XLA Ops:
  0.6 20.2 %copy-start.2 = (bf16[1,192,8192]{2,1,0:T(8,128)(2,1)S(1)}, bf16[1,192,8192]{2,1,0:T(8,128)(2,1)}, u32[]{:S(2)}) copy-start(bf16[1,192,8192]{2,1,0:T(8,128)(2,1)} %down_ref.2) | copy-start | bytes 9437188
  2.9 19.5 %copy-start.11 = (s32[64]{0:T(128)S(1)}, s32[64]{0:T(128)}, u32[]{:S(2)}) copy-start(s32[64]{0:T(128)} %get-tuple-element.57.table_ref) | copy-start | bytes 772
  2.9 11.4 %collective-permute-start = (bf16[8,4096]{1,0:T(8,128)(2,1)}, bf16[8,4096]{1,0:T(8,128)(2,1)S(1)}, u32[]{:S(2)}, u32[]{:S(2)}) collective-permute-start(bf16[8,4096]{1,0:T(8,128)(2,1)} %get-tuple-element.48), channel_id=1, source_target_pairs={{0,14},{2,12},{4,10},{6,8},{8,6},{10,4},{12,2},{14,0},{1,15},{3,13... | collective-permute-start | bytes 196616 | tf_op jit(solution)/shard_map/ppermute | solution.py:225
  8.9 6.5 %collective-permute-start.1 = (bf16[8,4096]{1,0:T(8,128)(2,1)}, bf16[8,4096]{1,0:T(8,128)(2,1)S(1)}, u32[]{:S(2)}, u32[]{:S(2)}) collective-permute-start(bf16[8,4096]{1,0:T(8,128)(2,1)} %get-tuple-element.49), channel_id=1, source_target_pairs={{0,12},{2,14},{4,8},{6,10},{8,4},{10,6},{12,0},{14,2},{1,13},{3,15... | collective-permute-start | bytes 196616 | tf_op jit(solution)/shard_map/ppermute | solution.py:225
  9.2 10.1 %collective-permute-start.2 = (bf16[8,4096]{1,0:T(8,128)(2,1)}, bf16[8,4096]{1,0:T(8,128)(2,1)S(1)}, u32[]{:S(2)}, u32[]{:S(2)}) collective-permute-start(bf16[8,4096]{1,0:T(8,128)(2,1)} %get-tuple-element.50), channel_id=1, source_target_pairs={{0,10},{2,8},{4,14},{6,12},{8,2},{10,0},{12,6},{14,4},{1,11},{3,9}... | collective-permute-start | bytes 196616 | tf_op jit(solution)/shard_map/ppermute | solution.py:225
  9.9 10.5 %collective-permute-start.3 = (bf16[8,4096]{1,0:T(8,128)(2,1)}, bf16[8,4096]{1,0:T(8,128)(2,1)S(1)}, u32[]{:S(2)}, u32[]{:S(2)}) collective-permute-start(bf16[8,4096]{1,0:T(8,128)(2,1)} %get-tuple-element.51), channel_id=1, source_target_pairs={{0,8},{2,10},{4,12},{6,14},{8,0},{10,2},{12,4},{14,6},{1,9},{3,11}... | collective-permute-start | bytes 196616 | tf_op jit(solution)/shard_map/ppermute | solution.py:225
  11.9 8.5 %collective-permute-start.4 = (bf16[8,4096]{1,0:T(8,128)(2,1)}, bf16[8,4096]{1,0:T(8,128)(2,1)S(1)}, u32[]{:S(2)}, u32[]{:S(2)}) collective-permute-start(bf16[8,4096]{1,0:T(8,128)(2,1)} %get-tuple-element.52), channel_id=1, source_target_pairs={{0,6},{2,4},{4,2},{6,0},{8,14},{10,12},{12,10},{14,8},{1,7},{3,5},... | collective-permute-start | bytes 196616 | tf_op jit(solution)/shard_map/ppermute | solution.py:225
  14.2 6.6 %collective-permute-start.5 = (bf16[8,4096]{1,0:T(8,128)(2,1)}, bf16[8,4096]{1,0:T(8,128)(2,1)S(1)}, u32[]{:S(2)}, u32[]{:S(2)}) collective-permute-start(bf16[8,4096]{1,0:T(8,128)(2,1)} %get-tuple-element.53), channel_id=1, source_target_pairs={{0,4},{2,6},{4,0},{6,2},{8,12},{10,14},{12,8},{14,10},{1,5},{3,7},... | collective-permute-start | bytes 196616 | tf_op jit(solution)/shard_map/ppermute | solution.py:225
  15.4 5.4 %collective-permute-start.6 = (bf16[8,4096]{1,0:T(8,128)(2,1)}, bf16[8,4096]{1,0:T(8,128)(2,1)S(1)}, u32[]{:S(2)}, u32[]{:S(2)}) collective-permute-start(bf16[8,4096]{1,0:T(8,128)(2,1)} %get-tuple-element.54), channel_id=1, source_target_pairs={{0,2},{2,0},{4,6},{6,4},{8,10},{10,8},{12,14},{14,12},{1,3},{3,1},... | collective-permute-start | bytes 196616 | tf_op jit(solution)/shard_map/ppermute | solution.py:225
  20.8 0.8 %copy-start.6 = (bf16[8,4096]{1,0:T(8,128)(2,1)S(1)}, bf16[8,4096]{1,0:T(8,128)(2,1)}, u32[]{:S(2)}) copy-start(bf16[8,4096]{1,0:T(8,128)(2,1)} %get-tuple-element.55.ret_refs_7_) | copy-start | bytes 196612
  21.7 1.9 %copy-start.9 = (bf16[1,64,4096]{2,1,0:T(8,128)(2,1)S(1)}, bf16[1,64,4096]{2,1,0:T(8,128)(2,1)}, u32[]{:S(2)}) copy-start(bf16[1,64,4096]{2,1,0:T(8,128)(2,1)} %uq_ref.1) | copy-start | bytes 1572868
  21.7 2.0 %copy-start.10 = (bf16[1,2,64,512]{3,2,1,0:T(8,128)(2,1)S(1)}, bf16[1,2,64,512]{3,2,1,0:T(8,128)(2,1)}, u32[]{:S(2)}) copy-start(bf16[1,2,64,512]{3,2,1,0:T(8,128)(2,1)} %ukv_ref.1) | copy-start | bytes 393220
  22.3 1.3 %collective-permute-start.7 = (f32[64,192]{1,0:T(8,128)S(1)}, f32[64,192]{1,0:T(8,128)S(1)}, u32[]{:S(2)}, u32[]{:S(2)}) collective-permute-start(f32[64,192]{1,0:T(8,128)S(1)} %shard_map.150.mine_ref), channel_id=1, source_target_pairs={{0,1},{1,0},{2,3},{3,2},{4,5},{5,4},{6,7},{7,6},{8,9},{9,8},{10,11... | collective-permute-start | bytes 147464 | tf_op jit(solution)/shard_map/ppermute | solution.py:232
  22.4 21.3 %copy-start = (bf16[32,4,96,128]{3,2,1,0:T(8,128)(2,1)S(1)}, bf16[32,4,96,128]{3,2,1,0:T(8,128)(2,1)}, u32[]{:S(2)}) copy-start(bf16[32,4,96,128]{3,2,1,0:T(8,128)(2,1)} %k_ref.1) | copy-start | bytes 9437188
  22.4 21.3 %copy-start.1 = (bf16[32,4,96,128]{3,2,1,0:T(8,128)(2,1)S(1)}, bf16[32,4,96,128]{3,2,1,0:T(8,128)(2,1)}, u32[]{:S(2)}) copy-start(bf16[32,4,96,128]{3,2,1,0:T(8,128)(2,1)} %v_ref.1) | copy-start | bytes 9437188
  22.4 21.3 %copy-start.5 = (bf16[32,4096]{1,0:T(8,128)(2,1)S(1)}, bf16[32,4096]{1,0:T(8,128)(2,1)}, u32[]{:S(2)}) copy-start(bf16[32,4096]{1,0:T(8,128)(2,1)} %pq_ref.1) | copy-start | bytes 786436
  22.4 21.3 %copy-start.7 = (bf16[32,512]{1,0:T(8,128)(2,1)S(1)}, bf16[32,512]{1,0:T(8,128)(2,1)}, u32[]{:S(2)}) copy-start(bf16[32,512]{1,0:T(8,128)(2,1)} %pk_ref.1) | copy-start | bytes 98308
  22.4 21.3 %copy-start.8 = (bf16[32,512]{1,0:T(8,128)(2,1)S(1)}, bf16[32,512]{1,0:T(8,128)(2,1)}, u32[]{:S(2)}) copy-start(bf16[32,512]{1,0:T(8,128)(2,1)} %pv_ref.1) | copy-start | bytes 98308
  23.9 9.4 %collective-permute-start.8 = (bf16[8,5120]{1,0:T(8,128)(2,1)S(1)}, bf16[8,5120]{1,0:T(8,128)(2,1)S(1)}, u32[]{:S(2)}, u32[]{:S(2)}) collective-permute-start(bf16[8,5120]{1,0:T(8,128)(2,1)S(1)} %get-tuple-element.63), channel_id=1, source_target_pairs={{0,14},{2,12},{4,10},{6,8},{8,6},{10,4},{12,2},{14,0},{1,15},{3,13... | collective-permute-start | bytes 245768 | tf_op jit(solution)/shard_map/ppermute | solution.py:225
  28.0 10.2 %collective-permute-start.9 = (bf16[8,5120]{1,0:T(8,128)(2,1)S(1)}, bf16[8,5120]{1,0:T(8,128)(2,1)S(1)}, u32[]{:S(2)}, u32[]{:S(2)}) collective-permute-start(bf16[8,5120]{1,0:T(8,128)(2,1)S(1)} %get-tuple-element.64), channel_id=1, source_target_pairs={{0,12},{2,14},{4,8},{6,10},{8,4},{10,6},{12,0},{14,2},{1,13},{3,15... | collective-permute-start | bytes 245768 | tf_op jit(solution)/shard_map/ppermute | solution.py:225
  28.0 13.9 %collective-permute-start.10 = (bf16[8,5120]{1,0:T(8,128)(2,1)S(1)}, bf16[8,5120]{1,0:T(8,128)(2,1)S(1)}, u32[]{:S(2)}, u32[]{:S(2)}) collective-permute-start(bf16[8,5120]{1,0:T(8,128)(2,1)S(1)} %get-tuple-element.65), channel_id=1, source_target_pairs={{0,10},{2,8},{4,14},{6,12},{8,2},{10,0},{12,6},{14,4},{1,11},{3,9}... | collective-permute-start | bytes 245768 | tf_op jit(solution)/shard_map/ppermute | solution.py:225
  30.3 12.2 %collective-permute-start.11 = (bf16[8,5120]{1,0:T(8,128)(2,1)S(1)}, bf16[8,5120]{1,0:T(8,128)(2,1)S(1)}, u32[]{:S(2)}, u32[]{:S(2)}) collective-permute-start(bf16[8,5120]{1,0:T(8,128)(2,1)S(1)} %get-tuple-element.66), channel_id=1, source_target_pairs={{0,8},{2,10},{4,12},{6,14},{8,0},{10,2},{12,4},{14,6},{1,9},{3,11}... | collective-permute-start | bytes 245768 | tf_op jit(solution)/shard_map/ppermute | solution.py:225
  31.6 10.9 %collective-permute-start.12 = (bf16[8,5120]{1,0:T(8,128)(2,1)S(1)}, bf16[8,5120]{1,0:T(8,128)(2,1)S(1)}, u32[]{:S(2)}, u32[]{:S(2)}) collective-permute-start(bf16[8,5120]{1,0:T(8,128)(2,1)S(1)} %get-tuple-element.67), channel_id=1, source_target_pairs={{0,6},{2,4},{4,2},{6,0},{8,14},{10,12},{12,10},{14,8},{1,7},{3,5},... | collective-permute-start | bytes 245768 | tf_op jit(solution)/shard_map/ppermute | solution.py:225
  33.3 10.4 %collective-permute-start.13 = (bf16[8,5120]{1,0:T(8,128)(2,1)S(1)}, bf16[8,5120]{1,0:T(8,128)(2,1)S(1)}, u32[]{:S(2)}, u32[]{:S(2)}) collective-permute-start(bf16[8,5120]{1,0:T(8,128)(2,1)S(1)} %get-tuple-element.68), channel_id=1, source_target_pairs={{0,4},{2,6},{4,0},{6,2},{8,12},{10,14},{12,8},{14,10},{1,5},{3,7},... | collective-permute-start | bytes 245768 | tf_op jit(solution)/shard_map/ppermute | solution.py:225
  38.2 5.5 %collective-permute-start.14 = (bf16[8,5120]{1,0:T(8,128)(2,1)S(1)}, bf16[8,5120]{1,0:T(8,128)(2,1)S(1)}, u32[]{:S(2)}, u32[]{:S(2)}) collective-permute-start(bf16[8,5120]{1,0:T(8,128)(2,1)S(1)} %get-tuple-element.69), channel_id=1, source_target_pairs={{0,2},{2,0},{4,6},{6,4},{8,10},{10,8},{12,14},{14,12},{1,3},{3,1},... | collective-permute-start | bytes 245768 | tf_op jit(solution)/shard_map/ppermute | solution.py:225
  43.7 19.6 %copy-start.4 = (bf16[1,64,4096]{2,1,0:T(8,128)(2,1)S(1)}, bf16[1,64,4096]{2,1,0:T(8,128)(2,1)}, u32[]{:S(2)}) copy-start(bf16[1,64,4096]{2,1,0:T(8,128)(2,1)} %down_ref.3) | copy-start | bytes 1572868
  43.7 21.2 %copy-start.3 = (bf16[1,64,4096]{2,1,0:T(8,128)(2,1)S(1)}, bf16[1,64,4096]{2,1,0:T(8,128)(2,1)}, u32[]{:S(2)}) copy-start(bf16[1,64,4096]{2,1,0:T(8,128)(2,1)} %uo_ref.1) | copy-start | bytes 1572868
  48.4 8.5 %collective-permute-start.15 = (bf16[8,4096]{1,0:T(8,128)(2,1)S(1)}, bf16[8,4096]{1,0:T(8,128)(2,1)S(1)}, u32[]{:S(2)}, u32[]{:S(2)}) collective-permute-start(bf16[8,4096]{1,0:T(8,128)(2,1)S(1)} %get-tuple-element.76), channel_id=1, source_target_pairs={{0,14},{2,12},{4,10},{6,8},{8,6},{10,4},{12,2},{14,0},{1,15},{3,13... | collective-permute-start | bytes 196616 | tf_op jit(solution)/shard_map/ppermute | solution.py:225
  51.6 7.0 %collective-permute-start.16 = (bf16[8,4096]{1,0:T(8,128)(2,1)S(1)}, bf16[8,4096]{1,0:T(8,128)(2,1)S(1)}, u32[]{:S(2)}, u32[]{:S(2)}) collective-permute-start(bf16[8,4096]{1,0:T(8,128)(2,1)S(1)} %get-tuple-element.77), channel_id=1, source_target_pairs={{0,12},{2,14},{4,8},{6,10},{8,4},{10,6},{12,0},{14,2},{1,13},{3,15... | collective-permute-start | bytes 196616 | tf_op jit(solution)/shard_map/ppermute | solution.py:225
  52.7 9.7 %collective-permute-start.17 = (bf16[8,4096]{1,0:T(8,128)(2,1)S(1)}, bf16[8,4096]{1,0:T(8,128)(2,1)S(1)}, u32[]{:S(2)}, u32[]{:S(2)}) collective-permute-start(bf16[8,4096]{1,0:T(8,128)(2,1)S(1)} %get-tuple-element.78), channel_id=1, source_target_pairs={{0,10},{2,8},{4,14},{6,12},{8,2},{10,0},{12,6},{14,4},{1,11},{3,9}... | collective-permute-start | bytes 196616 | tf_op jit(solution)/shard_map/ppermute | solution.py:225
  53.5 9.2 %collective-permute-start.18 = (bf16[8,4096]{1,0:T(8,128)(2,1)S(1)}, bf16[8,4096]{1,0:T(8,128)(2,1)S(1)}, u32[]{:S(2)}, u32[]{:S(2)}) collective-permute-start(bf16[8,4096]{1,0:T(8,128)(2,1)S(1)} %get-tuple-element.79), channel_id=1, source_target_pairs={{0,8},{2,10},{4,12},{6,14},{8,0},{10,2},{12,4},{14,6},{1,9},{3,11}... | collective-permute-start | bytes 196616 | tf_op jit(solution)/shard_map/ppermute | solution.py:225
  56.0 6.7 %collective-permute-start.19 = (bf16[8,4096]{1,0:T(8,128)(2,1)S(1)}, bf16[8,4096]{1,0:T(8,128)(2,1)S(1)}, u32[]{:S(2)}, u32[]{:S(2)}) collective-permute-start(bf16[8,4096]{1,0:T(8,128)(2,1)S(1)} %get-tuple-element.80), channel_id=1, source_target_pairs={{0,6},{2,4},{4,2},{6,0},{8,14},{10,12},{12,10},{14,8},{1,7},{3,5},... | collective-permute-start | bytes 196616 | tf_op jit(solution)/shard_map/ppermute | solution.py:225
  56.9 6.5 %collective-permute-start.20 = (bf16[8,4096]{1,0:T(8,128)(2,1)S(1)}, bf16[8,4096]{1,0:T(8,128)(2,1)S(1)}, u32[]{:S(2)}, u32[]{:S(2)}) collective-permute-start(bf16[8,4096]{1,0:T(8,128)(2,1)S(1)} %get-tuple-element.81), channel_id=1, source_target_pairs={{0,4},{2,6},{4,0},{6,2},{8,12},{10,14},{12,8},{14,10},{1,5},{3,7},... | collective-permute-start | bytes 196616 | tf_op jit(solution)/shard_map/ppermute | solution.py:225
  58.6 4.7 %collective-permute-start.21 = (bf16[8,4096]{1,0:T(8,128)(2,1)S(1)}, bf16[8,4096]{1,0:T(8,128)(2,1)S(1)}, u32[]{:S(2)}, u32[]{:S(2)}) collective-permute-start(bf16[8,4096]{1,0:T(8,128)(2,1)S(1)} %get-tuple-element.82), channel_id=1, source_target_pairs={{0,2},{2,0},{4,6},{6,4},{8,10},{10,8},{12,14},{14,12},{1,3},{3,1},... | collective-permute-start | bytes 196616 | tf_op jit(solution)/shard_map/ppermute | solution.py:225
  63.6 1.3 %collective-permute-start.22 = (f32[64,64]{1,0:T(8,128)S(1)}, f32[64,64]{1,0:T(8,128)S(1)}, u32[]{:S(2)}, u32[]{:S(2)}) collective-permute-start(f32[64,64]{1,0:T(8,128)S(1)} %shard_map.154.mine_ref), channel_id=1, source_target_pairs={{0,1},{1,0},{2,3},{3,2},{4,5},{5,4},{6,7},{7,6},{8,9},{9,8},{10,11... | collective-permute-start | bytes 49160 | tf_op jit(solution)/shard_map/ppermute | solution.py:232
  65.2 9.4 %collective-permute-start.23 = (bf16[8,4096]{1,0:T(8,128)(2,1)S(1)}, bf16[8,4096]{1,0:T(8,128)(2,1)S(1)}, u32[]{:S(2)}, u32[]{:S(2)}) collective-permute-start(bf16[8,4096]{1,0:T(8,128)(2,1)S(1)} %get-tuple-element.84), channel_id=1, source_target_pairs={{0,14},{2,12},{4,10},{6,8},{8,6},{10,4},{12,2},{14,0},{1,15},{3,13... | collective-permute-start | bytes 196616 | tf_op jit(solution)/shard_map/ppermute | solution.py:225
  69.3 6.6 %collective-permute-start.24 = (bf16[8,4096]{1,0:T(8,128)(2,1)S(1)}, bf16[8,4096]{1,0:T(8,128)(2,1)S(1)}, u32[]{:S(2)}, u32[]{:S(2)}) collective-permute-start(bf16[8,4096]{1,0:T(8,128)(2,1)S(1)} %get-tuple-element.85), channel_id=1, source_target_pairs={{0,12},{2,14},{4,8},{6,10},{8,4},{10,6},{12,0},{14,2},{1,13},{3,15... | collective-permute-start | bytes 196616 | tf_op jit(solution)/shard_map/ppermute | solution.py:225
  69.5 10.9 %collective-permute-start.25 = (bf16[8,4096]{1,0:T(8,128)(2,1)S(1)}, bf16[8,4096]{1,0:T(8,128)(2,1)S(1)}, u32[]{:S(2)}, u32[]{:S(2)}) collective-permute-start(bf16[8,4096]{1,0:T(8,128)(2,1)S(1)} %get-tuple-element.86), channel_id=1, source_target_pairs={{0,10},{2,8},{4,14},{6,12},{8,2},{10,0},{12,6},{14,4},{1,11},{3,9}... | collective-permute-start | bytes 196616 | tf_op jit(solution)/shard_map/ppermute | solution.py:225
  71.7 9.4 %collective-permute-start.26 = (bf16[8,4096]{1,0:T(8,128)(2,1)S(1)}, bf16[8,4096]{1,0:T(8,128)(2,1)S(1)}, u32[]{:S(2)}, u32[]{:S(2)}) collective-permute-start(bf16[8,4096]{1,0:T(8,128)(2,1)S(1)} %get-tuple-element.87), channel_id=1, source_target_pairs={{0,8},{2,10},{4,12},{6,14},{8,0},{10,2},{12,4},{14,6},{1,9},{3,11}... | collective-permute-start | bytes 196616 | tf_op jit(solution)/shard_map/ppermute | solution.py:225
  72.9 8.2 %collective-permute-start.27 = (bf16[8,4096]{1,0:T(8,128)(2,1)S(1)}, bf16[8,4096]{1,0:T(8,128)(2,1)S(1)}, u32[]{:S(2)}, u32[]{:S(2)}) collective-permute-start(bf16[8,4096]{1,0:T(8,128)(2,1)S(1)} %get-tuple-element.88), channel_id=1, source_target_pairs={{0,6},{2,4},{4,2},{6,0},{8,14},{10,12},{12,10},{14,8},{1,7},{3,5},... | collective-permute-start | bytes 196616 | tf_op jit(solution)/shard_map/ppermute | solution.py:225
  74.6 6.6 %collective-permute-start.28 = (bf16[8,4096]{1,0:T(8,128)(2,1)S(1)}, bf16[8,4096]{1,0:T(8,128)(2,1)S(1)}, u32[]{:S(2)}, u32[]{:S(2)}) collective-permute-start(bf16[8,4096]{1,0:T(8,128)(2,1)S(1)} %get-tuple-element.89), channel_id=1, source_target_pairs={{0,4},{2,6},{4,0},{6,2},{8,12},{10,14},{12,8},{14,10},{1,5},{3,7},... | collective-permute-start | bytes 196616 | tf_op jit(solution)/shard_map/ppermute | solution.py:225
  75.9 5.3 %collective-permute-start.29 = (bf16[8,4096]{1,0:T(8,128)(2,1)S(1)}, bf16[8,4096]{1,0:T(8,128)(2,1)S(1)}, u32[]{:S(2)}, u32[]{:S(2)}) collective-permute-start(bf16[8,4096]{1,0:T(8,128)(2,1)S(1)} %get-tuple-element.90), channel_id=1, source_target_pairs={{0,2},{2,0},{4,6},{6,4},{8,10},{10,8},{12,14},{14,12},{1,3},{3,1},... | collective-permute-start | bytes 196616 | tf_op jit(solution)/shard_map/ppermute | solution.py:225

commit v6 on v5

--- a/solution.py
+++ b/solution.py
@@ -48,21 +48,25 @@
     return row
 
 
+def distances(count):
+    return sorted(range(1, count), key=lambda d: (d >> 1 & 1, d), reverse=True) + [0]
+
+
 def joined(refs):
     if len(refs) == 1:
         return refs[0][...]
-    return jnp.concatenate([ref[...].astype(F32) for ref in reversed(refs)], axis=0).astype(BF16)
+    listed = sorted(zip(distances(len(refs)), refs), key=lambda pair: pair[0])
+    return jnp.concatenate([ref[...].astype(F32) for _, ref in listed], axis=0).astype(BF16)
 
 
 def store_blocks(refs, value, columns=slice(None)):
     rows = value.shape[0] // len(refs)
-    for i, ref in enumerate(refs):
-        first = (len(refs) - 1 - i) * rows
-        ref[:, columns] = value[first : first + rows].astype(BF16)
+    for d, ref in zip(distances(len(refs)), refs):
+        ref[:, columns] = value[d * rows : (d + 1) * rows].astype(BF16)
 
 
 def pack_body(capacity, by_distance, tenant_hbm, slot_hbm, len_hbm, x_hbm, table_ref, *refs):
-    packed_refs, (tenant_ref, slot_ref, len_ref, count_ref, x_ref, sems) = refs[:-6], refs[-6:]
+    packed_refs, (tenant_ref, slot_ref, len_ref, x_ref, sems) = refs[:-5], refs[-5:]
     slots = sum(ref.shape[0] for ref in packed_refs)
     rows, width = x_ref.shape
     here = lax.axis_index("wide") if by_distance else 0
@@ -75,21 +79,17 @@
     ]
     for copy in copies:
         copy.start()
-    for d in range(slots // capacity):
-        count_ref[d] = 0
     for copy in copies[:3]:
         copy.wait()
     first = lax.axis_index("wide") * rows
-    lane = iota((1, rows), 1)
-    dest = jnp.zeros((1, rows), jnp.int32)
-    for r in range(rows):
-        holder = slot_ref[tenant_ref[first + r]]
-        place = count_ref[holder]
-        count_ref[holder] = place + 1
-        slot = (holder ^ here) * capacity + place
-        table_ref[r] = slot
-        table_ref[rows + r] = len_ref[r]
-        dest = jnp.where(lane == r, slot, dest)
+    holder = scalars(lambda r: slot_ref[tenant_ref[first + r]], rows)
+    sublane, lane = iota((rows, rows), 0), iota((rows, rows), 1)
+    holder_col = jnp.sum(jnp.where(sublane == lane, holder, 0), axis=1, keepdims=True)
+    earlier = (holder_col == holder) & (sublane < lane)
+    place = jnp.sum(earlier.astype(jnp.int32), axis=0, keepdims=True)
+    dest = (holder ^ here) * capacity + place
+    table_ref[0:1] = dest
+    table_ref[1:2] = scalars(lambda r: len_ref[r], rows)
     chosen = (iota((slots, rows), 0) == dest).astype(F32).astype(BF16)
     copies[3].wait()
     store_blocks(packed_refs, dot(chosen, x_ref[...]))
@@ -124,8 +124,7 @@
     lines = bias_ref.shape[0]
     rows, slots = home_ref.shape
     shift = group.bit_length() - 1
-    dest_row = scalars(lambda r: table_ref[r], rows)
-    len_row = scalars(lambda r: table_ref[rows + r], rows)
+    dest_row, len_row = table_ref[0:1], table_ref[1:2]
     mine = (iota((lines, rows), 0) >> shift) == iota((lines, rows), 1)
     len_line = jnp.sum(jnp.where(mine, len_row, 0), axis=1, keepdims=True)
     eye = iota((rows, rows), 0) == iota((rows, rows), 1)
@@ -153,6 +152,12 @@
         for h in range(group):
             line_ref[slot, pl.ds(h, rows, stride=group), :] = part(h)
         return line_ref[slot]
+
+    def beside(value, r, side):
+        lines = value[r * group : (r + 1) * group]
+        pair = [jnp.zeros_like(lines)] * 2
+        pair[side] = lines
+        return jnp.concatenate(pair, axis=1)
 
     for g in range(heads):
         slot = 4 * (g % 2)
@@ -172,7 +177,14 @@
         new_value = lines_of(slot + 2, lambda h: new_value)
         own = jnp.sum(query * new_key, axis=1, keepdims=True) * scale
         score = jnp.concatenate(
-            [dot_t(query[r * group : (r + 1) * group].astype(BF16), k_ref[r, g]) for r in range(rows)], axis=0
+            [
+                dot_t(
+                    jnp.concatenate([beside(query, r, 0), beside(query, r + 1, 1)], axis=0).astype(BF16),
+                    jnp.concatenate([k_ref[r, g], k_ref[r + 1, g]], axis=1),
+                )
+                for r in range(0, rows, 2)
+            ],
+            axis=0,
         )
         score = score * scale + bias
         highest = jnp.maximum(jnp.max(score, axis=1, keepdims=True), own)
@@ -222,8 +234,8 @@
         )
         return (moved.reshape(slots, width),)
     moved = [
-        lax.ppermute(block, "wide", [(k, k ^ (wide_count - 1 - i)) for k in range(wide_count)])
-        for i, block in enumerate(blocks[:-1])
+        lax.ppermute(block, "wide", [(k, k ^ d) for k in range(wide_count)])
+        for d, block in zip(distances(wide_count), blocks[:-1])
     ]
     return (*moved, blocks[-1])
 
@@ -267,14 +279,12 @@
 
     table, *packed = call(
         functools.partial(pack_body, capacity, by_distance),
-        (struct((2 * rows,), jnp.int32), *blocks_of(half)),
+        (struct((2, rows), jnp.int32), *blocks_of(half)),
         [HBM] * 4,
-        (SMEM, *[VMEM] * count),
         scratch=[
             pltpu.SMEM(tenant.shape, jnp.int32),
             pltpu.SMEM(slot_of_adapter.shape, jnp.int32),
             pltpu.SMEM((rows,), jnp.int32),
-            pltpu.SMEM((wide_count,), jnp.int32),
             pltpu.VMEM((rows, half), BF16),
             DMA((4,)),
         ],
@@ -282,11 +292,6 @@
         moved=40000000,
     )(tenant, slot_of_adapter, live_cache_length, normed_layer_input)
     received = exchange(packed, wide_count)
-    rank_part = call(
-        down_body, struct((slots, stacked_down_weight.shape[1]), F32), [(VMEM,) * count, VMEM], moved=4000000, limit=16
-    )(received, stacked_down_weight)
-    rank_other = other_core(rank_part)
-    table, rank_part = lax.optimization_barrier((table, rank_part))
     prepared = (
         struct((lines, cache_size), F32),
         struct((rows, slots), BF16),
@@ -294,9 +299,13 @@
         struct((rows, slots), BF16),
     )
     prepared = call(
-        functools.partial(prep_body, group), prepared, [SMEM], flops=10**9, moved=20000000, limit=16
+        functools.partial(prep_body, group), prepared, [VMEM], flops=10**9, moved=20000000, limit=16
     )(table)
-    rank_other, prepared = lax.optimization_barrier((rank_other, prepared))
+    received, prepared = lax.optimization_barrier((received, prepared))
+    rank_part = call(
+        down_body, struct((slots, stacked_down_weight.shape[1]), F32), [(VMEM,) * count, VMEM], moved=4000000, limit=16
+    )(received, stacked_down_weight)
+    rank_other = other_core(rank_part)
     home = prepared[3]
     terms = call(
         functools.partial(up_body, group),

time: 82.3 us -> 77.7 us (0.944)
  starting transfers between devices: 52.1 us -> 45.9 us
  waiting for transfers between devices: 18.3 us -> 21 us
  Pallas kernels: 9.97 us -> 9.08 us
    ppermute x28, starting transfers between devices: 52 us -> 45.8 us  [exchange(): lax.ppermute(block, 'wide', [(k, k ^ d) for k in range(wide_count)])]
    ppermute x28, waiting for transfers between devices: 16.6 us -> 18.5 us  [exchange(): lax.ppermute(block, 'wide', [(k, k ^ d) for k in range(wide_count)])]
  transfers between devices with their start and end apart: 30 -> 30, of which waited for: 16 -> 15; matrix products, arithmetic and copies ran while one was open for 0% -> 0% of each run, Pallas kernels for 1% -> 0%
where the time goes in v6:
time: 77.7 us; the launch traced here: 77.5 us
  starting transfers between devices  45.9 us (59%)
  waiting for transfers between devices  21 us (27%)
  Pallas kernels  9.08 us (12%)
  between operations  0.84 us (1%)
    ppermute x28, starting transfers between devices, exchange(): lax.ppermute(block, 'wide', [(k, k ^ d) for k in range(wide_count)])  45.8 us
    ppermute x28, waiting for transfers between devices, exchange(): lax.ppermute(block, 'wide', [(k, k ^ d) for k in range(wide_count)])  18.5 us
    pallas_call x1, Pallas kernels, shards(): call(functools.partial(attend_body, group), [*blocks_of(query_width), str...  4.34 us
    ppermute x2, waiting for transfers between devices, other_core(): return lax.ppermute(value, 'tp', [(0, 1), (1, 0)])  2.44 us
    pallas_call x1, Pallas kernels, shards(): call(functools.partial(pack_body, capacity, by_distance), (struct((2, row...  2.19 us
  transfers between devices with their start and end apart: 30, of which 15 were waited for; matrix products, arithmetic and copies ran while one was open for 0% of the time, Pallas kernels for 0%

profile of v6, /device:TPU:0, one launch (start us, length us, event | category | flops | bytes accessed | tf_op | source)
XLA Modules:
  0.0 77.5 jit_solution(12808011810934029084)
XLA Ops:
  0.6 2.2 %shard_map.149 = (s32[2,32]{1,0:T(2,128)}, bf16[8,4096]{1,0:T(8,128)(2,1)}, bf16[8,4096]{1,0:T(8,128)(2,1)}, bf16[8,4096]{1,0:T(8,128)(2,1)}, bf16[8,4096]{1,0:T...) custom-call(s32[256]{0:T(256)} %tenant_hbm.1, ...), custom_call_target="tpu_custom_call" | custom-call | flops 1000000000 | bytes 40000000 | tf_op jit(solution)/shard_map/pallas_call | solution.py:280
  2.9 6.1 %collective-permute-start = (bf16[8,4096]{1,0:T(8,128)(2,1)}, bf16[8,4096]{1,0:T(8,128)(2,1)S(1)}, u32[]{:S(2)}, u32[]{:S(2)}) collective-permute-start(bf16[8,4096]{1,0:T(8,128)(2,1)} %get-tuple-element.52), channel_id=1, source_target_pairs={{0,14},{2,12},{4,10},{6,8},{8,6},{10,4},{12,2},{14,0},{1,15},{3,13... | collective-permute-start | bytes 196616 | tf_op jit(solution)/shard_map/ppermute | solution.py:237
  8.9 0.2 collective-permute-start.1
  9.1 1.9 %collective-permute-start.3 = (bf16[8,4096]{1,0:T(8,128)(2,1)}, bf16[8,4096]{1,0:T(8,128)(2,1)S(1)}, u32[]{:S(2)}, u32[]{:S(2)}) collective-permute-start(bf16[8,4096]{1,0:T(8,128)(2,1)} %get-tuple-element.55), channel_id=1, source_target_pairs={{0,4},{2,6},{4,0},{6,2},{8,12},{10,14},{12,8},{14,10},{1,5},{3,7},... | collective-permute-start | bytes 196616 | tf_op jit(solution)/shard_map/ppermute | solution.py:237
  11.0 3.2 %collective-permute-start.4 = (bf16[8,4096]{1,0:T(8,128)(2,1)}, bf16[8,4096]{1,0:T(8,128)(2,1)S(1)}, u32[]{:S(2)}, u32[]{:S(2)}) collective-permute-start(bf16[8,4096]{1,0:T(8,128)(2,1)} %get-tuple-element.56), channel_id=1, source_target_pairs={{0,10},{2,8},{4,14},{6,12},{8,2},{10,0},{12,6},{14,4},{1,11},{3,9}... | collective-permute-start | bytes 196616 | tf_op jit(solution)/shard_map/ppermute | solution.py:237
  14.2 0.0 collective-permute-done.ret_refs_0_
  14.2 0.8 %collective-permute-start.5 = (bf16[8,4096]{1,0:T(8,128)(2,1)}, bf16[8,4096]{1,0:T(8,128)(2,1)S(1)}, u32[]{:S(2)}, u32[]{:S(2)}) collective-permute-start(bf16[8,4096]{1,0:T(8,128)(2,1)} %get-tuple-element.57), channel_id=1, source_target_pairs={{0,8},{2,10},{4,12},{6,14},{8,0},{10,2},{12,4},{14,6},{1,9},{3,11}... | collective-permute-start | bytes 196616 | tf_op jit(solution)/shard_map/ppermute | solution.py:237
  15.0 0.9 %collective-permute-done.1.ret_refs_1_ = bf16[8,4096]{1,0:T(8,128)(2,1)S(1)} collective-permute-done((bf16[8,4096]{1,0:T(8,128)(2,1)}, bf16[8,4096]{1,0:T(8,128)(2,1)S(1)}, u32[]{:S(2)}, u32[]{:S(2)}) %collective-permute-start.1) | collective-permute-done | bytes 65568 | tf_op jit(solution)/shard_map/ppermute | solution.py:237
  15.9 0.1 collective-permute-start.6
  16.1 0.7 copy-done.11
  16.7 0.2 shard_map.150
  16.9 0.0 collective-permute-done.3.ret_refs_3_
  16.9 3.1 %collective-permute-done.4.ret_refs_4_ = bf16[8,4096]{1,0:T(8,128)(2,1)S(1)} collective-permute-done((bf16[8,4096]{1,0:T(8,128)(2,1)}, bf16[8,4096]{1,0:T(8,128)(2,1)S(1)}, u32[]{:S(2)}, u32[]{:S(2)}) %collective-permute-start.4) | collective-permute-done | bytes 65568 | tf_op jit(solution)/shard_map/ppermute | solution.py:237
  20.1 1.1 %collective-permute-done.5.ret_refs_5_ = bf16[8,4096]{1,0:T(8,128)(2,1)S(1)} collective-permute-done((bf16[8,4096]{1,0:T(8,128)(2,1)}, bf16[8,4096]{1,0:T(8,128)(2,1)S(1)}, u32[]{:S(2)}, u32[]{:S(2)}) %collective-permute-start.5) | collective-permute-done | bytes 65568 | tf_op jit(solution)/shard_map/ppermute | solution.py:237
  21.2 0.0 copy-start
  21.2 0.0 copy-start.1
  21.2 0.0 copy-start.5
  21.2 0.0 copy-start.7
  21.2 0.0 copy-start.8
  21.3 0.6 shard_map.151.mine_ref
  21.9 0.1 collective-permute-start.7
  22.0 1.2 %collective-permute-done.7.other_ref = f32[64,192]{1,0:T(8,128)S(1)} collective-permute-done((f32[64,192]{1,0:T(8,128)S(1)}, f32[64,192]{1,0:T(8,128)S(1)}, u32[]{:S(2)}, u32[]{:S(2)}) %collective-permute-start.7) | collective-permute-done | bytes 49184 | tf_op jit(solution)/shard_map/ppermute | solution.py:244
  23.2 0.3 shard_map.152
  23.5 2.7 %collective-permute-start.8 = (bf16[8,5120]{1,0:T(8,128)(2,1)S(1)}, bf16[8,5120]{1,0:T(8,128)(2,1)S(1)}, u32[]{:S(2)}, u32[]{:S(2)}) collective-permute-start(bf16[8,5120]{1,0:T(8,128)(2,1)S(1)} %get-tuple-element.73), channel_id=1, source_target_pairs={{0,14},{2,12},{4,10},{6,8},{8,6},{10,4},{12,2},{14,0},{1,15},{3,13... | collective-permute-start | bytes 245768 | tf_op jit(solution)/shard_map/ppermute | solution.py:237
  26.3 1.4 %collective-permute-start.9 = (bf16[8,5120]{1,0:T(8,128)(2,1)S(1)}, bf16[8,5120]{1,0:T(8,128)(2,1)S(1)}, u32[]{:S(2)}, u32[]{:S(2)}) collective-permute-start(bf16[8,5120]{1,0:T(8,128)(2,1)S(1)} %get-tuple-element.74), channel_id=1, source_target_pairs={{0,12},{2,14},{4,8},{6,10},{8,4},{10,6},{12,0},{14,2},{1,13},{3,15... | collective-permute-start | bytes 245768 | tf_op jit(solution)/shard_map/ppermute | solution.py:237
  27.7 2.6 %collective-permute-start.11 = (bf16[8,5120]{1,0:T(8,128)(2,1)S(1)}, bf16[8,5120]{1,0:T(8,128)(2,1)S(1)}, u32[]{:S(2)}, u32[]{:S(2)}) collective-permute-start(bf16[8,5120]{1,0:T(8,128)(2,1)S(1)} %get-tuple-element.76), channel_id=1, source_target_pairs={{0,4},{2,6},{4,0},{6,2},{8,12},{10,14},{12,8},{14,10},{1,5},{3,7},... | collective-permute-start | bytes 245768 | tf_op jit(solution)/shard_map/ppermute | solution.py:237
  30.3 1.2 %collective-permute-start.12 = (bf16[8,5120]{1,0:T(8,128)(2,1)S(1)}, bf16[8,5120]{1,0:T(8,128)(2,1)S(1)}, u32[]{:S(2)}, u32[]{:S(2)}) collective-permute-start(bf16[8,5120]{1,0:T(8,128)(2,1)S(1)} %get-tuple-element.77), channel_id=1, source_target_pairs={{0,10},{2,8},{4,14},{6,12},{8,2},{10,0},{12,6},{14,4},{1,11},{3,9}... | collective-permute-start | bytes 245768 | tf_op jit(solution)/shard_map/ppermute | solution.py:237
  31.5 0.0 collective-permute-done.8.ret_refs_0_
  31.5 2.0 %collective-permute-start.13 = (bf16[8,5120]{1,0:T(8,128)(2,1)S(1)}, bf16[8,5120]{1,0:T(8,128)(2,1)S(1)}, u32[]{:S(2)}, u32[]{:S(2)}) collective-permute-start(bf16[8,5120]{1,0:T(8,128)(2,1)S(1)} %get-tuple-element.78), channel_id=1, source_target_pairs={{0,8},{2,10},{4,12},{6,14},{8,0},{10,2},{12,4},{14,6},{1,9},{3,11}... | collective-permute-start | bytes 245768 | tf_op jit(solution)/shard_map/ppermute | solution.py:237
  33.6 1.2 %collective-permute-start.14 = (bf16[8,5120]{1,0:T(8,128)(2,1)S(1)}, bf16[8,5120]{1,0:T(8,128)(2,1)S(1)}, u32[]{:S(2)}, u32[]{:S(2)}) collective-permute-start(bf16[8,5120]{1,0:T(8,128)(2,1)S(1)} %get-tuple-element.79), channel_id=1, source_target_pairs={{0,2},{2,0},{4,6},{6,4},{8,10},{10,8},{12,14},{14,12},{1,3},{3,1},... | collective-permute-start | bytes 245768 | tf_op jit(solution)/shard_map/ppermute | solution.py:237
  34.7 1.9 %collective-permute-done.10.ret_refs_2_ = bf16[8,5120]{1,0:T(8,128)(2,1)S(1)} collective-permute-done((bf16[8,5120]{1,0:T(8,128)(2,1)S(1)}, bf16[8,5120]{1,0:T(8,128)(2,1)S(1)}, u32[]{:S(2)}, u32[]{:S(2)}) %collective-permute-start.10) | collective-permute-done | bytes 81952 | tf_op jit(solution)/shard_map/ppermute | solution.py:237
  36.6 1.6 %collective-permute-done.11.ret_refs_3_ = bf16[8,5120]{1,0:T(8,128)(2,1)S(1)} collective-permute-done((bf16[8,5120]{1,0:T(8,128)(2,1)S(1)}, bf16[8,5120]{1,0:T(8,128)(2,1)S(1)}, u32[]{:S(2)}, u32[]{:S(2)}) %collective-permute-start.11) | collective-permute-done | bytes 81952 | tf_op jit(solution)/shard_map/ppermute | solution.py:237
  38.2 2.2 %collective-permute-done.12.ret_refs_4_ = bf16[8,5120]{1,0:T(8,128)(2,1)S(1)} collective-permute-done((bf16[8,5120]{1,0:T(8,128)(2,1)S(1)}, bf16[8,5120]{1,0:T(8,128)(2,1)S(1)}, u32[]{:S(2)}, u32[]{:S(2)}) %collective-permute-start.12) | collective-permute-done | bytes 81952 | tf_op jit(solution)/shard_map/ppermute | solution.py:237
  40.4 0.1 collective-permute-done.13.ret_refs_5_
  40.5 0.0 collective-permute-done.14.ret_refs_6_
  40.5 0.0 copy-start.4
  40.5 0.0 copy-start.3
  40.5 4.3 %shard_map.153 = (bf16[8,4096]{1,0:T(8,128)(2,1)S(1)}, bf16[8,4096]{1,0:T(8,128)(2,1)S(1)}, bf16[8,4096]{1,0:T(8,128)(2,1)S(1)}, bf16[8,4096]{1,0:T(8,128)(2,1)S...) custom-call(bf16[8,5120]{1,0:T(8,128)(2,1)S(1)} %collective-permute-, ...), custom_call_target="tpu_custom_call" | custom-call | bytes 8000000 | tf_op jit(solution)/shard_map/pallas_call | solution.py:319
  44.9 2.8 %collective-permute-start.15 = (bf16[8,4096]{1,0:T(8,128)(2,1)S(1)}, bf16[8,4096]{1,0:T(8,128)(2,1)S(1)}, u32[]{:S(2)}, u32[]{:S(2)}) collective-permute-start(bf16[8,4096]{1,0:T(8,128)(2,1)S(1)} %get-tuple-element.86), channel_id=1, source_target_pairs={{0,14},{2,12},{4,10},{6,8},{8,6},{10,4},{12,2},{14,0},{1,15},{3,13... | collective-permute-start | bytes 196616 | tf_op jit(solution)/shard_map/ppermute | solution.py:237
  47.7 1.8 %collective-permute-start.16 = (bf16[8,4096]{1,0:T(8,128)(2,1)S(1)}, bf16[8,4096]{1,0:T(8,128)(2,1)S(1)}, u32[]{:S(2)}, u32[]{:S(2)}) collective-permute-start(bf16[8,4096]{1,0:T(8,128)(2,1)S(1)} %get-tuple-element.87), channel_id=1, source_target_pairs={{0,12},{2,14},{4,8},{6,10},{8,4},{10,6},{12,0},{14,2},{1,13},{3,15... | collective-permute-start | bytes 196616 | tf_op jit(solution)/shard_map/ppermute | solution.py:237
  49.5 0.0 collective-permute-start.17
  49.5 2.1 %collective-permute-start.18 = (bf16[8,4096]{1,0:T(8,128)(2,1)S(1)}, bf16[8,4096]{1,0:T(8,128)(2,1)S(1)}, u32[]{:S(2)}, u32[]{:S(2)}) collective-permute-start(bf16[8,4096]{1,0:T(8,128)(2,1)S(1)} %get-tuple-element.89), channel_id=1, source_target_pairs={{0,4},{2,6},{4,0},{6,2},{8,12},{10,14},{12,8},{14,10},{1,5},{3,7},... | collective-permute-start | bytes 196616 | tf_op jit(solution)/shard_map/ppermute | solution.py:237
  51.6 1.4 %collective-permute-start.19 = (bf16[8,4096]{1,0:T(8,128)(2,1)S(1)}, bf16[8,4096]{1,0:T(8,128)(2,1)S(1)}, u32[]{:S(2)}, u32[]{:S(2)}) collective-permute-start(bf16[8,4096]{1,0:T(8,128)(2,1)S(1)} %get-tuple-element.90), channel_id=1, source_target_pairs={{0,10},{2,8},{4,14},{6,12},{8,2},{10,0},{12,6},{14,4},{1,11},{3,9}... | collective-permute-start | bytes 196616 | tf_op jit(solution)/shard_map/ppermute | solution.py:237
  53.0 0.0 collective-permute-done.15.ret_refs_0_
  53.0 2.3 %collective-permute-start.20 = (bf16[8,4096]{1,0:T(8,128)(2,1)S(1)}, bf16[8,4096]{1,0:T(8,128)(2,1)S(1)}, u32[]{:S(2)}, u32[]{:S(2)}) collective-permute-start(bf16[8,4096]{1,0:T(8,128)(2,1)S(1)} %get-tuple-element.91), channel_id=1, source_target_pairs={{0,8},{2,10},{4,12},{6,14},{8,0},{10,2},{12,4},{14,6},{1,9},{3,11}... | collective-permute-start | bytes 196616 | tf_op jit(solution)/shard_map/ppermute | solution.py:237
  55.3 0.0 collective-permute-done.16.ret_refs_1_
  55.3 0.7 collective-permute-start.21
  56.0 0.2 collective-permute-done.18.ret_refs_3_
  56.2 1.9 %collective-permute-done.19.ret_refs_4_ = bf16[8,4096]{1,0:T(8,128)(2,1)S(1)} collective-permute-done((bf16[8,4096]{1,0:T(8,128)(2,1)S(1)}, bf16[8,4096]{1,0:T(8,128)(2,1)S(1)}, u32[]{:S(2)}, u32[]{:S(2)}) %collective-permute-start.19) | collective-permute-done | bytes 65568 | tf_op jit(solution)/shard_map/ppermute | solution.py:237
  58.1 0.3 collective-permute-done.20.ret_refs_5_
  58.4 1.2 %collective-permute-done.21.ret_refs_6_ = bf16[8,4096]{1,0:T(8,128)(2,1)S(1)} collective-permute-done((bf16[8,4096]{1,0:T(8,128)(2,1)S(1)}, bf16[8,4096]{1,0:T(8,128)(2,1)S(1)}, u32[]{:S(2)}, u32[]{:S(2)}) %collective-permute-start.21) | collective-permute-done | bytes 65568 | tf_op jit(solution)/shard_map/ppermute | solution.py:237
  59.6 0.3 shard_map.154.mine_ref
  59.9 0.1 collective-permute-start.22
  60.0 1.2 %collective-permute-done.22.other_ref = f32[64,64]{1,0:T(8,128)S(1)} collective-permute-done((f32[64,64]{1,0:T(8,128)S(1)}, f32[64,64]{1,0:T(8,128)S(1)}, u32[]{:S(2)}, u32[]{:S(2)}) %collective-permute-start.22) | collective-permute-done | bytes 16416 | tf_op jit(solution)/shard_map/ppermute | solution.py:244
  61.2 0.3 shard_map.155
  61.5 2.3 %collective-permute-start.23 = (bf16[8,4096]{1,0:T(8,128)(2,1)S(1)}, bf16[8,4096]{1,0:T(8,128)(2,1)S(1)}, u32[]{:S(2)}, u32[]{:S(2)}) collective-permute-start(bf16[8,4096]{1,0:T(8,128)(2,1)S(1)} %get-tuple-element.94), channel_id=1, source_target_pairs={{0,14},{2,12},{4,10},{6,8},{8,6},{10,4},{12,2},{14,0},{1,15},{3,13... | collective-permute-start | bytes 196616 | tf_op jit(solution)/shard_map/ppermute | solution.py:237
  63.8 1.7 %collective-permute-start.24 = (bf16[8,4096]{1,0:T(8,128)(2,1)S(1)}, bf16[8,4096]{1,0:T(8,128)(2,1)S(1)}, u32[]{:S(2)}, u32[]{:S(2)}) collective-permute-start(bf16[8,4096]{1,0:T(8,128)(2,1)S(1)} %get-tuple-element.95), channel_id=1, source_target_pairs={{0,12},{2,14},{4,8},{6,10},{8,4},{10,6},{12,0},{14,2},{1,13},{3,15... | collective-permute-start | bytes 196616 | tf_op jit(solution)/shard_map/ppermute | solution.py:237
  65.5 2.8 %collective-permute-start.26 = (bf16[8,4096]{1,0:T(8,128)(2,1)S(1)}, bf16[8,4096]{1,0:T(8,128)(2,1)S(1)}, u32[]{:S(2)}, u32[]{:S(2)}) collective-permute-start(bf16[8,4096]{1,0:T(8,128)(2,1)S(1)} %get-tuple-element.97), channel_id=1, source_target_pairs={{0,4},{2,6},{4,0},{6,2},{8,12},{10,14},{12,8},{14,10},{1,5},{3,7},... | collective-permute-start | bytes 196616 | tf_op jit(solution)/shard_map/ppermute | solution.py:237
  68.3 0.8 %collective-permute-start.27 = (bf16[8,4096]{1,0:T(8,128)(2,1)S(1)}, bf16[8,4096]{1,0:T(8,128)(2,1)S(1)}, u32[]{:S(2)}, u32[]{:S(2)}) collective-permute-start(bf16[8,4096]{1,0:T(8,128)(2,1)S(1)} %get-tuple-element.98), channel_id=1, source_target_pairs={{0,10},{2,8},{4,14},{6,12},{8,2},{10,0},{12,6},{14,4},{1,11},{3,9}... | collective-permute-start | bytes 196616 | tf_op jit(solution)/shard_map/ppermute | solution.py:237
  69.1 2.2 %collective-permute-start.28 = (bf16[8,4096]{1,0:T(8,128)(2,1)S(1)}, bf16[8,4096]{1,0:T(8,128)(2,1)S(1)}, u32[]{:S(2)}, u32[]{:S(2)}) collective-permute-start(bf16[8,4096]{1,0:T(8,128)(2,1)S(1)} %get-tuple-element.99), channel_id=1, source_target_pairs={{0,8},{2,10},{4,12},{6,14},{8,0},{10,2},{12,4},{14,6},{1,9},{3,11}... | collective-permute-start | bytes 196616 | tf_op jit(solution)/shard_map/ppermute | solution.py:237
  71.3 1.4 %collective-permute-start.29 = (bf16[8,4096]{1,0:T(8,128)(2,1)S(1)}, bf16[8,4096]{1,0:T(8,128)(2,1)S(1)}, u32[]{:S(2)}, u32[]{:S(2)}) collective-permute-start(bf16[8,4096]{1,0:T(8,128)(2,1)S(1)} %get-tuple-element.100), channel_id=1, source_target_pairs={{0,2},{2,0},{4,6},{6,4},{8,10},{10,8},{12,14},{14,12},{1,3},{3,1},... | collective-permute-start | bytes 196616 | tf_op jit(solution)/shard_map/ppermute | solution.py:237
  72.7 1.0 %collective-permute-done.26.ret_refs_3_ = bf16[8,4096]{1,0:T(8,128)(2,1)S(1)} collective-permute-done((bf16[8,4096]{1,0:T(8,128)(2,1)S(1)}, bf16[8,4096]{1,0:T(8,128)(2,1)S(1)}, u32[]{:S(2)}, u32[]{:S(2)}) %collective-permute-start.26) | collective-permute-done | bytes 65568 | tf_op jit(solution)/shard_map/ppermute | solution.py:237
  73.7 3.0 %collective-permute-done.27.ret_refs_4_ = bf16[8,4096]{1,0:T(8,128)(2,1)S(1)} collective-permute-done((bf16[8,4096]{1,0:T(8,128)(2,1)S(1)}, bf16[8,4096]{1,0:T(8,128)(2,1)S(1)}, u32[]{:S(2)}, u32[]{:S(2)}) %collective-permute-start.27) | collective-permute-done | bytes 65568 | tf_op jit(solution)/shard_map/ppermute | solution.py:237
  76.6 0.9 %shard_map.156 = bf16[32,4096]{1,0:T(8,128)(2,1)} custom-call(bf16[32,64]{1,0:T(8,128)(2,1)S(1)} %get-tuple-element.84.home_ref, bf16[8,4096]{1,0:T(8,128)(2,1)S(1)} %collective-permute-done.23.ret_refs_0_, bf16[8,4096]{1,0:T(8,128)(2,1)S(1)} %collective-permute-done.24.ret_refs_1_, bf16[8,4096]{1,0:T(8,128)(2,1)S(1)} %collective-permute-done.25.ret_refs_2_, ...), custom_call_target="tpu_custom_call" | custom-call | bytes 1000000 | tf_op jit(solution)/shard_map/pallas_call | solution.py:339
  (28 shorter events, 0.1 us)
Async XLA Ops:
  0.6 20.6 %copy-start.2 = (bf16[1,192,8192]{2,1,0:T(8,128)(2,1)S(1)}, bf16[1,192,8192]{2,1,0:T(8,128)(2,1)}, u32[]{:S(2)}) copy-start(bf16[1,192,8192]{2,1,0:T(8,128)(2,1)} %down_ref.2) | copy-start | bytes 9437188
  2.8 18.3 %copy-start.6 = (bf16[8,4096]{1,0:T(8,128)(2,1)S(1)}, bf16[8,4096]{1,0:T(8,128)(2,1)}, u32[]{:S(2)}) copy-start(bf16[8,4096]{1,0:T(8,128)(2,1)} %get-tuple-element.72.ret_refs_7_) | copy-start | bytes 196612
  2.9 11.4 %collective-permute-start = (bf16[8,4096]{1,0:T(8,128)(2,1)}, bf16[8,4096]{1,0:T(8,128)(2,1)S(1)}, u32[]{:S(2)}, u32[]{:S(2)}) collective-permute-start(bf16[8,4096]{1,0:T(8,128)(2,1)} %get-tuple-element.52), channel_id=1, source_target_pairs={{0,14},{2,12},{4,10},{6,8},{8,6},{10,4},{12,2},{14,0},{1,15},{3,13... | collective-permute-start | bytes 196616 | tf_op jit(solution)/shard_map/ppermute | solution.py:237
  8.9 7.0 %collective-permute-start.1 = (bf16[8,4096]{1,0:T(8,128)(2,1)}, bf16[8,4096]{1,0:T(8,128)(2,1)S(1)}, u32[]{:S(2)}, u32[]{:S(2)}) collective-permute-start(bf16[8,4096]{1,0:T(8,128)(2,1)} %get-tuple-element.53), channel_id=1, source_target_pairs={{0,12},{2,14},{4,8},{6,10},{8,4},{10,6},{12,0},{14,2},{1,13},{3,15... | collective-permute-start | bytes 196616 | tf_op jit(solution)/shard_map/ppermute | solution.py:237
  9.1 7.7 %collective-permute-start.2 = (bf16[8,4096]{1,0:T(8,128)(2,1)}, bf16[8,4096]{1,0:T(8,128)(2,1)S(1)}, u32[]{:S(2)}, u32[]{:S(2)}) collective-permute-start(bf16[8,4096]{1,0:T(8,128)(2,1)} %get-tuple-element.54), channel_id=1, source_target_pairs={{0,6},{2,4},{4,2},{6,0},{8,14},{10,12},{12,10},{14,8},{1,7},{3,5},... | collective-permute-start | bytes 196616 | tf_op jit(solution)/shard_map/ppermute | solution.py:237
  9.1 7.8 %collective-permute-start.3 = (bf16[8,4096]{1,0:T(8,128)(2,1)}, bf16[8,4096]{1,0:T(8,128)(2,1)S(1)}, u32[]{:S(2)}, u32[]{:S(2)}) collective-permute-start(bf16[8,4096]{1,0:T(8,128)(2,1)} %get-tuple-element.55), channel_id=1, source_target_pairs={{0,4},{2,6},{4,0},{6,2},{8,12},{10,14},{12,8},{14,10},{1,5},{3,7},... | collective-permute-start | bytes 196616 | tf_op jit(solution)/shard_map/ppermute | solution.py:237
  11.0 9.0 %collective-permute-start.4 = (bf16[8,4096]{1,0:T(8,128)(2,1)}, bf16[8,4096]{1,0:T(8,128)(2,1)S(1)}, u32[]{:S(2)}, u32[]{:S(2)}) collective-permute-start(bf16[8,4096]{1,0:T(8,128)(2,1)} %get-tuple-element.56), channel_id=1, source_target_pairs={{0,10},{2,8},{4,14},{6,12},{8,2},{10,0},{12,6},{14,4},{1,11},{3,9}... | collective-permute-start | bytes 196616 | tf_op jit(solution)/shard_map/ppermute | solution.py:237
  14.2 7.0 %collective-permute-start.5 = (bf16[8,4096]{1,0:T(8,128)(2,1)}, bf16[8,4096]{1,0:T(8,128)(2,1)S(1)}, u32[]{:S(2)}, u32[]{:S(2)}) collective-permute-start(bf16[8,4096]{1,0:T(8,128)(2,1)} %get-tuple-element.57), channel_id=1, source_target_pairs={{0,8},{2,10},{4,12},{6,14},{8,0},{10,2},{12,4},{14,6},{1,9},{3,11}... | collective-permute-start | bytes 196616 | tf_op jit(solution)/shard_map/ppermute | solution.py:237
  15.9 5.2 %collective-permute-start.6 = (bf16[8,4096]{1,0:T(8,128)(2,1)}, bf16[8,4096]{1,0:T(8,128)(2,1)S(1)}, u32[]{:S(2)}, u32[]{:S(2)}) collective-permute-start(bf16[8,4096]{1,0:T(8,128)(2,1)} %get-tuple-element.58), channel_id=1, source_target_pairs={{0,2},{2,0},{4,6},{6,4},{8,10},{10,8},{12,14},{14,12},{1,3},{3,1},... | collective-permute-start | bytes 196616 | tf_op jit(solution)/shard_map/ppermute | solution.py:237
  16.1 0.7 copy-start.11
  16.7 6.5 %copy-start.9 = (bf16[1,64,4096]{2,1,0:T(8,128)(2,1)S(1)}, bf16[1,64,4096]{2,1,0:T(8,128)(2,1)}, u32[]{:S(2)}) copy-start(bf16[1,64,4096]{2,1,0:T(8,128)(2,1)} %uq_ref.1) | copy-start | bytes 1572868
  16.7 6.5 %copy-start.10 = (bf16[1,2,64,512]{3,2,1,0:T(8,128)(2,1)S(1)}, bf16[1,2,64,512]{3,2,1,0:T(8,128)(2,1)}, u32[]{:S(2)}) copy-start(bf16[1,2,64,512]{3,2,1,0:T(8,128)(2,1)} %ukv_ref.1) | copy-start | bytes 393220
  21.2 19.3 %copy-start = (bf16[32,4,96,128]{3,2,1,0:T(8,128)(2,1)S(1)}, bf16[32,4,96,128]{3,2,1,0:T(8,128)(2,1)}, u32[]{:S(2)}) copy-start(bf16[32,4,96,128]{3,2,1,0:T(8,128)(2,1)} %k_ref.1) | copy-start | bytes 9437188
  21.2 19.3 %copy-start.1 = (bf16[32,4,96,128]{3,2,1,0:T(8,128)(2,1)S(1)}, bf16[32,4,96,128]{3,2,1,0:T(8,128)(2,1)}, u32[]{:S(2)}) copy-start(bf16[32,4,96,128]{3,2,1,0:T(8,128)(2,1)} %v_ref.1) | copy-start | bytes 9437188
  21.2 19.3 %copy-start.5 = (bf16[32,4096]{1,0:T(8,128)(2,1)S(1)}, bf16[32,4096]{1,0:T(8,128)(2,1)}, u32[]{:S(2)}) copy-start(bf16[32,4096]{1,0:T(8,128)(2,1)} %pq_ref.1) | copy-start | bytes 786436
  21.2 19.3 %copy-start.7 = (bf16[32,512]{1,0:T(8,128)(2,1)S(1)}, bf16[32,512]{1,0:T(8,128)(2,1)}, u32[]{:S(2)}) copy-start(bf16[32,512]{1,0:T(8,128)(2,1)} %pk_ref.1) | copy-start | bytes 98308
  21.2 19.3 %copy-start.8 = (bf16[32,512]{1,0:T(8,128)(2,1)S(1)}, bf16[32,512]{1,0:T(8,128)(2,1)}, u32[]{:S(2)}) copy-start(bf16[32,512]{1,0:T(8,128)(2,1)} %pv_ref.1) | copy-start | bytes 98308
  21.9 1.3 %collective-permute-start.7 = (f32[64,192]{1,0:T(8,128)S(1)}, f32[64,192]{1,0:T(8,128)S(1)}, u32[]{:S(2)}, u32[]{:S(2)}) collective-permute-start(f32[64,192]{1,0:T(8,128)S(1)} %shard_map.151.mine_ref), channel_id=1, source_target_pairs={{0,1},{1,0},{2,3},{3,2},{4,5},{5,4},{6,7},{7,6},{8,9},{9,8},{10,11... | collective-permute-start | bytes 147464 | tf_op jit(solution)/shard_map/ppermute | solution.py:244
  23.5 8.0 %collective-permute-start.8 = (bf16[8,5120]{1,0:T(8,128)(2,1)S(1)}, bf16[8,5120]{1,0:T(8,128)(2,1)S(1)}, u32[]{:S(2)}, u32[]{:S(2)}) collective-permute-start(bf16[8,5120]{1,0:T(8,128)(2,1)S(1)} %get-tuple-element.73), channel_id=1, source_target_pairs={{0,14},{2,12},{4,10},{6,8},{8,6},{10,4},{12,2},{14,0},{1,15},{3,13... | collective-permute-start | bytes 245768 | tf_op jit(solution)/shard_map/ppermute | solution.py:237
  26.3 7.3 %collective-permute-start.9 = (bf16[8,5120]{1,0:T(8,128)(2,1)S(1)}, bf16[8,5120]{1,0:T(8,128)(2,1)S(1)}, u32[]{:S(2)}, u32[]{:S(2)}) collective-permute-start(bf16[8,5120]{1,0:T(8,128)(2,1)S(1)} %get-tuple-element.74), channel_id=1, source_target_pairs={{0,12},{2,14},{4,8},{6,10},{8,4},{10,6},{12,0},{14,2},{1,13},{3,15... | collective-permute-start | bytes 245768 | tf_op jit(solution)/shard_map/ppermute | solution.py:237
  27.7 8.9 %collective-permute-start.10 = (bf16[8,5120]{1,0:T(8,128)(2,1)S(1)}, bf16[8,5120]{1,0:T(8,128)(2,1)S(1)}, u32[]{:S(2)}, u32[]{:S(2)}) collective-permute-start(bf16[8,5120]{1,0:T(8,128)(2,1)S(1)} %get-tuple-element.75), channel_id=1, source_target_pairs={{0,6},{2,4},{4,2},{6,0},{8,14},{10,12},{12,10},{14,8},{1,7},{3,5},... | collective-permute-start | bytes 245768 | tf_op jit(solution)/shard_map/ppermute | solution.py:237
  27.7 10.5 %collective-permute-start.11 = (bf16[8,5120]{1,0:T(8,128)(2,1)S(1)}, bf16[8,5120]{1,0:T(8,128)(2,1)S(1)}, u32[]{:S(2)}, u32[]{:S(2)}) collective-permute-start(bf16[8,5120]{1,0:T(8,128)(2,1)S(1)} %get-tuple-element.76), channel_id=1, source_target_pairs={{0,4},{2,6},{4,0},{6,2},{8,12},{10,14},{12,8},{14,10},{1,5},{3,7},... | collective-permute-start | bytes 245768 | tf_op jit(solution)/shard_map/ppermute | solution.py:237
  30.3 10.0 %collective-permute-start.12 = (bf16[8,5120]{1,0:T(8,128)(2,1)S(1)}, bf16[8,5120]{1,0:T(8,128)(2,1)S(1)}, u32[]{:S(2)}, u32[]{:S(2)}) collective-permute-start(bf16[8,5120]{1,0:T(8,128)(2,1)S(1)} %get-tuple-element.77), channel_id=1, source_target_pairs={{0,10},{2,8},{4,14},{6,12},{8,2},{10,0},{12,6},{14,4},{1,11},{3,9}... | collective-permute-start | bytes 245768 | tf_op jit(solution)/shard_map/ppermute | solution.py:237
  31.5 8.9 %collective-permute-start.13 = (bf16[8,5120]{1,0:T(8,128)(2,1)S(1)}, bf16[8,5120]{1,0:T(8,128)(2,1)S(1)}, u32[]{:S(2)}, u32[]{:S(2)}) collective-permute-start(bf16[8,5120]{1,0:T(8,128)(2,1)S(1)} %get-tuple-element.78), channel_id=1, source_target_pairs={{0,8},{2,10},{4,12},{6,14},{8,0},{10,2},{12,4},{14,6},{1,9},{3,11}... | collective-permute-start | bytes 245768 | tf_op jit(solution)/shard_map/ppermute | solution.py:237
  33.6 6.9 %collective-permute-start.14 = (bf16[8,5120]{1,0:T(8,128)(2,1)S(1)}, bf16[8,5120]{1,0:T(8,128)(2,1)S(1)}, u32[]{:S(2)}, u32[]{:S(2)}) collective-permute-start(bf16[8,5120]{1,0:T(8,128)(2,1)S(1)} %get-tuple-element.79), channel_id=1, source_target_pairs={{0,2},{2,0},{4,6},{6,4},{8,10},{10,8},{12,14},{14,12},{1,3},{3,1},... | collective-permute-start | bytes 245768 | tf_op jit(solution)/shard_map/ppermute | solution.py:237
  40.5 19.1 %copy-start.4 = (bf16[1,64,4096]{2,1,0:T(8,128)(2,1)S(1)}, bf16[1,64,4096]{2,1,0:T(8,128)(2,1)}, u32[]{:S(2)}) copy-start(bf16[1,64,4096]{2,1,0:T(8,128)(2,1)} %down_ref.3) | copy-start | bytes 1572868
  40.5 20.7 %copy-start.3 = (bf16[1,64,4096]{2,1,0:T(8,128)(2,1)S(1)}, bf16[1,64,4096]{2,1,0:T(8,128)(2,1)}, u32[]{:S(2)}) copy-start(bf16[1,64,4096]{2,1,0:T(8,128)(2,1)} %uo_ref.1) | copy-start | bytes 1572868
  44.9 8.1 %collective-permute-start.15 = (bf16[8,4096]{1,0:T(8,128)(2,1)S(1)}, bf16[8,4096]{1,0:T(8,128)(2,1)S(1)}, u32[]{:S(2)}, u32[]{:S(2)}) collective-permute-start(bf16[8,4096]{1,0:T(8,128)(2,1)S(1)} %get-tuple-element.86), channel_id=1, source_target_pairs={{0,14},{2,12},{4,10},{6,8},{8,6},{10,4},{12,2},{14,0},{1,15},{3,13... | collective-permute-start | bytes 196616 | tf_op jit(solution)/shard_map/ppermute | solution.py:237
  47.7 7.6 %collective-permute-start.16 = (bf16[8,4096]{1,0:T(8,128)(2,1)S(1)}, bf16[8,4096]{1,0:T(8,128)(2,1)S(1)}, u32[]{:S(2)}, u32[]{:S(2)}) collective-permute-start(bf16[8,4096]{1,0:T(8,128)(2,1)S(1)} %get-tuple-element.87), channel_id=1, source_target_pairs={{0,12},{2,14},{4,8},{6,10},{8,4},{10,6},{12,0},{14,2},{1,13},{3,15... | collective-permute-start | bytes 196616 | tf_op jit(solution)/shard_map/ppermute | solution.py:237
  49.5 6.5 %collective-permute-start.17 = (bf16[8,4096]{1,0:T(8,128)(2,1)S(1)}, bf16[8,4096]{1,0:T(8,128)(2,1)S(1)}, u32[]{:S(2)}, u32[]{:S(2)}) collective-permute-start(bf16[8,4096]{1,0:T(8,128)(2,1)S(1)} %get-tuple-element.88), channel_id=1, source_target_pairs={{0,6},{2,4},{4,2},{6,0},{8,14},{10,12},{12,10},{14,8},{1,7},{3,5},... | collective-permute-start | bytes 196616 | tf_op jit(solution)/shard_map/ppermute | solution.py:237
  49.5 6.7 %collective-permute-start.18 = (bf16[8,4096]{1,0:T(8,128)(2,1)S(1)}, bf16[8,4096]{1,0:T(8,128)(2,1)S(1)}, u32[]{:S(2)}, u32[]{:S(2)}) collective-permute-start(bf16[8,4096]{1,0:T(8,128)(2,1)S(1)} %get-tuple-element.89), channel_id=1, source_target_pairs={{0,4},{2,6},{4,0},{6,2},{8,12},{10,14},{12,8},{14,10},{1,5},{3,7},... | collective-permute-start | bytes 196616 | tf_op jit(solution)/shard_map/ppermute | solution.py:237
  51.6 6.5 %collective-permute-start.19 = (bf16[8,4096]{1,0:T(8,128)(2,1)S(1)}, bf16[8,4096]{1,0:T(8,128)(2,1)S(1)}, u32[]{:S(2)}, u32[]{:S(2)}) collective-permute-start(bf16[8,4096]{1,0:T(8,128)(2,1)S(1)} %get-tuple-element.90), channel_id=1, source_target_pairs={{0,10},{2,8},{4,14},{6,12},{8,2},{10,0},{12,6},{14,4},{1,11},{3,9}... | collective-permute-start | bytes 196616 | tf_op jit(solution)/shard_map/ppermute | solution.py:237
  53.0 5.4 %collective-permute-start.20 = (bf16[8,4096]{1,0:T(8,128)(2,1)S(1)}, bf16[8,4096]{1,0:T(8,128)(2,1)S(1)}, u32[]{:S(2)}, u32[]{:S(2)}) collective-permute-start(bf16[8,4096]{1,0:T(8,128)(2,1)S(1)} %get-tuple-element.91), channel_id=1, source_target_pairs={{0,8},{2,10},{4,12},{6,14},{8,0},{10,2},{12,4},{14,6},{1,9},{3,11}... | collective-permute-start | bytes 196616 | tf_op jit(solution)/shard_map/ppermute | solution.py:237
  55.3 4.3 %collective-permute-start.21 = (bf16[8,4096]{1,0:T(8,128)(2,1)S(1)}, bf16[8,4096]{1,0:T(8,128)(2,1)S(1)}, u32[]{:S(2)}, u32[]{:S(2)}) collective-permute-start(bf16[8,4096]{1,0:T(8,128)(2,1)S(1)} %get-tuple-element.92), channel_id=1, source_target_pairs={{0,2},{2,0},{4,6},{6,4},{8,10},{10,8},{12,14},{14,12},{1,3},{3,1},... | collective-permute-start | bytes 196616 | tf_op jit(solution)/shard_map/ppermute | solution.py:237
  59.9 1.3 %collective-permute-start.22 = (f32[64,64]{1,0:T(8,128)S(1)}, f32[64,64]{1,0:T(8,128)S(1)}, u32[]{:S(2)}, u32[]{:S(2)}) collective-permute-start(f32[64,64]{1,0:T(8,128)S(1)} %shard_map.154.mine_ref), channel_id=1, source_target_pairs={{0,1},{1,0},{2,3},{3,2},{4,5},{5,4},{6,7},{7,6},{8,9},{9,8},{10,11... | collective-permute-start | bytes 49160 | tf_op jit(solution)/shard_map/ppermute | solution.py:244
  61.5 7.6 %collective-permute-start.23 = (bf16[8,4096]{1,0:T(8,128)(2,1)S(1)}, bf16[8,4096]{1,0:T(8,128)(2,1)S(1)}, u32[]{:S(2)}, u32[]{:S(2)}) collective-permute-start(bf16[8,4096]{1,0:T(8,128)(2,1)S(1)} %get-tuple-element.94), channel_id=1, source_target_pairs={{0,14},{2,12},{4,10},{6,8},{8,6},{10,4},{12,2},{14,0},{1,15},{3,13... | collective-permute-start | bytes 196616 | tf_op jit(solution)/shard_map/ppermute | solution.py:237
  63.8 7.5 %collective-permute-start.24 = (bf16[8,4096]{1,0:T(8,128)(2,1)S(1)}, bf16[8,4096]{1,0:T(8,128)(2,1)S(1)}, u32[]{:S(2)}, u32[]{:S(2)}) collective-permute-start(bf16[8,4096]{1,0:T(8,128)(2,1)S(1)} %get-tuple-element.95), channel_id=1, source_target_pairs={{0,12},{2,14},{4,8},{6,10},{8,4},{10,6},{12,0},{14,2},{1,13},{3,15... | collective-permute-start | bytes 196616 | tf_op jit(solution)/shard_map/ppermute | solution.py:237
  65.5 7.2 %collective-permute-start.25 = (bf16[8,4096]{1,0:T(8,128)(2,1)S(1)}, bf16[8,4096]{1,0:T(8,128)(2,1)S(1)}, u32[]{:S(2)}, u32[]{:S(2)}) collective-permute-start(bf16[8,4096]{1,0:T(8,128)(2,1)S(1)} %get-tuple-element.96), channel_id=1, source_target_pairs={{0,6},{2,4},{4,2},{6,0},{8,14},{10,12},{12,10},{14,8},{1,7},{3,5},... | collective-permute-start | bytes 196616 | tf_op jit(solution)/shard_map/ppermute | solution.py:237
  65.5 8.2 %collective-permute-start.26 = (bf16[8,4096]{1,0:T(8,128)(2,1)S(1)}, bf16[8,4096]{1,0:T(8,128)(2,1)S(1)}, u32[]{:S(2)}, u32[]{:S(2)}) collective-permute-start(bf16[8,4096]{1,0:T(8,128)(2,1)S(1)} %get-tuple-element.97), channel_id=1, source_target_pairs={{0,4},{2,6},{4,0},{6,2},{8,12},{10,14},{12,8},{14,10},{1,5},{3,7},... | collective-permute-start | bytes 196616 | tf_op jit(solution)/shard_map/ppermute | solution.py:237
  68.3 8.4 %collective-permute-start.27 = (bf16[8,4096]{1,0:T(8,128)(2,1)S(1)}, bf16[8,4096]{1,0:T(8,128)(2,1)S(1)}, u32[]{:S(2)}, u32[]{:S(2)}) collective-permute-start(bf16[8,4096]{1,0:T(8,128)(2,1)S(1)} %get-tuple-element.98), channel_id=1, source_target_pairs={{0,10},{2,8},{4,14},{6,12},{8,2},{10,0},{12,6},{14,4},{1,11},{3,9}... | collective-permute-start | bytes 196616 | tf_op jit(solution)/shard_map/ppermute | solution.py:237
  69.1 7.6 %collective-permute-start.28 = (bf16[8,4096]{1,0:T(8,128)(2,1)S(1)}, bf16[8,4096]{1,0:T(8,128)(2,1)S(1)}, u32[]{:S(2)}, u32[]{:S(2)}) collective-permute-start(bf16[8,4096]{1,0:T(8,128)(2,1)S(1)} %get-tuple-element.99), channel_id=1, source_target_pairs={{0,8},{2,10},{4,12},{6,14},{8,0},{10,2},{12,4},{14,6},{1,9},{3,11}... | collective-permute-start | bytes 196616 | tf_op jit(solution)/shard_map/ppermute | solution.py:237
  71.3 5.3 %collective-permute-start.29 = (bf16[8,4096]{1,0:T(8,128)(2,1)S(1)}, bf16[8,4096]{1,0:T(8,128)(2,1)S(1)}, u32[]{:S(2)}, u32[]{:S(2)}) collective-permute-start(bf16[8,4096]{1,0:T(8,128)(2,1)S(1)} %get-tuple-element.100), channel_id=1, source_target_pairs={{0,2},{2,0},{4,6},{6,4},{8,10},{10,8},{12,14},{14,12},{1,3},{3,1},... | collective-permute-start | bytes 196616 | tf_op jit(solution)/shard_map/ppermute | solution.py:237

commit v7 on v6

--- a/solution.py
+++ b/solution.py
@@ -139,14 +139,16 @@
 def attend_body(
     group, ret_refs, k_ref, v_ref, pq_ref, pk_ref, pv_ref, bias_ref, take_ref, send_ref, home_ref, *refs,
 ):
-    packed_refs, (context_ref, ret_ref, line_ref) = refs[:-3], refs[-3:]
-    ret_ref[...] = joined(ret_refs)
+    packed_refs, (context_ref, term_ref, line_ref) = refs[:-3], refs[-3:]
     rows, heads, cache_size, head_dim = k_ref.shape
     take, send = take_ref[...], send_ref[...]
     bias = bias_ref[...]
     scale = head_dim ** (-0.5)
     k_base = heads * group * head_dim
     v_base = k_base + heads * head_dim
+    term_ref[...] = dot(take, joined(ret_refs))
+    for base, plain in ((0, pq_ref), (k_base, pk_ref), (v_base, pv_ref)):
+        term_ref[:, base : base + plain.shape[1]] += plain[...].astype(F32)
 
     def lines_of(slot, part):
         for h in range(group):
@@ -162,16 +164,13 @@
     for g in range(heads):
         slot = 4 * (g % 2)
         columns = slice(g * group * head_dim, (g + 1) * group * head_dim)
-        query_rows = pq_ref[:, columns].astype(F32) + dot(take, ret_ref[:, columns])
+        query_rows = term_ref[:, columns]
         query = lines_of(slot, lambda h: query_rows[:, h * head_dim : (h + 1) * head_dim])
         query = query.astype(BF16).astype(F32)
         key_columns = slice(g * head_dim, (g + 1) * head_dim)
         new_key, new_value = (
-            (
-                plain[:, key_columns].astype(F32)
-                + dot(take, ret_ref[:, base + g * head_dim : base + (g + 1) * head_dim])
-            ).astype(BF16).astype(F32)
-            for base, plain in ((k_base, pk_ref), (v_base, pv_ref))
+            term_ref[:, base + g * head_dim : base + (g + 1) * head_dim].astype(BF16).astype(F32)
+            for base in (k_base, v_base)
         )
         new_key = lines_of(slot + 1, lambda h: new_key)
         new_value = lines_of(slot + 2, lambda h: new_value)
@@ -201,7 +200,7 @@
             [line_ref[slot + 3, pl.ds(h, rows, stride=group), :] for h in range(group)], axis=1
         ).astype(BF16)
         context_ref[:, columns] = context
-        store_blocks(packed_refs, dot(send, context), columns)
+    store_blocks(packed_refs, dot(send, context_ref[...]))
 
 
 def output_up_body(mine_ref, other_ref, uo_ref, *out_refs):
@@ -321,7 +320,7 @@
         [*blocks_of(query_width), struct((rows, query_width), BF16)],
         [(VMEM,) * count] + [VMEM] * (5 + len(prepared)),
         scratch=[
-            pltpu.VMEM((slots, kv_heads * (group + 2) * head_dim), BF16),
+            pltpu.VMEM((rows, kv_heads * (group + 2) * head_dim), F32),
             pltpu.VMEM((8, lines, head_dim), F32),
         ],
         moved=8000000,

time: 77.7 us -> 77 us (level)
  no operation moved by 1% of the time
where the time goes in v7:
time: 77 us; the launch traced here: 76.9 us
  starting transfers between devices  45.9 us (60%)
  waiting for transfers between devices  21 us (27%)
  Pallas kernels  8.39 us (11%)
  between operations  0.84 us (1%)
    ppermute x28, starting transfers between devices, exchange(): lax.ppermute(block, 'wide', [(k, k ^ d) for k in range(wide_count)])  45.8 us
    ppermute x28, waiting for transfers between devices, exchange(): lax.ppermute(block, 'wide', [(k, k ^ d) for k in range(wide_count)])  18.5 us
    pallas_call x1, Pallas kernels, shards(): call(functools.partial(attend_body, group), [*blocks_of(query_width), str...  3.65 us
    ppermute x2, waiting for transfers between devices, other_core(): return lax.ppermute(value, 'tp', [(0, 1), (1, 0)])  2.44 us
    pallas_call x1, Pallas kernels, shards(): call(functools.partial(pack_body, capacity, by_distance), (struct((2, row...  2.19 us
  transfers between devices with their start and end apart: 30, of which 15 were waited for; matrix products, arithmetic and copies ran while one was open for 0% of the time, Pallas kernels for 0%

profile of v7, /device:TPU:0, one launch (start us, length us, event | category | flops | bytes accessed | tf_op | source)
XLA Modules:
  0.0 76.9 jit_solution(9093395199469959484)
XLA Ops:
  0.6 2.2 %shard_map.149 = (s32[2,32]{1,0:T(2,128)}, bf16[8,4096]{1,0:T(8,128)(2,1)}, bf16[8,4096]{1,0:T(8,128)(2,1)}, bf16[8,4096]{1,0:T(8,128)(2,1)}, bf16[8,4096]{1,0:T...) custom-call(s32[256]{0:T(256)} %tenant_hbm.1, ...), custom_call_target="tpu_custom_call" | custom-call | flops 1000000000 | bytes 40000000 | tf_op jit(solution)/shard_map/pallas_call | solution.py:279
  2.9 6.1 %collective-permute-start = (bf16[8,4096]{1,0:T(8,128)(2,1)}, bf16[8,4096]{1,0:T(8,128)(2,1)S(1)}, u32[]{:S(2)}, u32[]{:S(2)}) collective-permute-start(bf16[8,4096]{1,0:T(8,128)(2,1)} %get-tuple-element.52), channel_id=1, source_target_pairs={{0,14},{2,12},{4,10},{6,8},{8,6},{10,4},{12,2},{14,0},{1,15},{3,13... | collective-permute-start | bytes 196616 | tf_op jit(solution)/shard_map/ppermute | solution.py:236
  8.9 0.2 collective-permute-start.1
  9.1 0.0 collective-permute-start.2
  9.1 1.9 %collective-permute-start.3 = (bf16[8,4096]{1,0:T(8,128)(2,1)}, bf16[8,4096]{1,0:T(8,128)(2,1)S(1)}, u32[]{:S(2)}, u32[]{:S(2)}) collective-permute-start(bf16[8,4096]{1,0:T(8,128)(2,1)} %get-tuple-element.55), channel_id=1, source_target_pairs={{0,4},{2,6},{4,0},{6,2},{8,12},{10,14},{12,8},{14,10},{1,5},{3,7},... | collective-permute-start | bytes 196616 | tf_op jit(solution)/shard_map/ppermute | solution.py:236
  11.0 3.2 %collective-permute-start.4 = (bf16[8,4096]{1,0:T(8,128)(2,1)}, bf16[8,4096]{1,0:T(8,128)(2,1)S(1)}, u32[]{:S(2)}, u32[]{:S(2)}) collective-permute-start(bf16[8,4096]{1,0:T(8,128)(2,1)} %get-tuple-element.56), channel_id=1, source_target_pairs={{0,10},{2,8},{4,14},{6,12},{8,2},{10,0},{12,6},{14,4},{1,11},{3,9}... | collective-permute-start | bytes 196616 | tf_op jit(solution)/shard_map/ppermute | solution.py:236
  14.2 0.0 collective-permute-done.ret_refs_0_
  14.2 0.8 %collective-permute-start.5 = (bf16[8,4096]{1,0:T(8,128)(2,1)}, bf16[8,4096]{1,0:T(8,128)(2,1)S(1)}, u32[]{:S(2)}, u32[]{:S(2)}) collective-permute-start(bf16[8,4096]{1,0:T(8,128)(2,1)} %get-tuple-element.57), channel_id=1, source_target_pairs={{0,8},{2,10},{4,12},{6,14},{8,0},{10,2},{12,4},{14,6},{1,9},{3,11}... | collective-permute-start | bytes 196616 | tf_op jit(solution)/shard_map/ppermute | solution.py:236
  15.0 0.9 %collective-permute-done.1.ret_refs_1_ = bf16[8,4096]{1,0:T(8,128)(2,1)S(1)} collective-permute-done((bf16[8,4096]{1,0:T(8,128)(2,1)}, bf16[8,4096]{1,0:T(8,128)(2,1)S(1)}, u32[]{:S(2)}, u32[]{:S(2)}) %collective-permute-start.1) | collective-permute-done | bytes 65568 | tf_op jit(solution)/shard_map/ppermute | solution.py:236
  15.9 0.1 collective-permute-start.6
  16.1 0.7 copy-done.11
  16.7 0.2 shard_map.150
  16.9 0.0 collective-permute-done.3.ret_refs_3_
  16.9 3.1 %collective-permute-done.4.ret_refs_4_ = bf16[8,4096]{1,0:T(8,128)(2,1)S(1)} collective-permute-done((bf16[8,4096]{1,0:T(8,128)(2,1)}, bf16[8,4096]{1,0:T(8,128)(2,1)S(1)}, u32[]{:S(2)}, u32[]{:S(2)}) %collective-permute-start.4) | collective-permute-done | bytes 65568 | tf_op jit(solution)/shard_map/ppermute | solution.py:236
  20.1 1.1 %collective-permute-done.5.ret_refs_5_ = bf16[8,4096]{1,0:T(8,128)(2,1)S(1)} collective-permute-done((bf16[8,4096]{1,0:T(8,128)(2,1)}, bf16[8,4096]{1,0:T(8,128)(2,1)S(1)}, u32[]{:S(2)}, u32[]{:S(2)}) %collective-permute-start.5) | collective-permute-done | bytes 65568 | tf_op jit(solution)/shard_map/ppermute | solution.py:236
  21.2 0.0 copy-start
  21.2 0.0 copy-start.1
  21.2 0.0 copy-start.5
  21.2 0.0 copy-start.7
  21.2 0.0 copy-start.8
  21.3 0.6 shard_map.151.mine_ref
  21.9 0.1 collective-permute-start.7
  22.0 1.2 %collective-permute-done.7.other_ref = f32[64,192]{1,0:T(8,128)S(1)} collective-permute-done((f32[64,192]{1,0:T(8,128)S(1)}, f32[64,192]{1,0:T(8,128)S(1)}, u32[]{:S(2)}, u32[]{:S(2)}) %collective-permute-start.7) | collective-permute-done | bytes 49184 | tf_op jit(solution)/shard_map/ppermute | solution.py:243
  23.2 0.3 shard_map.152
  23.5 2.7 %collective-permute-start.8 = (bf16[8,5120]{1,0:T(8,128)(2,1)S(1)}, bf16[8,5120]{1,0:T(8,128)(2,1)S(1)}, u32[]{:S(2)}, u32[]{:S(2)}) collective-permute-start(bf16[8,5120]{1,0:T(8,128)(2,1)S(1)} %get-tuple-element.73), channel_id=1, source_target_pairs={{0,14},{2,12},{4,10},{6,8},{8,6},{10,4},{12,2},{14,0},{1,15},{3,13... | collective-permute-start | bytes 245768 | tf_op jit(solution)/shard_map/ppermute | solution.py:236
  26.3 1.4 %collective-permute-start.9 = (bf16[8,5120]{1,0:T(8,128)(2,1)S(1)}, bf16[8,5120]{1,0:T(8,128)(2,1)S(1)}, u32[]{:S(2)}, u32[]{:S(2)}) collective-permute-start(bf16[8,5120]{1,0:T(8,128)(2,1)S(1)} %get-tuple-element.74), channel_id=1, source_target_pairs={{0,12},{2,14},{4,8},{6,10},{8,4},{10,6},{12,0},{14,2},{1,13},{3,15... | collective-permute-start | bytes 245768 | tf_op jit(solution)/shard_map/ppermute | solution.py:236
  27.7 2.6 %collective-permute-start.11 = (bf16[8,5120]{1,0:T(8,128)(2,1)S(1)}, bf16[8,5120]{1,0:T(8,128)(2,1)S(1)}, u32[]{:S(2)}, u32[]{:S(2)}) collective-permute-start(bf16[8,5120]{1,0:T(8,128)(2,1)S(1)} %get-tuple-element.76), channel_id=1, source_target_pairs={{0,4},{2,6},{4,0},{6,2},{8,12},{10,14},{12,8},{14,10},{1,5},{3,7},... | collective-permute-start | bytes 245768 | tf_op jit(solution)/shard_map/ppermute | solution.py:236
  30.3 1.2 %collective-permute-start.12 = (bf16[8,5120]{1,0:T(8,128)(2,1)S(1)}, bf16[8,5120]{1,0:T(8,128)(2,1)S(1)}, u32[]{:S(2)}, u32[]{:S(2)}) collective-permute-start(bf16[8,5120]{1,0:T(8,128)(2,1)S(1)} %get-tuple-element.77), channel_id=1, source_target_pairs={{0,10},{2,8},{4,14},{6,12},{8,2},{10,0},{12,6},{14,4},{1,11},{3,9}... | collective-permute-start | bytes 245768 | tf_op jit(solution)/shard_map/ppermute | solution.py:236
  31.5 2.0 %collective-permute-start.13 = (bf16[8,5120]{1,0:T(8,128)(2,1)S(1)}, bf16[8,5120]{1,0:T(8,128)(2,1)S(1)}, u32[]{:S(2)}, u32[]{:S(2)}) collective-permute-start(bf16[8,5120]{1,0:T(8,128)(2,1)S(1)} %get-tuple-element.78), channel_id=1, source_target_pairs={{0,8},{2,10},{4,12},{6,14},{8,0},{10,2},{12,4},{14,6},{1,9},{3,11}... | collective-permute-start | bytes 245768 | tf_op jit(solution)/shard_map/ppermute | solution.py:236
  33.6 1.2 %collective-permute-start.14 = (bf16[8,5120]{1,0:T(8,128)(2,1)S(1)}, bf16[8,5120]{1,0:T(8,128)(2,1)S(1)}, u32[]{:S(2)}, u32[]{:S(2)}) collective-permute-start(bf16[8,5120]{1,0:T(8,128)(2,1)S(1)} %get-tuple-element.79), channel_id=1, source_target_pairs={{0,2},{2,0},{4,6},{6,4},{8,10},{10,8},{12,14},{14,12},{1,3},{3,1},... | collective-permute-start | bytes 245768 | tf_op jit(solution)/shard_map/ppermute | solution.py:236
  34.7 1.9 %collective-permute-done.10.ret_refs_2_ = bf16[8,5120]{1,0:T(8,128)(2,1)S(1)} collective-permute-done((bf16[8,5120]{1,0:T(8,128)(2,1)S(1)}, bf16[8,5120]{1,0:T(8,128)(2,1)S(1)}, u32[]{:S(2)}, u32[]{:S(2)}) %collective-permute-start.10) | collective-permute-done | bytes 81952 | tf_op jit(solution)/shard_map/ppermute | solution.py:236
  36.6 1.6 %collective-permute-done.11.ret_refs_3_ = bf16[8,5120]{1,0:T(8,128)(2,1)S(1)} collective-permute-done((bf16[8,5120]{1,0:T(8,128)(2,1)S(1)}, bf16[8,5120]{1,0:T(8,128)(2,1)S(1)}, u32[]{:S(2)}, u32[]{:S(2)}) %collective-permute-start.11) | collective-permute-done | bytes 81952 | tf_op jit(solution)/shard_map/ppermute | solution.py:236
  38.2 2.2 %collective-permute-done.12.ret_refs_4_ = bf16[8,5120]{1,0:T(8,128)(2,1)S(1)} collective-permute-done((bf16[8,5120]{1,0:T(8,128)(2,1)S(1)}, bf16[8,5120]{1,0:T(8,128)(2,1)S(1)}, u32[]{:S(2)}, u32[]{:S(2)}) %collective-permute-start.12) | collective-permute-done | bytes 81952 | tf_op jit(solution)/shard_map/ppermute | solution.py:236
  40.4 0.1 collective-permute-done.13.ret_refs_5_
  40.5 0.0 collective-permute-done.14.ret_refs_6_
  40.5 0.0 copy-start.4
  40.5 0.0 copy-start.3
  40.5 3.7 %shard_map.153 = (bf16[8,4096]{1,0:T(8,128)(2,1)S(1)}, bf16[8,4096]{1,0:T(8,128)(2,1)S(1)}, bf16[8,4096]{1,0:T(8,128)(2,1)S(1)}, bf16[8,4096]{1,0:T(8,128)(2,1)S...) custom-call(bf16[8,5120]{1,0:T(8,128)(2,1)S(1)} %collective-permute-, ...), custom_call_target="tpu_custom_call" | custom-call | bytes 8000000 | tf_op jit(solution)/shard_map/pallas_call | solution.py:318
  44.2 2.8 %collective-permute-start.15 = (bf16[8,4096]{1,0:T(8,128)(2,1)S(1)}, bf16[8,4096]{1,0:T(8,128)(2,1)S(1)}, u32[]{:S(2)}, u32[]{:S(2)}) collective-permute-start(bf16[8,4096]{1,0:T(8,128)(2,1)S(1)} %get-tuple-element.86), channel_id=1, source_target_pairs={{0,14},{2,12},{4,10},{6,8},{8,6},{10,4},{12,2},{14,0},{1,15},{3,13... | collective-permute-start | bytes 196616 | tf_op jit(solution)/shard_map/ppermute | solution.py:236
  47.0 1.8 %collective-permute-start.16 = (bf16[8,4096]{1,0:T(8,128)(2,1)S(1)}, bf16[8,4096]{1,0:T(8,128)(2,1)S(1)}, u32[]{:S(2)}, u32[]{:S(2)}) collective-permute-start(bf16[8,4096]{1,0:T(8,128)(2,1)S(1)} %get-tuple-element.87), channel_id=1, source_target_pairs={{0,12},{2,14},{4,8},{6,10},{8,4},{10,6},{12,0},{14,2},{1,13},{3,15... | collective-permute-start | bytes 196616 | tf_op jit(solution)/shard_map/ppermute | solution.py:236
  48.8 2.1 %collective-permute-start.18 = (bf16[8,4096]{1,0:T(8,128)(2,1)S(1)}, bf16[8,4096]{1,0:T(8,128)(2,1)S(1)}, u32[]{:S(2)}, u32[]{:S(2)}) collective-permute-start(bf16[8,4096]{1,0:T(8,128)(2,1)S(1)} %get-tuple-element.89), channel_id=1, source_target_pairs={{0,4},{2,6},{4,0},{6,2},{8,12},{10,14},{12,8},{14,10},{1,5},{3,7},... | collective-permute-start | bytes 196616 | tf_op jit(solution)/shard_map/ppermute | solution.py:236
  50.9 1.4 %collective-permute-start.19 = (bf16[8,4096]{1,0:T(8,128)(2,1)S(1)}, bf16[8,4096]{1,0:T(8,128)(2,1)S(1)}, u32[]{:S(2)}, u32[]{:S(2)}) collective-permute-start(bf16[8,4096]{1,0:T(8,128)(2,1)S(1)} %get-tuple-element.90), channel_id=1, source_target_pairs={{0,10},{2,8},{4,14},{6,12},{8,2},{10,0},{12,6},{14,4},{1,11},{3,9}... | collective-permute-start | bytes 196616 | tf_op jit(solution)/shard_map/ppermute | solution.py:236
  52.3 0.0 collective-permute-done.15.ret_refs_0_
  52.3 2.4 %collective-permute-start.20 = (bf16[8,4096]{1,0:T(8,128)(2,1)S(1)}, bf16[8,4096]{1,0:T(8,128)(2,1)S(1)}, u32[]{:S(2)}, u32[]{:S(2)}) collective-permute-start(bf16[8,4096]{1,0:T(8,128)(2,1)S(1)} %get-tuple-element.91), channel_id=1, source_target_pairs={{0,8},{2,10},{4,12},{6,14},{8,0},{10,2},{12,4},{14,6},{1,9},{3,11}... | collective-permute-start | bytes 196616 | tf_op jit(solution)/shard_map/ppermute | solution.py:236
  54.7 0.7 collective-permute-start.21
  55.3 0.0 collective-permute-done.17.ret_refs_2_
  55.3 0.2 collective-permute-done.18.ret_refs_3_
  55.5 1.9 %collective-permute-done.19.ret_refs_4_ = bf16[8,4096]{1,0:T(8,128)(2,1)S(1)} collective-permute-done((bf16[8,4096]{1,0:T(8,128)(2,1)S(1)}, bf16[8,4096]{1,0:T(8,128)(2,1)S(1)}, u32[]{:S(2)}, u32[]{:S(2)}) %collective-permute-start.19) | collective-permute-done | bytes 65568 | tf_op jit(solution)/shard_map/ppermute | solution.py:236
  57.4 0.3 collective-permute-done.20.ret_refs_5_
  57.7 1.2 %collective-permute-done.21.ret_refs_6_ = bf16[8,4096]{1,0:T(8,128)(2,1)S(1)} collective-permute-done((bf16[8,4096]{1,0:T(8,128)(2,1)S(1)}, bf16[8,4096]{1,0:T(8,128)(2,1)S(1)}, u32[]{:S(2)}, u32[]{:S(2)}) %collective-permute-start.21) | collective-permute-done | bytes 65568 | tf_op jit(solution)/shard_map/ppermute | solution.py:236
  58.9 0.3 shard_map.154.mine_ref
  59.2 0.1 collective-permute-start.22
  59.3 1.2 %collective-permute-done.22.other_ref = f32[64,64]{1,0:T(8,128)S(1)} collective-permute-done((f32[64,64]{1,0:T(8,128)S(1)}, f32[64,64]{1,0:T(8,128)S(1)}, u32[]{:S(2)}, u32[]{:S(2)}) %collective-permute-start.22) | collective-permute-done | bytes 16416 | tf_op jit(solution)/shard_map/ppermute | solution.py:243
  60.5 0.3 shard_map.155
  60.8 2.3 %collective-permute-start.23 = (bf16[8,4096]{1,0:T(8,128)(2,1)S(1)}, bf16[8,4096]{1,0:T(8,128)(2,1)S(1)}, u32[]{:S(2)}, u32[]{:S(2)}) collective-permute-start(bf16[8,4096]{1,0:T(8,128)(2,1)S(1)} %get-tuple-element.94), channel_id=1, source_target_pairs={{0,14},{2,12},{4,10},{6,8},{8,6},{10,4},{12,2},{14,0},{1,15},{3,13... | collective-permute-start | bytes 196616 | tf_op jit(solution)/shard_map/ppermute | solution.py:236
  63.1 1.7 %collective-permute-start.24 = (bf16[8,4096]{1,0:T(8,128)(2,1)S(1)}, bf16[8,4096]{1,0:T(8,128)(2,1)S(1)}, u32[]{:S(2)}, u32[]{:S(2)}) collective-permute-start(bf16[8,4096]{1,0:T(8,128)(2,1)S(1)} %get-tuple-element.95), channel_id=1, source_target_pairs={{0,12},{2,14},{4,8},{6,10},{8,4},{10,6},{12,0},{14,2},{1,13},{3,15... | collective-permute-start | bytes 196616 | tf_op jit(solution)/shard_map/ppermute | solution.py:236
  64.8 0.0 collective-permute-start.25
  64.8 2.8 %collective-permute-start.26 = (bf16[8,4096]{1,0:T(8,128)(2,1)S(1)}, bf16[8,4096]{1,0:T(8,128)(2,1)S(1)}, u32[]{:S(2)}, u32[]{:S(2)}) collective-permute-start(bf16[8,4096]{1,0:T(8,128)(2,1)S(1)} %get-tuple-element.97), channel_id=1, source_target_pairs={{0,4},{2,6},{4,0},{6,2},{8,12},{10,14},{12,8},{14,10},{1,5},{3,7},... | collective-permute-start | bytes 196616 | tf_op jit(solution)/shard_map/ppermute | solution.py:236
  67.6 0.8 %collective-permute-start.27 = (bf16[8,4096]{1,0:T(8,128)(2,1)S(1)}, bf16[8,4096]{1,0:T(8,128)(2,1)S(1)}, u32[]{:S(2)}, u32[]{:S(2)}) collective-permute-start(bf16[8,4096]{1,0:T(8,128)(2,1)S(1)} %get-tuple-element.98), channel_id=1, source_target_pairs={{0,10},{2,8},{4,14},{6,12},{8,2},{10,0},{12,6},{14,4},{1,11},{3,9}... | collective-permute-start | bytes 196616 | tf_op jit(solution)/shard_map/ppermute | solution.py:236
  68.4 2.2 %collective-permute-start.28 = (bf16[8,4096]{1,0:T(8,128)(2,1)S(1)}, bf16[8,4096]{1,0:T(8,128)(2,1)S(1)}, u32[]{:S(2)}, u32[]{:S(2)}) collective-permute-start(bf16[8,4096]{1,0:T(8,128)(2,1)S(1)} %get-tuple-element.99), channel_id=1, source_target_pairs={{0,8},{2,10},{4,12},{6,14},{8,0},{10,2},{12,4},{14,6},{1,9},{3,11}... | collective-permute-start | bytes 196616 | tf_op jit(solution)/shard_map/ppermute | solution.py:236
  70.6 1.4 %collective-permute-start.29 = (bf16[8,4096]{1,0:T(8,128)(2,1)S(1)}, bf16[8,4096]{1,0:T(8,128)(2,1)S(1)}, u32[]{:S(2)}, u32[]{:S(2)}) collective-permute-start(bf16[8,4096]{1,0:T(8,128)(2,1)S(1)} %get-tuple-element.100), channel_id=1, source_target_pairs={{0,2},{2,0},{4,6},{6,4},{8,10},{10,8},{12,14},{14,12},{1,3},{3,1},... | collective-permute-start | bytes 196616 | tf_op jit(solution)/shard_map/ppermute | solution.py:236
  72.0 1.0 %collective-permute-done.26.ret_refs_3_ = bf16[8,4096]{1,0:T(8,128)(2,1)S(1)} collective-permute-done((bf16[8,4096]{1,0:T(8,128)(2,1)S(1)}, bf16[8,4096]{1,0:T(8,128)(2,1)S(1)}, u32[]{:S(2)}, u32[]{:S(2)}) %collective-permute-start.26) | collective-permute-done | bytes 65568 | tf_op jit(solution)/shard_map/ppermute | solution.py:236
  73.0 3.0 %collective-permute-done.27.ret_refs_4_ = bf16[8,4096]{1,0:T(8,128)(2,1)S(1)} collective-permute-done((bf16[8,4096]{1,0:T(8,128)(2,1)S(1)}, bf16[8,4096]{1,0:T(8,128)(2,1)S(1)}, u32[]{:S(2)}, u32[]{:S(2)}) %collective-permute-start.27) | collective-permute-done | bytes 65568 | tf_op jit(solution)/shard_map/ppermute | solution.py:236
  76.0 0.9 %shard_map.156 = bf16[32,4096]{1,0:T(8,128)(2,1)} custom-call(bf16[32,64]{1,0:T(8,128)(2,1)S(1)} %get-tuple-element.84.home_ref, bf16[8,4096]{1,0:T(8,128)(2,1)S(1)} %collective-permute-done.23.ret_refs_0_, bf16[8,4096]{1,0:T(8,128)(2,1)S(1)} %collective-permute-done.24.ret_refs_1_, bf16[8,4096]{1,0:T(8,128)(2,1)S(1)} %collective-permute-done.25.ret_refs_2_, ...), custom_call_target="tpu_custom_call" | custom-call | bytes 1000000 | tf_op jit(solution)/shard_map/pallas_call | solution.py:338
  (28 shorter events, 0.1 us)
Async XLA Ops:
  0.6 20.6 %copy-start.2 = (bf16[1,192,8192]{2,1,0:T(8,128)(2,1)S(1)}, bf16[1,192,8192]{2,1,0:T(8,128)(2,1)}, u32[]{:S(2)}) copy-start(bf16[1,192,8192]{2,1,0:T(8,128)(2,1)} %down_ref.2) | copy-start | bytes 9437188
  2.8 18.3 %copy-start.6 = (bf16[8,4096]{1,0:T(8,128)(2,1)S(1)}, bf16[8,4096]{1,0:T(8,128)(2,1)}, u32[]{:S(2)}) copy-start(bf16[8,4096]{1,0:T(8,128)(2,1)} %get-tuple-element.72.ret_refs_7_) | copy-start | bytes 196612
  2.9 11.4 %collective-permute-start = (bf16[8,4096]{1,0:T(8,128)(2,1)}, bf16[8,4096]{1,0:T(8,128)(2,1)S(1)}, u32[]{:S(2)}, u32[]{:S(2)}) collective-permute-start(bf16[8,4096]{1,0:T(8,128)(2,1)} %get-tuple-element.52), channel_id=1, source_target_pairs={{0,14},{2,12},{4,10},{6,8},{8,6},{10,4},{12,2},{14,0},{1,15},{3,13... | collective-permute-start | bytes 196616 | tf_op jit(solution)/shard_map/ppermute | solution.py:236
  8.9 7.0 %collective-permute-start.1 = (bf16[8,4096]{1,0:T(8,128)(2,1)}, bf16[8,4096]{1,0:T(8,128)(2,1)S(1)}, u32[]{:S(2)}, u32[]{:S(2)}) collective-permute-start(bf16[8,4096]{1,0:T(8,128)(2,1)} %get-tuple-element.53), channel_id=1, source_target_pairs={{0,12},{2,14},{4,8},{6,10},{8,4},{10,6},{12,0},{14,2},{1,13},{3,15... | collective-permute-start | bytes 196616 | tf_op jit(solution)/shard_map/ppermute | solution.py:236
  9.1 7.7 %collective-permute-start.2 = (bf16[8,4096]{1,0:T(8,128)(2,1)}, bf16[8,4096]{1,0:T(8,128)(2,1)S(1)}, u32[]{:S(2)}, u32[]{:S(2)}) collective-permute-start(bf16[8,4096]{1,0:T(8,128)(2,1)} %get-tuple-element.54), channel_id=1, source_target_pairs={{0,6},{2,4},{4,2},{6,0},{8,14},{10,12},{12,10},{14,8},{1,7},{3,5},... | collective-permute-start | bytes 196616 | tf_op jit(solution)/shard_map/ppermute | solution.py:236
  9.1 7.8 %collective-permute-start.3 = (bf16[8,4096]{1,0:T(8,128)(2,1)}, bf16[8,4096]{1,0:T(8,128)(2,1)S(1)}, u32[]{:S(2)}, u32[]{:S(2)}) collective-permute-start(bf16[8,4096]{1,0:T(8,128)(2,1)} %get-tuple-element.55), channel_id=1, source_target_pairs={{0,4},{2,6},{4,0},{6,2},{8,12},{10,14},{12,8},{14,10},{1,5},{3,7},... | collective-permute-start | bytes 196616 | tf_op jit(solution)/shard_map/ppermute | solution.py:236
  11.0 9.0 %collective-permute-start.4 = (bf16[8,4096]{1,0:T(8,128)(2,1)}, bf16[8,4096]{1,0:T(8,128)(2,1)S(1)}, u32[]{:S(2)}, u32[]{:S(2)}) collective-permute-start(bf16[8,4096]{1,0:T(8,128)(2,1)} %get-tuple-element.56), channel_id=1, source_target_pairs={{0,10},{2,8},{4,14},{6,12},{8,2},{10,0},{12,6},{14,4},{1,11},{3,9}... | collective-permute-start | bytes 196616 | tf_op jit(solution)/shard_map/ppermute | solution.py:236
  14.2 7.0 %collective-permute-start.5 = (bf16[8,4096]{1,0:T(8,128)(2,1)}, bf16[8,4096]{1,0:T(8,128)(2,1)S(1)}, u32[]{:S(2)}, u32[]{:S(2)}) collective-permute-start(bf16[8,4096]{1,0:T(8,128)(2,1)} %get-tuple-element.57), channel_id=1, source_target_pairs={{0,8},{2,10},{4,12},{6,14},{8,0},{10,2},{12,4},{14,6},{1,9},{3,11}... | collective-permute-start | bytes 196616 | tf_op jit(solution)/shard_map/ppermute | solution.py:236
  15.9 5.2 %collective-permute-start.6 = (bf16[8,4096]{1,0:T(8,128)(2,1)}, bf16[8,4096]{1,0:T(8,128)(2,1)S(1)}, u32[]{:S(2)}, u32[]{:S(2)}) collective-permute-start(bf16[8,4096]{1,0:T(8,128)(2,1)} %get-tuple-element.58), channel_id=1, source_target_pairs={{0,2},{2,0},{4,6},{6,4},{8,10},{10,8},{12,14},{14,12},{1,3},{3,1},... | collective-permute-start | bytes 196616 | tf_op jit(solution)/shard_map/ppermute | solution.py:236
  16.1 0.7 copy-start.11
  16.7 6.5 %copy-start.9 = (bf16[1,64,4096]{2,1,0:T(8,128)(2,1)S(1)}, bf16[1,64,4096]{2,1,0:T(8,128)(2,1)}, u32[]{:S(2)}) copy-start(bf16[1,64,4096]{2,1,0:T(8,128)(2,1)} %uq_ref.1) | copy-start | bytes 1572868
  16.7 6.5 %copy-start.10 = (bf16[1,2,64,512]{3,2,1,0:T(8,128)(2,1)S(1)}, bf16[1,2,64,512]{3,2,1,0:T(8,128)(2,1)}, u32[]{:S(2)}) copy-start(bf16[1,2,64,512]{3,2,1,0:T(8,128)(2,1)} %ukv_ref.1) | copy-start | bytes 393220
  21.2 19.3 %copy-start = (bf16[32,4,96,128]{3,2,1,0:T(8,128)(2,1)S(1)}, bf16[32,4,96,128]{3,2,1,0:T(8,128)(2,1)}, u32[]{:S(2)}) copy-start(bf16[32,4,96,128]{3,2,1,0:T(8,128)(2,1)} %k_ref.1) | copy-start | bytes 9437188
  21.2 19.3 %copy-start.1 = (bf16[32,4,96,128]{3,2,1,0:T(8,128)(2,1)S(1)}, bf16[32,4,96,128]{3,2,1,0:T(8,128)(2,1)}, u32[]{:S(2)}) copy-start(bf16[32,4,96,128]{3,2,1,0:T(8,128)(2,1)} %v_ref.1) | copy-start | bytes 9437188
  21.2 19.3 %copy-start.5 = (bf16[32,4096]{1,0:T(8,128)(2,1)S(1)}, bf16[32,4096]{1,0:T(8,128)(2,1)}, u32[]{:S(2)}) copy-start(bf16[32,4096]{1,0:T(8,128)(2,1)} %pq_ref.1) | copy-start | bytes 786436
  21.2 19.3 %copy-start.7 = (bf16[32,512]{1,0:T(8,128)(2,1)S(1)}, bf16[32,512]{1,0:T(8,128)(2,1)}, u32[]{:S(2)}) copy-start(bf16[32,512]{1,0:T(8,128)(2,1)} %pk_ref.1) | copy-start | bytes 98308
  21.2 19.3 %copy-start.8 = (bf16[32,512]{1,0:T(8,128)(2,1)S(1)}, bf16[32,512]{1,0:T(8,128)(2,1)}, u32[]{:S(2)}) copy-start(bf16[32,512]{1,0:T(8,128)(2,1)} %pv_ref.1) | copy-start | bytes 98308
  21.9 1.3 %collective-permute-start.7 = (f32[64,192]{1,0:T(8,128)S(1)}, f32[64,192]{1,0:T(8,128)S(1)}, u32[]{:S(2)}, u32[]{:S(2)}) collective-permute-start(f32[64,192]{1,0:T(8,128)S(1)} %shard_map.151.mine_ref), channel_id=1, source_target_pairs={{0,1},{1,0},{2,3},{3,2},{4,5},{5,4},{6,7},{7,6},{8,9},{9,8},{10,11... | collective-permute-start | bytes 147464 | tf_op jit(solution)/shard_map/ppermute | solution.py:243
  23.5 8.0 %collective-permute-start.8 = (bf16[8,5120]{1,0:T(8,128)(2,1)S(1)}, bf16[8,5120]{1,0:T(8,128)(2,1)S(1)}, u32[]{:S(2)}, u32[]{:S(2)}) collective-permute-start(bf16[8,5120]{1,0:T(8,128)(2,1)S(1)} %get-tuple-element.73), channel_id=1, source_target_pairs={{0,14},{2,12},{4,10},{6,8},{8,6},{10,4},{12,2},{14,0},{1,15},{3,13... | collective-permute-start | bytes 245768 | tf_op jit(solution)/shard_map/ppermute | solution.py:236
  26.3 7.3 %collective-permute-start.9 = (bf16[8,5120]{1,0:T(8,128)(2,1)S(1)}, bf16[8,5120]{1,0:T(8,128)(2,1)S(1)}, u32[]{:S(2)}, u32[]{:S(2)}) collective-permute-start(bf16[8,5120]{1,0:T(8,128)(2,1)S(1)} %get-tuple-element.74), channel_id=1, source_target_pairs={{0,12},{2,14},{4,8},{6,10},{8,4},{10,6},{12,0},{14,2},{1,13},{3,15... | collective-permute-start | bytes 245768 | tf_op jit(solution)/shard_map/ppermute | solution.py:236
  27.7 8.9 %collective-permute-start.10 = (bf16[8,5120]{1,0:T(8,128)(2,1)S(1)}, bf16[8,5120]{1,0:T(8,128)(2,1)S(1)}, u32[]{:S(2)}, u32[]{:S(2)}) collective-permute-start(bf16[8,5120]{1,0:T(8,128)(2,1)S(1)} %get-tuple-element.75), channel_id=1, source_target_pairs={{0,6},{2,4},{4,2},{6,0},{8,14},{10,12},{12,10},{14,8},{1,7},{3,5},... | collective-permute-start | bytes 245768 | tf_op jit(solution)/shard_map/ppermute | solution.py:236
  27.7 10.5 %collective-permute-start.11 = (bf16[8,5120]{1,0:T(8,128)(2,1)S(1)}, bf16[8,5120]{1,0:T(8,128)(2,1)S(1)}, u32[]{:S(2)}, u32[]{:S(2)}) collective-permute-start(bf16[8,5120]{1,0:T(8,128)(2,1)S(1)} %get-tuple-element.76), channel_id=1, source_target_pairs={{0,4},{2,6},{4,0},{6,2},{8,12},{10,14},{12,8},{14,10},{1,5},{3,7},... | collective-permute-start | bytes 245768 | tf_op jit(solution)/shard_map/ppermute | solution.py:236
  30.3 10.0 %collective-permute-start.12 = (bf16[8,5120]{1,0:T(8,128)(2,1)S(1)}, bf16[8,5120]{1,0:T(8,128)(2,1)S(1)}, u32[]{:S(2)}, u32[]{:S(2)}) collective-permute-start(bf16[8,5120]{1,0:T(8,128)(2,1)S(1)} %get-tuple-element.77), channel_id=1, source_target_pairs={{0,10},{2,8},{4,14},{6,12},{8,2},{10,0},{12,6},{14,4},{1,11},{3,9}... | collective-permute-start | bytes 245768 | tf_op jit(solution)/shard_map/ppermute | solution.py:236
  31.5 8.9 %collective-permute-start.13 = (bf16[8,5120]{1,0:T(8,128)(2,1)S(1)}, bf16[8,5120]{1,0:T(8,128)(2,1)S(1)}, u32[]{:S(2)}, u32[]{:S(2)}) collective-permute-start(bf16[8,5120]{1,0:T(8,128)(2,1)S(1)} %get-tuple-element.78), channel_id=1, source_target_pairs={{0,8},{2,10},{4,12},{6,14},{8,0},{10,2},{12,4},{14,6},{1,9},{3,11}... | collective-permute-start | bytes 245768 | tf_op jit(solution)/shard_map/ppermute | solution.py:236
  33.6 6.9 %collective-permute-start.14 = (bf16[8,5120]{1,0:T(8,128)(2,1)S(1)}, bf16[8,5120]{1,0:T(8,128)(2,1)S(1)}, u32[]{:S(2)}, u32[]{:S(2)}) collective-permute-start(bf16[8,5120]{1,0:T(8,128)(2,1)S(1)} %get-tuple-element.79), channel_id=1, source_target_pairs={{0,2},{2,0},{4,6},{6,4},{8,10},{10,8},{12,14},{14,12},{1,3},{3,1},... | collective-permute-start | bytes 245768 | tf_op jit(solution)/shard_map/ppermute | solution.py:236
  40.5 18.4 %copy-start.4 = (bf16[1,64,4096]{2,1,0:T(8,128)(2,1)S(1)}, bf16[1,64,4096]{2,1,0:T(8,128)(2,1)}, u32[]{:S(2)}) copy-start(bf16[1,64,4096]{2,1,0:T(8,128)(2,1)} %down_ref.3) | copy-start | bytes 1572868
  40.5 20.0 %copy-start.3 = (bf16[1,64,4096]{2,1,0:T(8,128)(2,1)S(1)}, bf16[1,64,4096]{2,1,0:T(8,128)(2,1)}, u32[]{:S(2)}) copy-start(bf16[1,64,4096]{2,1,0:T(8,128)(2,1)} %uo_ref.1) | copy-start | bytes 1572868
  44.2 8.1 %collective-permute-start.15 = (bf16[8,4096]{1,0:T(8,128)(2,1)S(1)}, bf16[8,4096]{1,0:T(8,128)(2,1)S(1)}, u32[]{:S(2)}, u32[]{:S(2)}) collective-permute-start(bf16[8,4096]{1,0:T(8,128)(2,1)S(1)} %get-tuple-element.86), channel_id=1, source_target_pairs={{0,14},{2,12},{4,10},{6,8},{8,6},{10,4},{12,2},{14,0},{1,15},{3,13... | collective-permute-start | bytes 196616 | tf_op jit(solution)/shard_map/ppermute | solution.py:236
  47.0 7.7 %collective-permute-start.16 = (bf16[8,4096]{1,0:T(8,128)(2,1)S(1)}, bf16[8,4096]{1,0:T(8,128)(2,1)S(1)}, u32[]{:S(2)}, u32[]{:S(2)}) collective-permute-start(bf16[8,4096]{1,0:T(8,128)(2,1)S(1)} %get-tuple-element.87), channel_id=1, source_target_pairs={{0,12},{2,14},{4,8},{6,10},{8,4},{10,6},{12,0},{14,2},{1,13},{3,15... | collective-permute-start | bytes 196616 | tf_op jit(solution)/shard_map/ppermute | solution.py:236
  48.8 6.5 %collective-permute-start.17 = (bf16[8,4096]{1,0:T(8,128)(2,1)S(1)}, bf16[8,4096]{1,0:T(8,128)(2,1)S(1)}, u32[]{:S(2)}, u32[]{:S(2)}) collective-permute-start(bf16[8,4096]{1,0:T(8,128)(2,1)S(1)} %get-tuple-element.88), channel_id=1, source_target_pairs={{0,6},{2,4},{4,2},{6,0},{8,14},{10,12},{12,10},{14,8},{1,7},{3,5},... | collective-permute-start | bytes 196616 | tf_op jit(solution)/shard_map/ppermute | solution.py:236
  48.8 6.7 %collective-permute-start.18 = (bf16[8,4096]{1,0:T(8,128)(2,1)S(1)}, bf16[8,4096]{1,0:T(8,128)(2,1)S(1)}, u32[]{:S(2)}, u32[]{:S(2)}) collective-permute-start(bf16[8,4096]{1,0:T(8,128)(2,1)S(1)} %get-tuple-element.89), channel_id=1, source_target_pairs={{0,4},{2,6},{4,0},{6,2},{8,12},{10,14},{12,8},{14,10},{1,5},{3,7},... | collective-permute-start | bytes 196616 | tf_op jit(solution)/shard_map/ppermute | solution.py:236
  50.9 6.5 %collective-permute-start.19 = (bf16[8,4096]{1,0:T(8,128)(2,1)S(1)}, bf16[8,4096]{1,0:T(8,128)(2,1)S(1)}, u32[]{:S(2)}, u32[]{:S(2)}) collective-permute-start(bf16[8,4096]{1,0:T(8,128)(2,1)S(1)} %get-tuple-element.90), channel_id=1, source_target_pairs={{0,10},{2,8},{4,14},{6,12},{8,2},{10,0},{12,6},{14,4},{1,11},{3,9}... | collective-permute-start | bytes 196616 | tf_op jit(solution)/shard_map/ppermute | solution.py:236
  52.3 5.4 %collective-permute-start.20 = (bf16[8,4096]{1,0:T(8,128)(2,1)S(1)}, bf16[8,4096]{1,0:T(8,128)(2,1)S(1)}, u32[]{:S(2)}, u32[]{:S(2)}) collective-permute-start(bf16[8,4096]{1,0:T(8,128)(2,1)S(1)} %get-tuple-element.91), channel_id=1, source_target_pairs={{0,8},{2,10},{4,12},{6,14},{8,0},{10,2},{12,4},{14,6},{1,9},{3,11}... | collective-permute-start | bytes 196616 | tf_op jit(solution)/shard_map/ppermute | solution.py:236
  54.7 4.3 %collective-permute-start.21 = (bf16[8,4096]{1,0:T(8,128)(2,1)S(1)}, bf16[8,4096]{1,0:T(8,128)(2,1)S(1)}, u32[]{:S(2)}, u32[]{:S(2)}) collective-permute-start(bf16[8,4096]{1,0:T(8,128)(2,1)S(1)} %get-tuple-element.92), channel_id=1, source_target_pairs={{0,2},{2,0},{4,6},{6,4},{8,10},{10,8},{12,14},{14,12},{1,3},{3,1},... | collective-permute-start | bytes 196616 | tf_op jit(solution)/shard_map/ppermute | solution.py:236
  59.2 1.3 %collective-permute-start.22 = (f32[64,64]{1,0:T(8,128)S(1)}, f32[64,64]{1,0:T(8,128)S(1)}, u32[]{:S(2)}, u32[]{:S(2)}) collective-permute-start(f32[64,64]{1,0:T(8,128)S(1)} %shard_map.154.mine_ref), channel_id=1, source_target_pairs={{0,1},{1,0},{2,3},{3,2},{4,5},{5,4},{6,7},{7,6},{8,9},{9,8},{10,11... | collective-permute-start | bytes 49160 | tf_op jit(solution)/shard_map/ppermute | solution.py:243
  60.8 7.6 %collective-permute-start.23 = (bf16[8,4096]{1,0:T(8,128)(2,1)S(1)}, bf16[8,4096]{1,0:T(8,128)(2,1)S(1)}, u32[]{:S(2)}, u32[]{:S(2)}) collective-permute-start(bf16[8,4096]{1,0:T(8,128)(2,1)S(1)} %get-tuple-element.94), channel_id=1, source_target_pairs={{0,14},{2,12},{4,10},{6,8},{8,6},{10,4},{12,2},{14,0},{1,15},{3,13... | collective-permute-start | bytes 196616 | tf_op jit(solution)/shard_map/ppermute | solution.py:236
  63.1 7.5 %collective-permute-start.24 = (bf16[8,4096]{1,0:T(8,128)(2,1)S(1)}, bf16[8,4096]{1,0:T(8,128)(2,1)S(1)}, u32[]{:S(2)}, u32[]{:S(2)}) collective-permute-start(bf16[8,4096]{1,0:T(8,128)(2,1)S(1)} %get-tuple-element.95), channel_id=1, source_target_pairs={{0,12},{2,14},{4,8},{6,10},{8,4},{10,6},{12,0},{14,2},{1,13},{3,15... | collective-permute-start | bytes 196616 | tf_op jit(solution)/shard_map/ppermute | solution.py:236
  64.8 7.2 %collective-permute-start.25 = (bf16[8,4096]{1,0:T(8,128)(2,1)S(1)}, bf16[8,4096]{1,0:T(8,128)(2,1)S(1)}, u32[]{:S(2)}, u32[]{:S(2)}) collective-permute-start(bf16[8,4096]{1,0:T(8,128)(2,1)S(1)} %get-tuple-element.96), channel_id=1, source_target_pairs={{0,6},{2,4},{4,2},{6,0},{8,14},{10,12},{12,10},{14,8},{1,7},{3,5},... | collective-permute-start | bytes 196616 | tf_op jit(solution)/shard_map/ppermute | solution.py:236
  64.8 8.2 %collective-permute-start.26 = (bf16[8,4096]{1,0:T(8,128)(2,1)S(1)}, bf16[8,4096]{1,0:T(8,128)(2,1)S(1)}, u32[]{:S(2)}, u32[]{:S(2)}) collective-permute-start(bf16[8,4096]{1,0:T(8,128)(2,1)S(1)} %get-tuple-element.97), channel_id=1, source_target_pairs={{0,4},{2,6},{4,0},{6,2},{8,12},{10,14},{12,8},{14,10},{1,5},{3,7},... | collective-permute-start | bytes 196616 | tf_op jit(solution)/shard_map/ppermute | solution.py:236
  67.6 8.4 %collective-permute-start.27 = (bf16[8,4096]{1,0:T(8,128)(2,1)S(1)}, bf16[8,4096]{1,0:T(8,128)(2,1)S(1)}, u32[]{:S(2)}, u32[]{:S(2)}) collective-permute-start(bf16[8,4096]{1,0:T(8,128)(2,1)S(1)} %get-tuple-element.98), channel_id=1, source_target_pairs={{0,10},{2,8},{4,14},{6,12},{8,2},{10,0},{12,6},{14,4},{1,11},{3,9}... | collective-permute-start | bytes 196616 | tf_op jit(solution)/shard_map/ppermute | solution.py:236
  68.4 7.6 %collective-permute-start.28 = (bf16[8,4096]{1,0:T(8,128)(2,1)S(1)}, bf16[8,4096]{1,0:T(8,128)(2,1)S(1)}, u32[]{:S(2)}, u32[]{:S(2)}) collective-permute-start(bf16[8,4096]{1,0:T(8,128)(2,1)S(1)} %get-tuple-element.99), channel_id=1, source_target_pairs={{0,8},{2,10},{4,12},{6,14},{8,0},{10,2},{12,4},{14,6},{1,9},{3,11}... | collective-permute-start | bytes 196616 | tf_op jit(solution)/shard_map/ppermute | solution.py:236
  70.6 5.3 %collective-permute-start.29 = (bf16[8,4096]{1,0:T(8,128)(2,1)S(1)}, bf16[8,4096]{1,0:T(8,128)(2,1)S(1)}, u32[]{:S(2)}, u32[]{:S(2)}) collective-permute-start(bf16[8,4096]{1,0:T(8,128)(2,1)S(1)} %get-tuple-element.100), channel_id=1, source_target_pairs={{0,2},{2,0},{4,6},{6,4},{8,10},{10,8},{12,14},{14,12},{1,3},{3,1},... | collective-permute-start | bytes 196616 | tf_op jit(solution)/shard_map/ppermute | solution.py:236

commit v8 on v7

--- a/solution.py
+++ b/solution.py
@@ -8,6 +8,7 @@
 from jax.sharding import PartitionSpec as P
 
 ADAPTER_SCALE = 0.5
+SEND_ORDER = (7, 2, 5, 4, 3, 6, 1)
 F32 = jnp.float32
 BF16 = jnp.bfloat16
 VMEM = pl.BlockSpec(memory_space=pltpu.VMEM)
@@ -49,7 +50,7 @@
 
 
 def distances(count):
-    return sorted(range(1, count), key=lambda d: (d >> 1 & 1, d), reverse=True) + [0]
+    return [d for d in SEND_ORDER if d < count] + [0]
 
 
 def joined(refs):

time: 77 us -> 75.2 us (0.977)
  waiting for transfers between devices: 21 us -> 16.7 us
  starting transfers between devices: 45.9 us -> 48.3 us
    ppermute x28, waiting for transfers between devices: 18.5 us -> 14.3 us  [exchange(): lax.ppermute(block, 'wide', [(k, k ^ d) for k in range(wide_count)])]
    ppermute x28, starting transfers between devices: 45.8 us -> 48.2 us  [exchange(): lax.ppermute(block, 'wide', [(k, k ^ d) for k in range(wide_count)])]
  transfers between devices with their start and end apart: 30 -> 30, of which waited for: 15 -> 12; matrix products, arithmetic and copies ran while one was open for 0% -> 0% of each run, Pallas kernels for 0% -> 0%
where the time goes in v8:
time: 75.2 us; the launch traced here: 75 us
  starting transfers between devices  48.3 us (64%)
  waiting for transfers between devices  16.7 us (22%)
  Pallas kernels  8.41 us (11%)
  between operations  0.84 us (1%)
    ppermute x28, starting transfers between devices, exchange(): lax.ppermute(block, 'wide', [(k, k ^ d) for k in range(wide_count)])  48.2 us
    ppermute x28, waiting for transfers between devices, exchange(): lax.ppermute(block, 'wide', [(k, k ^ d) for k in range(wide_count)])  14.3 us
    pallas_call x1, Pallas kernels, shards(): call(functools.partial(attend_body, group), [*blocks_of(query_width), str...  3.65 us
    ppermute x2, waiting for transfers between devices, other_core(): return lax.ppermute(value, 'tp', [(0, 1), (1, 0)])  2.44 us
    pallas_call x1, Pallas kernels, shards(): call(functools.partial(pack_body, capacity, by_distance), (struct((2, row...  2.19 us
  transfers between devices with their start and end apart: 30, of which 12 were waited for; matrix products, arithmetic and copies ran while one was open for 0% of the time, Pallas kernels for 0%

profile of v8, /device:TPU:0, one launch (start us, length us, event | category | flops | bytes accessed | tf_op | source)
XLA Modules:
  0.0 75.0 jit_solution(9238385824470955658)
XLA Ops:
  0.6 2.2 %shard_map.149 = (s32[2,32]{1,0:T(2,128)}, bf16[8,4096]{1,0:T(8,128)(2,1)}, bf16[8,4096]{1,0:T(8,128)(2,1)}, bf16[8,4096]{1,0:T(8,128)(2,1)}, bf16[8,4096]{1,0:T...) custom-call(s32[256]{0:T(256)} %tenant_hbm.1, ...), custom_call_target="tpu_custom_call" | custom-call | flops 1000000000 | bytes 40000000 | tf_op jit(solution)/shard_map/pallas_call | solution.py:280
  2.9 6.1 %collective-permute-start = (bf16[8,4096]{1,0:T(8,128)(2,1)}, bf16[8,4096]{1,0:T(8,128)(2,1)S(1)}, u32[]{:S(2)}, u32[]{:S(2)}) collective-permute-start(bf16[8,4096]{1,0:T(8,128)(2,1)} %get-tuple-element.52), channel_id=1, source_target_pairs={{0,14},{2,12},{4,10},{6,8},{8,6},{10,4},{12,2},{14,0},{1,15},{3,13... | collective-permute-start | bytes 196616 | tf_op jit(solution)/shard_map/ppermute | solution.py:237
  8.9 0.0 collective-permute-start.1
  8.9 0.6 collective-permute-start.2
  9.6 2.2 %collective-permute-start.3 = (bf16[8,4096]{1,0:T(8,128)(2,1)}, bf16[8,4096]{1,0:T(8,128)(2,1)S(1)}, u32[]{:S(2)}, u32[]{:S(2)}) collective-permute-start(bf16[8,4096]{1,0:T(8,128)(2,1)} %get-tuple-element.55), channel_id=1, source_target_pairs={{0,8},{2,10},{4,12},{6,14},{8,0},{10,2},{12,4},{14,6},{1,9},{3,11}... | collective-permute-start | bytes 196616 | tf_op jit(solution)/shard_map/ppermute | solution.py:237
  11.8 3.0 %collective-permute-start.4 = (bf16[8,4096]{1,0:T(8,128)(2,1)}, bf16[8,4096]{1,0:T(8,128)(2,1)S(1)}, u32[]{:S(2)}, u32[]{:S(2)}) collective-permute-start(bf16[8,4096]{1,0:T(8,128)(2,1)} %get-tuple-element.56), channel_id=1, source_target_pairs={{0,6},{2,4},{4,2},{6,0},{8,14},{10,12},{12,10},{14,8},{1,7},{3,5},... | collective-permute-start | bytes 196616 | tf_op jit(solution)/shard_map/ppermute | solution.py:237
  14.8 0.0 collective-permute-done.ret_refs_0_
  14.8 1.1 %collective-permute-start.5 = (bf16[8,4096]{1,0:T(8,128)(2,1)}, bf16[8,4096]{1,0:T(8,128)(2,1)S(1)}, u32[]{:S(2)}, u32[]{:S(2)}) collective-permute-start(bf16[8,4096]{1,0:T(8,128)(2,1)} %get-tuple-element.57), channel_id=1, source_target_pairs={{0,12},{2,14},{4,8},{6,10},{8,4},{10,6},{12,0},{14,2},{1,13},{3,15... | collective-permute-start | bytes 196616 | tf_op jit(solution)/shard_map/ppermute | solution.py:237
  15.9 1.5 %collective-permute-start.6 = (bf16[8,4096]{1,0:T(8,128)(2,1)}, bf16[8,4096]{1,0:T(8,128)(2,1)S(1)}, u32[]{:S(2)}, u32[]{:S(2)}) collective-permute-start(bf16[8,4096]{1,0:T(8,128)(2,1)} %get-tuple-element.58), channel_id=1, source_target_pairs={{0,2},{2,0},{4,6},{6,4},{8,10},{10,8},{12,14},{14,12},{1,3},{3,1},... | collective-permute-start | bytes 196616 | tf_op jit(solution)/shard_map/ppermute | solution.py:237
  17.4 0.7 copy-done.11
  18.0 0.2 shard_map.150
  18.2 1.1 %collective-permute-done.2.ret_refs_2_ = bf16[8,4096]{1,0:T(8,128)(2,1)S(1)} collective-permute-done((bf16[8,4096]{1,0:T(8,128)(2,1)}, bf16[8,4096]{1,0:T(8,128)(2,1)S(1)}, u32[]{:S(2)}, u32[]{:S(2)}) %collective-permute-start.2) | collective-permute-done | bytes 65568 | tf_op jit(solution)/shard_map/ppermute | solution.py:237
  19.3 0.0 collective-permute-done.3.ret_refs_3_
  19.3 0.0 collective-permute-done.4.ret_refs_4_
  19.3 1.7 %collective-permute-done.5.ret_refs_5_ = bf16[8,4096]{1,0:T(8,128)(2,1)S(1)} collective-permute-done((bf16[8,4096]{1,0:T(8,128)(2,1)}, bf16[8,4096]{1,0:T(8,128)(2,1)S(1)}, u32[]{:S(2)}, u32[]{:S(2)}) %collective-permute-start.5) | collective-permute-done | bytes 65568 | tf_op jit(solution)/shard_map/ppermute | solution.py:237
  21.0 0.0 collective-permute-done.6.ret_refs_6_
  21.1 0.0 copy-start
  21.1 0.0 copy-start.1
  21.1 0.0 copy-start.5
  21.1 0.0 copy-start.7
  21.1 0.0 copy-start.8
  21.1 0.6 shard_map.151.mine_ref
  21.7 0.1 collective-permute-start.7
  21.8 1.2 %collective-permute-done.7.other_ref = f32[64,192]{1,0:T(8,128)S(1)} collective-permute-done((f32[64,192]{1,0:T(8,128)S(1)}, f32[64,192]{1,0:T(8,128)S(1)}, u32[]{:S(2)}, u32[]{:S(2)}) %collective-permute-start.7) | collective-permute-done | bytes 49184 | tf_op jit(solution)/shard_map/ppermute | solution.py:244
  23.1 0.3 shard_map.152
  23.4 2.2 %collective-permute-start.8 = (bf16[8,5120]{1,0:T(8,128)(2,1)S(1)}, bf16[8,5120]{1,0:T(8,128)(2,1)S(1)}, u32[]{:S(2)}, u32[]{:S(2)}) collective-permute-start(bf16[8,5120]{1,0:T(8,128)(2,1)S(1)} %get-tuple-element.73), channel_id=1, source_target_pairs={{0,14},{2,12},{4,10},{6,8},{8,6},{10,4},{12,2},{14,0},{1,15},{3,13... | collective-permute-start | bytes 245768 | tf_op jit(solution)/shard_map/ppermute | solution.py:237
  25.6 3.1 %collective-permute-start.10 = (bf16[8,5120]{1,0:T(8,128)(2,1)S(1)}, bf16[8,5120]{1,0:T(8,128)(2,1)S(1)}, u32[]{:S(2)}, u32[]{:S(2)}) collective-permute-start(bf16[8,5120]{1,0:T(8,128)(2,1)S(1)} %get-tuple-element.75), channel_id=1, source_target_pairs={{0,10},{2,8},{4,14},{6,12},{8,2},{10,0},{12,6},{14,4},{1,11},{3,9}... | collective-permute-start | bytes 245768 | tf_op jit(solution)/shard_map/ppermute | solution.py:237
  28.7 0.5 collective-permute-start.11
  29.3 2.2 %collective-permute-start.12 = (bf16[8,5120]{1,0:T(8,128)(2,1)S(1)}, bf16[8,5120]{1,0:T(8,128)(2,1)S(1)}, u32[]{:S(2)}, u32[]{:S(2)}) collective-permute-start(bf16[8,5120]{1,0:T(8,128)(2,1)S(1)} %get-tuple-element.77), channel_id=1, source_target_pairs={{0,6},{2,4},{4,2},{6,0},{8,14},{10,12},{12,10},{14,8},{1,7},{3,5},... | collective-permute-start | bytes 245768 | tf_op jit(solution)/shard_map/ppermute | solution.py:237
  31.4 0.1 collective-permute-done.8.ret_refs_0_
  31.5 2.0 %collective-permute-start.13 = (bf16[8,5120]{1,0:T(8,128)(2,1)S(1)}, bf16[8,5120]{1,0:T(8,128)(2,1)S(1)}, u32[]{:S(2)}, u32[]{:S(2)}) collective-permute-start(bf16[8,5120]{1,0:T(8,128)(2,1)S(1)} %get-tuple-element.78), channel_id=1, source_target_pairs={{0,12},{2,14},{4,8},{6,10},{8,4},{10,6},{12,0},{14,2},{1,13},{3,15... | collective-permute-start | bytes 245768 | tf_op jit(solution)/shard_map/ppermute | solution.py:237
  33.6 1.2 %collective-permute-start.14 = (bf16[8,5120]{1,0:T(8,128)(2,1)S(1)}, bf16[8,5120]{1,0:T(8,128)(2,1)S(1)}, u32[]{:S(2)}, u32[]{:S(2)}) collective-permute-start(bf16[8,5120]{1,0:T(8,128)(2,1)S(1)} %get-tuple-element.79), channel_id=1, source_target_pairs={{0,2},{2,0},{4,6},{6,4},{8,10},{10,8},{12,14},{14,12},{1,3},{3,1},... | collective-permute-start | bytes 245768 | tf_op jit(solution)/shard_map/ppermute | solution.py:237
  34.8 1.4 %collective-permute-done.10.ret_refs_2_ = bf16[8,5120]{1,0:T(8,128)(2,1)S(1)} collective-permute-done((bf16[8,5120]{1,0:T(8,128)(2,1)S(1)}, bf16[8,5120]{1,0:T(8,128)(2,1)S(1)}, u32[]{:S(2)}, u32[]{:S(2)}) %collective-permute-start.10) | collective-permute-done | bytes 81952 | tf_op jit(solution)/shard_map/ppermute | solution.py:237
  36.2 3.4 %collective-permute-done.11.ret_refs_3_ = bf16[8,5120]{1,0:T(8,128)(2,1)S(1)} collective-permute-done((bf16[8,5120]{1,0:T(8,128)(2,1)S(1)}, bf16[8,5120]{1,0:T(8,128)(2,1)S(1)}, u32[]{:S(2)}, u32[]{:S(2)}) %collective-permute-start.11) | collective-permute-done | bytes 81952 | tf_op jit(solution)/shard_map/ppermute | solution.py:237
  39.6 0.0 collective-permute-done.12.ret_refs_4_
  39.6 0.0 collective-permute-done.13.ret_refs_5_
  39.6 0.0 collective-permute-done.14.ret_refs_6_
  39.7 0.0 copy-start.4
  39.7 0.0 copy-start.3
  39.7 3.7 %shard_map.153 = (bf16[8,4096]{1,0:T(8,128)(2,1)S(1)}, bf16[8,4096]{1,0:T(8,128)(2,1)S(1)}, bf16[8,4096]{1,0:T(8,128)(2,1)S(1)}, bf16[8,4096]{1,0:T(8,128)(2,1)S...) custom-call(bf16[8,5120]{1,0:T(8,128)(2,1)S(1)} %collective-permute-, ...), custom_call_target="tpu_custom_call" | custom-call | bytes 8000000 | tf_op jit(solution)/shard_map/pallas_call | solution.py:319
  43.4 2.4 %collective-permute-start.15 = (bf16[8,4096]{1,0:T(8,128)(2,1)S(1)}, bf16[8,4096]{1,0:T(8,128)(2,1)S(1)}, u32[]{:S(2)}, u32[]{:S(2)}) collective-permute-start(bf16[8,4096]{1,0:T(8,128)(2,1)S(1)} %get-tuple-element.86), channel_id=1, source_target_pairs={{0,14},{2,12},{4,10},{6,8},{8,6},{10,4},{12,2},{14,0},{1,15},{3,13... | collective-permute-start | bytes 196616 | tf_op jit(solution)/shard_map/ppermute | solution.py:237
  45.7 1.0 %collective-permute-start.16 = (bf16[8,4096]{1,0:T(8,128)(2,1)S(1)}, bf16[8,4096]{1,0:T(8,128)(2,1)S(1)}, u32[]{:S(2)}, u32[]{:S(2)}) collective-permute-start(bf16[8,4096]{1,0:T(8,128)(2,1)S(1)} %get-tuple-element.87), channel_id=1, source_target_pairs={{0,4},{2,6},{4,0},{6,2},{8,12},{10,14},{12,8},{14,10},{1,5},{3,7},... | collective-permute-start | bytes 196616 | tf_op jit(solution)/shard_map/ppermute | solution.py:237
  46.7 1.9 %collective-permute-start.17 = (bf16[8,4096]{1,0:T(8,128)(2,1)S(1)}, bf16[8,4096]{1,0:T(8,128)(2,1)S(1)}, u32[]{:S(2)}, u32[]{:S(2)}) collective-permute-start(bf16[8,4096]{1,0:T(8,128)(2,1)S(1)} %get-tuple-element.88), channel_id=1, source_target_pairs={{0,10},{2,8},{4,14},{6,12},{8,2},{10,0},{12,6},{14,4},{1,11},{3,9}... | collective-permute-start | bytes 196616 | tf_op jit(solution)/shard_map/ppermute | solution.py:237
  48.6 1.2 %collective-permute-start.18 = (bf16[8,4096]{1,0:T(8,128)(2,1)S(1)}, bf16[8,4096]{1,0:T(8,128)(2,1)S(1)}, u32[]{:S(2)}, u32[]{:S(2)}) collective-permute-start(bf16[8,4096]{1,0:T(8,128)(2,1)S(1)} %get-tuple-element.89), channel_id=1, source_target_pairs={{0,8},{2,10},{4,12},{6,14},{8,0},{10,2},{12,4},{14,6},{1,9},{3,11}... | collective-permute-start | bytes 196616 | tf_op jit(solution)/shard_map/ppermute | solution.py:237
  49.9 1.7 %collective-permute-start.19 = (bf16[8,4096]{1,0:T(8,128)(2,1)S(1)}, bf16[8,4096]{1,0:T(8,128)(2,1)S(1)}, u32[]{:S(2)}, u32[]{:S(2)}) collective-permute-start(bf16[8,4096]{1,0:T(8,128)(2,1)S(1)} %get-tuple-element.90), channel_id=1, source_target_pairs={{0,6},{2,4},{4,2},{6,0},{8,14},{10,12},{12,10},{14,8},{1,7},{3,5},... | collective-permute-start | bytes 196616 | tf_op jit(solution)/shard_map/ppermute | solution.py:237
  51.6 1.9 %collective-permute-start.20 = (bf16[8,4096]{1,0:T(8,128)(2,1)S(1)}, bf16[8,4096]{1,0:T(8,128)(2,1)S(1)}, u32[]{:S(2)}, u32[]{:S(2)}) collective-permute-start(bf16[8,4096]{1,0:T(8,128)(2,1)S(1)} %get-tuple-element.91), channel_id=1, source_target_pairs={{0,12},{2,14},{4,8},{6,10},{8,4},{10,6},{12,0},{14,2},{1,13},{3,15... | collective-permute-start | bytes 196616 | tf_op jit(solution)/shard_map/ppermute | solution.py:237
  53.4 1.1 %collective-permute-start.21 = (bf16[8,4096]{1,0:T(8,128)(2,1)S(1)}, bf16[8,4096]{1,0:T(8,128)(2,1)S(1)}, u32[]{:S(2)}, u32[]{:S(2)}) collective-permute-start(bf16[8,4096]{1,0:T(8,128)(2,1)S(1)} %get-tuple-element.92), channel_id=1, source_target_pairs={{0,2},{2,0},{4,6},{6,4},{8,10},{10,8},{12,14},{14,12},{1,3},{3,1},... | collective-permute-start | bytes 196616 | tf_op jit(solution)/shard_map/ppermute | solution.py:237
  54.5 1.5 %collective-permute-done.17.ret_refs_2_ = bf16[8,4096]{1,0:T(8,128)(2,1)S(1)} collective-permute-done((bf16[8,4096]{1,0:T(8,128)(2,1)S(1)}, bf16[8,4096]{1,0:T(8,128)(2,1)S(1)}, u32[]{:S(2)}, u32[]{:S(2)}) %collective-permute-start.17) | collective-permute-done | bytes 65568 | tf_op jit(solution)/shard_map/ppermute | solution.py:237
  56.0 0.9 %collective-permute-done.18.ret_refs_3_ = bf16[8,4096]{1,0:T(8,128)(2,1)S(1)} collective-permute-done((bf16[8,4096]{1,0:T(8,128)(2,1)S(1)}, bf16[8,4096]{1,0:T(8,128)(2,1)S(1)}, u32[]{:S(2)}, u32[]{:S(2)}) %collective-permute-start.18) | collective-permute-done | bytes 65568 | tf_op jit(solution)/shard_map/ppermute | solution.py:237
  57.0 0.8 %collective-permute-done.20.ret_refs_5_ = bf16[8,4096]{1,0:T(8,128)(2,1)S(1)} collective-permute-done((bf16[8,4096]{1,0:T(8,128)(2,1)S(1)}, bf16[8,4096]{1,0:T(8,128)(2,1)S(1)}, u32[]{:S(2)}, u32[]{:S(2)}) %collective-permute-start.20) | collective-permute-done | bytes 65568 | tf_op jit(solution)/shard_map/ppermute | solution.py:237
  57.7 0.3 shard_map.154.mine_ref
  58.0 0.1 collective-permute-start.22
  58.1 1.2 %collective-permute-done.22.other_ref = f32[64,64]{1,0:T(8,128)S(1)} collective-permute-done((f32[64,64]{1,0:T(8,128)S(1)}, f32[64,64]{1,0:T(8,128)S(1)}, u32[]{:S(2)}, u32[]{:S(2)}) %collective-permute-start.22) | collective-permute-done | bytes 16416 | tf_op jit(solution)/shard_map/ppermute | solution.py:244
  59.3 0.3 shard_map.155
  59.6 2.4 %collective-permute-start.23 = (bf16[8,4096]{1,0:T(8,128)(2,1)S(1)}, bf16[8,4096]{1,0:T(8,128)(2,1)S(1)}, u32[]{:S(2)}, u32[]{:S(2)}) collective-permute-start(bf16[8,4096]{1,0:T(8,128)(2,1)S(1)} %get-tuple-element.94), channel_id=1, source_target_pairs={{0,14},{2,12},{4,10},{6,8},{8,6},{10,4},{12,2},{14,0},{1,15},{3,13... | collective-permute-start | bytes 196616 | tf_op jit(solution)/shard_map/ppermute | solution.py:237
  62.0 0.2 collective-permute-start.24
  62.3 2.7 %collective-permute-start.25 = (bf16[8,4096]{1,0:T(8,128)(2,1)S(1)}, bf16[8,4096]{1,0:T(8,128)(2,1)S(1)}, u32[]{:S(2)}, u32[]{:S(2)}) collective-permute-start(bf16[8,4096]{1,0:T(8,128)(2,1)S(1)} %get-tuple-element.96), channel_id=1, source_target_pairs={{0,10},{2,8},{4,14},{6,12},{8,2},{10,0},{12,6},{14,4},{1,11},{3,9}... | collective-permute-start | bytes 196616 | tf_op jit(solution)/shard_map/ppermute | solution.py:237
  65.0 0.9 %collective-permute-start.26 = (bf16[8,4096]{1,0:T(8,128)(2,1)S(1)}, bf16[8,4096]{1,0:T(8,128)(2,1)S(1)}, u32[]{:S(2)}, u32[]{:S(2)}) collective-permute-start(bf16[8,4096]{1,0:T(8,128)(2,1)S(1)} %get-tuple-element.97), channel_id=1, source_target_pairs={{0,8},{2,10},{4,12},{6,14},{8,0},{10,2},{12,4},{14,6},{1,9},{3,11}... | collective-permute-start | bytes 196616 | tf_op jit(solution)/shard_map/ppermute | solution.py:237
  65.9 2.0 %collective-permute-start.27 = (bf16[8,4096]{1,0:T(8,128)(2,1)S(1)}, bf16[8,4096]{1,0:T(8,128)(2,1)S(1)}, u32[]{:S(2)}, u32[]{:S(2)}) collective-permute-start(bf16[8,4096]{1,0:T(8,128)(2,1)S(1)} %get-tuple-element.98), channel_id=1, source_target_pairs={{0,6},{2,4},{4,2},{6,0},{8,14},{10,12},{12,10},{14,8},{1,7},{3,5},... | collective-permute-start | bytes 196616 | tf_op jit(solution)/shard_map/ppermute | solution.py:237
  67.9 1.9 %collective-permute-start.28 = (bf16[8,4096]{1,0:T(8,128)(2,1)S(1)}, bf16[8,4096]{1,0:T(8,128)(2,1)S(1)}, u32[]{:S(2)}, u32[]{:S(2)}) collective-permute-start(bf16[8,4096]{1,0:T(8,128)(2,1)S(1)} %get-tuple-element.99), channel_id=1, source_target_pairs={{0,12},{2,14},{4,8},{6,10},{8,4},{10,6},{12,0},{14,2},{1,13},{3,15... | collective-permute-start | bytes 196616 | tf_op jit(solution)/shard_map/ppermute | solution.py:237
  69.8 1.0 %collective-permute-start.29 = (bf16[8,4096]{1,0:T(8,128)(2,1)S(1)}, bf16[8,4096]{1,0:T(8,128)(2,1)S(1)}, u32[]{:S(2)}, u32[]{:S(2)}) collective-permute-start(bf16[8,4096]{1,0:T(8,128)(2,1)S(1)} %get-tuple-element.100), channel_id=1, source_target_pairs={{0,2},{2,0},{4,6},{6,4},{8,10},{10,8},{12,14},{14,12},{1,3},{3,1},... | collective-permute-start | bytes 196616 | tf_op jit(solution)/shard_map/ppermute | solution.py:237
  70.8 1.1 %collective-permute-done.25.ret_refs_2_ = bf16[8,4096]{1,0:T(8,128)(2,1)S(1)} collective-permute-done((bf16[8,4096]{1,0:T(8,128)(2,1)S(1)}, bf16[8,4096]{1,0:T(8,128)(2,1)S(1)}, u32[]{:S(2)}, u32[]{:S(2)}) %collective-permute-start.25) | collective-permute-done | bytes 65568 | tf_op jit(solution)/shard_map/ppermute | solution.py:237
  71.9 2.3 %collective-permute-done.26.ret_refs_3_ = bf16[8,4096]{1,0:T(8,128)(2,1)S(1)} collective-permute-done((bf16[8,4096]{1,0:T(8,128)(2,1)S(1)}, bf16[8,4096]{1,0:T(8,128)(2,1)S(1)}, u32[]{:S(2)}, u32[]{:S(2)}) %collective-permute-start.26) | collective-permute-done | bytes 65568 | tf_op jit(solution)/shard_map/ppermute | solution.py:237
  74.1 0.9 %shard_map.156 = bf16[32,4096]{1,0:T(8,128)(2,1)} custom-call(bf16[32,64]{1,0:T(8,128)(2,1)S(1)} %get-tuple-element.84.home_ref, bf16[8,4096]{1,0:T(8,128)(2,1)S(1)} %collective-permute-done.23.ret_refs_0_, bf16[8,4096]{1,0:T(8,128)(2,1)S(1)} %collective-permute-done.24.ret_refs_1_, bf16[8,4096]{1,0:T(8,128)(2,1)S(1)} %collective-permute-done.25.ret_refs_2_, ...), custom_call_target="tpu_custom_call" | custom-call | bytes 1000000 | tf_op jit(solution)/shard_map/pallas_call | solution.py:339
  (28 shorter events, 0.1 us)
Async XLA Ops:
  0.6 20.4 %copy-start.2 = (bf16[1,192,8192]{2,1,0:T(8,128)(2,1)S(1)}, bf16[1,192,8192]{2,1,0:T(8,128)(2,1)}, u32[]{:S(2)}) copy-start(bf16[1,192,8192]{2,1,0:T(8,128)(2,1)} %down_ref.2) | copy-start | bytes 9437188
  2.8 18.2 %copy-start.6 = (bf16[8,4096]{1,0:T(8,128)(2,1)S(1)}, bf16[8,4096]{1,0:T(8,128)(2,1)}, u32[]{:S(2)}) copy-start(bf16[8,4096]{1,0:T(8,128)(2,1)} %get-tuple-element.72.ret_refs_7_) | copy-start | bytes 196612
  2.9 11.9 %collective-permute-start = (bf16[8,4096]{1,0:T(8,128)(2,1)}, bf16[8,4096]{1,0:T(8,128)(2,1)S(1)}, u32[]{:S(2)}, u32[]{:S(2)}) collective-permute-start(bf16[8,4096]{1,0:T(8,128)(2,1)} %get-tuple-element.52), channel_id=1, source_target_pairs={{0,14},{2,12},{4,10},{6,8},{8,6},{10,4},{12,2},{14,0},{1,15},{3,13... | collective-permute-start | bytes 196616 | tf_op jit(solution)/shard_map/ppermute | solution.py:237
  8.9 6.9 %collective-permute-start.1 = (bf16[8,4096]{1,0:T(8,128)(2,1)}, bf16[8,4096]{1,0:T(8,128)(2,1)S(1)}, u32[]{:S(2)}, u32[]{:S(2)}) collective-permute-start(bf16[8,4096]{1,0:T(8,128)(2,1)} %get-tuple-element.53), channel_id=1, source_target_pairs={{0,4},{2,6},{4,0},{6,2},{8,12},{10,14},{12,8},{14,10},{1,5},{3,7},... | collective-permute-start | bytes 196616 | tf_op jit(solution)/shard_map/ppermute | solution.py:237
  8.9 10.4 %collective-permute-start.2 = (bf16[8,4096]{1,0:T(8,128)(2,1)}, bf16[8,4096]{1,0:T(8,128)(2,1)S(1)}, u32[]{:S(2)}, u32[]{:S(2)}) collective-permute-start(bf16[8,4096]{1,0:T(8,128)(2,1)} %get-tuple-element.54), channel_id=1, source_target_pairs={{0,10},{2,8},{4,14},{6,12},{8,2},{10,0},{12,6},{14,4},{1,11},{3,9}... | collective-permute-start | bytes 196616 | tf_op jit(solution)/shard_map/ppermute | solution.py:237
  9.6 9.8 %collective-permute-start.3 = (bf16[8,4096]{1,0:T(8,128)(2,1)}, bf16[8,4096]{1,0:T(8,128)(2,1)S(1)}, u32[]{:S(2)}, u32[]{:S(2)}) collective-permute-start(bf16[8,4096]{1,0:T(8,128)(2,1)} %get-tuple-element.55), channel_id=1, source_target_pairs={{0,8},{2,10},{4,12},{6,14},{8,0},{10,2},{12,4},{14,6},{1,9},{3,11}... | collective-permute-start | bytes 196616 | tf_op jit(solution)/shard_map/ppermute | solution.py:237
  11.8 7.5 %collective-permute-start.4 = (bf16[8,4096]{1,0:T(8,128)(2,1)}, bf16[8,4096]{1,0:T(8,128)(2,1)S(1)}, u32[]{:S(2)}, u32[]{:S(2)}) collective-permute-start(bf16[8,4096]{1,0:T(8,128)(2,1)} %get-tuple-element.56), channel_id=1, source_target_pairs={{0,6},{2,4},{4,2},{6,0},{8,14},{10,12},{12,10},{14,8},{1,7},{3,5},... | collective-permute-start | bytes 196616 | tf_op jit(solution)/shard_map/ppermute | solution.py:237
  14.8 6.3 %collective-permute-start.5 = (bf16[8,4096]{1,0:T(8,128)(2,1)}, bf16[8,4096]{1,0:T(8,128)(2,1)S(1)}, u32[]{:S(2)}, u32[]{:S(2)}) collective-permute-start(bf16[8,4096]{1,0:T(8,128)(2,1)} %get-tuple-element.57), channel_id=1, source_target_pairs={{0,12},{2,14},{4,8},{6,10},{8,4},{10,6},{12,0},{14,2},{1,13},{3,15... | collective-permute-start | bytes 196616 | tf_op jit(solution)/shard_map/ppermute | solution.py:237
  15.9 5.2 %collective-permute-start.6 = (bf16[8,4096]{1,0:T(8,128)(2,1)}, bf16[8,4096]{1,0:T(8,128)(2,1)S(1)}, u32[]{:S(2)}, u32[]{:S(2)}) collective-permute-start(bf16[8,4096]{1,0:T(8,128)(2,1)} %get-tuple-element.58), channel_id=1, source_target_pairs={{0,2},{2,0},{4,6},{6,4},{8,10},{10,8},{12,14},{14,12},{1,3},{3,1},... | collective-permute-start | bytes 196616 | tf_op jit(solution)/shard_map/ppermute | solution.py:237
  17.4 0.7 copy-start.11
  18.0 5.0 %copy-start.9 = (bf16[1,64,4096]{2,1,0:T(8,128)(2,1)S(1)}, bf16[1,64,4096]{2,1,0:T(8,128)(2,1)}, u32[]{:S(2)}) copy-start(bf16[1,64,4096]{2,1,0:T(8,128)(2,1)} %uq_ref.1) | copy-start | bytes 1572868
  18.0 5.0 %copy-start.10 = (bf16[1,2,64,512]{3,2,1,0:T(8,128)(2,1)S(1)}, bf16[1,2,64,512]{3,2,1,0:T(8,128)(2,1)}, u32[]{:S(2)}) copy-start(bf16[1,2,64,512]{3,2,1,0:T(8,128)(2,1)} %ukv_ref.1) | copy-start | bytes 393220
  21.1 18.6 %copy-start = (bf16[32,4,96,128]{3,2,1,0:T(8,128)(2,1)S(1)}, bf16[32,4,96,128]{3,2,1,0:T(8,128)(2,1)}, u32[]{:S(2)}) copy-start(bf16[32,4,96,128]{3,2,1,0:T(8,128)(2,1)} %k_ref.1) | copy-start | bytes 9437188
  21.1 18.6 %copy-start.1 = (bf16[32,4,96,128]{3,2,1,0:T(8,128)(2,1)S(1)}, bf16[32,4,96,128]{3,2,1,0:T(8,128)(2,1)}, u32[]{:S(2)}) copy-start(bf16[32,4,96,128]{3,2,1,0:T(8,128)(2,1)} %v_ref.1) | copy-start | bytes 9437188
  21.1 18.6 %copy-start.5 = (bf16[32,4096]{1,0:T(8,128)(2,1)S(1)}, bf16[32,4096]{1,0:T(8,128)(2,1)}, u32[]{:S(2)}) copy-start(bf16[32,4096]{1,0:T(8,128)(2,1)} %pq_ref.1) | copy-start | bytes 786436
  21.1 18.6 %copy-start.7 = (bf16[32,512]{1,0:T(8,128)(2,1)S(1)}, bf16[32,512]{1,0:T(8,128)(2,1)}, u32[]{:S(2)}) copy-start(bf16[32,512]{1,0:T(8,128)(2,1)} %pk_ref.1) | copy-start | bytes 98308
  21.1 18.6 %copy-start.8 = (bf16[32,512]{1,0:T(8,128)(2,1)S(1)}, bf16[32,512]{1,0:T(8,128)(2,1)}, u32[]{:S(2)}) copy-start(bf16[32,512]{1,0:T(8,128)(2,1)} %pv_ref.1) | copy-start | bytes 98308
  21.7 1.3 %collective-permute-start.7 = (f32[64,192]{1,0:T(8,128)S(1)}, f32[64,192]{1,0:T(8,128)S(1)}, u32[]{:S(2)}, u32[]{:S(2)}) collective-permute-start(f32[64,192]{1,0:T(8,128)S(1)} %shard_map.151.mine_ref), channel_id=1, source_target_pairs={{0,1},{1,0},{2,3},{3,2},{4,5},{5,4},{6,7},{7,6},{8,9},{9,8},{10,11... | collective-permute-start | bytes 147464 | tf_op jit(solution)/shard_map/ppermute | solution.py:244
  23.4 8.1 %collective-permute-start.8 = (bf16[8,5120]{1,0:T(8,128)(2,1)S(1)}, bf16[8,5120]{1,0:T(8,128)(2,1)S(1)}, u32[]{:S(2)}, u32[]{:S(2)}) collective-permute-start(bf16[8,5120]{1,0:T(8,128)(2,1)S(1)} %get-tuple-element.73), channel_id=1, source_target_pairs={{0,14},{2,12},{4,10},{6,8},{8,6},{10,4},{12,2},{14,0},{1,15},{3,13... | collective-permute-start | bytes 245768 | tf_op jit(solution)/shard_map/ppermute | solution.py:237
  25.6 8.0 %collective-permute-start.9 = (bf16[8,5120]{1,0:T(8,128)(2,1)S(1)}, bf16[8,5120]{1,0:T(8,128)(2,1)S(1)}, u32[]{:S(2)}, u32[]{:S(2)}) collective-permute-start(bf16[8,5120]{1,0:T(8,128)(2,1)S(1)} %get-tuple-element.74), channel_id=1, source_target_pairs={{0,4},{2,6},{4,0},{6,2},{8,12},{10,14},{12,8},{14,10},{1,5},{3,7},... | collective-permute-start | bytes 245768 | tf_op jit(solution)/shard_map/ppermute | solution.py:237
  25.6 10.6 %collective-permute-start.10 = (bf16[8,5120]{1,0:T(8,128)(2,1)S(1)}, bf16[8,5120]{1,0:T(8,128)(2,1)S(1)}, u32[]{:S(2)}, u32[]{:S(2)}) collective-permute-start(bf16[8,5120]{1,0:T(8,128)(2,1)S(1)} %get-tuple-element.75), channel_id=1, source_target_pairs={{0,10},{2,8},{4,14},{6,12},{8,2},{10,0},{12,6},{14,4},{1,11},{3,9}... | collective-permute-start | bytes 245768 | tf_op jit(solution)/shard_map/ppermute | solution.py:237
  28.7 10.9 %collective-permute-start.11 = (bf16[8,5120]{1,0:T(8,128)(2,1)S(1)}, bf16[8,5120]{1,0:T(8,128)(2,1)S(1)}, u32[]{:S(2)}, u32[]{:S(2)}) collective-permute-start(bf16[8,5120]{1,0:T(8,128)(2,1)S(1)} %get-tuple-element.76), channel_id=1, source_target_pairs={{0,8},{2,10},{4,12},{6,14},{8,0},{10,2},{12,4},{14,6},{1,9},{3,11}... | collective-permute-start | bytes 245768 | tf_op jit(solution)/shard_map/ppermute | solution.py:237
  29.3 10.3 %collective-permute-start.12 = (bf16[8,5120]{1,0:T(8,128)(2,1)S(1)}, bf16[8,5120]{1,0:T(8,128)(2,1)S(1)}, u32[]{:S(2)}, u32[]{:S(2)}) collective-permute-start(bf16[8,5120]{1,0:T(8,128)(2,1)S(1)} %get-tuple-element.77), channel_id=1, source_target_pairs={{0,6},{2,4},{4,2},{6,0},{8,14},{10,12},{12,10},{14,8},{1,7},{3,5},... | collective-permute-start | bytes 245768 | tf_op jit(solution)/shard_map/ppermute | solution.py:237
  31.5 8.1 %collective-permute-start.13 = (bf16[8,5120]{1,0:T(8,128)(2,1)S(1)}, bf16[8,5120]{1,0:T(8,128)(2,1)S(1)}, u32[]{:S(2)}, u32[]{:S(2)}) collective-permute-start(bf16[8,5120]{1,0:T(8,128)(2,1)S(1)} %get-tuple-element.78), channel_id=1, source_target_pairs={{0,12},{2,14},{4,8},{6,10},{8,4},{10,6},{12,0},{14,2},{1,13},{3,15... | collective-permute-start | bytes 245768 | tf_op jit(solution)/shard_map/ppermute | solution.py:237
  33.6 6.1 %collective-permute-start.14 = (bf16[8,5120]{1,0:T(8,128)(2,1)S(1)}, bf16[8,5120]{1,0:T(8,128)(2,1)S(1)}, u32[]{:S(2)}, u32[]{:S(2)}) collective-permute-start(bf16[8,5120]{1,0:T(8,128)(2,1)S(1)} %get-tuple-element.79), channel_id=1, source_target_pairs={{0,2},{2,0},{4,6},{6,4},{8,10},{10,8},{12,14},{14,12},{1,3},{3,1},... | collective-permute-start | bytes 245768 | tf_op jit(solution)/shard_map/ppermute | solution.py:237
  39.7 18.1 %copy-start.4 = (bf16[1,64,4096]{2,1,0:T(8,128)(2,1)S(1)}, bf16[1,64,4096]{2,1,0:T(8,128)(2,1)}, u32[]{:S(2)}) copy-start(bf16[1,64,4096]{2,1,0:T(8,128)(2,1)} %down_ref.3) | copy-start | bytes 1572868
  39.7 19.6 %copy-start.3 = (bf16[1,64,4096]{2,1,0:T(8,128)(2,1)S(1)}, bf16[1,64,4096]{2,1,0:T(8,128)(2,1)}, u32[]{:S(2)}) copy-start(bf16[1,64,4096]{2,1,0:T(8,128)(2,1)} %uo_ref.1) | copy-start | bytes 1572868
  43.4 8.2 %collective-permute-start.15 = (bf16[8,4096]{1,0:T(8,128)(2,1)S(1)}, bf16[8,4096]{1,0:T(8,128)(2,1)S(1)}, u32[]{:S(2)}, u32[]{:S(2)}) collective-permute-start(bf16[8,4096]{1,0:T(8,128)(2,1)S(1)} %get-tuple-element.86), channel_id=1, source_target_pairs={{0,14},{2,12},{4,10},{6,8},{8,6},{10,4},{12,2},{14,0},{1,15},{3,13... | collective-permute-start | bytes 196616 | tf_op jit(solution)/shard_map/ppermute | solution.py:237
  45.7 7.7 %collective-permute-start.16 = (bf16[8,4096]{1,0:T(8,128)(2,1)S(1)}, bf16[8,4096]{1,0:T(8,128)(2,1)S(1)}, u32[]{:S(2)}, u32[]{:S(2)}) collective-permute-start(bf16[8,4096]{1,0:T(8,128)(2,1)S(1)} %get-tuple-element.87), channel_id=1, source_target_pairs={{0,4},{2,6},{4,0},{6,2},{8,12},{10,14},{12,8},{14,10},{1,5},{3,7},... | collective-permute-start | bytes 196616 | tf_op jit(solution)/shard_map/ppermute | solution.py:237
  46.7 9.3 %collective-permute-start.17 = (bf16[8,4096]{1,0:T(8,128)(2,1)S(1)}, bf16[8,4096]{1,0:T(8,128)(2,1)S(1)}, u32[]{:S(2)}, u32[]{:S(2)}) collective-permute-start(bf16[8,4096]{1,0:T(8,128)(2,1)S(1)} %get-tuple-element.88), channel_id=1, source_target_pairs={{0,10},{2,8},{4,14},{6,12},{8,2},{10,0},{12,6},{14,4},{1,11},{3,9}... | collective-permute-start | bytes 196616 | tf_op jit(solution)/shard_map/ppermute | solution.py:237
  48.6 8.3 %collective-permute-start.18 = (bf16[8,4096]{1,0:T(8,128)(2,1)S(1)}, bf16[8,4096]{1,0:T(8,128)(2,1)S(1)}, u32[]{:S(2)}, u32[]{:S(2)}) collective-permute-start(bf16[8,4096]{1,0:T(8,128)(2,1)S(1)} %get-tuple-element.89), channel_id=1, source_target_pairs={{0,8},{2,10},{4,12},{6,14},{8,0},{10,2},{12,4},{14,6},{1,9},{3,11}... | collective-permute-start | bytes 196616 | tf_op jit(solution)/shard_map/ppermute | solution.py:237
  49.9 7.1 %collective-permute-start.19 = (bf16[8,4096]{1,0:T(8,128)(2,1)S(1)}, bf16[8,4096]{1,0:T(8,128)(2,1)S(1)}, u32[]{:S(2)}, u32[]{:S(2)}) collective-permute-start(bf16[8,4096]{1,0:T(8,128)(2,1)S(1)} %get-tuple-element.90), channel_id=1, source_target_pairs={{0,6},{2,4},{4,2},{6,0},{8,14},{10,12},{12,10},{14,8},{1,7},{3,5},... | collective-permute-start | bytes 196616 | tf_op jit(solution)/shard_map/ppermute | solution.py:237
  51.6 6.2 %collective-permute-start.20 = (bf16[8,4096]{1,0:T(8,128)(2,1)S(1)}, bf16[8,4096]{1,0:T(8,128)(2,1)S(1)}, u32[]{:S(2)}, u32[]{:S(2)}) collective-permute-start(bf16[8,4096]{1,0:T(8,128)(2,1)S(1)} %get-tuple-element.91), channel_id=1, source_target_pairs={{0,12},{2,14},{4,8},{6,10},{8,4},{10,6},{12,0},{14,2},{1,13},{3,15... | collective-permute-start | bytes 196616 | tf_op jit(solution)/shard_map/ppermute | solution.py:237
  53.4 4.3 %collective-permute-start.21 = (bf16[8,4096]{1,0:T(8,128)(2,1)S(1)}, bf16[8,4096]{1,0:T(8,128)(2,1)S(1)}, u32[]{:S(2)}, u32[]{:S(2)}) collective-permute-start(bf16[8,4096]{1,0:T(8,128)(2,1)S(1)} %get-tuple-element.92), channel_id=1, source_target_pairs={{0,2},{2,0},{4,6},{6,4},{8,10},{10,8},{12,14},{14,12},{1,3},{3,1},... | collective-permute-start | bytes 196616 | tf_op jit(solution)/shard_map/ppermute | solution.py:237
  58.0 1.3 %collective-permute-start.22 = (f32[64,64]{1,0:T(8,128)S(1)}, f32[64,64]{1,0:T(8,128)S(1)}, u32[]{:S(2)}, u32[]{:S(2)}) collective-permute-start(f32[64,64]{1,0:T(8,128)S(1)} %shard_map.154.mine_ref), channel_id=1, source_target_pairs={{0,1},{1,0},{2,3},{3,2},{4,5},{5,4},{6,7},{7,6},{8,9},{9,8},{10,11... | collective-permute-start | bytes 49160 | tf_op jit(solution)/shard_map/ppermute | solution.py:244
  59.6 8.3 %collective-permute-start.23 = (bf16[8,4096]{1,0:T(8,128)(2,1)S(1)}, bf16[8,4096]{1,0:T(8,128)(2,1)S(1)}, u32[]{:S(2)}, u32[]{:S(2)}) collective-permute-start(bf16[8,4096]{1,0:T(8,128)(2,1)S(1)} %get-tuple-element.94), channel_id=1, source_target_pairs={{0,14},{2,12},{4,10},{6,8},{8,6},{10,4},{12,2},{14,0},{1,15},{3,13... | collective-permute-start | bytes 196616 | tf_op jit(solution)/shard_map/ppermute | solution.py:237
  62.0 7.8 %collective-permute-start.24 = (bf16[8,4096]{1,0:T(8,128)(2,1)S(1)}, bf16[8,4096]{1,0:T(8,128)(2,1)S(1)}, u32[]{:S(2)}, u32[]{:S(2)}) collective-permute-start(bf16[8,4096]{1,0:T(8,128)(2,1)S(1)} %get-tuple-element.95), channel_id=1, source_target_pairs={{0,4},{2,6},{4,0},{6,2},{8,12},{10,14},{12,8},{14,10},{1,5},{3,7},... | collective-permute-start | bytes 196616 | tf_op jit(solution)/shard_map/ppermute | solution.py:237
  62.3 9.6 %collective-permute-start.25 = (bf16[8,4096]{1,0:T(8,128)(2,1)S(1)}, bf16[8,4096]{1,0:T(8,128)(2,1)S(1)}, u32[]{:S(2)}, u32[]{:S(2)}) collective-permute-start(bf16[8,4096]{1,0:T(8,128)(2,1)S(1)} %get-tuple-element.96), channel_id=1, source_target_pairs={{0,10},{2,8},{4,14},{6,12},{8,2},{10,0},{12,6},{14,4},{1,11},{3,9}... | collective-permute-start | bytes 196616 | tf_op jit(solution)/shard_map/ppermute | solution.py:237
  65.0 9.2 %collective-permute-start.26 = (bf16[8,4096]{1,0:T(8,128)(2,1)S(1)}, bf16[8,4096]{1,0:T(8,128)(2,1)S(1)}, u32[]{:S(2)}, u32[]{:S(2)}) collective-permute-start(bf16[8,4096]{1,0:T(8,128)(2,1)S(1)} %get-tuple-element.97), channel_id=1, source_target_pairs={{0,8},{2,10},{4,12},{6,14},{8,0},{10,2},{12,4},{14,6},{1,9},{3,11}... | collective-permute-start | bytes 196616 | tf_op jit(solution)/shard_map/ppermute | solution.py:237
  65.9 8.2 %collective-permute-start.27 = (bf16[8,4096]{1,0:T(8,128)(2,1)S(1)}, bf16[8,4096]{1,0:T(8,128)(2,1)S(1)}, u32[]{:S(2)}, u32[]{:S(2)}) collective-permute-start(bf16[8,4096]{1,0:T(8,128)(2,1)S(1)} %get-tuple-element.98), channel_id=1, source_target_pairs={{0,6},{2,4},{4,2},{6,0},{8,14},{10,12},{12,10},{14,8},{1,7},{3,5},... | collective-permute-start | bytes 196616 | tf_op jit(solution)/shard_map/ppermute | solution.py:237
  67.9 6.3 %collective-permute-start.28 = (bf16[8,4096]{1,0:T(8,128)(2,1)S(1)}, bf16[8,4096]{1,0:T(8,128)(2,1)S(1)}, u32[]{:S(2)}, u32[]{:S(2)}) collective-permute-start(bf16[8,4096]{1,0:T(8,128)(2,1)S(1)} %get-tuple-element.99), channel_id=1, source_target_pairs={{0,12},{2,14},{4,8},{6,10},{8,4},{10,6},{12,0},{14,2},{1,13},{3,15... | collective-permute-start | bytes 196616 | tf_op jit(solution)/shard_map/ppermute | solution.py:237
  69.8 4.3 %collective-permute-start.29 = (bf16[8,4096]{1,0:T(8,128)(2,1)S(1)}, bf16[8,4096]{1,0:T(8,128)(2,1)S(1)}, u32[]{:S(2)}, u32[]{:S(2)}) collective-permute-start(bf16[8,4096]{1,0:T(8,128)(2,1)S(1)} %get-tuple-element.100), channel_id=1, source_target_pairs={{0,2},{2,0},{4,6},{6,4},{8,10},{10,8},{12,14},{14,12},{1,3},{3,1},... | collective-permute-start | bytes 196616 | tf_op jit(solution)/shard_map/ppermute | solution.py:237

commit v9 on v8

--- a/solution.py
+++ b/solution.py
@@ -162,8 +162,9 @@
         pair[side] = lines
         return jnp.concatenate(pair, axis=1)
 
+    held = []
     for g in range(heads):
-        slot = 4 * (g % 2)
+        slot = 4 * g
         columns = slice(g * group * head_dim, (g + 1) * group * head_dim)
         query_rows = term_ref[:, columns]
         query = lines_of(slot, lambda h: query_rows[:, h * head_dim : (h + 1) * head_dim])
@@ -186,6 +187,12 @@
             ],
             axis=0,
         )
+        held.append((own, score))
+    for g in range(heads):
+        slot = 4 * g
+        columns = slice(g * group * head_dim, (g + 1) * group * head_dim)
+        own, score = held[g]
+        new_value = line_ref[slot + 2]
         score = score * scale + bias
         highest = jnp.maximum(jnp.max(score, axis=1, keepdims=True), own)
         raised = jnp.exp(score - highest)
@@ -322,7 +329,7 @@
         [(VMEM,) * count] + [VMEM] * (5 + len(prepared)),
         scratch=[
             pltpu.VMEM((rows, kv_heads * (group + 2) * head_dim), F32),
-            pltpu.VMEM((8, lines, head_dim), F32),
+            pltpu.VMEM((4 * kv_heads, lines, head_dim), F32),
         ],
         moved=8000000,
         limit=16,

time: 75.2 us -> 74.4 us (0.989)
  Pallas kernels: 8.41 us -> 7.58 us
    pallas_call x1, Pallas kernels: 3.65 us -> 2.84 us  [shards(): call(functools.partial(attend_body, group), [*blocks_of(query_width), str...]
where the time goes in v9:
time: 74.4 us; the launch traced here: 74.2 us
  starting transfers between devices  48.3 us (65%)
  waiting for transfers between devices  16.7 us (22%)
  Pallas kernels  7.58 us (10%)
  between operations  0.84 us (1%)
    ppermute x28, starting transfers between devices, exchange(): lax.ppermute(block, 'wide', [(k, k ^ d) for k in range(wide_count)])  48.2 us
    ppermute x28, waiting for transfers between devices, exchange(): lax.ppermute(block, 'wide', [(k, k ^ d) for k in range(wide_count)])  14.3 us
    pallas_call x1, Pallas kernels, shards(): call(functools.partial(attend_body, group), [*blocks_of(query_width), str...  2.84 us
    ppermute x2, waiting for transfers between devices, other_core(): return lax.ppermute(value, 'tp', [(0, 1), (1, 0)])  2.44 us
    pallas_call x1, Pallas kernels, shards(): call(functools.partial(pack_body, capacity, by_distance), (struct((2, row...  2.19 us
  transfers between devices with their start and end apart: 30, of which 12 were waited for; matrix products, arithmetic and copies ran while one was open for 0% of the time, Pallas kernels for 0%

profile of v9, /device:TPU:0, one launch (start us, length us, event | category | flops | bytes accessed | tf_op | source)
XLA Modules:
  0.0 74.2 jit_solution(16613825940273061399)
XLA Ops:
  0.6 2.2 %shard_map.149 = (s32[2,32]{1,0:T(2,128)}, bf16[8,4096]{1,0:T(8,128)(2,1)}, bf16[8,4096]{1,0:T(8,128)(2,1)}, bf16[8,4096]{1,0:T(8,128)(2,1)}, bf16[8,4096]{1,0:T...) custom-call(s32[256]{0:T(256)} %tenant_hbm.1, ...), custom_call_target="tpu_custom_call" | custom-call | flops 1000000000 | bytes 40000000 | tf_op jit(solution)/shard_map/pallas_call | solution.py:287
  2.9 6.1 %collective-permute-start = (bf16[8,4096]{1,0:T(8,128)(2,1)}, bf16[8,4096]{1,0:T(8,128)(2,1)S(1)}, u32[]{:S(2)}, u32[]{:S(2)}) collective-permute-start(bf16[8,4096]{1,0:T(8,128)(2,1)} %get-tuple-element.52), channel_id=1, source_target_pairs={{0,14},{2,12},{4,10},{6,8},{8,6},{10,4},{12,2},{14,0},{1,15},{3,13... | collective-permute-start | bytes 196616 | tf_op jit(solution)/shard_map/ppermute | solution.py:244
  8.9 0.0 collective-permute-start.1
  8.9 0.6 collective-permute-start.2
  9.6 2.2 %collective-permute-start.3 = (bf16[8,4096]{1,0:T(8,128)(2,1)}, bf16[8,4096]{1,0:T(8,128)(2,1)S(1)}, u32[]{:S(2)}, u32[]{:S(2)}) collective-permute-start(bf16[8,4096]{1,0:T(8,128)(2,1)} %get-tuple-element.55), channel_id=1, source_target_pairs={{0,8},{2,10},{4,12},{6,14},{8,0},{10,2},{12,4},{14,6},{1,9},{3,11}... | collective-permute-start | bytes 196616 | tf_op jit(solution)/shard_map/ppermute | solution.py:244
  11.8 3.0 %collective-permute-start.4 = (bf16[8,4096]{1,0:T(8,128)(2,1)}, bf16[8,4096]{1,0:T(8,128)(2,1)S(1)}, u32[]{:S(2)}, u32[]{:S(2)}) collective-permute-start(bf16[8,4096]{1,0:T(8,128)(2,1)} %get-tuple-element.56), channel_id=1, source_target_pairs={{0,6},{2,4},{4,2},{6,0},{8,14},{10,12},{12,10},{14,8},{1,7},{3,5},... | collective-permute-start | bytes 196616 | tf_op jit(solution)/shard_map/ppermute | solution.py:244
  14.8 0.0 collective-permute-done.ret_refs_0_
  14.8 1.1 %collective-permute-start.5 = (bf16[8,4096]{1,0:T(8,128)(2,1)}, bf16[8,4096]{1,0:T(8,128)(2,1)S(1)}, u32[]{:S(2)}, u32[]{:S(2)}) collective-permute-start(bf16[8,4096]{1,0:T(8,128)(2,1)} %get-tuple-element.57), channel_id=1, source_target_pairs={{0,12},{2,14},{4,8},{6,10},{8,4},{10,6},{12,0},{14,2},{1,13},{3,15... | collective-permute-start | bytes 196616 | tf_op jit(solution)/shard_map/ppermute | solution.py:244
  15.9 0.0 collective-permute-done.1.ret_refs_1_
  15.9 1.5 %collective-permute-start.6 = (bf16[8,4096]{1,0:T(8,128)(2,1)}, bf16[8,4096]{1,0:T(8,128)(2,1)S(1)}, u32[]{:S(2)}, u32[]{:S(2)}) collective-permute-start(bf16[8,4096]{1,0:T(8,128)(2,1)} %get-tuple-element.58), channel_id=1, source_target_pairs={{0,2},{2,0},{4,6},{6,4},{8,10},{10,8},{12,14},{14,12},{1,3},{3,1},... | collective-permute-start | bytes 196616 | tf_op jit(solution)/shard_map/ppermute | solution.py:244
  17.4 0.7 copy-done.11
  18.0 0.2 shard_map.150
  18.2 1.1 %collective-permute-done.2.ret_refs_2_ = bf16[8,4096]{1,0:T(8,128)(2,1)S(1)} collective-permute-done((bf16[8,4096]{1,0:T(8,128)(2,1)}, bf16[8,4096]{1,0:T(8,128)(2,1)S(1)}, u32[]{:S(2)}, u32[]{:S(2)}) %collective-permute-start.2) | collective-permute-done | bytes 65568 | tf_op jit(solution)/shard_map/ppermute | solution.py:244
  19.3 0.0 collective-permute-done.3.ret_refs_3_
  19.3 0.0 collective-permute-done.4.ret_refs_4_
  19.3 1.7 %collective-permute-done.5.ret_refs_5_ = bf16[8,4096]{1,0:T(8,128)(2,1)S(1)} collective-permute-done((bf16[8,4096]{1,0:T(8,128)(2,1)}, bf16[8,4096]{1,0:T(8,128)(2,1)S(1)}, u32[]{:S(2)}, u32[]{:S(2)}) %collective-permute-start.5) | collective-permute-done | bytes 65568 | tf_op jit(solution)/shard_map/ppermute | solution.py:244
  21.0 0.0 collective-permute-done.6.ret_refs_6_
  21.1 0.0 copy-start
  21.1 0.0 copy-start.1
  21.1 0.0 copy-start.5
  21.1 0.0 copy-start.7
  21.1 0.0 copy-start.8
  21.1 0.6 shard_map.151.mine_ref
  21.7 0.1 collective-permute-start.7
  21.8 1.2 %collective-permute-done.7.other_ref = f32[64,192]{1,0:T(8,128)S(1)} collective-permute-done((f32[64,192]{1,0:T(8,128)S(1)}, f32[64,192]{1,0:T(8,128)S(1)}, u32[]{:S(2)}, u32[]{:S(2)}) %collective-permute-start.7) | collective-permute-done | bytes 49184 | tf_op jit(solution)/shard_map/ppermute | solution.py:251
  23.1 0.3 shard_map.152
  23.4 2.2 %collective-permute-start.8 = (bf16[8,5120]{1,0:T(8,128)(2,1)S(1)}, bf16[8,5120]{1,0:T(8,128)(2,1)S(1)}, u32[]{:S(2)}, u32[]{:S(2)}) collective-permute-start(bf16[8,5120]{1,0:T(8,128)(2,1)S(1)} %get-tuple-element.73), channel_id=1, source_target_pairs={{0,14},{2,12},{4,10},{6,8},{8,6},{10,4},{12,2},{14,0},{1,15},{3,13... | collective-permute-start | bytes 245768 | tf_op jit(solution)/shard_map/ppermute | solution.py:244
  25.6 0.0 collective-permute-start.9
  25.6 3.1 %collective-permute-start.10 = (bf16[8,5120]{1,0:T(8,128)(2,1)S(1)}, bf16[8,5120]{1,0:T(8,128)(2,1)S(1)}, u32[]{:S(2)}, u32[]{:S(2)}) collective-permute-start(bf16[8,5120]{1,0:T(8,128)(2,1)S(1)} %get-tuple-element.75), channel_id=1, source_target_pairs={{0,10},{2,8},{4,14},{6,12},{8,2},{10,0},{12,6},{14,4},{1,11},{3,9}... | collective-permute-start | bytes 245768 | tf_op jit(solution)/shard_map/ppermute | solution.py:244
  28.7 0.5 collective-permute-start.11
  29.3 2.2 %collective-permute-start.12 = (bf16[8,5120]{1,0:T(8,128)(2,1)S(1)}, bf16[8,5120]{1,0:T(8,128)(2,1)S(1)}, u32[]{:S(2)}, u32[]{:S(2)}) collective-permute-start(bf16[8,5120]{1,0:T(8,128)(2,1)S(1)} %get-tuple-element.77), channel_id=1, source_target_pairs={{0,6},{2,4},{4,2},{6,0},{8,14},{10,12},{12,10},{14,8},{1,7},{3,5},... | collective-permute-start | bytes 245768 | tf_op jit(solution)/shard_map/ppermute | solution.py:244
  31.4 0.1 collective-permute-done.8.ret_refs_0_
  31.5 2.0 %collective-permute-start.13 = (bf16[8,5120]{1,0:T(8,128)(2,1)S(1)}, bf16[8,5120]{1,0:T(8,128)(2,1)S(1)}, u32[]{:S(2)}, u32[]{:S(2)}) collective-permute-start(bf16[8,5120]{1,0:T(8,128)(2,1)S(1)} %get-tuple-element.78), channel_id=1, source_target_pairs={{0,12},{2,14},{4,8},{6,10},{8,4},{10,6},{12,0},{14,2},{1,13},{3,15... | collective-permute-start | bytes 245768 | tf_op jit(solution)/shard_map/ppermute | solution.py:244
  33.6 1.2 %collective-permute-start.14 = (bf16[8,5120]{1,0:T(8,128)(2,1)S(1)}, bf16[8,5120]{1,0:T(8,128)(2,1)S(1)}, u32[]{:S(2)}, u32[]{:S(2)}) collective-permute-start(bf16[8,5120]{1,0:T(8,128)(2,1)S(1)} %get-tuple-element.79), channel_id=1, source_target_pairs={{0,2},{2,0},{4,6},{6,4},{8,10},{10,8},{12,14},{14,12},{1,3},{3,1},... | collective-permute-start | bytes 245768 | tf_op jit(solution)/shard_map/ppermute | solution.py:244
  34.8 1.4 %collective-permute-done.10.ret_refs_2_ = bf16[8,5120]{1,0:T(8,128)(2,1)S(1)} collective-permute-done((bf16[8,5120]{1,0:T(8,128)(2,1)S(1)}, bf16[8,5120]{1,0:T(8,128)(2,1)S(1)}, u32[]{:S(2)}, u32[]{:S(2)}) %collective-permute-start.10) | collective-permute-done | bytes 81952 | tf_op jit(solution)/shard_map/ppermute | solution.py:244
  36.2 3.4 %collective-permute-done.11.ret_refs_3_ = bf16[8,5120]{1,0:T(8,128)(2,1)S(1)} collective-permute-done((bf16[8,5120]{1,0:T(8,128)(2,1)S(1)}, bf16[8,5120]{1,0:T(8,128)(2,1)S(1)}, u32[]{:S(2)}, u32[]{:S(2)}) %collective-permute-start.11) | collective-permute-done | bytes 81952 | tf_op jit(solution)/shard_map/ppermute | solution.py:244
  39.6 0.0 collective-permute-done.12.ret_refs_4_
  39.7 0.0 copy-start.4
  39.7 0.0 copy-start.3
  39.7 2.8 %shard_map.153 = (bf16[8,4096]{1,0:T(8,128)(2,1)S(1)}, bf16[8,4096]{1,0:T(8,128)(2,1)S(1)}, bf16[8,4096]{1,0:T(8,128)(2,1)S(1)}, bf16[8,4096]{1,0:T(8,128)(2,1)S...) custom-call(bf16[8,5120]{1,0:T(8,128)(2,1)S(1)} %collective-permute-, ...), custom_call_target="tpu_custom_call" | custom-call | bytes 8000000 | tf_op jit(solution)/shard_map/pallas_call | solution.py:326
  42.5 2.4 %collective-permute-start.15 = (bf16[8,4096]{1,0:T(8,128)(2,1)S(1)}, bf16[8,4096]{1,0:T(8,128)(2,1)S(1)}, u32[]{:S(2)}, u32[]{:S(2)}) collective-permute-start(bf16[8,4096]{1,0:T(8,128)(2,1)S(1)} %get-tuple-element.86), channel_id=1, source_target_pairs={{0,14},{2,12},{4,10},{6,8},{8,6},{10,4},{12,2},{14,0},{1,15},{3,13... | collective-permute-start | bytes 196616 | tf_op jit(solution)/shard_map/ppermute | solution.py:244
  44.9 1.0 %collective-permute-start.16 = (bf16[8,4096]{1,0:T(8,128)(2,1)S(1)}, bf16[8,4096]{1,0:T(8,128)(2,1)S(1)}, u32[]{:S(2)}, u32[]{:S(2)}) collective-permute-start(bf16[8,4096]{1,0:T(8,128)(2,1)S(1)} %get-tuple-element.87), channel_id=1, source_target_pairs={{0,4},{2,6},{4,0},{6,2},{8,12},{10,14},{12,8},{14,10},{1,5},{3,7},... | collective-permute-start | bytes 196616 | tf_op jit(solution)/shard_map/ppermute | solution.py:244
  45.9 1.9 %collective-permute-start.17 = (bf16[8,4096]{1,0:T(8,128)(2,1)S(1)}, bf16[8,4096]{1,0:T(8,128)(2,1)S(1)}, u32[]{:S(2)}, u32[]{:S(2)}) collective-permute-start(bf16[8,4096]{1,0:T(8,128)(2,1)S(1)} %get-tuple-element.88), channel_id=1, source_target_pairs={{0,10},{2,8},{4,14},{6,12},{8,2},{10,0},{12,6},{14,4},{1,11},{3,9}... | collective-permute-start | bytes 196616 | tf_op jit(solution)/shard_map/ppermute | solution.py:244
  47.8 1.2 %collective-permute-start.18 = (bf16[8,4096]{1,0:T(8,128)(2,1)S(1)}, bf16[8,4096]{1,0:T(8,128)(2,1)S(1)}, u32[]{:S(2)}, u32[]{:S(2)}) collective-permute-start(bf16[8,4096]{1,0:T(8,128)(2,1)S(1)} %get-tuple-element.89), channel_id=1, source_target_pairs={{0,8},{2,10},{4,12},{6,14},{8,0},{10,2},{12,4},{14,6},{1,9},{3,11}... | collective-permute-start | bytes 196616 | tf_op jit(solution)/shard_map/ppermute | solution.py:244
  49.0 1.7 %collective-permute-start.19 = (bf16[8,4096]{1,0:T(8,128)(2,1)S(1)}, bf16[8,4096]{1,0:T(8,128)(2,1)S(1)}, u32[]{:S(2)}, u32[]{:S(2)}) collective-permute-start(bf16[8,4096]{1,0:T(8,128)(2,1)S(1)} %get-tuple-element.90), channel_id=1, source_target_pairs={{0,6},{2,4},{4,2},{6,0},{8,14},{10,12},{12,10},{14,8},{1,7},{3,5},... | collective-permute-start | bytes 196616 | tf_op jit(solution)/shard_map/ppermute | solution.py:244
  50.7 1.9 %collective-permute-start.20 = (bf16[8,4096]{1,0:T(8,128)(2,1)S(1)}, bf16[8,4096]{1,0:T(8,128)(2,1)S(1)}, u32[]{:S(2)}, u32[]{:S(2)}) collective-permute-start(bf16[8,4096]{1,0:T(8,128)(2,1)S(1)} %get-tuple-element.91), channel_id=1, source_target_pairs={{0,12},{2,14},{4,8},{6,10},{8,4},{10,6},{12,0},{14,2},{1,13},{3,15... | collective-permute-start | bytes 196616 | tf_op jit(solution)/shard_map/ppermute | solution.py:244
  52.6 1.1 %collective-permute-start.21 = (bf16[8,4096]{1,0:T(8,128)(2,1)S(1)}, bf16[8,4096]{1,0:T(8,128)(2,1)S(1)}, u32[]{:S(2)}, u32[]{:S(2)}) collective-permute-start(bf16[8,4096]{1,0:T(8,128)(2,1)S(1)} %get-tuple-element.92), channel_id=1, source_target_pairs={{0,2},{2,0},{4,6},{6,4},{8,10},{10,8},{12,14},{14,12},{1,3},{3,1},... | collective-permute-start | bytes 196616 | tf_op jit(solution)/shard_map/ppermute | solution.py:244
  53.7 1.5 %collective-permute-done.17.ret_refs_2_ = bf16[8,4096]{1,0:T(8,128)(2,1)S(1)} collective-permute-done((bf16[8,4096]{1,0:T(8,128)(2,1)S(1)}, bf16[8,4096]{1,0:T(8,128)(2,1)S(1)}, u32[]{:S(2)}, u32[]{:S(2)}) %collective-permute-start.17) | collective-permute-done | bytes 65568 | tf_op jit(solution)/shard_map/ppermute | solution.py:244
  55.2 0.9 %collective-permute-done.18.ret_refs_3_ = bf16[8,4096]{1,0:T(8,128)(2,1)S(1)} collective-permute-done((bf16[8,4096]{1,0:T(8,128)(2,1)S(1)}, bf16[8,4096]{1,0:T(8,128)(2,1)S(1)}, u32[]{:S(2)}, u32[]{:S(2)}) %collective-permute-start.18) | collective-permute-done | bytes 65568 | tf_op jit(solution)/shard_map/ppermute | solution.py:244
  56.2 0.8 %collective-permute-done.20.ret_refs_5_ = bf16[8,4096]{1,0:T(8,128)(2,1)S(1)} collective-permute-done((bf16[8,4096]{1,0:T(8,128)(2,1)S(1)}, bf16[8,4096]{1,0:T(8,128)(2,1)S(1)}, u32[]{:S(2)}, u32[]{:S(2)}) %collective-permute-start.20) | collective-permute-done | bytes 65568 | tf_op jit(solution)/shard_map/ppermute | solution.py:244
  56.9 0.3 shard_map.154.mine_ref
  57.2 0.1 collective-permute-start.22
  57.3 1.2 %collective-permute-done.22.other_ref = f32[64,64]{1,0:T(8,128)S(1)} collective-permute-done((f32[64,64]{1,0:T(8,128)S(1)}, f32[64,64]{1,0:T(8,128)S(1)}, u32[]{:S(2)}, u32[]{:S(2)}) %collective-permute-start.22) | collective-permute-done | bytes 16416 | tf_op jit(solution)/shard_map/ppermute | solution.py:251
  58.5 0.3 shard_map.155
  58.8 2.4 %collective-permute-start.23 = (bf16[8,4096]{1,0:T(8,128)(2,1)S(1)}, bf16[8,4096]{1,0:T(8,128)(2,1)S(1)}, u32[]{:S(2)}, u32[]{:S(2)}) collective-permute-start(bf16[8,4096]{1,0:T(8,128)(2,1)S(1)} %get-tuple-element.94), channel_id=1, source_target_pairs={{0,14},{2,12},{4,10},{6,8},{8,6},{10,4},{12,2},{14,0},{1,15},{3,13... | collective-permute-start | bytes 196616 | tf_op jit(solution)/shard_map/ppermute | solution.py:244
  61.2 0.2 collective-permute-start.24
  61.4 2.7 %collective-permute-start.25 = (bf16[8,4096]{1,0:T(8,128)(2,1)S(1)}, bf16[8,4096]{1,0:T(8,128)(2,1)S(1)}, u32[]{:S(2)}, u32[]{:S(2)}) collective-permute-start(bf16[8,4096]{1,0:T(8,128)(2,1)S(1)} %get-tuple-element.96), channel_id=1, source_target_pairs={{0,10},{2,8},{4,14},{6,12},{8,2},{10,0},{12,6},{14,4},{1,11},{3,9}... | collective-permute-start | bytes 196616 | tf_op jit(solution)/shard_map/ppermute | solution.py:244
  64.1 1.0 %collective-permute-start.26 = (bf16[8,4096]{1,0:T(8,128)(2,1)S(1)}, bf16[8,4096]{1,0:T(8,128)(2,1)S(1)}, u32[]{:S(2)}, u32[]{:S(2)}) collective-permute-start(bf16[8,4096]{1,0:T(8,128)(2,1)S(1)} %get-tuple-element.97), channel_id=1, source_target_pairs={{0,8},{2,10},{4,12},{6,14},{8,0},{10,2},{12,4},{14,6},{1,9},{3,11}... | collective-permute-start | bytes 196616 | tf_op jit(solution)/shard_map/ppermute | solution.py:244
  65.1 2.0 %collective-permute-start.27 = (bf16[8,4096]{1,0:T(8,128)(2,1)S(1)}, bf16[8,4096]{1,0:T(8,128)(2,1)S(1)}, u32[]{:S(2)}, u32[]{:S(2)}) collective-permute-start(bf16[8,4096]{1,0:T(8,128)(2,1)S(1)} %get-tuple-element.98), channel_id=1, source_target_pairs={{0,6},{2,4},{4,2},{6,0},{8,14},{10,12},{12,10},{14,8},{1,7},{3,5},... | collective-permute-start | bytes 196616 | tf_op jit(solution)/shard_map/ppermute | solution.py:244
  67.1 1.9 %collective-permute-start.28 = (bf16[8,4096]{1,0:T(8,128)(2,1)S(1)}, bf16[8,4096]{1,0:T(8,128)(2,1)S(1)}, u32[]{:S(2)}, u32[]{:S(2)}) collective-permute-start(bf16[8,4096]{1,0:T(8,128)(2,1)S(1)} %get-tuple-element.99), channel_id=1, source_target_pairs={{0,12},{2,14},{4,8},{6,10},{8,4},{10,6},{12,0},{14,2},{1,13},{3,15... | collective-permute-start | bytes 196616 | tf_op jit(solution)/shard_map/ppermute | solution.py:244
  69.0 1.0 %collective-permute-start.29 = (bf16[8,4096]{1,0:T(8,128)(2,1)S(1)}, bf16[8,4096]{1,0:T(8,128)(2,1)S(1)}, u32[]{:S(2)}, u32[]{:S(2)}) collective-permute-start(bf16[8,4096]{1,0:T(8,128)(2,1)S(1)} %get-tuple-element.100), channel_id=1, source_target_pairs={{0,2},{2,0},{4,6},{6,4},{8,10},{10,8},{12,14},{14,12},{1,3},{3,1},... | collective-permute-start | bytes 196616 | tf_op jit(solution)/shard_map/ppermute | solution.py:244
  70.0 0.8 %collective-permute-done.25.ret_refs_2_ = bf16[8,4096]{1,0:T(8,128)(2,1)S(1)} collective-permute-done((bf16[8,4096]{1,0:T(8,128)(2,1)S(1)}, bf16[8,4096]{1,0:T(8,128)(2,1)S(1)}, u32[]{:S(2)}, u32[]{:S(2)}) %collective-permute-start.25) | collective-permute-done | bytes 65568 | tf_op jit(solution)/shard_map/ppermute | solution.py:244
  70.8 2.5 %collective-permute-done.26.ret_refs_3_ = bf16[8,4096]{1,0:T(8,128)(2,1)S(1)} collective-permute-done((bf16[8,4096]{1,0:T(8,128)(2,1)S(1)}, bf16[8,4096]{1,0:T(8,128)(2,1)S(1)}, u32[]{:S(2)}, u32[]{:S(2)}) %collective-permute-start.26) | collective-permute-done | bytes 65568 | tf_op jit(solution)/shard_map/ppermute | solution.py:244
  73.3 0.9 %shard_map.156 = bf16[32,4096]{1,0:T(8,128)(2,1)} custom-call(bf16[32,64]{1,0:T(8,128)(2,1)S(1)} %get-tuple-element.84.home_ref, bf16[8,4096]{1,0:T(8,128)(2,1)S(1)} %collective-permute-done.23.ret_refs_0_, bf16[8,4096]{1,0:T(8,128)(2,1)S(1)} %collective-permute-done.24.ret_refs_1_, bf16[8,4096]{1,0:T(8,128)(2,1)S(1)} %collective-permute-done.25.ret_refs_2_, ...), custom_call_target="tpu_custom_call" | custom-call | bytes 1000000 | tf_op jit(solution)/shard_map/pallas_call | solution.py:346
  (28 shorter events, 0.1 us)
Async XLA Ops:
  0.6 20.4 %copy-start.2 = (bf16[1,192,8192]{2,1,0:T(8,128)(2,1)S(1)}, bf16[1,192,8192]{2,1,0:T(8,128)(2,1)}, u32[]{:S(2)}) copy-start(bf16[1,192,8192]{2,1,0:T(8,128)(2,1)} %down_ref.2) | copy-start | bytes 9437188
  2.8 18.2 %copy-start.6 = (bf16[8,4096]{1,0:T(8,128)(2,1)S(1)}, bf16[8,4096]{1,0:T(8,128)(2,1)}, u32[]{:S(2)}) copy-start(bf16[8,4096]{1,0:T(8,128)(2,1)} %get-tuple-element.72.ret_refs_7_) | copy-start | bytes 196612
  2.9 11.9 %collective-permute-start = (bf16[8,4096]{1,0:T(8,128)(2,1)}, bf16[8,4096]{1,0:T(8,128)(2,1)S(1)}, u32[]{:S(2)}, u32[]{:S(2)}) collective-permute-start(bf16[8,4096]{1,0:T(8,128)(2,1)} %get-tuple-element.52), channel_id=1, source_target_pairs={{0,14},{2,12},{4,10},{6,8},{8,6},{10,4},{12,2},{14,0},{1,15},{3,13... | collective-permute-start | bytes 196616 | tf_op jit(solution)/shard_map/ppermute | solution.py:244
  8.9 6.9 %collective-permute-start.1 = (bf16[8,4096]{1,0:T(8,128)(2,1)}, bf16[8,4096]{1,0:T(8,128)(2,1)S(1)}, u32[]{:S(2)}, u32[]{:S(2)}) collective-permute-start(bf16[8,4096]{1,0:T(8,128)(2,1)} %get-tuple-element.53), channel_id=1, source_target_pairs={{0,4},{2,6},{4,0},{6,2},{8,12},{10,14},{12,8},{14,10},{1,5},{3,7},... | collective-permute-start | bytes 196616 | tf_op jit(solution)/shard_map/ppermute | solution.py:244
  8.9 10.4 %collective-permute-start.2 = (bf16[8,4096]{1,0:T(8,128)(2,1)}, bf16[8,4096]{1,0:T(8,128)(2,1)S(1)}, u32[]{:S(2)}, u32[]{:S(2)}) collective-permute-start(bf16[8,4096]{1,0:T(8,128)(2,1)} %get-tuple-element.54), channel_id=1, source_target_pairs={{0,10},{2,8},{4,14},{6,12},{8,2},{10,0},{12,6},{14,4},{1,11},{3,9}... | collective-permute-start | bytes 196616 | tf_op jit(solution)/shard_map/ppermute | solution.py:244
  9.6 9.8 %collective-permute-start.3 = (bf16[8,4096]{1,0:T(8,128)(2,1)}, bf16[8,4096]{1,0:T(8,128)(2,1)S(1)}, u32[]{:S(2)}, u32[]{:S(2)}) collective-permute-start(bf16[8,4096]{1,0:T(8,128)(2,1)} %get-tuple-element.55), channel_id=1, source_target_pairs={{0,8},{2,10},{4,12},{6,14},{8,0},{10,2},{12,4},{14,6},{1,9},{3,11}... | collective-permute-start | bytes 196616 | tf_op jit(solution)/shard_map/ppermute | solution.py:244
  11.8 7.5 %collective-permute-start.4 = (bf16[8,4096]{1,0:T(8,128)(2,1)}, bf16[8,4096]{1,0:T(8,128)(2,1)S(1)}, u32[]{:S(2)}, u32[]{:S(2)}) collective-permute-start(bf16[8,4096]{1,0:T(8,128)(2,1)} %get-tuple-element.56), channel_id=1, source_target_pairs={{0,6},{2,4},{4,2},{6,0},{8,14},{10,12},{12,10},{14,8},{1,7},{3,5},... | collective-permute-start | bytes 196616 | tf_op jit(solution)/shard_map/ppermute | solution.py:244
  14.8 6.3 %collective-permute-start.5 = (bf16[8,4096]{1,0:T(8,128)(2,1)}, bf16[8,4096]{1,0:T(8,128)(2,1)S(1)}, u32[]{:S(2)}, u32[]{:S(2)}) collective-permute-start(bf16[8,4096]{1,0:T(8,128)(2,1)} %get-tuple-element.57), channel_id=1, source_target_pairs={{0,12},{2,14},{4,8},{6,10},{8,4},{10,6},{12,0},{14,2},{1,13},{3,15... | collective-permute-start | bytes 196616 | tf_op jit(solution)/shard_map/ppermute | solution.py:244
  15.9 5.2 %collective-permute-start.6 = (bf16[8,4096]{1,0:T(8,128)(2,1)}, bf16[8,4096]{1,0:T(8,128)(2,1)S(1)}, u32[]{:S(2)}, u32[]{:S(2)}) collective-permute-start(bf16[8,4096]{1,0:T(8,128)(2,1)} %get-tuple-element.58), channel_id=1, source_target_pairs={{0,2},{2,0},{4,6},{6,4},{8,10},{10,8},{12,14},{14,12},{1,3},{3,1},... | collective-permute-start | bytes 196616 | tf_op jit(solution)/shard_map/ppermute | solution.py:244
  17.4 0.7 copy-start.11
  18.0 5.0 %copy-start.9 = (bf16[1,64,4096]{2,1,0:T(8,128)(2,1)S(1)}, bf16[1,64,4096]{2,1,0:T(8,128)(2,1)}, u32[]{:S(2)}) copy-start(bf16[1,64,4096]{2,1,0:T(8,128)(2,1)} %uq_ref.1) | copy-start | bytes 1572868
  18.0 5.0 %copy-start.10 = (bf16[1,2,64,512]{3,2,1,0:T(8,128)(2,1)S(1)}, bf16[1,2,64,512]{3,2,1,0:T(8,128)(2,1)}, u32[]{:S(2)}) copy-start(bf16[1,2,64,512]{3,2,1,0:T(8,128)(2,1)} %ukv_ref.1) | copy-start | bytes 393220
  21.1 18.6 %copy-start = (bf16[32,4,96,128]{3,2,1,0:T(8,128)(2,1)S(1)}, bf16[32,4,96,128]{3,2,1,0:T(8,128)(2,1)}, u32[]{:S(2)}) copy-start(bf16[32,4,96,128]{3,2,1,0:T(8,128)(2,1)} %k_ref.1) | copy-start | bytes 9437188
  21.1 18.6 %copy-start.1 = (bf16[32,4,96,128]{3,2,1,0:T(8,128)(2,1)S(1)}, bf16[32,4,96,128]{3,2,1,0:T(8,128)(2,1)}, u32[]{:S(2)}) copy-start(bf16[32,4,96,128]{3,2,1,0:T(8,128)(2,1)} %v_ref.1) | copy-start | bytes 9437188
  21.1 18.6 %copy-start.5 = (bf16[32,4096]{1,0:T(8,128)(2,1)S(1)}, bf16[32,4096]{1,0:T(8,128)(2,1)}, u32[]{:S(2)}) copy-start(bf16[32,4096]{1,0:T(8,128)(2,1)} %pq_ref.1) | copy-start | bytes 786436
  21.1 18.6 %copy-start.7 = (bf16[32,512]{1,0:T(8,128)(2,1)S(1)}, bf16[32,512]{1,0:T(8,128)(2,1)}, u32[]{:S(2)}) copy-start(bf16[32,512]{1,0:T(8,128)(2,1)} %pk_ref.1) | copy-start | bytes 98308
  21.1 18.6 %copy-start.8 = (bf16[32,512]{1,0:T(8,128)(2,1)S(1)}, bf16[32,512]{1,0:T(8,128)(2,1)}, u32[]{:S(2)}) copy-start(bf16[32,512]{1,0:T(8,128)(2,1)} %pv_ref.1) | copy-start | bytes 98308
  21.7 1.3 %collective-permute-start.7 = (f32[64,192]{1,0:T(8,128)S(1)}, f32[64,192]{1,0:T(8,128)S(1)}, u32[]{:S(2)}, u32[]{:S(2)}) collective-permute-start(f32[64,192]{1,0:T(8,128)S(1)} %shard_map.151.mine_ref), channel_id=1, source_target_pairs={{0,1},{1,0},{2,3},{3,2},{4,5},{5,4},{6,7},{7,6},{8,9},{9,8},{10,11... | collective-permute-start | bytes 147464 | tf_op jit(solution)/shard_map/ppermute | solution.py:251
  23.4 8.1 %collective-permute-start.8 = (bf16[8,5120]{1,0:T(8,128)(2,1)S(1)}, bf16[8,5120]{1,0:T(8,128)(2,1)S(1)}, u32[]{:S(2)}, u32[]{:S(2)}) collective-permute-start(bf16[8,5120]{1,0:T(8,128)(2,1)S(1)} %get-tuple-element.73), channel_id=1, source_target_pairs={{0,14},{2,12},{4,10},{6,8},{8,6},{10,4},{12,2},{14,0},{1,15},{3,13... | collective-permute-start | bytes 245768 | tf_op jit(solution)/shard_map/ppermute | solution.py:244
  25.6 8.0 %collective-permute-start.9 = (bf16[8,5120]{1,0:T(8,128)(2,1)S(1)}, bf16[8,5120]{1,0:T(8,128)(2,1)S(1)}, u32[]{:S(2)}, u32[]{:S(2)}) collective-permute-start(bf16[8,5120]{1,0:T(8,128)(2,1)S(1)} %get-tuple-element.74), channel_id=1, source_target_pairs={{0,4},{2,6},{4,0},{6,2},{8,12},{10,14},{12,8},{14,10},{1,5},{3,7},... | collective-permute-start | bytes 245768 | tf_op jit(solution)/shard_map/ppermute | solution.py:244
  25.6 10.6 %collective-permute-start.10 = (bf16[8,5120]{1,0:T(8,128)(2,1)S(1)}, bf16[8,5120]{1,0:T(8,128)(2,1)S(1)}, u32[]{:S(2)}, u32[]{:S(2)}) collective-permute-start(bf16[8,5120]{1,0:T(8,128)(2,1)S(1)} %get-tuple-element.75), channel_id=1, source_target_pairs={{0,10},{2,8},{4,14},{6,12},{8,2},{10,0},{12,6},{14,4},{1,11},{3,9}... | collective-permute-start | bytes 245768 | tf_op jit(solution)/shard_map/ppermute | solution.py:244
  28.7 10.9 %collective-permute-start.11 = (bf16[8,5120]{1,0:T(8,128)(2,1)S(1)}, bf16[8,5120]{1,0:T(8,128)(2,1)S(1)}, u32[]{:S(2)}, u32[]{:S(2)}) collective-permute-start(bf16[8,5120]{1,0:T(8,128)(2,1)S(1)} %get-tuple-element.76), channel_id=1, source_target_pairs={{0,8},{2,10},{4,12},{6,14},{8,0},{10,2},{12,4},{14,6},{1,9},{3,11}... | collective-permute-start | bytes 245768 | tf_op jit(solution)/shard_map/ppermute | solution.py:244
  29.3 10.3 %collective-permute-start.12 = (bf16[8,5120]{1,0:T(8,128)(2,1)S(1)}, bf16[8,5120]{1,0:T(8,128)(2,1)S(1)}, u32[]{:S(2)}, u32[]{:S(2)}) collective-permute-start(bf16[8,5120]{1,0:T(8,128)(2,1)S(1)} %get-tuple-element.77), channel_id=1, source_target_pairs={{0,6},{2,4},{4,2},{6,0},{8,14},{10,12},{12,10},{14,8},{1,7},{3,5},... | collective-permute-start | bytes 245768 | tf_op jit(solution)/shard_map/ppermute | solution.py:244
  31.5 8.1 %collective-permute-start.13 = (bf16[8,5120]{1,0:T(8,128)(2,1)S(1)}, bf16[8,5120]{1,0:T(8,128)(2,1)S(1)}, u32[]{:S(2)}, u32[]{:S(2)}) collective-permute-start(bf16[8,5120]{1,0:T(8,128)(2,1)S(1)} %get-tuple-element.78), channel_id=1, source_target_pairs={{0,12},{2,14},{4,8},{6,10},{8,4},{10,6},{12,0},{14,2},{1,13},{3,15... | collective-permute-start | bytes 245768 | tf_op jit(solution)/shard_map/ppermute | solution.py:244
  33.6 6.1 %collective-permute-start.14 = (bf16[8,5120]{1,0:T(8,128)(2,1)S(1)}, bf16[8,5120]{1,0:T(8,128)(2,1)S(1)}, u32[]{:S(2)}, u32[]{:S(2)}) collective-permute-start(bf16[8,5120]{1,0:T(8,128)(2,1)S(1)} %get-tuple-element.79), channel_id=1, source_target_pairs={{0,2},{2,0},{4,6},{6,4},{8,10},{10,8},{12,14},{14,12},{1,3},{3,1},... | collective-permute-start | bytes 245768 | tf_op jit(solution)/shard_map/ppermute | solution.py:244
  39.7 17.2 %copy-start.4 = (bf16[1,64,4096]{2,1,0:T(8,128)(2,1)S(1)}, bf16[1,64,4096]{2,1,0:T(8,128)(2,1)}, u32[]{:S(2)}) copy-start(bf16[1,64,4096]{2,1,0:T(8,128)(2,1)} %down_ref.3) | copy-start | bytes 1572868
  39.7 18.8 %copy-start.3 = (bf16[1,64,4096]{2,1,0:T(8,128)(2,1)S(1)}, bf16[1,64,4096]{2,1,0:T(8,128)(2,1)}, u32[]{:S(2)}) copy-start(bf16[1,64,4096]{2,1,0:T(8,128)(2,1)} %uo_ref.1) | copy-start | bytes 1572868
  42.5 8.2 %collective-permute-start.15 = (bf16[8,4096]{1,0:T(8,128)(2,1)S(1)}, bf16[8,4096]{1,0:T(8,128)(2,1)S(1)}, u32[]{:S(2)}, u32[]{:S(2)}) collective-permute-start(bf16[8,4096]{1,0:T(8,128)(2,1)S(1)} %get-tuple-element.86), channel_id=1, source_target_pairs={{0,14},{2,12},{4,10},{6,8},{8,6},{10,4},{12,2},{14,0},{1,15},{3,13... | collective-permute-start | bytes 196616 | tf_op jit(solution)/shard_map/ppermute | solution.py:244
  44.9 7.7 %collective-permute-start.16 = (bf16[8,4096]{1,0:T(8,128)(2,1)S(1)}, bf16[8,4096]{1,0:T(8,128)(2,1)S(1)}, u32[]{:S(2)}, u32[]{:S(2)}) collective-permute-start(bf16[8,4096]{1,0:T(8,128)(2,1)S(1)} %get-tuple-element.87), channel_id=1, source_target_pairs={{0,4},{2,6},{4,0},{6,2},{8,12},{10,14},{12,8},{14,10},{1,5},{3,7},... | collective-permute-start | bytes 196616 | tf_op jit(solution)/shard_map/ppermute | solution.py:244
  45.9 9.3 %collective-permute-start.17 = (bf16[8,4096]{1,0:T(8,128)(2,1)S(1)}, bf16[8,4096]{1,0:T(8,128)(2,1)S(1)}, u32[]{:S(2)}, u32[]{:S(2)}) collective-permute-start(bf16[8,4096]{1,0:T(8,128)(2,1)S(1)} %get-tuple-element.88), channel_id=1, source_target_pairs={{0,10},{2,8},{4,14},{6,12},{8,2},{10,0},{12,6},{14,4},{1,11},{3,9}... | collective-permute-start | bytes 196616 | tf_op jit(solution)/shard_map/ppermute | solution.py:244
  47.8 8.3 %collective-permute-start.18 = (bf16[8,4096]{1,0:T(8,128)(2,1)S(1)}, bf16[8,4096]{1,0:T(8,128)(2,1)S(1)}, u32[]{:S(2)}, u32[]{:S(2)}) collective-permute-start(bf16[8,4096]{1,0:T(8,128)(2,1)S(1)} %get-tuple-element.89), channel_id=1, source_target_pairs={{0,8},{2,10},{4,12},{6,14},{8,0},{10,2},{12,4},{14,6},{1,9},{3,11}... | collective-permute-start | bytes 196616 | tf_op jit(solution)/shard_map/ppermute | solution.py:244
  49.0 7.1 %collective-permute-start.19 = (bf16[8,4096]{1,0:T(8,128)(2,1)S(1)}, bf16[8,4096]{1,0:T(8,128)(2,1)S(1)}, u32[]{:S(2)}, u32[]{:S(2)}) collective-permute-start(bf16[8,4096]{1,0:T(8,128)(2,1)S(1)} %get-tuple-element.90), channel_id=1, source_target_pairs={{0,6},{2,4},{4,2},{6,0},{8,14},{10,12},{12,10},{14,8},{1,7},{3,5},... | collective-permute-start | bytes 196616 | tf_op jit(solution)/shard_map/ppermute | solution.py:244
  50.7 6.2 %collective-permute-start.20 = (bf16[8,4096]{1,0:T(8,128)(2,1)S(1)}, bf16[8,4096]{1,0:T(8,128)(2,1)S(1)}, u32[]{:S(2)}, u32[]{:S(2)}) collective-permute-start(bf16[8,4096]{1,0:T(8,128)(2,1)S(1)} %get-tuple-element.91), channel_id=1, source_target_pairs={{0,12},{2,14},{4,8},{6,10},{8,4},{10,6},{12,0},{14,2},{1,13},{3,15... | collective-permute-start | bytes 196616 | tf_op jit(solution)/shard_map/ppermute | solution.py:244
  52.6 4.3 %collective-permute-start.21 = (bf16[8,4096]{1,0:T(8,128)(2,1)S(1)}, bf16[8,4096]{1,0:T(8,128)(2,1)S(1)}, u32[]{:S(2)}, u32[]{:S(2)}) collective-permute-start(bf16[8,4096]{1,0:T(8,128)(2,1)S(1)} %get-tuple-element.92), channel_id=1, source_target_pairs={{0,2},{2,0},{4,6},{6,4},{8,10},{10,8},{12,14},{14,12},{1,3},{3,1},... | collective-permute-start | bytes 196616 | tf_op jit(solution)/shard_map/ppermute | solution.py:244
  57.2 1.3 %collective-permute-start.22 = (f32[64,64]{1,0:T(8,128)S(1)}, f32[64,64]{1,0:T(8,128)S(1)}, u32[]{:S(2)}, u32[]{:S(2)}) collective-permute-start(f32[64,64]{1,0:T(8,128)S(1)} %shard_map.154.mine_ref), channel_id=1, source_target_pairs={{0,1},{1,0},{2,3},{3,2},{4,5},{5,4},{6,7},{7,6},{8,9},{9,8},{10,11... | collective-permute-start | bytes 49160 | tf_op jit(solution)/shard_map/ppermute | solution.py:251
  58.8 8.3 %collective-permute-start.23 = (bf16[8,4096]{1,0:T(8,128)(2,1)S(1)}, bf16[8,4096]{1,0:T(8,128)(2,1)S(1)}, u32[]{:S(2)}, u32[]{:S(2)}) collective-permute-start(bf16[8,4096]{1,0:T(8,128)(2,1)S(1)} %get-tuple-element.94), channel_id=1, source_target_pairs={{0,14},{2,12},{4,10},{6,8},{8,6},{10,4},{12,2},{14,0},{1,15},{3,13... | collective-permute-start | bytes 196616 | tf_op jit(solution)/shard_map/ppermute | solution.py:244
  61.2 7.8 %collective-permute-start.24 = (bf16[8,4096]{1,0:T(8,128)(2,1)S(1)}, bf16[8,4096]{1,0:T(8,128)(2,1)S(1)}, u32[]{:S(2)}, u32[]{:S(2)}) collective-permute-start(bf16[8,4096]{1,0:T(8,128)(2,1)S(1)} %get-tuple-element.95), channel_id=1, source_target_pairs={{0,4},{2,6},{4,0},{6,2},{8,12},{10,14},{12,8},{14,10},{1,5},{3,7},... | collective-permute-start | bytes 196616 | tf_op jit(solution)/shard_map/ppermute | solution.py:244
  61.4 9.3 %collective-permute-start.25 = (bf16[8,4096]{1,0:T(8,128)(2,1)S(1)}, bf16[8,4096]{1,0:T(8,128)(2,1)S(1)}, u32[]{:S(2)}, u32[]{:S(2)}) collective-permute-start(bf16[8,4096]{1,0:T(8,128)(2,1)S(1)} %get-tuple-element.96), channel_id=1, source_target_pairs={{0,10},{2,8},{4,14},{6,12},{8,2},{10,0},{12,6},{14,4},{1,11},{3,9}... | collective-permute-start | bytes 196616 | tf_op jit(solution)/shard_map/ppermute | solution.py:244
  64.1 9.2 %collective-permute-start.26 = (bf16[8,4096]{1,0:T(8,128)(2,1)S(1)}, bf16[8,4096]{1,0:T(8,128)(2,1)S(1)}, u32[]{:S(2)}, u32[]{:S(2)}) collective-permute-start(bf16[8,4096]{1,0:T(8,128)(2,1)S(1)} %get-tuple-element.97), channel_id=1, source_target_pairs={{0,8},{2,10},{4,12},{6,14},{8,0},{10,2},{12,4},{14,6},{1,9},{3,11}... | collective-permute-start | bytes 196616 | tf_op jit(solution)/shard_map/ppermute | solution.py:244
  65.1 8.2 %collective-permute-start.27 = (bf16[8,4096]{1,0:T(8,128)(2,1)S(1)}, bf16[8,4096]{1,0:T(8,128)(2,1)S(1)}, u32[]{:S(2)}, u32[]{:S(2)}) collective-permute-start(bf16[8,4096]{1,0:T(8,128)(2,1)S(1)} %get-tuple-element.98), channel_id=1, source_target_pairs={{0,6},{2,4},{4,2},{6,0},{8,14},{10,12},{12,10},{14,8},{1,7},{3,5},... | collective-permute-start | bytes 196616 | tf_op jit(solution)/shard_map/ppermute | solution.py:244
  67.1 6.3 %collective-permute-start.28 = (bf16[8,4096]{1,0:T(8,128)(2,1)S(1)}, bf16[8,4096]{1,0:T(8,128)(2,1)S(1)}, u32[]{:S(2)}, u32[]{:S(2)}) collective-permute-start(bf16[8,4096]{1,0:T(8,128)(2,1)S(1)} %get-tuple-element.99), channel_id=1, source_target_pairs={{0,12},{2,14},{4,8},{6,10},{8,4},{10,6},{12,0},{14,2},{1,13},{3,15... | collective-permute-start | bytes 196616 | tf_op jit(solution)/shard_map/ppermute | solution.py:244
  69.0 4.3 %collective-permute-start.29 = (bf16[8,4096]{1,0:T(8,128)(2,1)S(1)}, bf16[8,4096]{1,0:T(8,128)(2,1)S(1)}, u32[]{:S(2)}, u32[]{:S(2)}) collective-permute-start(bf16[8,4096]{1,0:T(8,128)(2,1)S(1)} %get-tuple-element.100), channel_id=1, source_target_pairs={{0,2},{2,0},{4,6},{6,4},{8,10},{10,8},{12,14},{14,12},{1,3},{3,1},... | collective-permute-start | bytes 196616 | tf_op jit(solution)/shard_map/ppermute | solution.py:244

commit v10 on v9

--- a/solution.py
+++ b/solution.py
@@ -192,7 +192,6 @@
         slot = 4 * g
         columns = slice(g * group * head_dim, (g + 1) * group * head_dim)
         own, score = held[g]
-        new_value = line_ref[slot + 2]
         score = score * scale + bias
         highest = jnp.maximum(jnp.max(score, axis=1, keepdims=True), own)
         raised = jnp.exp(score - highest)
@@ -200,6 +199,12 @@
         inverse = 1.0 / (jnp.sum(raised, axis=1, keepdims=True) + own_raised)
         weight = raised * inverse
         own_weight = (own_raised * inverse).astype(BF16).astype(F32)
+        held[g] = weight, own_weight
+    for g in range(heads):
+        slot = 4 * g
+        columns = slice(g * group * head_dim, (g + 1) * group * head_dim)
+        weight, own_weight = held[g]
+        new_value = line_ref[slot + 2]
         attended = jnp.concatenate(
             [dot(weight[r * group : (r + 1) * group].astype(BF16), v_ref[r, g]) for r in range(rows)], axis=0
         )

time: 74.4 us -> 74.4 us (level)
  no operation moved by 1% of the time
where the time goes in v10:
time: 74.4 us; the launch traced here: 74.2 us
  starting transfers between devices  48.3 us (65%)
  waiting for transfers between devices  16.7 us (22%)
  Pallas kernels  7.58 us (10%)
  between operations  0.84 us (1%)
    ppermute x28, starting transfers between devices, exchange(): lax.ppermute(block, 'wide', [(k, k ^ d) for k in range(wide_count)])  48.2 us
    ppermute x28, waiting for transfers between devices, exchange(): lax.ppermute(block, 'wide', [(k, k ^ d) for k in range(wide_count)])  14.3 us
    pallas_call x1, Pallas kernels, shards(): call(functools.partial(attend_body, group), [*blocks_of(query_width), str...  2.84 us
    ppermute x2, waiting for transfers between devices, other_core(): return lax.ppermute(value, 'tp', [(0, 1), (1, 0)])  2.44 us
    pallas_call x1, Pallas kernels, shards(): call(functools.partial(pack_body, capacity, by_distance), (struct((2, row...  2.19 us
  transfers between devices with their start and end apart: 30, of which 12 were waited for; matrix products, arithmetic and copies ran while one was open for 0% of the time, Pallas kernels for 0%

profile of v10, /device:TPU:0, one launch (start us, length us, event | category | flops | bytes accessed | tf_op | source)
XLA Modules:
  0.0 74.2 jit_solution(17120412336616504521)
XLA Ops:
  0.6 2.2 %shard_map.149 = (s32[2,32]{1,0:T(2,128)}, bf16[8,4096]{1,0:T(8,128)(2,1)}, bf16[8,4096]{1,0:T(8,128)(2,1)}, bf16[8,4096]{1,0:T(8,128)(2,1)}, bf16[8,4096]{1,0:T...) custom-call(s32[256]{0:T(256)} %tenant_hbm.1, ...), custom_call_target="tpu_custom_call" | custom-call | flops 1000000000 | bytes 40000000 | tf_op jit(solution)/shard_map/pallas_call | solution.py:292
  2.9 6.1 %collective-permute-start = (bf16[8,4096]{1,0:T(8,128)(2,1)}, bf16[8,4096]{1,0:T(8,128)(2,1)S(1)}, u32[]{:S(2)}, u32[]{:S(2)}) collective-permute-start(bf16[8,4096]{1,0:T(8,128)(2,1)} %get-tuple-element.52), channel_id=1, source_target_pairs={{0,14},{2,12},{4,10},{6,8},{8,6},{10,4},{12,2},{14,0},{1,15},{3,13... | collective-permute-start | bytes 196616 | tf_op jit(solution)/shard_map/ppermute | solution.py:249
  8.9 0.0 collective-permute-start.1
  8.9 0.6 collective-permute-start.2
  9.6 2.2 %collective-permute-start.3 = (bf16[8,4096]{1,0:T(8,128)(2,1)}, bf16[8,4096]{1,0:T(8,128)(2,1)S(1)}, u32[]{:S(2)}, u32[]{:S(2)}) collective-permute-start(bf16[8,4096]{1,0:T(8,128)(2,1)} %get-tuple-element.55), channel_id=1, source_target_pairs={{0,8},{2,10},{4,12},{6,14},{8,0},{10,2},{12,4},{14,6},{1,9},{3,11}... | collective-permute-start | bytes 196616 | tf_op jit(solution)/shard_map/ppermute | solution.py:249
  11.8 3.0 %collective-permute-start.4 = (bf16[8,4096]{1,0:T(8,128)(2,1)}, bf16[8,4096]{1,0:T(8,128)(2,1)S(1)}, u32[]{:S(2)}, u32[]{:S(2)}) collective-permute-start(bf16[8,4096]{1,0:T(8,128)(2,1)} %get-tuple-element.56), channel_id=1, source_target_pairs={{0,6},{2,4},{4,2},{6,0},{8,14},{10,12},{12,10},{14,8},{1,7},{3,5},... | collective-permute-start | bytes 196616 | tf_op jit(solution)/shard_map/ppermute | solution.py:249
  14.8 0.0 collective-permute-done.ret_refs_0_
  14.8 1.1 %collective-permute-start.5 = (bf16[8,4096]{1,0:T(8,128)(2,1)}, bf16[8,4096]{1,0:T(8,128)(2,1)S(1)}, u32[]{:S(2)}, u32[]{:S(2)}) collective-permute-start(bf16[8,4096]{1,0:T(8,128)(2,1)} %get-tuple-element.57), channel_id=1, source_target_pairs={{0,12},{2,14},{4,8},{6,10},{8,4},{10,6},{12,0},{14,2},{1,13},{3,15... | collective-permute-start | bytes 196616 | tf_op jit(solution)/shard_map/ppermute | solution.py:249
  15.9 0.0 collective-permute-done.1.ret_refs_1_
  15.9 1.5 %collective-permute-start.6 = (bf16[8,4096]{1,0:T(8,128)(2,1)}, bf16[8,4096]{1,0:T(8,128)(2,1)S(1)}, u32[]{:S(2)}, u32[]{:S(2)}) collective-permute-start(bf16[8,4096]{1,0:T(8,128)(2,1)} %get-tuple-element.58), channel_id=1, source_target_pairs={{0,2},{2,0},{4,6},{6,4},{8,10},{10,8},{12,14},{14,12},{1,3},{3,1},... | collective-permute-start | bytes 196616 | tf_op jit(solution)/shard_map/ppermute | solution.py:249
  17.4 0.7 copy-done.11
  18.0 0.2 shard_map.150
  18.2 1.1 %collective-permute-done.2.ret_refs_2_ = bf16[8,4096]{1,0:T(8,128)(2,1)S(1)} collective-permute-done((bf16[8,4096]{1,0:T(8,128)(2,1)}, bf16[8,4096]{1,0:T(8,128)(2,1)S(1)}, u32[]{:S(2)}, u32[]{:S(2)}) %collective-permute-start.2) | collective-permute-done | bytes 65568 | tf_op jit(solution)/shard_map/ppermute | solution.py:249
  19.3 0.0 collective-permute-done.3.ret_refs_3_
  19.3 0.0 collective-permute-done.4.ret_refs_4_
  19.3 1.7 %collective-permute-done.5.ret_refs_5_ = bf16[8,4096]{1,0:T(8,128)(2,1)S(1)} collective-permute-done((bf16[8,4096]{1,0:T(8,128)(2,1)}, bf16[8,4096]{1,0:T(8,128)(2,1)S(1)}, u32[]{:S(2)}, u32[]{:S(2)}) %collective-permute-start.5) | collective-permute-done | bytes 65568 | tf_op jit(solution)/shard_map/ppermute | solution.py:249
  21.0 0.0 collective-permute-done.6.ret_refs_6_
  21.1 0.0 copy-start
  21.1 0.0 copy-start.1
  21.1 0.0 copy-start.5
  21.1 0.0 copy-start.7
  21.1 0.0 copy-start.8
  21.1 0.6 shard_map.151.mine_ref
  21.7 0.1 collective-permute-start.7
  21.8 1.2 %collective-permute-done.7.other_ref = f32[64,192]{1,0:T(8,128)S(1)} collective-permute-done((f32[64,192]{1,0:T(8,128)S(1)}, f32[64,192]{1,0:T(8,128)S(1)}, u32[]{:S(2)}, u32[]{:S(2)}) %collective-permute-start.7) | collective-permute-done | bytes 49184 | tf_op jit(solution)/shard_map/ppermute | solution.py:256
  23.1 0.3 shard_map.152
  23.4 2.2 %collective-permute-start.8 = (bf16[8,5120]{1,0:T(8,128)(2,1)S(1)}, bf16[8,5120]{1,0:T(8,128)(2,1)S(1)}, u32[]{:S(2)}, u32[]{:S(2)}) collective-permute-start(bf16[8,5120]{1,0:T(8,128)(2,1)S(1)} %get-tuple-element.73), channel_id=1, source_target_pairs={{0,14},{2,12},{4,10},{6,8},{8,6},{10,4},{12,2},{14,0},{1,15},{3,13... | collective-permute-start | bytes 245768 | tf_op jit(solution)/shard_map/ppermute | solution.py:249
  25.6 0.0 collective-permute-start.9
  25.6 3.1 %collective-permute-start.10 = (bf16[8,5120]{1,0:T(8,128)(2,1)S(1)}, bf16[8,5120]{1,0:T(8,128)(2,1)S(1)}, u32[]{:S(2)}, u32[]{:S(2)}) collective-permute-start(bf16[8,5120]{1,0:T(8,128)(2,1)S(1)} %get-tuple-element.75), channel_id=1, source_target_pairs={{0,10},{2,8},{4,14},{6,12},{8,2},{10,0},{12,6},{14,4},{1,11},{3,9}... | collective-permute-start | bytes 245768 | tf_op jit(solution)/shard_map/ppermute | solution.py:249
  28.7 0.5 collective-permute-start.11
  29.3 2.2 %collective-permute-start.12 = (bf16[8,5120]{1,0:T(8,128)(2,1)S(1)}, bf16[8,5120]{1,0:T(8,128)(2,1)S(1)}, u32[]{:S(2)}, u32[]{:S(2)}) collective-permute-start(bf16[8,5120]{1,0:T(8,128)(2,1)S(1)} %get-tuple-element.77), channel_id=1, source_target_pairs={{0,6},{2,4},{4,2},{6,0},{8,14},{10,12},{12,10},{14,8},{1,7},{3,5},... | collective-permute-start | bytes 245768 | tf_op jit(solution)/shard_map/ppermute | solution.py:249
  31.4 0.1 collective-permute-done.8.ret_refs_0_
  31.5 2.0 %collective-permute-start.13 = (bf16[8,5120]{1,0:T(8,128)(2,1)S(1)}, bf16[8,5120]{1,0:T(8,128)(2,1)S(1)}, u32[]{:S(2)}, u32[]{:S(2)}) collective-permute-start(bf16[8,5120]{1,0:T(8,128)(2,1)S(1)} %get-tuple-element.78), channel_id=1, source_target_pairs={{0,12},{2,14},{4,8},{6,10},{8,4},{10,6},{12,0},{14,2},{1,13},{3,15... | collective-permute-start | bytes 245768 | tf_op jit(solution)/shard_map/ppermute | solution.py:249
  33.6 1.2 %collective-permute-start.14 = (bf16[8,5120]{1,0:T(8,128)(2,1)S(1)}, bf16[8,5120]{1,0:T(8,128)(2,1)S(1)}, u32[]{:S(2)}, u32[]{:S(2)}) collective-permute-start(bf16[8,5120]{1,0:T(8,128)(2,1)S(1)} %get-tuple-element.79), channel_id=1, source_target_pairs={{0,2},{2,0},{4,6},{6,4},{8,10},{10,8},{12,14},{14,12},{1,3},{3,1},... | collective-permute-start | bytes 245768 | tf_op jit(solution)/shard_map/ppermute | solution.py:249
  34.8 1.4 %collective-permute-done.10.ret_refs_2_ = bf16[8,5120]{1,0:T(8,128)(2,1)S(1)} collective-permute-done((bf16[8,5120]{1,0:T(8,128)(2,1)S(1)}, bf16[8,5120]{1,0:T(8,128)(2,1)S(1)}, u32[]{:S(2)}, u32[]{:S(2)}) %collective-permute-start.10) | collective-permute-done | bytes 81952 | tf_op jit(solution)/shard_map/ppermute | solution.py:249
  36.2 3.4 %collective-permute-done.11.ret_refs_3_ = bf16[8,5120]{1,0:T(8,128)(2,1)S(1)} collective-permute-done((bf16[8,5120]{1,0:T(8,128)(2,1)S(1)}, bf16[8,5120]{1,0:T(8,128)(2,1)S(1)}, u32[]{:S(2)}, u32[]{:S(2)}) %collective-permute-start.11) | collective-permute-done | bytes 81952 | tf_op jit(solution)/shard_map/ppermute | solution.py:249
  39.6 0.0 collective-permute-done.12.ret_refs_4_
  39.7 0.0 copy-start.4
  39.7 0.0 copy-start.3
  39.7 2.8 %shard_map.153 = (bf16[8,4096]{1,0:T(8,128)(2,1)S(1)}, bf16[8,4096]{1,0:T(8,128)(2,1)S(1)}, bf16[8,4096]{1,0:T(8,128)(2,1)S(1)}, bf16[8,4096]{1,0:T(8,128)(2,1)S...) custom-call(bf16[8,5120]{1,0:T(8,128)(2,1)S(1)} %collective-permute-, ...), custom_call_target="tpu_custom_call" | custom-call | bytes 8000000 | tf_op jit(solution)/shard_map/pallas_call | solution.py:331
  42.5 2.4 %collective-permute-start.15 = (bf16[8,4096]{1,0:T(8,128)(2,1)S(1)}, bf16[8,4096]{1,0:T(8,128)(2,1)S(1)}, u32[]{:S(2)}, u32[]{:S(2)}) collective-permute-start(bf16[8,4096]{1,0:T(8,128)(2,1)S(1)} %get-tuple-element.86), channel_id=1, source_target_pairs={{0,14},{2,12},{4,10},{6,8},{8,6},{10,4},{12,2},{14,0},{1,15},{3,13... | collective-permute-start | bytes 196616 | tf_op jit(solution)/shard_map/ppermute | solution.py:249
  44.9 1.0 %collective-permute-start.16 = (bf16[8,4096]{1,0:T(8,128)(2,1)S(1)}, bf16[8,4096]{1,0:T(8,128)(2,1)S(1)}, u32[]{:S(2)}, u32[]{:S(2)}) collective-permute-start(bf16[8,4096]{1,0:T(8,128)(2,1)S(1)} %get-tuple-element.87), channel_id=1, source_target_pairs={{0,4},{2,6},{4,0},{6,2},{8,12},{10,14},{12,8},{14,10},{1,5},{3,7},... | collective-permute-start | bytes 196616 | tf_op jit(solution)/shard_map/ppermute | solution.py:249
  45.9 1.9 %collective-permute-start.17 = (bf16[8,4096]{1,0:T(8,128)(2,1)S(1)}, bf16[8,4096]{1,0:T(8,128)(2,1)S(1)}, u32[]{:S(2)}, u32[]{:S(2)}) collective-permute-start(bf16[8,4096]{1,0:T(8,128)(2,1)S(1)} %get-tuple-element.88), channel_id=1, source_target_pairs={{0,10},{2,8},{4,14},{6,12},{8,2},{10,0},{12,6},{14,4},{1,11},{3,9}... | collective-permute-start | bytes 196616 | tf_op jit(solution)/shard_map/ppermute | solution.py:249
  47.8 1.2 %collective-permute-start.18 = (bf16[8,4096]{1,0:T(8,128)(2,1)S(1)}, bf16[8,4096]{1,0:T(8,128)(2,1)S(1)}, u32[]{:S(2)}, u32[]{:S(2)}) collective-permute-start(bf16[8,4096]{1,0:T(8,128)(2,1)S(1)} %get-tuple-element.89), channel_id=1, source_target_pairs={{0,8},{2,10},{4,12},{6,14},{8,0},{10,2},{12,4},{14,6},{1,9},{3,11}... | collective-permute-start | bytes 196616 | tf_op jit(solution)/shard_map/ppermute | solution.py:249
  49.0 1.7 %collective-permute-start.19 = (bf16[8,4096]{1,0:T(8,128)(2,1)S(1)}, bf16[8,4096]{1,0:T(8,128)(2,1)S(1)}, u32[]{:S(2)}, u32[]{:S(2)}) collective-permute-start(bf16[8,4096]{1,0:T(8,128)(2,1)S(1)} %get-tuple-element.90), channel_id=1, source_target_pairs={{0,6},{2,4},{4,2},{6,0},{8,14},{10,12},{12,10},{14,8},{1,7},{3,5},... | collective-permute-start | bytes 196616 | tf_op jit(solution)/shard_map/ppermute | solution.py:249
  50.7 1.9 %collective-permute-start.20 = (bf16[8,4096]{1,0:T(8,128)(2,1)S(1)}, bf16[8,4096]{1,0:T(8,128)(2,1)S(1)}, u32[]{:S(2)}, u32[]{:S(2)}) collective-permute-start(bf16[8,4096]{1,0:T(8,128)(2,1)S(1)} %get-tuple-element.91), channel_id=1, source_target_pairs={{0,12},{2,14},{4,8},{6,10},{8,4},{10,6},{12,0},{14,2},{1,13},{3,15... | collective-permute-start | bytes 196616 | tf_op jit(solution)/shard_map/ppermute | solution.py:249
  52.6 1.1 %collective-permute-start.21 = (bf16[8,4096]{1,0:T(8,128)(2,1)S(1)}, bf16[8,4096]{1,0:T(8,128)(2,1)S(1)}, u32[]{:S(2)}, u32[]{:S(2)}) collective-permute-start(bf16[8,4096]{1,0:T(8,128)(2,1)S(1)} %get-tuple-element.92), channel_id=1, source_target_pairs={{0,2},{2,0},{4,6},{6,4},{8,10},{10,8},{12,14},{14,12},{1,3},{3,1},... | collective-permute-start | bytes 196616 | tf_op jit(solution)/shard_map/ppermute | solution.py:249
  53.7 1.5 %collective-permute-done.17.ret_refs_2_ = bf16[8,4096]{1,0:T(8,128)(2,1)S(1)} collective-permute-done((bf16[8,4096]{1,0:T(8,128)(2,1)S(1)}, bf16[8,4096]{1,0:T(8,128)(2,1)S(1)}, u32[]{:S(2)}, u32[]{:S(2)}) %collective-permute-start.17) | collective-permute-done | bytes 65568 | tf_op jit(solution)/shard_map/ppermute | solution.py:249
  55.2 0.9 %collective-permute-done.18.ret_refs_3_ = bf16[8,4096]{1,0:T(8,128)(2,1)S(1)} collective-permute-done((bf16[8,4096]{1,0:T(8,128)(2,1)S(1)}, bf16[8,4096]{1,0:T(8,128)(2,1)S(1)}, u32[]{:S(2)}, u32[]{:S(2)}) %collective-permute-start.18) | collective-permute-done | bytes 65568 | tf_op jit(solution)/shard_map/ppermute | solution.py:249
  56.2 0.8 %collective-permute-done.20.ret_refs_5_ = bf16[8,4096]{1,0:T(8,128)(2,1)S(1)} collective-permute-done((bf16[8,4096]{1,0:T(8,128)(2,1)S(1)}, bf16[8,4096]{1,0:T(8,128)(2,1)S(1)}, u32[]{:S(2)}, u32[]{:S(2)}) %collective-permute-start.20) | collective-permute-done | bytes 65568 | tf_op jit(solution)/shard_map/ppermute | solution.py:249
  56.9 0.3 shard_map.154.mine_ref
  57.2 0.1 collective-permute-start.22
  57.3 1.2 %collective-permute-done.22.other_ref = f32[64,64]{1,0:T(8,128)S(1)} collective-permute-done((f32[64,64]{1,0:T(8,128)S(1)}, f32[64,64]{1,0:T(8,128)S(1)}, u32[]{:S(2)}, u32[]{:S(2)}) %collective-permute-start.22) | collective-permute-done | bytes 16416 | tf_op jit(solution)/shard_map/ppermute | solution.py:256
  58.5 0.3 shard_map.155
  58.8 2.4 %collective-permute-start.23 = (bf16[8,4096]{1,0:T(8,128)(2,1)S(1)}, bf16[8,4096]{1,0:T(8,128)(2,1)S(1)}, u32[]{:S(2)}, u32[]{:S(2)}) collective-permute-start(bf16[8,4096]{1,0:T(8,128)(2,1)S(1)} %get-tuple-element.94), channel_id=1, source_target_pairs={{0,14},{2,12},{4,10},{6,8},{8,6},{10,4},{12,2},{14,0},{1,15},{3,13... | collective-permute-start | bytes 196616 | tf_op jit(solution)/shard_map/ppermute | solution.py:249
  61.2 0.2 collective-permute-start.24
  61.4 2.7 %collective-permute-start.25 = (bf16[8,4096]{1,0:T(8,128)(2,1)S(1)}, bf16[8,4096]{1,0:T(8,128)(2,1)S(1)}, u32[]{:S(2)}, u32[]{:S(2)}) collective-permute-start(bf16[8,4096]{1,0:T(8,128)(2,1)S(1)} %get-tuple-element.96), channel_id=1, source_target_pairs={{0,10},{2,8},{4,14},{6,12},{8,2},{10,0},{12,6},{14,4},{1,11},{3,9}... | collective-permute-start | bytes 196616 | tf_op jit(solution)/shard_map/ppermute | solution.py:249
  64.1 1.0 %collective-permute-start.26 = (bf16[8,4096]{1,0:T(8,128)(2,1)S(1)}, bf16[8,4096]{1,0:T(8,128)(2,1)S(1)}, u32[]{:S(2)}, u32[]{:S(2)}) collective-permute-start(bf16[8,4096]{1,0:T(8,128)(2,1)S(1)} %get-tuple-element.97), channel_id=1, source_target_pairs={{0,8},{2,10},{4,12},{6,14},{8,0},{10,2},{12,4},{14,6},{1,9},{3,11}... | collective-permute-start | bytes 196616 | tf_op jit(solution)/shard_map/ppermute | solution.py:249
  65.1 2.0 %collective-permute-start.27 = (bf16[8,4096]{1,0:T(8,128)(2,1)S(1)}, bf16[8,4096]{1,0:T(8,128)(2,1)S(1)}, u32[]{:S(2)}, u32[]{:S(2)}) collective-permute-start(bf16[8,4096]{1,0:T(8,128)(2,1)S(1)} %get-tuple-element.98), channel_id=1, source_target_pairs={{0,6},{2,4},{4,2},{6,0},{8,14},{10,12},{12,10},{14,8},{1,7},{3,5},... | collective-permute-start | bytes 196616 | tf_op jit(solution)/shard_map/ppermute | solution.py:249
  67.1 1.9 %collective-permute-start.28 = (bf16[8,4096]{1,0:T(8,128)(2,1)S(1)}, bf16[8,4096]{1,0:T(8,128)(2,1)S(1)}, u32[]{:S(2)}, u32[]{:S(2)}) collective-permute-start(bf16[8,4096]{1,0:T(8,128)(2,1)S(1)} %get-tuple-element.99), channel_id=1, source_target_pairs={{0,12},{2,14},{4,8},{6,10},{8,4},{10,6},{12,0},{14,2},{1,13},{3,15... | collective-permute-start | bytes 196616 | tf_op jit(solution)/shard_map/ppermute | solution.py:249
  69.0 1.0 %collective-permute-start.29 = (bf16[8,4096]{1,0:T(8,128)(2,1)S(1)}, bf16[8,4096]{1,0:T(8,128)(2,1)S(1)}, u32[]{:S(2)}, u32[]{:S(2)}) collective-permute-start(bf16[8,4096]{1,0:T(8,128)(2,1)S(1)} %get-tuple-element.100), channel_id=1, source_target_pairs={{0,2},{2,0},{4,6},{6,4},{8,10},{10,8},{12,14},{14,12},{1,3},{3,1},... | collective-permute-start | bytes 196616 | tf_op jit(solution)/shard_map/ppermute | solution.py:249
  70.0 0.8 %collective-permute-done.25.ret_refs_2_ = bf16[8,4096]{1,0:T(8,128)(2,1)S(1)} collective-permute-done((bf16[8,4096]{1,0:T(8,128)(2,1)S(1)}, bf16[8,4096]{1,0:T(8,128)(2,1)S(1)}, u32[]{:S(2)}, u32[]{:S(2)}) %collective-permute-start.25) | collective-permute-done | bytes 65568 | tf_op jit(solution)/shard_map/ppermute | solution.py:249
  70.8 2.5 %collective-permute-done.26.ret_refs_3_ = bf16[8,4096]{1,0:T(8,128)(2,1)S(1)} collective-permute-done((bf16[8,4096]{1,0:T(8,128)(2,1)S(1)}, bf16[8,4096]{1,0:T(8,128)(2,1)S(1)}, u32[]{:S(2)}, u32[]{:S(2)}) %collective-permute-start.26) | collective-permute-done | bytes 65568 | tf_op jit(solution)/shard_map/ppermute | solution.py:249
  73.3 0.9 %shard_map.156 = bf16[32,4096]{1,0:T(8,128)(2,1)} custom-call(bf16[32,64]{1,0:T(8,128)(2,1)S(1)} %get-tuple-element.84.home_ref, bf16[8,4096]{1,0:T(8,128)(2,1)S(1)} %collective-permute-done.23.ret_refs_0_, bf16[8,4096]{1,0:T(8,128)(2,1)S(1)} %collective-permute-done.24.ret_refs_1_, bf16[8,4096]{1,0:T(8,128)(2,1)S(1)} %collective-permute-done.25.ret_refs_2_, ...), custom_call_target="tpu_custom_call" | custom-call | bytes 1000000 | tf_op jit(solution)/shard_map/pallas_call | solution.py:351
  (28 shorter events, 0.1 us)
Async XLA Ops:
  0.6 20.4 %copy-start.2 = (bf16[1,192,8192]{2,1,0:T(8,128)(2,1)S(1)}, bf16[1,192,8192]{2,1,0:T(8,128)(2,1)}, u32[]{:S(2)}) copy-start(bf16[1,192,8192]{2,1,0:T(8,128)(2,1)} %down_ref.2) | copy-start | bytes 9437188
  2.8 18.2 %copy-start.6 = (bf16[8,4096]{1,0:T(8,128)(2,1)S(1)}, bf16[8,4096]{1,0:T(8,128)(2,1)}, u32[]{:S(2)}) copy-start(bf16[8,4096]{1,0:T(8,128)(2,1)} %get-tuple-element.72.ret_refs_7_) | copy-start | bytes 196612
  2.9 11.9 %collective-permute-start = (bf16[8,4096]{1,0:T(8,128)(2,1)}, bf16[8,4096]{1,0:T(8,128)(2,1)S(1)}, u32[]{:S(2)}, u32[]{:S(2)}) collective-permute-start(bf16[8,4096]{1,0:T(8,128)(2,1)} %get-tuple-element.52), channel_id=1, source_target_pairs={{0,14},{2,12},{4,10},{6,8},{8,6},{10,4},{12,2},{14,0},{1,15},{3,13... | collective-permute-start | bytes 196616 | tf_op jit(solution)/shard_map/ppermute | solution.py:249
  8.9 6.9 %collective-permute-start.1 = (bf16[8,4096]{1,0:T(8,128)(2,1)}, bf16[8,4096]{1,0:T(8,128)(2,1)S(1)}, u32[]{:S(2)}, u32[]{:S(2)}) collective-permute-start(bf16[8,4096]{1,0:T(8,128)(2,1)} %get-tuple-element.53), channel_id=1, source_target_pairs={{0,4},{2,6},{4,0},{6,2},{8,12},{10,14},{12,8},{14,10},{1,5},{3,7},... | collective-permute-start | bytes 196616 | tf_op jit(solution)/shard_map/ppermute | solution.py:249
  8.9 10.4 %collective-permute-start.2 = (bf16[8,4096]{1,0:T(8,128)(2,1)}, bf16[8,4096]{1,0:T(8,128)(2,1)S(1)}, u32[]{:S(2)}, u32[]{:S(2)}) collective-permute-start(bf16[8,4096]{1,0:T(8,128)(2,1)} %get-tuple-element.54), channel_id=1, source_target_pairs={{0,10},{2,8},{4,14},{6,12},{8,2},{10,0},{12,6},{14,4},{1,11},{3,9}... | collective-permute-start | bytes 196616 | tf_op jit(solution)/shard_map/ppermute | solution.py:249
  9.6 9.8 %collective-permute-start.3 = (bf16[8,4096]{1,0:T(8,128)(2,1)}, bf16[8,4096]{1,0:T(8,128)(2,1)S(1)}, u32[]{:S(2)}, u32[]{:S(2)}) collective-permute-start(bf16[8,4096]{1,0:T(8,128)(2,1)} %get-tuple-element.55), channel_id=1, source_target_pairs={{0,8},{2,10},{4,12},{6,14},{8,0},{10,2},{12,4},{14,6},{1,9},{3,11}... | collective-permute-start | bytes 196616 | tf_op jit(solution)/shard_map/ppermute | solution.py:249
  11.8 7.5 %collective-permute-start.4 = (bf16[8,4096]{1,0:T(8,128)(2,1)}, bf16[8,4096]{1,0:T(8,128)(2,1)S(1)}, u32[]{:S(2)}, u32[]{:S(2)}) collective-permute-start(bf16[8,4096]{1,0:T(8,128)(2,1)} %get-tuple-element.56), channel_id=1, source_target_pairs={{0,6},{2,4},{4,2},{6,0},{8,14},{10,12},{12,10},{14,8},{1,7},{3,5},... | collective-permute-start | bytes 196616 | tf_op jit(solution)/shard_map/ppermute | solution.py:249
  14.8 6.3 %collective-permute-start.5 = (bf16[8,4096]{1,0:T(8,128)(2,1)}, bf16[8,4096]{1,0:T(8,128)(2,1)S(1)}, u32[]{:S(2)}, u32[]{:S(2)}) collective-permute-start(bf16[8,4096]{1,0:T(8,128)(2,1)} %get-tuple-element.57), channel_id=1, source_target_pairs={{0,12},{2,14},{4,8},{6,10},{8,4},{10,6},{12,0},{14,2},{1,13},{3,15... | collective-permute-start | bytes 196616 | tf_op jit(solution)/shard_map/ppermute | solution.py:249
  15.9 5.2 %collective-permute-start.6 = (bf16[8,4096]{1,0:T(8,128)(2,1)}, bf16[8,4096]{1,0:T(8,128)(2,1)S(1)}, u32[]{:S(2)}, u32[]{:S(2)}) collective-permute-start(bf16[8,4096]{1,0:T(8,128)(2,1)} %get-tuple-element.58), channel_id=1, source_target_pairs={{0,2},{2,0},{4,6},{6,4},{8,10},{10,8},{12,14},{14,12},{1,3},{3,1},... | collective-permute-start | bytes 196616 | tf_op jit(solution)/shard_map/ppermute | solution.py:249
  17.4 0.7 copy-start.11
  18.0 5.0 %copy-start.9 = (bf16[1,64,4096]{2,1,0:T(8,128)(2,1)S(1)}, bf16[1,64,4096]{2,1,0:T(8,128)(2,1)}, u32[]{:S(2)}) copy-start(bf16[1,64,4096]{2,1,0:T(8,128)(2,1)} %uq_ref.1) | copy-start | bytes 1572868
  18.0 5.0 %copy-start.10 = (bf16[1,2,64,512]{3,2,1,0:T(8,128)(2,1)S(1)}, bf16[1,2,64,512]{3,2,1,0:T(8,128)(2,1)}, u32[]{:S(2)}) copy-start(bf16[1,2,64,512]{3,2,1,0:T(8,128)(2,1)} %ukv_ref.1) | copy-start | bytes 393220
  21.1 18.6 %copy-start = (bf16[32,4,96,128]{3,2,1,0:T(8,128)(2,1)S(1)}, bf16[32,4,96,128]{3,2,1,0:T(8,128)(2,1)}, u32[]{:S(2)}) copy-start(bf16[32,4,96,128]{3,2,1,0:T(8,128)(2,1)} %k_ref.1) | copy-start | bytes 9437188
  21.1 18.6 %copy-start.1 = (bf16[32,4,96,128]{3,2,1,0:T(8,128)(2,1)S(1)}, bf16[32,4,96,128]{3,2,1,0:T(8,128)(2,1)}, u32[]{:S(2)}) copy-start(bf16[32,4,96,128]{3,2,1,0:T(8,128)(2,1)} %v_ref.1) | copy-start | bytes 9437188
  21.1 18.6 %copy-start.5 = (bf16[32,4096]{1,0:T(8,128)(2,1)S(1)}, bf16[32,4096]{1,0:T(8,128)(2,1)}, u32[]{:S(2)}) copy-start(bf16[32,4096]{1,0:T(8,128)(2,1)} %pq_ref.1) | copy-start | bytes 786436
  21.1 18.6 %copy-start.7 = (bf16[32,512]{1,0:T(8,128)(2,1)S(1)}, bf16[32,512]{1,0:T(8,128)(2,1)}, u32[]{:S(2)}) copy-start(bf16[32,512]{1,0:T(8,128)(2,1)} %pk_ref.1) | copy-start | bytes 98308
  21.1 18.6 %copy-start.8 = (bf16[32,512]{1,0:T(8,128)(2,1)S(1)}, bf16[32,512]{1,0:T(8,128)(2,1)}, u32[]{:S(2)}) copy-start(bf16[32,512]{1,0:T(8,128)(2,1)} %pv_ref.1) | copy-start | bytes 98308
  21.7 1.3 %collective-permute-start.7 = (f32[64,192]{1,0:T(8,128)S(1)}, f32[64,192]{1,0:T(8,128)S(1)}, u32[]{:S(2)}, u32[]{:S(2)}) collective-permute-start(f32[64,192]{1,0:T(8,128)S(1)} %shard_map.151.mine_ref), channel_id=1, source_target_pairs={{0,1},{1,0},{2,3},{3,2},{4,5},{5,4},{6,7},{7,6},{8,9},{9,8},{10,11... | collective-permute-start | bytes 147464 | tf_op jit(solution)/shard_map/ppermute | solution.py:256
  23.4 8.1 %collective-permute-start.8 = (bf16[8,5120]{1,0:T(8,128)(2,1)S(1)}, bf16[8,5120]{1,0:T(8,128)(2,1)S(1)}, u32[]{:S(2)}, u32[]{:S(2)}) collective-permute-start(bf16[8,5120]{1,0:T(8,128)(2,1)S(1)} %get-tuple-element.73), channel_id=1, source_target_pairs={{0,14},{2,12},{4,10},{6,8},{8,6},{10,4},{12,2},{14,0},{1,15},{3,13... | collective-permute-start | bytes 245768 | tf_op jit(solution)/shard_map/ppermute | solution.py:249
  25.6 8.0 %collective-permute-start.9 = (bf16[8,5120]{1,0:T(8,128)(2,1)S(1)}, bf16[8,5120]{1,0:T(8,128)(2,1)S(1)}, u32[]{:S(2)}, u32[]{:S(2)}) collective-permute-start(bf16[8,5120]{1,0:T(8,128)(2,1)S(1)} %get-tuple-element.74), channel_id=1, source_target_pairs={{0,4},{2,6},{4,0},{6,2},{8,12},{10,14},{12,8},{14,10},{1,5},{3,7},... | collective-permute-start | bytes 245768 | tf_op jit(solution)/shard_map/ppermute | solution.py:249
  25.6 10.6 %collective-permute-start.10 = (bf16[8,5120]{1,0:T(8,128)(2,1)S(1)}, bf16[8,5120]{1,0:T(8,128)(2,1)S(1)}, u32[]{:S(2)}, u32[]{:S(2)}) collective-permute-start(bf16[8,5120]{1,0:T(8,128)(2,1)S(1)} %get-tuple-element.75), channel_id=1, source_target_pairs={{0,10},{2,8},{4,14},{6,12},{8,2},{10,0},{12,6},{14,4},{1,11},{3,9}... | collective-permute-start | bytes 245768 | tf_op jit(solution)/shard_map/ppermute | solution.py:249
  28.7 10.9 %collective-permute-start.11 = (bf16[8,5120]{1,0:T(8,128)(2,1)S(1)}, bf16[8,5120]{1,0:T(8,128)(2,1)S(1)}, u32[]{:S(2)}, u32[]{:S(2)}) collective-permute-start(bf16[8,5120]{1,0:T(8,128)(2,1)S(1)} %get-tuple-element.76), channel_id=1, source_target_pairs={{0,8},{2,10},{4,12},{6,14},{8,0},{10,2},{12,4},{14,6},{1,9},{3,11}... | collective-permute-start | bytes 245768 | tf_op jit(solution)/shard_map/ppermute | solution.py:249
  29.3 10.3 %collective-permute-start.12 = (bf16[8,5120]{1,0:T(8,128)(2,1)S(1)}, bf16[8,5120]{1,0:T(8,128)(2,1)S(1)}, u32[]{:S(2)}, u32[]{:S(2)}) collective-permute-start(bf16[8,5120]{1,0:T(8,128)(2,1)S(1)} %get-tuple-element.77), channel_id=1, source_target_pairs={{0,6},{2,4},{4,2},{6,0},{8,14},{10,12},{12,10},{14,8},{1,7},{3,5},... | collective-permute-start | bytes 245768 | tf_op jit(solution)/shard_map/ppermute | solution.py:249
  31.5 8.1 %collective-permute-start.13 = (bf16[8,5120]{1,0:T(8,128)(2,1)S(1)}, bf16[8,5120]{1,0:T(8,128)(2,1)S(1)}, u32[]{:S(2)}, u32[]{:S(2)}) collective-permute-start(bf16[8,5120]{1,0:T(8,128)(2,1)S(1)} %get-tuple-element.78), channel_id=1, source_target_pairs={{0,12},{2,14},{4,8},{6,10},{8,4},{10,6},{12,0},{14,2},{1,13},{3,15... | collective-permute-start | bytes 245768 | tf_op jit(solution)/shard_map/ppermute | solution.py:249
  33.6 6.1 %collective-permute-start.14 = (bf16[8,5120]{1,0:T(8,128)(2,1)S(1)}, bf16[8,5120]{1,0:T(8,128)(2,1)S(1)}, u32[]{:S(2)}, u32[]{:S(2)}) collective-permute-start(bf16[8,5120]{1,0:T(8,128)(2,1)S(1)} %get-tuple-element.79), channel_id=1, source_target_pairs={{0,2},{2,0},{4,6},{6,4},{8,10},{10,8},{12,14},{14,12},{1,3},{3,1},... | collective-permute-start | bytes 245768 | tf_op jit(solution)/shard_map/ppermute | solution.py:249
  39.7 17.2 %copy-start.4 = (bf16[1,64,4096]{2,1,0:T(8,128)(2,1)S(1)}, bf16[1,64,4096]{2,1,0:T(8,128)(2,1)}, u32[]{:S(2)}) copy-start(bf16[1,64,4096]{2,1,0:T(8,128)(2,1)} %down_ref.3) | copy-start | bytes 1572868
  39.7 18.8 %copy-start.3 = (bf16[1,64,4096]{2,1,0:T(8,128)(2,1)S(1)}, bf16[1,64,4096]{2,1,0:T(8,128)(2,1)}, u32[]{:S(2)}) copy-start(bf16[1,64,4096]{2,1,0:T(8,128)(2,1)} %uo_ref.1) | copy-start | bytes 1572868
  42.5 8.2 %collective-permute-start.15 = (bf16[8,4096]{1,0:T(8,128)(2,1)S(1)}, bf16[8,4096]{1,0:T(8,128)(2,1)S(1)}, u32[]{:S(2)}, u32[]{:S(2)}) collective-permute-start(bf16[8,4096]{1,0:T(8,128)(2,1)S(1)} %get-tuple-element.86), channel_id=1, source_target_pairs={{0,14},{2,12},{4,10},{6,8},{8,6},{10,4},{12,2},{14,0},{1,15},{3,13... | collective-permute-start | bytes 196616 | tf_op jit(solution)/shard_map/ppermute | solution.py:249
  44.9 7.7 %collective-permute-start.16 = (bf16[8,4096]{1,0:T(8,128)(2,1)S(1)}, bf16[8,4096]{1,0:T(8,128)(2,1)S(1)}, u32[]{:S(2)}, u32[]{:S(2)}) collective-permute-start(bf16[8,4096]{1,0:T(8,128)(2,1)S(1)} %get-tuple-element.87), channel_id=1, source_target_pairs={{0,4},{2,6},{4,0},{6,2},{8,12},{10,14},{12,8},{14,10},{1,5},{3,7},... | collective-permute-start | bytes 196616 | tf_op jit(solution)/shard_map/ppermute | solution.py:249
  45.9 9.3 %collective-permute-start.17 = (bf16[8,4096]{1,0:T(8,128)(2,1)S(1)}, bf16[8,4096]{1,0:T(8,128)(2,1)S(1)}, u32[]{:S(2)}, u32[]{:S(2)}) collective-permute-start(bf16[8,4096]{1,0:T(8,128)(2,1)S(1)} %get-tuple-element.88), channel_id=1, source_target_pairs={{0,10},{2,8},{4,14},{6,12},{8,2},{10,0},{12,6},{14,4},{1,11},{3,9}... | collective-permute-start | bytes 196616 | tf_op jit(solution)/shard_map/ppermute | solution.py:249
  47.8 8.3 %collective-permute-start.18 = (bf16[8,4096]{1,0:T(8,128)(2,1)S(1)}, bf16[8,4096]{1,0:T(8,128)(2,1)S(1)}, u32[]{:S(2)}, u32[]{:S(2)}) collective-permute-start(bf16[8,4096]{1,0:T(8,128)(2,1)S(1)} %get-tuple-element.89), channel_id=1, source_target_pairs={{0,8},{2,10},{4,12},{6,14},{8,0},{10,2},{12,4},{14,6},{1,9},{3,11}... | collective-permute-start | bytes 196616 | tf_op jit(solution)/shard_map/ppermute | solution.py:249
  49.0 7.1 %collective-permute-start.19 = (bf16[8,4096]{1,0:T(8,128)(2,1)S(1)}, bf16[8,4096]{1,0:T(8,128)(2,1)S(1)}, u32[]{:S(2)}, u32[]{:S(2)}) collective-permute-start(bf16[8,4096]{1,0:T(8,128)(2,1)S(1)} %get-tuple-element.90), channel_id=1, source_target_pairs={{0,6},{2,4},{4,2},{6,0},{8,14},{10,12},{12,10},{14,8},{1,7},{3,5},... | collective-permute-start | bytes 196616 | tf_op jit(solution)/shard_map/ppermute | solution.py:249
  50.7 6.2 %collective-permute-start.20 = (bf16[8,4096]{1,0:T(8,128)(2,1)S(1)}, bf16[8,4096]{1,0:T(8,128)(2,1)S(1)}, u32[]{:S(2)}, u32[]{:S(2)}) collective-permute-start(bf16[8,4096]{1,0:T(8,128)(2,1)S(1)} %get-tuple-element.91), channel_id=1, source_target_pairs={{0,12},{2,14},{4,8},{6,10},{8,4},{10,6},{12,0},{14,2},{1,13},{3,15... | collective-permute-start | bytes 196616 | tf_op jit(solution)/shard_map/ppermute | solution.py:249
  52.6 4.3 %collective-permute-start.21 = (bf16[8,4096]{1,0:T(8,128)(2,1)S(1)}, bf16[8,4096]{1,0:T(8,128)(2,1)S(1)}, u32[]{:S(2)}, u32[]{:S(2)}) collective-permute-start(bf16[8,4096]{1,0:T(8,128)(2,1)S(1)} %get-tuple-element.92), channel_id=1, source_target_pairs={{0,2},{2,0},{4,6},{6,4},{8,10},{10,8},{12,14},{14,12},{1,3},{3,1},... | collective-permute-start | bytes 196616 | tf_op jit(solution)/shard_map/ppermute | solution.py:249
  57.2 1.3 %collective-permute-start.22 = (f32[64,64]{1,0:T(8,128)S(1)}, f32[64,64]{1,0:T(8,128)S(1)}, u32[]{:S(2)}, u32[]{:S(2)}) collective-permute-start(f32[64,64]{1,0:T(8,128)S(1)} %shard_map.154.mine_ref), channel_id=1, source_target_pairs={{0,1},{1,0},{2,3},{3,2},{4,5},{5,4},{6,7},{7,6},{8,9},{9,8},{10,11... | collective-permute-start | bytes 49160 | tf_op jit(solution)/shard_map/ppermute | solution.py:256
  58.8 8.3 %collective-permute-start.23 = (bf16[8,4096]{1,0:T(8,128)(2,1)S(1)}, bf16[8,4096]{1,0:T(8,128)(2,1)S(1)}, u32[]{:S(2)}, u32[]{:S(2)}) collective-permute-start(bf16[8,4096]{1,0:T(8,128)(2,1)S(1)} %get-tuple-element.94), channel_id=1, source_target_pairs={{0,14},{2,12},{4,10},{6,8},{8,6},{10,4},{12,2},{14,0},{1,15},{3,13... | collective-permute-start | bytes 196616 | tf_op jit(solution)/shard_map/ppermute | solution.py:249
  61.2 7.8 %collective-permute-start.24 = (bf16[8,4096]{1,0:T(8,128)(2,1)S(1)}, bf16[8,4096]{1,0:T(8,128)(2,1)S(1)}, u32[]{:S(2)}, u32[]{:S(2)}) collective-permute-start(bf16[8,4096]{1,0:T(8,128)(2,1)S(1)} %get-tuple-element.95), channel_id=1, source_target_pairs={{0,4},{2,6},{4,0},{6,2},{8,12},{10,14},{12,8},{14,10},{1,5},{3,7},... | collective-permute-start | bytes 196616 | tf_op jit(solution)/shard_map/ppermute | solution.py:249
  61.4 9.3 %collective-permute-start.25 = (bf16[8,4096]{1,0:T(8,128)(2,1)S(1)}, bf16[8,4096]{1,0:T(8,128)(2,1)S(1)}, u32[]{:S(2)}, u32[]{:S(2)}) collective-permute-start(bf16[8,4096]{1,0:T(8,128)(2,1)S(1)} %get-tuple-element.96), channel_id=1, source_target_pairs={{0,10},{2,8},{4,14},{6,12},{8,2},{10,0},{12,6},{14,4},{1,11},{3,9}... | collective-permute-start | bytes 196616 | tf_op jit(solution)/shard_map/ppermute | solution.py:249
  64.1 9.2 %collective-permute-start.26 = (bf16[8,4096]{1,0:T(8,128)(2,1)S(1)}, bf16[8,4096]{1,0:T(8,128)(2,1)S(1)}, u32[]{:S(2)}, u32[]{:S(2)}) collective-permute-start(bf16[8,4096]{1,0:T(8,128)(2,1)S(1)} %get-tuple-element.97), channel_id=1, source_target_pairs={{0,8},{2,10},{4,12},{6,14},{8,0},{10,2},{12,4},{14,6},{1,9},{3,11}... | collective-permute-start | bytes 196616 | tf_op jit(solution)/shard_map/ppermute | solution.py:249
  65.1 8.2 %collective-permute-start.27 = (bf16[8,4096]{1,0:T(8,128)(2,1)S(1)}, bf16[8,4096]{1,0:T(8,128)(2,1)S(1)}, u32[]{:S(2)}, u32[]{:S(2)}) collective-permute-start(bf16[8,4096]{1,0:T(8,128)(2,1)S(1)} %get-tuple-element.98), channel_id=1, source_target_pairs={{0,6},{2,4},{4,2},{6,0},{8,14},{10,12},{12,10},{14,8},{1,7},{3,5},... | collective-permute-start | bytes 196616 | tf_op jit(solution)/shard_map/ppermute | solution.py:249
  67.1 6.3 %collective-permute-start.28 = (bf16[8,4096]{1,0:T(8,128)(2,1)S(1)}, bf16[8,4096]{1,0:T(8,128)(2,1)S(1)}, u32[]{:S(2)}, u32[]{:S(2)}) collective-permute-start(bf16[8,4096]{1,0:T(8,128)(2,1)S(1)} %get-tuple-element.99), channel_id=1, source_target_pairs={{0,12},{2,14},{4,8},{6,10},{8,4},{10,6},{12,0},{14,2},{1,13},{3,15... | collective-permute-start | bytes 196616 | tf_op jit(solution)/shard_map/ppermute | solution.py:249
  69.0 4.3 %collective-permute-start.29 = (bf16[8,4096]{1,0:T(8,128)(2,1)S(1)}, bf16[8,4096]{1,0:T(8,128)(2,1)S(1)}, u32[]{:S(2)}, u32[]{:S(2)}) collective-permute-start(bf16[8,4096]{1,0:T(8,128)(2,1)S(1)} %get-tuple-element.100), channel_id=1, source_target_pairs={{0,2},{2,0},{4,6},{6,4},{8,10},{10,8},{12,14},{14,12},{1,3},{3,1},... | collective-permute-start | bytes 196616 | tf_op jit(solution)/shard_map/ppermute | solution.py:249
